TPU v7x, 32 devices: a whole 2x2x4 slice. The times are simulated.
32 devices in a mesh: dp: 8 (over z, y), fsdp: 4 (over x, core).
Axes of the slice: x: 2, y: 2, z: 4, core: 2. Of those that a mesh axis runs over, the one named last changes fastest.
Arguments:
- tokens: bfloat16 [4, 32, 1024, 512], P('fsdp', 'dp'), may hold values from -6 to 6
- segment_ids: int32 [4, 32, 1024], P('fsdp', 'dp'), may hold values from 0 to 3, never falling along the last dimension, each value on 1 to 512 neighbouring positions
- pad_tokens: int32 [4, 32], P('fsdp'), may hold values from 0 to 256, as said below
- cotangent: bfloat16 [4, 32, 1024, 512], P('fsdp', 'dp'), may hold values from -6 to 6
- project_in: bfloat16 [512, 1536], P(('dp', 'fsdp')), may hold values from -0.25 to 0.25
- project_out: bfloat16 [512, 512], P(('dp', 'fsdp')), may hold values from -2 to 2
- router_weight: bfloat16 [512, 4], P(('dp', 'fsdp')), may hold values from -0.125 to 0.125
- expert_in: bfloat16 [4, 512, 2048], P('fsdp', None, 'dp'), may hold values from -0.5 to 0.5
- expert_out: bfloat16 [4, 2048, 512], P('fsdp', 'dp'), may hold values from -0.125 to 0.125
- first_gain: bfloat16 [512], P(('dp', 'fsdp')), may hold values from 0.099609375 to 1.8984375
- first_bias: bfloat16 [512], P(('dp', 'fsdp')), may hold values from -0.5 to 0.5
- second_gain: bfloat16 [512], P(('dp', 'fsdp')), may hold values from 0.099609375 to 1.8984375
- second_bias: bfloat16 [512], P(('dp', 'fsdp')), may hold values from -0.5 to 0.5
Outputs:
- layer_output: bfloat16 [4, 32, 1024, 512], P('fsdp', 'dp')
- tokens_grad: float32 [4, 32, 1024, 512], P('fsdp', 'dp')
- project_in_grad: float32 [512, 1536], P(('dp', 'fsdp'))
- project_out_grad: float32 [512, 512], P(('dp', 'fsdp'))
- router_grad: float32 [512, 4], P(('dp', 'fsdp'))
- expert_in_grad: float32 [4, 512, 2048], P('fsdp', None, 'dp')
- expert_out_grad: float32 [4, 2048, 512], P('fsdp', 'dp')
- first_gain_grad: float32 [512], P(('dp', 'fsdp'))
- first_bias_grad: float32 [512], P(('dp', 'fsdp'))
- second_gain_grad: float32 [512], P(('dp', 'fsdp'))
- second_bias_grad: float32 [512], P(('dp', 'fsdp'))
Inputs may be any that keep to these rules, and one draw needn't show every extreme that they name: `pad_tokens`: in each of the 4 blocks some row of the group has no padding.
All inputs are finite; a program needn't handle non-finite values.
Results may differ from a plain program's by a relative error of at most 0.018.
Values may be sent and summed in bfloat16 or wider, within the bound.
No kernel may reach another device: no remote copies, remote signals or barrier semaphores. Data moves between devices by JAX's collectives and lax.ppermute only.
A program may use at most 256 MiB of HBM per device.

v0:
```python
import math

import jax
import jax.numpy as jnp
from jax import lax
from jax.sharding import PartitionSpec as P

HEAD_DIM = 64


NEGATIVE = -1e30


def layer_norm(values, gain_vec, shift_vec):
    centred = values - jnp.mean(values, axis=-1, keepdims=True)
    spread = jnp.mean(centred * centred, axis=-1, keepdims=True)
    return centred * lax.rsqrt(spread + 1e-05) * gain_vec + shift_vec


def activate(values):
    return jax.nn.gelu(values, approximate=True)


def allowed_block(seg_row, valid_row, begin_at, block_rows):
    end_at = begin_at + block_rows
    places = jnp.arange(end_at)
    rows_here = places[begin_at:end_at]
    same_doc = seg_row[begin_at:end_at][:, None] == seg_row[None, :end_at]
    earlier = places[None, :] <= rows_here[:, None]
    return same_doc & earlier & valid_row[None, :end_at] | (places[None, :] == rows_here[:, None])


def block_scores(query_blk, key_heads, allowed):
    scores = jnp.einsum(
        "qhd,khd->hqk", query_blk, key_heads, preferred_element_type=jnp.float32
    ) * (1.0 / math.sqrt(query_blk.shape[2]))
    return jnp.where(allowed[None], scores, NEGATIVE)


def attend_forward(packed):
    query_row, key_row, value_row, seg_row, valid_row = packed
    length, row_width = query_row.shape
    head_count = row_width // HEAD_DIM
    key_heads = key_row.reshape(length, head_count, HEAD_DIM)
    value_heads = value_row.reshape(length, head_count, HEAD_DIM)
    block_rows = min(512, length)
    outputs = []
    totals = []
    for begin_at in range(0, length, block_rows):
        end_at = begin_at + block_rows
        query_blk = query_row[begin_at:end_at].reshape(block_rows, head_count, HEAD_DIM)
        scores = block_scores(
            query_blk, key_heads[:end_at], allowed_block(seg_row, valid_row, begin_at, block_rows)
        )
        highest = jnp.max(scores, axis=-1, keepdims=True)
        raised = jnp.exp(scores - highest)
        row_total = jnp.sum(raised, axis=-1, keepdims=True)
        attn_prob = (raised / row_total).astype(jnp.bfloat16)
        outputs.append(
            jnp.einsum(
                "hqk,khd->qhd", attn_prob, value_heads[:end_at], preferred_element_type=jnp.float32
            ).reshape(block_rows, row_width)
        )
        totals.append((highest + jnp.log(row_total))[..., 0])
    return (jnp.concatenate(outputs, 0), jnp.concatenate(totals, 1))


def attend_backward(packed):
    query_row, key_row, value_row, seg_row, valid_row, log_total, grad_row = packed
    length, row_width = query_row.shape
    head_count = row_width // HEAD_DIM
    scale = 1.0 / math.sqrt(HEAD_DIM)
    key_heads = key_row.reshape(length, head_count, HEAD_DIM)
    value_heads = value_row.reshape(length, head_count, HEAD_DIM)
    block_rows = min(512, length)
    grad_keys = jnp.zeros((length, head_count, HEAD_DIM), jnp.float32)
    grad_values = jnp.zeros((length, head_count, HEAD_DIM), jnp.float32)
    grad_query = []
    for begin_at in range(0, length, block_rows):
        end_at = begin_at + block_rows
        query_blk = query_row[begin_at:end_at].reshape(block_rows, head_count, HEAD_DIM)
        keys_here = key_heads[:end_at]
        scores = block_scores(
            query_blk, keys_here, allowed_block(seg_row, valid_row, begin_at, block_rows)
        )
        attn_prob = jnp.exp(scores - log_total[:, begin_at:end_at, None])
        grad_block = grad_row[begin_at:end_at].reshape(block_rows, head_count, HEAD_DIM)
        grad_prob = jnp.einsum(
            "qhd,khd->hqk", grad_block, value_heads[:end_at], preferred_element_type=jnp.float32
        )
        grad_values = grad_values.at[:end_at].add(
            jnp.einsum(
                "hqk,qhd->khd",
                attn_prob.astype(jnp.bfloat16),
                grad_block,
                preferred_element_type=jnp.float32,
            )
        )
        inner_sum = jnp.sum(attn_prob * grad_prob, axis=-1, keepdims=True)
        grad_scores = (attn_prob * (grad_prob - inner_sum)).astype(jnp.bfloat16)
        grad_query.append(
            (
                jnp.einsum(
                    "hqk,khd->qhd", grad_scores, keys_here, preferred_element_type=jnp.float32
                )
                * scale
            ).reshape(block_rows, row_width)
        )
        grad_keys = grad_keys.at[:end_at].add(
            jnp.einsum("hqk,qhd->khd", grad_scores, query_blk, preferred_element_type=jnp.float32)
            * scale
        )
    return (
        jnp.concatenate(grad_query, 0).astype(jnp.bfloat16),
        grad_keys.reshape(length, row_width).astype(jnp.bfloat16),
        grad_values.reshape(length, row_width).astype(jnp.bfloat16),
    )


def run_experts(pooled, grad_result, weight_in, weight_out):
    pre_act = jnp.einsum("ned,edf->nef", pooled, weight_in, preferred_element_type=jnp.float32)
    act_value, pull_act = jax.vjp(activate, pre_act)
    act_low = act_value.astype(jnp.bfloat16)
    result = jnp.einsum(
        "nef,efd->ned", act_low, weight_out, preferred_element_type=jnp.float32
    ).astype(jnp.bfloat16)
    grad_act = jnp.einsum(
        "ned,efd->nef", grad_result, weight_out, preferred_element_type=jnp.float32
    )
    grad_pre = pull_act(grad_act)[0].astype(jnp.bfloat16)
    grad_in = jnp.einsum("ned,nef->edf", pooled, grad_pre, preferred_element_type=jnp.float32)
    grad_out = jnp.einsum("nef,ned->efd", act_low, grad_result, preferred_element_type=jnp.float32)
    grad_pooled = jnp.einsum(
        "nef,edf->ned", grad_pre, weight_in, preferred_element_type=jnp.float32
    ).astype(jnp.bfloat16)
    return (result, grad_pooled, grad_in, grad_out)


def per_device(
    tokens,
    segment_ids,
    pad_tokens,
    cotangent,
    project_in,
    project_out,
    router_weight,
    expert_in,
    expert_out,
    first_gain,
    first_bias,
    second_gain,
    second_bias,
):
    full_in, full_out, full_router, gain_one, shift_one, gain_two, shift_two = (
        lax.all_gather(project_in, ("dp", "fsdp"), axis=0, tiled=True),
        lax.all_gather(project_out, ("dp", "fsdp"), axis=0, tiled=True),
        lax.all_gather(router_weight, ("dp", "fsdp"), axis=0, tiled=True),
        lax.all_gather(first_gain, ("dp", "fsdp"), axis=0, tiled=True),
        lax.all_gather(first_bias, ("dp", "fsdp"), axis=0, tiled=True),
        lax.all_gather(second_gain, ("dp", "fsdp"), axis=0, tiled=True),
        lax.all_gather(second_bias, ("dp", "fsdp"), axis=0, tiled=True),
    )
    local_in, local_out = (
        lax.all_gather(expert_in, "dp", axis=2, tiled=True),
        lax.all_gather(expert_out, "dp", axis=1, tiled=True),
    )
    blocks_here, rows_here, length, model_width = tokens.shape
    group_size = pad_tokens.shape[1]
    data_index = lax.axis_index("dp")
    gain_one = gain_one.astype(jnp.float32)
    shift_one = shift_one.astype(jnp.float32)
    gain_two = gain_two.astype(jnp.float32)
    shift_two = shift_two.astype(jnp.float32)
    own_pads = lax.dynamic_slice_in_dim(pad_tokens, data_index * rows_here, rows_here, 1)
    places = jnp.arange(length)
    valid_rows = places[None, None, :] < (length - own_pads)[..., None]
    inputs = tokens.astype(jnp.float32)
    normed = layer_norm(inputs, gain_one, shift_one).astype(jnp.bfloat16)
    flat_count = blocks_here * rows_here
    joined = jnp.dot(
        normed.reshape(-1, model_width), full_in, preferred_element_type=jnp.float32
    ).astype(jnp.bfloat16)
    joined = joined.reshape(flat_count, length, 3 * model_width)
    query_all = joined[..., :model_width]
    key_all = joined[..., model_width : 2 * model_width]
    value_all = joined[..., 2 * model_width :]
    seg_flat = segment_ids.reshape(flat_count, length)
    valid_flat = valid_rows.reshape(flat_count, length)
    attended, log_totals = lax.map(
        attend_forward, (query_all, key_all, value_all, seg_flat, valid_flat)
    )
    attended = attended.astype(jnp.bfloat16)
    branch = jnp.dot(
        attended.reshape(-1, model_width), full_out, preferred_element_type=jnp.float32
    ).reshape(tokens.shape)
    hidden = inputs + branch
    mixed_in = layer_norm(hidden, gain_two, shift_two).astype(jnp.bfloat16)
    grouped, grouped_grad = (
        lax.all_to_all(mixed_in, "dp", split_axis=2, concat_axis=1, tiled=True),
        lax.all_to_all(cotangent, "dp", split_axis=2, concat_axis=1, tiled=True),
    )
    place_count = grouped.shape[2]
    global_place = data_index * place_count + jnp.arange(place_count)
    valid_group = global_place[None, None, :] < (length - pad_tokens)[..., None]
    logits = jnp.einsum("bgpd,de->bgpe", grouped, full_router, preferred_element_type=jnp.float32)
    keep_mask = valid_group[..., None]
    highest = jnp.max(jnp.where(keep_mask, logits, NEGATIVE), axis=1, keepdims=True)
    raised = jnp.exp(jnp.where(keep_mask, logits - highest, NEGATIVE))
    gate_values = raised / jnp.sum(raised, axis=1, keepdims=True)
    gate_low = gate_values.astype(jnp.bfloat16)
    expert_count = full_router.shape[1]
    pooled = jnp.einsum(
        "bgpe,bgpd->bped", gate_low, grouped, preferred_element_type=jnp.float32
    ).astype(jnp.bfloat16)
    grad_result = (
        group_size
        * jnp.einsum("bgpe,bgpd->bped", gate_low, grouped_grad, preferred_element_type=jnp.float32)
    ).astype(jnp.bfloat16)
    pooled = pooled.reshape(-1, expert_count, model_width)
    grad_result = grad_result.reshape(-1, expert_count, model_width)
    sent_pool, sent_grad = (
        lax.all_to_all(pooled, "fsdp", split_axis=1, concat_axis=0, tiled=True),
        lax.all_to_all(grad_result, "fsdp", split_axis=1, concat_axis=0, tiled=True),
    )
    result, grad_pooled, grad_in, grad_out = run_experts(sent_pool, sent_grad, local_in, local_out)
    result, grad_pooled = (
        lax.all_to_all(result, "fsdp", split_axis=0, concat_axis=1, tiled=True),
        lax.all_to_all(grad_pooled, "fsdp", split_axis=0, concat_axis=1, tiled=True),
    )
    grad_in, grad_out = (
        lax.psum_scatter(
            grad_in.astype(jnp.bfloat16), "dp", scatter_dimension=2, tiled=True
        ).astype(jnp.float32),
        lax.psum_scatter(
            grad_out.astype(jnp.bfloat16), "dp", scatter_dimension=1, tiled=True
        ).astype(jnp.float32),
    )
    result = result.reshape(blocks_here, place_count, expert_count, model_width)
    grad_pooled = grad_pooled.reshape(blocks_here, place_count, expert_count, model_width)
    spread = (
        group_size
        * jnp.einsum("bgpe,bped->bgpd", gate_low, result, preferred_element_type=jnp.float32)
    ).astype(jnp.bfloat16)
    grad_gates = group_size * jnp.einsum(
        "bgpd,bped->bgpe", grouped_grad, result, preferred_element_type=jnp.float32
    )
    grad_gates = grad_gates + jnp.einsum(
        "bped,bgpd->bgpe", grad_pooled, grouped, preferred_element_type=jnp.float32
    )
    grad_gates = lax.optimization_barrier(grad_gates.astype(jnp.bfloat16)).astype(jnp.float32)
    inner_sum = jnp.sum(gate_values * grad_gates, axis=1, keepdims=True)
    grad_logits = (gate_values * (grad_gates - inner_sum)).astype(jnp.bfloat16)
    grad_grouped = jnp.einsum(
        "bgpe,bped->bgpd", gate_low, grad_pooled, preferred_element_type=jnp.float32
    )
    grad_grouped = grad_grouped + jnp.einsum(
        "bgpe,de->bgpd", grad_logits, full_router, preferred_element_type=jnp.float32
    )
    grad_router = jnp.einsum(
        "bgpd,bgpe->de", grouped, grad_logits, preferred_element_type=jnp.float32
    )
    spread_rows, grad_mixed = (
        lax.all_to_all(spread, "dp", split_axis=1, concat_axis=2, tiled=True),
        lax.all_to_all(
            grad_grouped.astype(jnp.bfloat16), "dp", split_axis=1, concat_axis=2, tiled=True
        ),
    )
    layer_out = (hidden + spread_rows.astype(jnp.float32)).astype(jnp.bfloat16)
    _, pull_two = jax.vjp(layer_norm, hidden, gain_two, shift_two)
    grad_hidden_part, grad_gain_two, grad_shift_two = pull_two(grad_mixed.astype(jnp.float32))
    grad_hidden = cotangent.astype(jnp.float32) + grad_hidden_part
    grad_hidden_low = grad_hidden.astype(jnp.bfloat16).reshape(-1, model_width)
    grad_proj_out = jnp.einsum(
        "nd,ne->de",
        attended.reshape(-1, model_width),
        grad_hidden_low,
        preferred_element_type=jnp.float32,
    )
    grad_attended = jnp.einsum(
        "ne,de->nd", grad_hidden_low, full_out, preferred_element_type=jnp.float32
    ).astype(jnp.bfloat16)
    grad_attended = grad_attended.reshape(flat_count, length, model_width)
    grad_query, grad_keys, grad_values = lax.map(
        attend_backward,
        (query_all, key_all, value_all, seg_flat, valid_flat, log_totals, grad_attended),
    )
    grad_joined = jnp.concatenate((grad_query, grad_keys, grad_values), axis=-1).reshape(
        -1, 3 * model_width
    )
    grad_proj_in = jnp.einsum(
        "nd,ne->de",
        normed.reshape(-1, model_width),
        grad_joined,
        preferred_element_type=jnp.float32,
    )
    grad_normed = jnp.einsum(
        "ne,de->nd", grad_joined, full_in, preferred_element_type=jnp.float32
    ).reshape(tokens.shape)
    _, pull_one = jax.vjp(layer_norm, inputs, gain_one, shift_one)
    grad_inputs, grad_gain_one, grad_shift_one = pull_one(grad_normed)
    tokens_grad = grad_hidden + grad_inputs
    reduced = (
        lax.psum_scatter(grad_proj_in, ("dp", "fsdp"), scatter_dimension=0, tiled=True),
        lax.psum_scatter(grad_proj_out, ("dp", "fsdp"), scatter_dimension=0, tiled=True),
        lax.psum_scatter(grad_router, ("dp", "fsdp"), scatter_dimension=0, tiled=True),
        lax.psum_scatter(grad_gain_one, ("dp", "fsdp"), scatter_dimension=0, tiled=True),
        lax.psum_scatter(grad_shift_one, ("dp", "fsdp"), scatter_dimension=0, tiled=True),
        lax.psum_scatter(grad_gain_two, ("dp", "fsdp"), scatter_dimension=0, tiled=True),
        lax.psum_scatter(grad_shift_two, ("dp", "fsdp"), scatter_dimension=0, tiled=True),
    )
    return (
        layer_out,
        tokens_grad,
        reduced[0],
        reduced[1],
        reduced[2],
        grad_in,
        grad_out,
        reduced[3],
        reduced[4],
        reduced[5],
        reduced[6],
    )


def solution(mesh):
    in_specs = (
        P("fsdp", "dp", None, None),
        P("fsdp", "dp", None),
        P("fsdp", None),
        P("fsdp", "dp", None, None),
        P(("dp", "fsdp"), None),
        P(("dp", "fsdp"), None),
        P(("dp", "fsdp"), None),
        P("fsdp", None, "dp"),
        P("fsdp", "dp", None),
        P(("dp", "fsdp")),
        P(("dp", "fsdp")),
        P(("dp", "fsdp")),
        P(("dp", "fsdp")),
    )
    out_specs = (
        P("fsdp", "dp", None, None),
        P("fsdp", "dp", None, None),
        P(("dp", "fsdp"), None),
        P(("dp", "fsdp"), None),
        P(("dp", "fsdp"), None),
        P("fsdp", None, "dp"),
        P("fsdp", "dp", None),
        P(("dp", "fsdp")),
        P(("dp", "fsdp")),
        P(("dp", "fsdp")),
        P(("dp", "fsdp")),
    )
    return jax.shard_map(
        per_device, mesh=mesh, in_specs=in_specs, out_specs=out_specs, check_vma=False
    )
```

profile of v0, /device:TPU:0, one launch (start us, length us, event | category | flops | bytes accessed | tf_op | source)
XLA Modules:
  0.0 1494.5 jit_solution(6769413167146078132)
XLA Ops:
  12.2 42.1 %all-reduce.11 = (bf16[512]{0:T(512)(128)(2,1)S(1)}, bf16[512]{0:T(512)(128)(2,1)S(1)}, bf16[512]{0:T(512)(128)(2,1)S(1)}, bf16[512]{0:T(512)(128)(2,1)S(1)}) all-reduce(bf16[512]{0:T(512)(128)(2,1)S(1)} %dynamic-update-slice.13, bf16[512]{0:T(512)(128)(2,1)S(1)} %dynamic-update-slice.12, ...), channel_id=1, replica_groups=mesh['dp'=8,'fsdp'=4] {'dp','fsdp'}, use_global_device_ids=true, to_apply=%add.3 | all-reduce | flops 2048 | bytes 8192
  61.3 44.5 %all_gather.30 = bf16[512,512]{1,0:T(8,128)(2,1)} all-gather(bf16[16,512]{1,0:T(8,128)(2,1)S(1)} %copy-done.37), channel_id=1, replica_groups=mesh['dp'=8,'fsdp'=4] {'dp','fsdp'}, dimensions={0}, use_global_device_ids=true | all-gather | bytes 540672 | tf_op jit(solution)/shard_map/all_gather | solution.py:156
  108.9 8.9 convolution_convert_fusion
  141.4 110.9 %while.35 = (s32[]{:T(128)}, bf16[4,1024,512]{2,1,0:T(8,128)(2,1)}, f32[4,8,1024]{2,1,0:T(8,128)S(1)}, bf16[4,1024,512]{1,2,0:T(8,128)(2,1)}, s32[4,1024]{1,0:T(...) while((s32[]{:T(128)}, bf16[4,1024,512]{2,1,0:T(8,128)(2,1)}, ...), condition=%wide.region_7.8_spmd, body=%wide.region_2.7_spmd.sunk | while | flops 1692925952 | bytes 98933408 | solution.py:189
  280.7 86.6 %all-to-all-done = bf16[1,4,1024,512]{3,1,0,2:T(4,128)(2,1)} async-done(((bf16[1,4,1024,512]{3,1,0,2:T(4,128)(2,1)}), bf16[1,4,1024,512]{3,1,0,2:T(4,128)(2,1)}, u32[]{:S(2)}, u32[]{:S(2)}) %all-to-all-start) | async-done | bytes 4194336 | tf_op jit(solution)/shard_map/all_to_all | solution.py:199
  373.0 110.3 %all-gather = bf16[32,16,4]{1,2,0:T(4,128)(2,1)S(1)} all-gather(bf16[1,16,4]{1,2,0:T(4,128)(2,1)S(1)} %bitcast.484), channel_id=1, replica_groups=mesh['dp'=8,'fsdp'=4] {'dp','fsdp'}, dimensions={0}, use_global_device_ids=true | all-gather | bytes 4224 | tf_op jit(solution)/shard_map/all_gather | solution.py:157
  495.8 28.8 %all-to-all-start.1 = ((bf16[128,4,512]{2,0,1:T(8,128)(2,1)}), bf16[128,4,512]{2,0,1:T(8,128)(2,1)S(1)}, u32[]{:S(2)}, u32[]{:S(2)}) async-start(bf16[128,4,512]{2,0,1:T(8,128)(2,1)} %copy.126), calls=%async_computation.1 | async-start | bytes 1048576 | tf_op jit(solution)/shard_map/all_to_all | solution.py:222
  584.3 9.8 all-to-all-start.3
  620.6 68.3 %all-to-all-done.3 = bf16[1,32,128,512]{3,2,0,1:T(8,128)(2,1)} async-done(((bf16[1,32,128,512]{3,2,0,1:T(8,128)(2,1)}), bf16[1,32,128,512]{3,2,0,1:T(8,128)(2,1)}, u32[]{:S(2)}, u32[]{:S(2)}) %all-to-all-start.3) | async-done | bytes 4194336 | tf_op jit(solution)/shard_map/all_to_all | solution.py:263
  698.1 50.6 %reduce-scatter.16.cloned.1.call-done = f32[16,4]{1,0:T(8,128)} async-done(((f32[512,4]{1,0:T(8,128)}), f32[16,4]{1,0:T(8,128)}) %reduce-scatter.16.cloned.1.call-update) | async-done | bytes 272
  750.1 108.2 %reduce-scatter.14.cloned.1.call-done = bf16[1,256,512]{2,1,0:T(8,128)(2,1)} async-done(((bf16[1,2048,512]{2,1,0:T(8,128)(2,1)}), bf16[1,256,512]{2,1,0:T(8,128)(2,1)}) %reduce-scatter.14.cloned.1.call-update) | async-done | bytes 262160 | tf_op jit(solution)/shard_map/reduce_scatter | solution.py:234
  860.1 69.5 %reduce-scatter.12.cloned.1.call-done = bf16[1,512,256]{2,1,0:T(8,128)(2,1)} async-done(((bf16[1,512,2048]{2,1,0:T(8,128)(2,1)}), bf16[1,512,256]{2,1,0:T(8,128)(2,1)}) %reduce-scatter.12.cloned.1.call-update) | async-done | bytes 262160 | tf_op jit(solution)/shard_map/reduce_scatter | solution.py:231
  966.9 282.5 %while.36 = (s32[]{:T(128)}, bf16[4,1024,512]{2,1,0:T(8,128)(2,1)}, bf16[4,1024,512]{2,1,0:T(8,128)(2,1)}, bf16[4,1024,512]{2,1,0:T(8,128)(2,1)}, bf16[4,1024,51...) while((s32[]{:T(128)}, bf16[4,1024,512]{2,1,0:T(8,128)(2,1)}, ...), condition=%wide.region_18.19_spmd, body=%wide.region_15.18_spmd.sunk | while | flops 4106477568 | bytes 258841600 | solution.py:283
  996.5 11.4 multiply_reduce_fusion.6
  1008.0 8.7 fusion.290
  1067.0 11.4 multiply_reduce_fusion.6
  1137.5 11.4 multiply_reduce_fusion.6
  1208.0 11.4 multiply_reduce_fusion.6
  1219.4 8.7 fusion.290
  1268.8 9.7 fusion.141
  1288.5 39.7 %all-reduce.10 = (f32[512]{0:T(512)S(1)}, f32[512]{0:T(512)S(1)}, f32[512]{0:T(512)S(1)}, f32[512]{0:T(512)S(1)}) all-reduce(f32[512]{0:T(512)S(1)} %get-tuple-element.349, f32[512]{0:T(512)S(1)} %get-tuple-element.435, f32[512]{0:T(512)S(1)} %copy-done.39, ...), channel_id=7, replica_groups=mesh['dp'=8,'fsdp'=4] {'dp','fsdp'}, use_global_device_ids=true, to_apply=%region_27.28.clone | all-reduce | flops 2048 | bytes 16384
  1330.5 13.6 add_add_fusion.2
  1344.1 39.3 %reduce-scatter.10.cloned.1.call-done = f32[16,512]{1,0:T(8,128)} async-done(((f32[512,512]{1,0:T(8,128)}), f32[16,512]{1,0:T(8,128)}) %reduce-scatter.10.cloned.1.call-update) | async-done | bytes 32784 | tf_op jit(solution)/shard_map/reduce_scatter | solution.py:304
  1383.5 103.4 %reduce-scatter.8.cloned.1.call-done = f32[16,1536]{1,0:T(8,128)} async-done(((f32[512,1536]{1,0:T(8,128)}), f32[16,1536]{1,0:T(8,128)}) %reduce-scatter.8.cloned.1.call-update) | async-done | bytes 98320 | tf_op jit(solution)/shard_map/reduce_scatter | solution.py:303
  (513 shorter events, 579.3 us)
Async XLA Ops:
  8.0 100.9 %all-gather.5.cloned.1.call-start = ((), (), s32[]{:S(2)}) async-start(), calls=%async_computation.13 | async-start | bytes 1622016 | tf_op jit(solution)/shard_map/all_gather | solution.py:155
  54.3 51.5 %copy-start.34 = (f32[512]{0:T(512)}, f32[512]{0:T(512)S(1)}, u32[]{:S(2)}) copy-start(f32[512]{0:T(512)S(1)} %convert_element_type.254) | copy-start | bytes 6148
  59.6 46.2 %copy-start.22 = (f32[4,1024]{1,0:T(4,128)}, f32[4,1024]{1,0:T(4,128)S(1)}, u32[]{:S(2)}) copy-start(f32[4,1024]{1,0:T(4,128)S(1)} %broadcast_multiply_fusion.1) | copy-start | bytes 49156
  61.2 47.6 %copy-start.32 = (f32[4,1024]{1,0:T(4,128)}, f32[4,1024]{1,0:T(4,128)S(1)}, u32[]{:S(2)}) copy-start(f32[4,1024]{1,0:T(4,128)S(1)} %fusion.50) | copy-start | bytes 49156
  141.4 111.0 %copy-start.17 = (bf16[512,512]{1,0:T(8,128)(2,1)S(1)}, bf16[512,512]{1,0:T(8,128)(2,1)}, u32[]{:S(2)}) copy-start(bf16[512,512]{1,0:T(8,128)(2,1)} %all_gather.30) | copy-start | bytes 1572868
  268.7 98.5 %all-to-all-start = ((bf16[1,4,1024,512]{3,1,0,2:T(4,128)(2,1)}), bf16[1,4,1024,512]{3,1,0,2:T(4,128)(2,1)}, u32[]{:S(2)}, u32[]{:S(2)}) async-start(bf16[1,4,1024,512]{3,1,0,2:T(4,128)(2,1)} %copy.121), calls=%async_computation | async-start | bytes 8388608 | tf_op jit(solution)/shard_map/all_to_all | solution.py:199
  280.7 92.3 %copy-start.40 = (bf16[16,4]{0,1:T(4,128)(2,1)S(1)}, bf16[16,4]{0,1:T(4,128)(2,1)}, u32[]{:S(2)}) copy-start(bf16[16,4]{0,1:T(4,128)(2,1)} %param.35) | copy-start | bytes 388
  280.7 202.7 %copy-start.42 = (s32[1,32]{1,0:T(1,128)S(1)}, s32[1,32]{1,0:T(1,128)}, u32[]{:S(2)}) copy-start(s32[1,32]{1,0:T(1,128)} %param.31) | copy-start | bytes 388
  367.3 128.5 %all-to-all-start.4 = ((bf16[1,4,1024,512]{3,1,0,2:T(4,128)(2,1)}), bf16[1,4,1024,512]{3,1,0,2:T(4,128)(2,1)}, u32[]{:S(2)}, u32[]{:S(2)}) async-start(bf16[1,4,1024,512]{3,1,0,2:T(4,128)(2,1)} %copy.132), calls=%async_computation.4 | async-start | bytes 8388608 | tf_op jit(solution)/shard_map/all_to_all | solution.py:200
  371.8 173.6 %all-gather.7.cloned.1.call-start = ((), (), s32[]{:S(2)}) async-start(), calls=%async_computation.14 | async-start | bytes 2359296 | tf_op jit(solution)/shard_map/all_gather | solution.py:164
  372.4 178.0 %all-gather.9.cloned.1.call-start = ((), (), s32[]{:S(2)}) async-start(), calls=%async_computation.15 | async-start | bytes 2359296 | tf_op jit(solution)/shard_map/all_gather | solution.py:165
  495.8 46.1 %all-to-all-start.1 = ((bf16[128,4,512]{2,0,1:T(8,128)(2,1)}), bf16[128,4,512]{2,0,1:T(8,128)(2,1)S(1)}, u32[]{:S(2)}, u32[]{:S(2)}) async-start(bf16[128,4,512]{2,0,1:T(8,128)(2,1)} %copy.126), calls=%async_computation.1 | async-start | bytes 1048576 | tf_op jit(solution)/shard_map/all_to_all | solution.py:222
  542.0 15.5 %all-to-all-start.5 = ((bf16[128,4,512]{2,0,1:T(8,128)(2,1)}), bf16[128,4,512]{2,0,1:T(8,128)(2,1)S(1)}, u32[]{:S(2)}, u32[]{:S(2)}) async-start(bf16[128,4,512]{2,0,1:T(8,128)(2,1)} %copy.135), calls=%async_computation.5 | async-start | bytes 1048576 | tf_op jit(solution)/shard_map/all_to_all | solution.py:223
  557.4 14.4 all-to-all-start.2
  571.9 12.4 all-to-all-start.6
  584.3 104.6 %all-to-all-start.3 = ((bf16[1,32,128,512]{3,2,0,1:T(8,128)(2,1)}), bf16[1,32,128,512]{3,2,0,1:T(8,128)(2,1)}, u32[]{:S(2)}, u32[]{:S(2)}) async-start(bf16[1,32,128,512]{3,2,0,1:T(8,128)(2,1)} %copy.130), calls=%async_computation.3 | async-start | bytes 8388608 | tf_op jit(solution)/shard_map/all_to_all | solution.py:263
  594.1 154.6 %reduce-scatter.16.cloned.1.call-start = ((), (), s32[]{:S(2)}) async-start(), calls=%async_computation.20 | async-start | bytes 270336
  608.0 250.3 %reduce-scatter.14.cloned.1.call-start = ((), (), s32[]{:S(2)}) async-start(), calls=%async_computation.19 | async-start | bytes 2359296 | tf_op jit(solution)/shard_map/reduce_scatter | solution.py:234
  620.6 73.1 %copy-start.20 = (bf16[128,4,512]{2,0,1:T(8,128)(2,1)S(1)}, bf16[128,4,512]{2,0,1:T(8,128)(2,1)}, u32[]{:S(2)}) copy-start(bf16[128,4,512]{2,0,1:T(8,128)(2,1)} %copy-done.19) | copy-start | bytes 1572868
  689.0 249.1 %all-to-all-start.7 = ((bf16[1,32,128,512]{3,2,0,1:T(8,128)(2,1)}), bf16[1,32,128,512]{3,2,0,1:T(8,128)(2,1)}, u32[]{:S(2)}, u32[]{:S(2)}) async-start(bf16[1,32,128,512]{3,2,0,1:T(8,128)(2,1)} %copy.143), calls=%async_computation.7 | async-start | bytes 8388608 | tf_op jit(solution)/shard_map/all_to_all | solution.py:264
  693.7 235.9 %reduce-scatter.12.cloned.1.call-start = ((), (), s32[]{:S(2)}) async-start(), calls=%async_computation.18 | async-start | bytes 2359296 | tf_op jit(solution)/shard_map/reduce_scatter | solution.py:231
  698.0 685.5 %reduce-scatter.10.cloned.1.call-start = ((), (), s32[]{:S(2)}) async-start(), calls=%async_computation.17 | async-start | bytes 1081344 | tf_op jit(solution)/shard_map/reduce_scatter | solution.py:304
  1249.4 237.5 %reduce-scatter.8.cloned.1.call-start = ((), (), s32[]{:S(2)}) async-start(), calls=%async_computation.16 | async-start | bytes 3244032 | tf_op jit(solution)/shard_map/reduce_scatter | solution.py:303
  1284.3 46.3 %copy-start.31 = (f32[4,1024]{1,0:T(4,128)S(1)}, f32[4,1024]{1,0:T(4,128)}, u32[]{:S(2)}) copy-start(f32[4,1024]{1,0:T(4,128)} %copy-done.30) | copy-start | bytes 49156
  (68 other events, 418.7 us)
Sparse Core Ops, SparseCore 0:
  11.7 57.7 all-gather.4
  608.1 140.5 reduce-scatter.15
  752.7 105.5 reduce-scatter.13
  862.1 67.4 reduce-scatter.11
  1249.5 133.9 reduce-scatter.9
  1389.3 97.5 reduce-scatter.7
Sparse Core Ops, SparseCore 1:
  374.3 117.6 all-gather.6
  494.0 47.4 all-gather.8
where the time goes:
time: 1510 us; the launch traced here: 1490 us
  waiting for transfers between devices  530 us (35%)
  matrix products  296 us (20%)
  blocking collectives  237 us (16%)
  local copies, waits for them, and re-layouts  205 us (14%)
  other arithmetic  144 us (10%)
  starting transfers between devices  63.8 us (4%)
  between operations  16.6 us (1%)
    all_gather x1, blocking collectives, per_device(): lax.all_gather(router_weight, ('dp', 'fsdp'), axis=0, tiled=True)  110 us
    reduce_scatter x1, waiting for transfers between devices, per_device(): lax.psum_scatter(grad_out.astype(jnp.bfloat16), 'dp', scatter_dimension=1...  108 us
    reduce_scatter x1, waiting for transfers between devices, per_device(): lax.psum_scatter(grad_proj_in, ('dp', 'fsdp'), scatter_dimension=0, tiled...  103 us
    all_to_all x1, waiting for transfers between devices, per_device(): lax.all_to_all(mixed_in, 'dp', split_axis=2, concat_axis=1, tiled=True)  86.6 us
    unnamed x2, blocking collectives  81.8 us
    reduce_scatter x1, waiting for transfers between devices, per_device(): lax.psum_scatter(grad_in.astype(jnp.bfloat16), 'dp', scatter_dimension=2,...  69.5 us
    dot_general x16, matrix products, block_scores(): jnp.einsum('qhd,khd->hqk', query_blk, key_heads, preferred_element_type=j...  69.3 us
    all_to_all x1, waiting for transfers between devices, per_device(): lax.all_to_all(spread, 'dp', split_axis=1, concat_axis=2, tiled=True)  68.3 us
  transfers between devices with their start and end apart: 16, of which 8 were waited for; matrix products, arithmetic and copies ran while one was open for 11% of the time, Pallas kernels for 0%

commit v1 on v0

v1 whole, which is shorter than its diff:
```python
import functools, math
import jax, jax.numpy as jnp
from jax import lax
from jax.experimental import pallas as pl
from jax.experimental.pallas import tpu as pltpu
from jax.sharding import PartitionSpec as P

NEGATIVE = -1e30
QB = 128
F32 = jnp.float32
BF16 = jnp.bfloat16
NT = (((1,), (1,)), ((), ()))
TN = (((0,), (0,)), ((), ()))


def dot(a, b):
    return jnp.dot(a, b, preferred_element_type=F32)


def dot_nt(a, b):
    return lax.dot_general(a, b, NT, preferred_element_type=F32)


def dot_tn(a, b):
    return lax.dot_general(a, b, TN, preferred_element_type=F32)


def iota(shape, axis):
    return lax.broadcasted_iota(jnp.int32, shape, axis)


def split_heads(x):
    low = iota(x.shape, 1) < 64
    zero = jnp.zeros_like(x)
    return jnp.concatenate([jnp.where(low, x, zero), jnp.where(low, zero, x)], axis=0)


def join_heads(x):
    half = x.shape[0] // 2
    low = iota((half, x.shape[1]), 1) < 64
    return jnp.where(low, x[:half], x[half:])


def attn_fwd_kernel(width, begin, count, lo_ref, vlen_ref, start_ref, joined_ref, out_ref, bias_ref):
    row = pl.program_id(0)
    vlen = vlen_ref[row]

    def block(step, _):
        qb = step + begin
        lo = lo_ref[row, qb]
        base = pl.multiple_of(qb * QB, QB)
        first = pl.multiple_of(lo * QB, QB)
        own = pl.ds(base, QB)
        target = pl.ds(pl.multiple_of(step * QB, QB), QB)

        def variant(blocks):
            span = blocks * QB
            keys = pl.ds(first, span)
            begins = jnp.broadcast_to(start_ref[0, pl.ds(qb, 1), :], (QB, QB)).T
            i = base + iota((QB, QB), 0)
            for b in range(blocks):
                j = first + b * QB + iota((QB, QB), 1)
                ok = ((j >= begins) & (j <= i) & (j < vlen)) | (j == i)
                bias_ref[:, b * QB:(b + 1) * QB] = jnp.where(ok, 0.0, NEGATIVE)
            bias = bias_ref[:, :span]
            bias = jnp.concatenate([bias, bias], axis=0)
            at = [pl.ds(lane, 128) for lane in range(0, width, 128)]
            key_at = [pl.ds(width + lane, 128) for lane in range(0, width, 128)]
            value_at = [pl.ds(2 * width + lane, 128) for lane in range(0, width, 128)]
            query = [split_heads(joined_ref[0, own, lanes] * jnp.asarray(0.125, BF16)) for lanes in at]
            scores = [dot_nt(q, joined_ref[0, keys, lanes]) for q, lanes in zip(query, key_at)]
            scores = [s + bias for s in scores]
            tops = [jnp.max(s, axis=1, keepdims=True) for s in scores]
            raised = [jnp.exp(s - top) for s, top in zip(scores, tops)]
            totals = [jnp.sum(p, axis=1, keepdims=True) for p in raised]
            out = [dot(p.astype(BF16), joined_ref[0, keys, lanes]) for p, lanes in zip(raised, value_at)]
            for o, total, lanes in zip(out, totals, at):
                out_ref[0, target, lanes] = join_heads(o * (1.0 / total)).astype(BF16)

        for blocks in range(1, 6):
            pl.when(qb - lo + 1 == blocks)(functools.partial(variant, blocks))
        return 0

    lax.fori_loop(0, count, block, 0)


def attn_fwd(joined, starts, lows, vlens, begin, count):
    rows, length, triple = joined.shape
    width = triple // 3
    spec = pltpu.PrefetchScalarGridSpec(
        num_scalar_prefetch=2,
        grid=(rows,),
        in_specs=[
            pl.BlockSpec((1, length // QB, QB), lambda r, *_: (r, 0, 0)),
            pl.BlockSpec((1, length, triple), lambda r, *_: (r, 0, 0)),
        ],
        out_specs=pl.BlockSpec((1, count * QB, width), lambda r, *_: (r, 0, 0)),
        scratch_shapes=[pltpu.VMEM((QB, 5 * QB), F32)],
    )
    return pl.pallas_call(
        functools.partial(attn_fwd_kernel, width, begin, count),
        grid_spec=spec,
        out_shape=jax.ShapeDtypeStruct((rows, count * QB, width), BF16),
        compiler_params=pltpu.CompilerParams(vmem_limit_bytes=48 << 20),
        cost_estimate=pl.CostEstimate(flops=rows * count * QB * 400 * 8 * 256 * 4, bytes_accessed=rows * length * triple * 2, transcendentals=0),
        name="attend",
    )(lows, vlens, starts, joined)


def attn_bwd_kernel(width, length, begin, count, resume, lo_ref, vlen_ref, start_ref, joined_ref, grad_ref, *rest):
    if resume:
        dk_in, dv_in, *rest = rest
    dq_ref, dk_ref, dv_ref, bias_ref = rest
    row = pl.program_id(0)
    vlen = vlen_ref[row]
    dk_ref[...] = jnp.zeros_like(dk_ref)
    dv_ref[...] = jnp.zeros_like(dv_ref)
    if resume:
        n = dk_in.shape[1]
        dk_ref[0, :n] = dk_in[0]
        dv_ref[0, :n] = dv_in[0]

    def block(step, _):
        qb = step + begin
        lo = lo_ref[row, qb]
        base = pl.multiple_of(qb * QB, QB)
        first = pl.multiple_of(lo * QB, QB)
        own = pl.ds(base, QB)
        target = pl.ds(pl.multiple_of(step * QB, QB), QB)

        def variant(blocks):
            span = blocks * QB
            keys = pl.ds(first, span)
            begins = start_ref[0, pl.ds(qb, 1), :]
            i = base + iota((QB, QB), 1)
            for b in range(blocks):
                j = first + b * QB + iota((QB, QB), 0)
                ok = ((j >= begins) & (j <= i) & (j < vlen)) | (j == i)
                bias_ref[b * QB:(b + 1) * QB, :] = jnp.where(ok, 0.0, NEGATIVE)
            bias = bias_ref[:span, :]
            bias = jnp.concatenate([bias, bias], axis=1)
            at = [pl.ds(lane, 128) for lane in range(0, width, 128)]
            key_at = [pl.ds(width + lane, 128) for lane in range(0, width, 128)]
            value_at = [pl.ds(2 * width + lane, 128) for lane in range(0, width, 128)]
            query = [split_heads(joined_ref[0, own, lanes] * jnp.asarray(0.125, BF16)) for lanes in at]
            grads = [split_heads(grad_ref[0, target, lanes]) for lanes in at]
            scores = [dot_nt(joined_ref[0, keys, lanes], q) for q, lanes in zip(query, key_at)]
            change = [dot_nt(joined_ref[0, keys, lanes], g) for g, lanes in zip(grads, value_at)]
            scores = [s + bias for s in scores]
            tops = [jnp.max(s, axis=0, keepdims=True) for s in scores]
            prob = [jnp.exp(s - top) for s, top in zip(scores, tops)]
            totals = [1.0 / jnp.sum(p, axis=0, keepdims=True) for p in prob]
            prob = [p * total for p, total in zip(prob, totals)]
            scaled = [p * c for p, c in zip(prob, change)]
            sums = [jnp.sum(t, axis=0, keepdims=True) for t in scaled]
            moved = [(t - p * total).astype(BF16) for t, p, total in zip(scaled, prob, sums)]
            for p, g, lanes in zip(prob, grads, at):
                dv_ref[0, keys, lanes] += dot(p.astype(BF16), g)
            for m, q, lanes in zip(moved, query, at):
                dk_ref[0, keys, lanes] += dot(m, q)
            back = [dot_tn(m, joined_ref[0, keys, lanes]) for m, lanes in zip(moved, key_at)]
            for b, lanes in zip(back, at):
                dq_ref[0, target, lanes] = (join_heads(b) * 0.125).astype(BF16)

        for blocks in range(1, 6):
            pl.when(qb - lo + 1 == blocks)(functools.partial(variant, blocks))
        return 0

    lax.fori_loop(0, count, block, 0)


def attn_bwd(joined, grads, starts, lows, vlens, begin, count, carry=None):
    rows, length, triple = joined.shape
    width = triple // 3
    full = pl.BlockSpec((1, length, width), lambda r, *_: (r, 0, 0))
    part = pl.BlockSpec((1, count * QB, width), lambda r, *_: (r, 0, 0))
    ins = [
        pl.BlockSpec((1, length // QB, QB), lambda r, *_: (r, 0, 0)),
        pl.BlockSpec((1, length, triple), lambda r, *_: (r, 0, 0)),
        part,
    ]
    args = [lows, vlens, starts, joined, grads]
    reach = begin * QB + count * QB
    if carry is not None:
        ins += [pl.BlockSpec((1, carry[0].shape[1], width), lambda r, *_: (r, 0, 0))] * 2
        args += list(carry)
    outk = pl.BlockSpec((1, reach, width), lambda r, *_: (r, 0, 0))
    spec = pltpu.PrefetchScalarGridSpec(
        num_scalar_prefetch=2,
        grid=(rows,),
        in_specs=ins,
        out_specs=[part, outk, outk],
        scratch_shapes=[pltpu.VMEM((5 * QB, QB), F32)],
    )
    return pl.pallas_call(
        functools.partial(attn_bwd_kernel, width, length, begin, count, carry is not None),
        grid_spec=spec,
        out_shape=[
            jax.ShapeDtypeStruct((rows, count * QB, width), BF16),
            jax.ShapeDtypeStruct((rows, reach, width), F32),
            jax.ShapeDtypeStruct((rows, reach, width), F32),
        ],
        compiler_params=pltpu.CompilerParams(vmem_limit_bytes=56 << 20),
        cost_estimate=pl.CostEstimate(flops=rows * count * QB * 400 * 8 * 256 * 10, bytes_accessed=rows * length * triple * 4, transcendentals=0),
        name="attend_back",
    )(*args)


def normalise(values):
    centred = values - jnp.mean(values, axis=-1, keepdims=True)
    inverse = lax.rsqrt(jnp.mean(centred * centred, axis=-1, keepdims=True) + 1e-05)
    return centred * inverse, inverse


def pull_norm(scaled, hat, inverse):
    return inverse * (
        scaled
        - jnp.mean(scaled, axis=-1, keepdims=True)
        - hat * jnp.mean(scaled * hat, axis=-1, keepdims=True)
    )


def constant_spec(shape, *where):
    where = where or (0,) * len(shape)
    return pl.BlockSpec(shape, lambda *_: where)


def join_kernel(tokens_ref, gains_ref, weight_ref, joined_ref):
    hat, _ = normalise(tokens_ref[0].astype(F32))
    normed = (hat * gains_ref[0:1] + gains_ref[1:2]).astype(BF16)
    joined_ref[0] = dot(normed, weight_ref[...]).astype(BF16)


def join_tokens(tokens, gains, packed, tile=512):
    rows, length, width = tokens.shape
    return pl.pallas_call(
        join_kernel,
        grid=(rows, length // tile),
        in_specs=[
            pl.BlockSpec((1, tile, width), lambda r, t: (r, t, 0)),
            constant_spec(gains.shape),
            constant_spec((width, 3 * width)),
        ],
        out_specs=pl.BlockSpec((1, tile, 3 * width), lambda r, t: (r, t, 0)),
        out_shape=jax.ShapeDtypeStruct((rows, length, 3 * width), BF16),
        compiler_params=pltpu.CompilerParams(vmem_limit_bytes=40 << 20),
        cost_estimate=pl.CostEstimate(
            flops=rows * length * width * width * 6, bytes_accessed=rows * length * width * 8, transcendentals=0
        ),
        name="join",
    )(tokens, gains, packed)


def mixed_kernel(attended_ref, tokens_ref, gains_ref, weight_ref, router_ref, hidden_ref, mixed_ref, logits_ref):
    hidden = tokens_ref[0].astype(F32) + dot(attended_ref[0], weight_ref[...])
    hidden_ref[0] = hidden
    hat, _ = normalise(hidden)
    mixed = (hat * gains_ref[2:3] + gains_ref[3:4]).astype(BF16)
    mixed_ref[0] = mixed
    logits_ref[0] = dot_nt(router_ref[...], mixed)


def mix_tokens(attended, tokens, gains, packed, router, offset, tile=512):
    rows, span, width = attended.shape
    block = pl.BlockSpec((1, tile, width), lambda r, t: (r, t, 0))
    return pl.pallas_call(
        mixed_kernel,
        grid=(rows, span // tile),
        in_specs=[
            block,
            pl.BlockSpec((1, tile, width), lambda r, t: (r, t + offset // tile, 0)),
            constant_spec(gains.shape),
            constant_spec((width, width), 0, 3),
            constant_spec(router.shape),
        ],
        out_specs=[block, block, pl.BlockSpec((1, router.shape[0], tile), lambda r, t: (r, 0, t))],
        out_shape=[
            jax.ShapeDtypeStruct((rows, span, width), F32),
            jax.ShapeDtypeStruct((rows, span, width), BF16),
            jax.ShapeDtypeStruct((rows, router.shape[0], span), F32),
        ],
        compiler_params=pltpu.CompilerParams(vmem_limit_bytes=40 << 20),
        cost_estimate=pl.CostEstimate(
            flops=rows * span * width * width * 2, bytes_accessed=rows * span * width * 10, transcendentals=0
        ),
        name="mix",
    )(attended, tokens, gains, packed, router)


def pool_kernel(experts, scale, gates_ref, values_ref, out_ref):
    rows, places = values_ref.shape[0], values_ref.shape[1]
    sub = 16

    def step(s, _):
        here = pl.ds(pl.multiple_of(s * sub, sub), sub)
        gates = gates_ref[here, :].astype(BF16).astype(F32)
        values = [values_ref[r, here, :].astype(F32) for r in range(rows)]
        for e in range(experts):
            total = sum(gates[:, r * experts + e: r * experts + e + 1] * values[r] for r in range(rows))
            out_ref[0, e, here, :] = (scale * total).astype(BF16)
        return 0

    lax.fori_loop(0, places // sub, step, 0, unroll=2)


def pool_tokens(gates, values, owners, experts, scale):
    rows, span, width = values.shape
    places = span // owners
    return pl.pallas_call(
        functools.partial(pool_kernel, experts, scale),
        grid=(owners,),
        in_specs=[
            pl.BlockSpec((places, gates.shape[1]), lambda i: (i, 0)),
            pl.BlockSpec((rows, places, width), lambda i: (0, i, 0)),
        ],
        out_specs=pl.BlockSpec((1, experts, places, width), lambda i: (i, 0, 0, 0)),
        out_shape=jax.ShapeDtypeStruct((owners, experts, places, width), BF16),
        compiler_params=pltpu.CompilerParams(vmem_limit_bytes=40 << 20),
        cost_estimate=pl.CostEstimate(
            flops=rows * span * width * 200, bytes_accessed=rows * span * width * 8, transcendentals=0
        ),
        name="pool",
    )(gates, values)


CUBIC = 0.044715
SLOPE = math.sqrt(2.0 / math.pi)


def expert_kernel(steps, pooled_ref, weights_ref, result_ref, act_ref, slope_ref, total_ref):
    step = pl.program_id(0)
    blocks, places, width = pooled_ref.shape
    pooled = pooled_ref[...].reshape(blocks * places, width)
    pre = dot(pooled, weights_ref[0, 0])
    square = pre * pre
    bent = jnp.tanh(SLOPE * pre * (1.0 + CUBIC * square))
    half = 0.5 * (1.0 + bent)
    act = (pre * half).astype(BF16)
    act_ref[0] = act
    slope_ref[0] = half + 0.5 * pre * (1.0 - bent * bent) * (SLOPE * (1.0 + 3.0 * CUBIC * square))
    result = dot_nt(act, weights_ref[0, 1])

    @pl.when(step == 0)
    def _():
        total_ref[...] = result

    @pl.when(step > 0)
    def _():
        total_ref[...] += result

    @pl.when(step == steps - 1)
    def _():
        result_ref[...] = total_ref[...].astype(BF16).reshape(blocks, places, width)


def run_experts(pooled, weights):
    blocks, places, width = pooled.shape
    steps, _, _, tile = weights.shape
    count = blocks * places
    return pl.pallas_call(
        functools.partial(expert_kernel, steps),
        grid=(steps,),
        in_specs=[constant_spec(pooled.shape), pl.BlockSpec((1, 2, width, tile), lambda i: (i, 0, 0, 0))],
        out_specs=[
            constant_spec(pooled.shape),
            pl.BlockSpec((1, count, tile), lambda i: (i, 0, 0)),
            pl.BlockSpec((1, count, tile), lambda i: (i, 0, 0)),
        ],
        out_shape=[
            jax.ShapeDtypeStruct(pooled.shape, BF16),
            jax.ShapeDtypeStruct((steps, count, tile), BF16),
            jax.ShapeDtypeStruct((steps, count, tile), F32),
        ],
        scratch_shapes=[pltpu.VMEM((count, width), F32)],
        compiler_params=pltpu.CompilerParams(vmem_limit_bytes=40 << 20),
        cost_estimate=pl.CostEstimate(
            flops=count * width * tile * steps * 8, bytes_accessed=width * tile * steps * 8, transcendentals=0
        ),
        name="experts",
    )(pooled, weights)


def expert_back_kernel(steps, pooled_ref, grads_ref, result_ref, act_ref, slope_ref, weights_ref, back_ref, grad_ref, total_ref):
    step = pl.program_id(0)
    blocks, places, width = pooled_ref.shape
    count = blocks * places
    pooled = pooled_ref[...].reshape(count, width)
    grads = grads_ref[...].reshape(count, width)
    act = act_ref[0]
    grad_pre = (dot(grads, weights_ref[0, 1]) * slope_ref[0]).astype(BF16)
    grad_ref[0, 0] = dot_tn(pooled, grad_pre).astype(BF16)
    grad_ref[0, 1] = dot_tn(grads, act).astype(BF16)
    part = dot_nt(grad_pre, weights_ref[0, 0])

    @pl.when(step == 0)
    def _():
        total_ref[...] = part

    @pl.when(step > 0)
    def _():
        total_ref[...] += part

    @pl.when(step == steps - 1)
    def _():
        grad_pooled = total_ref[...].astype(BF16)
        back_ref[:, :places] = grad_pooled.reshape(blocks, places, width)
        result = result_ref[...].reshape(count, width)
        product = result.astype(F32) * grads.astype(F32) + grad_pooled.astype(F32) * pooled.astype(F32)
        high = product.astype(BF16)
        rest = (product - high.astype(F32)).astype(BF16)
        ones = jnp.ones((16, width), BF16)
        sums = dot_nt(ones, high) + dot_nt(ones, rest)
        top = sums.astype(BF16)
        low = (sums - top.astype(F32)).astype(BF16)
        for b in range(blocks):
            here = slice(b * places, b * places + places)
            fill = jnp.zeros((16, width - 2 * places), BF16)
            back_ref[b, places:] = jnp.concatenate([top[:, here], low[:, here], fill], axis=1)


def pull_experts(pooled, grads, result, act, slope, weights):
    blocks, places, width = pooled.shape
    steps, _, _, tile = weights.shape
    count = blocks * places
    return pl.pallas_call(
        functools.partial(expert_back_kernel, steps),
        grid=(steps,),
        in_specs=[constant_spec(pooled.shape)] * 3
        + [pl.BlockSpec((1, count, tile), lambda i: (i, 0, 0))] * 2
        + [pl.BlockSpec((1, 2, width, tile), lambda i: (i, 0, 0, 0))],
        out_specs=[
            constant_spec((blocks, places + 16, width)),
            pl.BlockSpec((1, 2, width, tile), lambda i: (i, 0, 0, 0)),
        ],
        out_shape=[
            jax.ShapeDtypeStruct((blocks, places + 16, width), BF16),
            jax.ShapeDtypeStruct(weights.shape, BF16),
        ],
        scratch_shapes=[pltpu.VMEM((count, width), F32)],
        compiler_params=pltpu.CompilerParams(vmem_limit_bytes=40 << 20),
        cost_estimate=pl.CostEstimate(
            flops=count * width * tile * steps * 12, bytes_accessed=width * tile * steps * 8, transcendentals=0
        ),
        name="pull_experts",
    )(pooled, grads, result, act, slope, weights)


def spread_kernel(experts, group, gates_ref, result_ref, grads_ref, hidden_ref, out_ref, change_ref):
    rows, places = grads_ref.shape[0], grads_ref.shape[1]
    sub = 16
    slots = gates_ref.shape[1]

    def step(s, _):
        here = pl.ds(pl.multiple_of(s * sub, sub), sub)
        results = [result_ref[0, e, here, :].astype(F32) * group for e in range(experts)]
        gates = gates_ref[here, :].astype(BF16).astype(F32)
        lane = iota((sub, slots), 1)
        changes = jnp.zeros((sub, slots), F32)
        for r in range(rows):
            grads = grads_ref[r, here, :].astype(F32)
            for e in range(experts):
                both = jnp.sum(grads * results[e], axis=1, keepdims=True)
                changes = jnp.where(lane == r * experts + e, both, changes)
            total = sum(gates[:, r * experts + e: r * experts + e + 1] * results[e] for e in range(experts))
            out_ref[r, here, :] = (hidden_ref[r, here, :] + total.astype(BF16).astype(F32)).astype(BF16)
        change_ref[here, :] = changes
        return 0

    lax.fori_loop(0, places // sub, step, 0, unroll=2)


def spread_tokens(gates, result, cotangent, hidden, group):
    rows, span, width = hidden.shape
    owners, experts, places, _ = result.shape
    block = pl.BlockSpec((rows, places, width), lambda i: (0, i, 0))
    slots = pl.BlockSpec((places, gates.shape[1]), lambda i: (i, 0))
    return pl.pallas_call(
        functools.partial(spread_kernel, experts, group),
        grid=(owners,),
        in_specs=[slots, pl.BlockSpec((1, experts, places, width), lambda i: (i, 0, 0, 0)), block, block],
        out_specs=[block, slots],
        out_shape=[jax.ShapeDtypeStruct((rows, span, width), BF16), jax.ShapeDtypeStruct(gates.shape, F32)],
        compiler_params=pltpu.CompilerParams(vmem_limit_bytes=40 << 20),
        cost_estimate=pl.CostEstimate(
            flops=rows * span * width * 200, bytes_accessed=rows * span * width * 10, transcendentals=0
        ),
        name="spread",
    )(gates, result, cotangent, hidden)


def router_kernel(experts, gates_ref, inner_ref, change_ref, pooled_ref, mixed_ref, router_ref, grad_ref, router_grad_ref, logits_ref, routed_ref):
    rows, places = mixed_ref.shape[0], mixed_ref.shape[1]
    sub = 16
    slots = gates_ref.shape[1]

    @pl.when(pl.program_id(0) == 0)
    def _():
        router_grad_ref[...] = jnp.zeros_like(router_grad_ref)

    def change(s, _):
        here = pl.ds(pl.multiple_of(s * sub, sub), sub)
        pooled = [pooled_ref[0, e, here, :].astype(F32) for e in range(experts)]
        lane = iota((sub, slots), 1)
        changes = jnp.zeros((sub, slots), F32)
        for r in range(rows):
            mixed = mixed_ref[r, here, :].astype(F32)
            for e in range(experts):
                both = jnp.sum(pooled[e] * mixed, axis=1, keepdims=True)
                changes = jnp.where(lane == r * experts + e, both, changes)
        changes = (changes + change_ref[here, :]).astype(BF16).astype(F32)
        logits_ref[here, :] = (gates_ref[here, :] * (changes - inner_ref[here, :])).astype(BF16)
        return 0

    lax.fori_loop(0, places // sub, change, 0, unroll=2)
    low = logits_ref[...]
    for r in range(rows):
        routed_ref[r] = dot(low, router_ref[r])
        router_grad_ref[...] += dot_tn(low, mixed_ref[r])[r * experts: r * experts + experts]

    def spread(s, _):
        here = pl.ds(pl.multiple_of(s * sub, sub), sub)
        pooled = [pooled_ref[0, e, here, :].astype(F32) for e in range(experts)]
        gates = gates_ref[here, :].astype(BF16).astype(F32)
        for r in range(rows):
            total = sum(
                (gates[:, r * experts + e: r * experts + e + 1] * pooled[e] for e in range(experts)),
                routed_ref[r, here, :],
            )
            grad_ref[r, here, :] = total.astype(BF16)
        return 0

    lax.fori_loop(0, places // sub, spread, 0, unroll=2)


def pull_gates(gates, inner, change, pooled, mixed, router):
    rows, span, width = mixed.shape
    owners, experts, depth, _ = pooled.shape
    places = span // owners
    block = pl.BlockSpec((rows, places, width), lambda i: (0, i, 0))
    slots = pl.BlockSpec((places, gates.shape[1]), lambda i: (i, 0))
    return pl.pallas_call(
        functools.partial(router_kernel, experts),
        grid=(owners,),
        in_specs=[
            slots,
            slots,
            slots,
            pl.BlockSpec((1, experts, depth, width), lambda i: (i, 0, 0, 0)),
            block,
            constant_spec(router.shape),
        ],
        out_specs=[block, constant_spec((experts, width))],
        out_shape=[
            jax.ShapeDtypeStruct((rows, span, width), BF16),
            jax.ShapeDtypeStruct((experts, width), F32),
        ],
        scratch_shapes=[pltpu.VMEM((places, gates.shape[1]), BF16), pltpu.VMEM((rows, places, width), F32)],
        compiler_params=pltpu.CompilerParams(vmem_limit_bytes=40 << 20),
        cost_estimate=pl.CostEstimate(
            flops=rows * span * width * 200, bytes_accessed=rows * span * width * 10, transcendentals=0
        ),
        name="pull_gates",
    )(gates, inner, change, pooled, mixed, router)


def hidden_kernel(grad_ref, hidden_ref, cotangent_ref, attended_ref, gains_ref, weight_ref, out_ref, low_ref, project_ref, sums_ref):
    @pl.when((pl.program_id(0) == 0) & (pl.program_id(1) == 0))
    def _():
        project_ref[...] = jnp.zeros_like(project_ref)
        sums_ref[...] = jnp.zeros_like(sums_ref)

    grads = grad_ref[0].astype(F32)
    hat, inverse = normalise(hidden_ref[0])
    sums_ref[0:1] += jnp.sum(grads * hat, axis=0, keepdims=True)
    sums_ref[1:2] += jnp.sum(grads, axis=0, keepdims=True)
    total = cotangent_ref[0].astype(F32) + pull_norm(grads * gains_ref[2:3], hat, inverse)
    out_ref[0] = total
    low = total.astype(BF16)
    project_ref[...] += dot_tn(attended_ref[0], low)
    low_ref[0] = dot_nt(low, weight_ref[...]).astype(BF16)


def pull_hidden(grad_mixed, hidden, cotangent, attended, gains, packed, offset, tile=512):
    rows, span, width = hidden.shape
    block = pl.BlockSpec((1, tile, width), lambda r, t: (r, t, 0))
    return pl.pallas_call(
        hidden_kernel,
        grid=(rows, span // tile),
        in_specs=[
            block,
            block,
            pl.BlockSpec((1, tile, width), lambda r, t: (r, t + offset // tile, 0)),
            block,
            constant_spec(gains.shape),
            constant_spec((width, width), 0, 3),
        ],
        out_specs=[block, block, constant_spec((width, width)), constant_spec((8, width))],
        out_shape=[
            jax.ShapeDtypeStruct((rows, span, width), F32),
            jax.ShapeDtypeStruct((rows, span, width), BF16),
            jax.ShapeDtypeStruct((width, width), F32),
            jax.ShapeDtypeStruct((8, width), F32),
        ],
        compiler_params=pltpu.CompilerParams(vmem_limit_bytes=48 << 20),
        cost_estimate=pl.CostEstimate(
            flops=rows * span * width * width * 4, bytes_accessed=rows * span * width * 16, transcendentals=0
        ),
        name="pull_hidden",
    )(grad_mixed, hidden, cotangent, attended, gains, packed)


def tokens_kernel(query_ref, keys_ref, values_ref, tokens_ref, hidden_ref, gains_ref, weight_ref, out_ref, project_ref, sums_ref):
    @pl.when((pl.program_id(0) == 0) & (pl.program_id(1) == 0))
    def _():
        project_ref[...] = jnp.zeros_like(project_ref)
        sums_ref[...] = jnp.zeros_like(sums_ref)

    width = tokens_ref.shape[2]
    hat, inverse = normalise(tokens_ref[0].astype(F32))
    normed = (hat * gains_ref[0:1] + gains_ref[1:2]).astype(BF16)
    parts = [query_ref[0], keys_ref[0].astype(BF16), values_ref[0].astype(BF16)]
    grads = jnp.zeros((normed.shape[0], width), F32)
    for i, part in enumerate(parts):
        lanes = slice(i * width, i * width + width)
        project_ref[:, lanes] += dot_tn(normed, part)
        grads += dot_nt(part, weight_ref[:, lanes])
    sums_ref[0:1] += jnp.sum(grads * hat, axis=0, keepdims=True)
    sums_ref[1:2] += jnp.sum(grads, axis=0, keepdims=True)
    out_ref[0] = hidden_ref[0] + pull_norm(grads * gains_ref[0:1], hat, inverse)


def pull_tokens(query, keys, values, tokens, hidden, gains, packed, tile=512):
    rows, length, width = tokens.shape
    block = pl.BlockSpec((1, tile, width), lambda r, t: (r, t, 0))
    return pl.pallas_call(
        tokens_kernel,
        grid=(rows, length // tile),
        in_specs=[block] * 5 + [constant_spec(gains.shape), constant_spec((width, 3 * width))],
        out_specs=[block, constant_spec((width, 3 * width)), constant_spec((8, width))],
        out_shape=[
            jax.ShapeDtypeStruct((rows, length, width), F32),
            jax.ShapeDtypeStruct((width, 3 * width), F32),
            jax.ShapeDtypeStruct((8, width), F32),
        ],
        compiler_params=pltpu.CompilerParams(vmem_limit_bytes=48 << 20),
        cost_estimate=pl.CostEstimate(
            flops=rows * length * width * width * 12, bytes_accessed=rows * length * width * 20, transcendentals=0
        ),
        name="pull_tokens",
    )(query, keys, values, tokens, hidden, gains, packed)


def ring_order(size):
    inner = 2 if size % 2 == 0 and size > 2 else 1
    outer = size // inner
    up = [z * inner for z in range(outer)]
    if inner == 1:
        return up
    return up + [z * inner + 1 for z in reversed(range(outer))]


def shift(value, order, step):
    count = len(order)
    return lax.ppermute(value, "dp", [(order[i], order[(i + step) % count]) for i in range(count)])


def flip(value, bit, axis="fsdp"):
    count = lax.axis_size(axis)
    return lax.ppermute(value, axis, [(i, i ^ bit) for i in range(count)])


def turn(value, step, axis="dp"):
    count = lax.axis_size(axis)
    return lax.ppermute(value, axis, [(i, (i + step) % count) for i in range(count)])


def take(values, index):
    return lax.dynamic_index_in_dim(values, index, 0, keepdims=False)


def put(values, value, index):
    return lax.dynamic_update_index_in_dim(values, value, index, 0)


def add(a, b):
    return (a.astype(F32) + b.astype(F32)).astype(BF16)


def place_of(order):
    places = [order.index(i) for i in range(len(order))]
    return jnp.array(places)[lax.axis_index("dp")], jnp.array(order)


def scatter_ring(values, order):
    count = len(order)
    here, table = place_of(order)
    half = values.shape[1] // 2
    parts = [(values[:, :half], 1), (values[:, half:], -1)]
    held = [take(part, table[(here - way) % count]) for part, way in parts]
    for step in range(count - 1):
        came = [shift(value, order, way) for value, (_, way) in zip(held, parts)]
        held = [
            add(value, take(part, table[(here - way * (2 + step)) % count])) for value, (part, way) in zip(came, parts)
        ]
    return jnp.concatenate(held, axis=0)


def gather_ring(value, order):
    count = len(order)
    here, table = place_of(order)
    whole = jnp.zeros((count,) + value.shape, value.dtype)
    whole = put(whole, value, table[here])
    ahead = behind = value
    for step in range(1, count // 2 + 1):
        ahead = shift(ahead, order, 1)
        whole = put(whole, ahead, table[(here - step) % count])
        if 2 * step < count:
            behind = shift(behind, order, -1)
            whole = put(whole, behind, table[(here + step) % count])
    return whole


def gather_all(value, order):
    whole = gather_ring(value, order)
    size = lax.axis_size("fsdp")
    here = lax.axis_index("fsdp")
    whole = whole[:, None]
    bit = size // 2
    while bit:
        other = flip(whole, bit)
        first = jnp.concatenate([whole, other], axis=1)
        second = jnp.concatenate([other, whole], axis=1)
        whole = jnp.where((here & bit) == 0, first, second)
        bit //= 2
    bits = size.bit_length() - 1
    shape = whole.shape
    whole = whole.reshape((shape[0],) + (2,) * bits + shape[2:])
    whole = whole.transpose((0,) + tuple(range(bits, 0, -1)) + tuple(range(bits + 1, bits + 1 + len(shape) - 2)))
    return whole.reshape((-1,) + shape[3:])


def scatter_all(values):
    owners, size = lax.axis_size("dp"), lax.axis_size("fsdp")
    bits = size.bit_length() - 1
    here = lax.axis_index("fsdp")
    width = values.shape[1]
    held = values.reshape((owners,) + (2,) * bits + (-1, width))
    for level in range(bits):
        axis = bits - level
        mine = (here >> level) & 1
        keep = lax.dynamic_index_in_dim(held, mine, axis, keepdims=False)
        give = lax.dynamic_index_in_dim(held, 1 - mine, axis, keepdims=False)
        held = add(keep, flip(give, 1 << level))
    data = lax.axis_index("dp")
    total = take(held, data).astype(F32)
    for step in range(1, owners):
        total += turn(take(held, (data + step) % owners), step).astype(F32)
    return total


def exchange(values):
    size = lax.axis_size("fsdp")
    here = lax.axis_index("fsdp")
    whole = values
    for bits in range(1, size):
        whole = put(whole, flip(take(values, here ^ bits), bits), here ^ bits)
    return whole


def per_device(
    tokens,
    segment_ids,
    pad_tokens,
    cotangent,
    project_in,
    project_out,
    router_weight,
    expert_in,
    expert_out,
    first_gain,
    first_bias,
    second_gain,
    second_bias,
):
    blocks_here, rows, length, width = tokens.shape
    tokens = tokens.reshape(rows, length, width)
    cotangent = cotangent.reshape(rows, length, width)
    segments = segment_ids.reshape(rows, length)
    group = pad_tokens.shape[1]
    owners = lax.axis_size("dp")
    experts = router_weight.shape[1]
    order = ring_order(owners)
    data_index = lax.axis_index("dp")
    places = length // owners

    vectors = jnp.stack([first_gain, first_bias, second_gain, second_bias], axis=1)
    small = jnp.concatenate([router_weight, vectors], axis=1)
    small = jnp.pad(small, ((0, 0), (0, 128 - small.shape[1])))
    packed = jnp.concatenate([project_in, project_out, small], axis=1)
    packed = gather_all(packed, order)
    weights = jnp.stack([expert_in[0], expert_out[0].T])
    packed, weights = lax.optimization_barrier((packed, weights))
    weights = gather_ring(weights, order)
    small = packed[:, 4 * width:].T
    router = jnp.pad(small[:experts], ((0, 16 - experts), (0, 0)))
    gains = jnp.pad(small[experts: experts + 4].astype(F32), ((0, 4), (0, 0)))

    own_pads = lax.dynamic_slice_in_dim(pad_tokens[0], data_index * rows, rows, 0)
    vlens = (length - own_pads).astype(jnp.int32)
    starts = jnp.zeros_like(segments)
    for doc in range(1, 4):
        before = jnp.sum((segments < doc).astype(jnp.int32), axis=1, keepdims=True)
        starts = jnp.where(segments == doc, before, starts)
    starts = starts.reshape(rows, length // QB, QB)
    lows = starts[:, :, 0] // QB

    joined = join_tokens(tokens, gains, packed)
    attended = attn_fwd(joined, starts, lows, vlens, 0, length // QB)
    hidden, mixed, logits = mix_tokens(attended, tokens, gains, packed, router, 0)

    logits = logits[:, :experts]
    valid = (jnp.arange(length)[None, :] < vlens[:, None])[:, None, :]
    highest = jnp.max(jnp.where(valid, logits, NEGATIVE), axis=0)
    total = jnp.sum(jnp.where(valid, jnp.exp(logits - highest), 0.0), axis=0)
    stats = jnp.stack([highest, total])
    stats = jnp.stack([stats] + [turn(stats, step) for step in range(1, owners)])
    tops = jnp.max(stats[:, 0], axis=0)
    total = jnp.sum(stats[:, 1] * jnp.exp(stats[:, 0] - tops), axis=0)
    gates = jnp.where(valid, jnp.exp(jnp.where(valid, logits - tops, NEGATIVE)) / total, 0.0)
    gates = gates.reshape(rows * experts, length).T

    pooled = exchange(scatter_ring(pool_tokens(gates, mixed, owners, experts, 1.0), order))
    result, act, slope = run_experts(pooled, weights)
    grad_result = exchange(scatter_ring(pool_tokens(gates, cotangent, owners, experts, float(group)), order))
    grad_pooled, grad_weights = pull_experts(pooled, grad_result, result, act, slope, weights)
    result = gather_ring(exchange(result), order)
    grad_pooled = gather_ring(exchange(grad_pooled), order)
    layer_out, change = spread_tokens(gates, result, cotangent, hidden, group)

    grad_pooled, grad_weights = lax.optimization_barrier((grad_pooled, grad_weights))
    grad_weights = lax.all_to_all(grad_weights, "dp", split_axis=0, concat_axis=0, tiled=True)
    grad_weights = jnp.sum(grad_weights.astype(F32), axis=0)
    inner = grad_pooled[:, :, places].astype(F32)
    inner = inner[..., :places] + inner[..., places: 2 * places]
    inner = inner.transpose(0, 2, 1).reshape(length, 1, experts)
    inner = jnp.broadcast_to(inner, (length, rows, experts)).reshape(length, rows * experts)
    spots = jnp.stack(
        [jnp.pad(router[:experts], ((r * experts, (rows - 1 - r) * experts), (0, 0))) for r in range(rows)]
    )
    grad_mixed, router_grad = pull_gates(gates, inner, change, grad_pooled, mixed, spots)
    grad_hidden, grad_attended, grad_proj_out, sums_two = pull_hidden(
        grad_mixed, hidden, cotangent, attended, gains, packed, 0
    )
    query, keys, values = attn_bwd(joined, grad_attended, starts, lows, vlens, 0, length // QB)
    tokens_grad, grad_proj_in, sums_one = pull_tokens(query, keys, values, tokens, grad_hidden, gains, packed)

    late = jnp.concatenate([router_grad, sums_one[:2], sums_two[:2]], axis=0).T
    late = jnp.pad(late, ((0, 0), (0, 128 - late.shape[1])))
    reduced = scatter_all(jnp.concatenate([grad_proj_in, grad_proj_out, late], axis=1).astype(BF16))
    late = reduced[:, 4 * width:]
    return (
        layer_out[None],
        tokens_grad[None],
        reduced[:, : 3 * width],
        reduced[:, 3 * width: 4 * width],
        late[:, :experts],
        grad_weights[0][None],
        grad_weights[1].T[None],
        late[:, experts],
        late[:, experts + 1],
        late[:, experts + 2],
        late[:, experts + 3],
    )


def solution(mesh):
    in_specs = (
        P("fsdp", "dp", None, None),
        P("fsdp", "dp", None),
        P("fsdp", None),
        P("fsdp", "dp", None, None),
        P(("dp", "fsdp"), None),
        P(("dp", "fsdp"), None),
        P(("dp", "fsdp"), None),
        P("fsdp", None, "dp"),
        P("fsdp", "dp", None),
        P(("dp", "fsdp")),
        P(("dp", "fsdp")),
        P(("dp", "fsdp")),
        P(("dp", "fsdp")),
    )
    out_specs = (
        P("fsdp", "dp", None, None),
        P("fsdp", "dp", None, None),
        P(("dp", "fsdp"), None),
        P(("dp", "fsdp"), None),
        P(("dp", "fsdp"), None),
        P("fsdp", None, "dp"),
        P("fsdp", "dp", None),
        P(("dp", "fsdp")),
        P(("dp", "fsdp")),
        P(("dp", "fsdp")),
        P(("dp", "fsdp")),
    )
    return jax.shard_map(
        per_device, mesh=mesh, in_specs=in_specs, out_specs=out_specs, check_vma=False
    )
```

time: 1510 us -> 641 us (0.42)
  waiting for transfers between devices: 530 us -> 179 us
  matrix products: 296 us -> 0 us
  blocking collectives: 237 us -> 0 us
  Pallas kernels: 0 us -> 213 us
  local copies, waits for them, and re-layouts: 205 us -> 56.1 us
  other arithmetic: 144 us -> 15.4 us
  between operations: 16.6 us -> 64.8 us
  starting transfers between devices: 63.8 us -> 103 us
    reduce_scatter x4 -> x0, waiting for transfers between devices: 320 us -> none  [the longest x1 108 us: per_device(): lax.psum_scatter(grad_out.astype(jnp.bfloat16), 'dp', scatter_dimension=1...]
    dot_general x77 -> x0, matrix products: 296 us -> none  [the longest x16 69.3 us: block_scores(): jnp.einsum('qhd,khd->hqk', query_blk, key_heads, preferred_element_type=j...]
    pallas_call x0 -> x12, Pallas kernels: none -> 213 us  [the longest x1 61.9 us: attn_bwd(): pl.pallas_call(functools.partial(attn_bwd_kernel, width, length, begin, c...]
    ppermute x0 -> x86, waiting for transfers between devices: none -> 179 us  [the longest x56 136 us: shift(): lax.ppermute(value, 'dp', [(order[i], order[(i + step) % count]) for i in...]
    all_to_all x8 -> x1, waiting for transfers between devices: 157 us -> 0.01 us  [per_device(): lax.all_to_all(grad_weights, 'dp', split_axis=0, concat_axis=0, tiled=True)]
    all_gather x2 -> x0, blocking collectives: 155 us -> none  [the longest x1 110 us: per_device(): lax.all_gather(router_weight, ('dp', 'fsdp'), axis=0, tiled=True)]
    ppermute x0 -> x86, starting transfers between devices: none -> 98.3 us  [the longest x56 69.6 us: shift(): lax.ppermute(value, 'dp', [(order[i], order[(i + step) % count]) for i in...]
    unnamed x2 -> x0, blocking collectives: 81.8 us -> none
  transfers between devices with their start and end apart: 16 -> 87, of which waited for: 8 -> 45; matrix products, arithmetic and copies ran while one was open for 11% -> 6% of each run, Pallas kernels for 0% -> 20%
where the time goes in v1:
time: 641 us; the launch traced here: 631 us
  Pallas kernels  213 us (33%)
  waiting for transfers between devices  179 us (28%)
  starting transfers between devices  103 us (16%)
  between operations  64.8 us (10%)
  local copies, waits for them, and re-layouts  56.1 us (9%)
  other arithmetic  15.4 us (2%)
    ppermute x56, waiting for transfers between devices, shift(): lax.ppermute(value, 'dp', [(order[i], order[(i + step) % count]) for i in...  136 us
    ppermute x56, starting transfers between devices, shift(): lax.ppermute(value, 'dp', [(order[i], order[(i + step) % count]) for i in...  69.6 us
    pallas_call x1, Pallas kernels, attn_bwd(): pl.pallas_call(functools.partial(attn_bwd_kernel, width, length, begin, c...  61.9 us
    ppermute x16, waiting for transfers between devices, flip(): return lax.ppermute(value, axis, [(i, i ^ bit) for i in range(count)])  34.3 us
    pallas_call x1, Pallas kernels, attn_fwd(): pl.pallas_call(functools.partial(attn_fwd_kernel, width, begin, count), g...  27.9 us
    unnamed x52, local copies, waits for them, and re-layouts  25.2 us
    pallas_call x1, Pallas kernels, pull_tokens(): pl.pallas_call(tokens_kernel, grid=(rows, length // tile), in_specs=[bloc...  24.4 us
    ppermute x14, starting transfers between devices, turn(): lax.ppermute(value, axis, [(i, (i + step) % count) for i in range(count)])  19.7 us
  transfers between devices with their start and end apart: 87, of which 45 were waited for; matrix products, arithmetic and copies ran while one was open for 6% of the time, Pallas kernels for 20%

profile of v1, /device:TPU:0, one launch (start us, length us, event | category | flops | bytes accessed | tf_op | source)
XLA Modules:
  0.0 630.9 jit_solution(17748341388084221893)
XLA Ops:
  100.8 11.5 %join.1.joined_ref = bf16[4,1024,1536]{2,1,0:T(8,128)(2,1)} custom-call(bf16[4,1024,512]{2,1,0:T(8,128)(2,1)S(1)} %bitcast.387, f32[8,512]{1,0:T(8,128)S(1)} %copy.128.gains_ref, bf16[512,2176]{1,0:T(8,128)(2,1)S(1)} %bitcast.377), custom_call_target="tpu_custom_call" | custom-call | flops 6442450944 | bytes 16777216 | tf_op jit(solution)/shard_map/join/pallas_call | solution.py:236
  112.3 27.9 %attend.1.attended_ref = bf16[4,1024,512]{2,1,0:T(8,128)(2,1)S(1)} custom-call(s32[4,8]{1,0:T(4,128)S(1)} %add_select_fusion.lo_ref, s32[4]{0:T(128)S(1)} %fusion.57.vlen_ref, s32[4,8,128]{2,1,0:T(8,128)S(1)} %select_select_fusion.start_ref, bf16[4,1024,1536]{2,1,0:T(8,128)(2,1)} %join.1.joined_ref), custom_call_target="tpu_custom_call" | custom-call | flops 13421772800 | bytes 12582912 | tf_op jit(solution)/shard_map/attend/pallas_call | solution.py:100
  140.2 9.6 %mix.1 = (f32[4,1024,512]{2,1,0:T(8,128)}, bf16[4,1024,512]{2,1,0:T(8,128)(2,1)S(1)}, f32[4,16,1024]{2,1,0:T(8,128)S(1)}) custom-call(bf16[4,1024,512]{2,1,0:T(8,128)(2,1)S(1)} %attend.1.attended_ref, bf16[4,1024,512]{2,1,0:T(8,128)(2,1)} %bitcast.385, f32[8,512]{1,0:T(8,128)S(1)} %copy.128.gains_ref, bf16[512,2176]{1,0:T(8,128)(2,1)S(1)} %bitcast.378, ...), custom_call_target="tpu_custom_call" | custom-call | flops 2147483648 | bytes 20971520 | tf_op jit(solution)/shard_map/mix/pallas_call | solution.py:266
  186.6 5.4 pool.3
  196.2 5.5 collective-permute-done.57
  218.0 12.6 %collective-permute-done.25 = bf16[2,128,512]{2,1,0:T(8,128)(2,1)S(1)} collective-permute-done((bf16[2,128,512]{2,1,0:T(8,128)(2,1)S(1)}, bf16[2,128,512]{2,1,0:T(8,128)(2,1)S(1)}, u32[]{:S(2)}, u32[]{:S(2)}) %collective-permute-start.25) | collective-permute-done | bytes 262176 | tf_op jit(solution)/shard_map/ppermute | solution.py:664
  252.1 13.4 %collective-permute-done.27 = bf16[2,128,512]{2,1,0:T(8,128)(2,1)S(1)} collective-permute-done((bf16[2,128,512]{2,1,0:T(8,128)(2,1)S(1)}, bf16[2,128,512]{2,1,0:T(8,128)(2,1)S(1)}, u32[]{:S(2)}, u32[]{:S(2)}) %collective-permute-start.27) | collective-permute-done | bytes 262176 | tf_op jit(solution)/shard_map/ppermute | solution.py:664
  286.8 11.9 %collective-permute-done.22 = bf16[2,128,512]{2,1,0:T(8,128)(2,1)S(1)} collective-permute-done((bf16[2,128,512]{2,1,0:T(8,128)(2,1)S(1)}, bf16[2,128,512]{2,1,0:T(8,128)(2,1)S(1)}, u32[]{:S(2)}, u32[]{:S(2)}) %collective-permute-start.22) | collective-permute-done | bytes 262176 | tf_op jit(solution)/shard_map/ppermute | solution.py:664
  313.9 9.1 %experts.1 = (bf16[4,128,512]{2,1,0:T(8,128)(2,1)S(1)}, bf16[8,512,256]{2,1,0:T(8,128)(2,1)S(1)}, f32[8,512,256]{2,1,0:T(8,128)S(1)}) custom-call(bf16[4,128,512]{2,1,0:T(8,128)(2,1)S(1)} %bitcast_dynamic-update-slice_fusion.33.pooled_ref, bf16[8,2,512,256]{3,2,1,0:T(8,128)(2,1)} %bitcast_dynamic-update-slice_fusion.16.weights_ref), custom_call_target="tpu_custom_call" | custom-call | flops 4294967296 | bytes 8388608 | tf_op jit(solution)/shard_map/experts/pallas_call | solution.py:360
  327.5 10.7 %pull_experts.1 = (bf16[4,144,512]{2,1,0:T(8,128)(2,1)S(1)}, bf16[8,2,512,256]{3,2,1,0:T(8,128)(2,1)S(1)}) custom-call(bf16[4,128,512]{2,1,0:T(8,128)(2,1)S(1)} %bitcast_dynamic-update-slice_fusion.33.pooled_ref, bf16[4,128,512]{2,1,0:T(8,128)(2,1)S(1)} %bitcast_dynamic-update-slice_fusion.27.grads_ref, ...), custom_call_target="tpu_custom_call" | custom-call | flops 6442450944 | bytes 8388608 | tf_op jit(solution)/shard_map/pull_experts/pallas_call | solution.py:425
  347.1 12.9 %collective-permute-start.44 = (bf16[4,128,512]{2,1,0:T(8,128)(2,1)S(1)}, bf16[4,128,512]{2,1,0:T(8,128)(2,1)S(1)}, u32[]{:S(2)}, u32[]{:S(2)}) collective-permute-start(bf16[4,128,512]{2,1,0:T(8,128)(2,1)S(1)} %bitcast_dynamic-update-slice_fusion.30), channel_id=1, source_target_pairs={{0,4},{8,0},{16,8},{24,16},{28,24},{20,28},{12,20},{4,12},{1,5},{9... | collective-permute-start | bytes 1572872 | tf_op jit(solution)/shard_map/ppermute | solution.py:664
  364.0 9.4 %collective-permute-done.44 = bf16[4,128,512]{2,1,0:T(8,128)(2,1)S(1)} collective-permute-done((bf16[4,128,512]{2,1,0:T(8,128)(2,1)S(1)}, bf16[4,128,512]{2,1,0:T(8,128)(2,1)S(1)}, u32[]{:S(2)}, u32[]{:S(2)}) %collective-permute-start.44) | collective-permute-done | bytes 524320 | tf_op jit(solution)/shard_map/ppermute | solution.py:664
  377.4 8.6 %collective-permute-done.71 = bf16[4,144,512]{2,1,0:T(8,128)(2,1)S(1)} collective-permute-done((bf16[4,144,512]{2,1,0:T(8,128)(2,1)S(1)}, bf16[4,144,512]{2,1,0:T(8,128)(2,1)S(1)}, u32[]{:S(2)}, u32[]{:S(2)}) %collective-permute-start.71) | collective-permute-done | bytes 589856 | tf_op jit(solution)/shard_map/ppermute | solution.py:664
  388.6 8.6 %collective-permute-done.46 = bf16[4,128,512]{2,1,0:T(8,128)(2,1)S(1)} collective-permute-done((bf16[4,128,512]{2,1,0:T(8,128)(2,1)S(1)}, bf16[4,128,512]{2,1,0:T(8,128)(2,1)S(1)}, u32[]{:S(2)}, u32[]{:S(2)}) %collective-permute-start.46) | collective-permute-done | bytes 524320 | tf_op jit(solution)/shard_map/ppermute | solution.py:664
  401.3 8.6 %collective-permute-done.73 = bf16[4,144,512]{2,1,0:T(8,128)(2,1)S(1)} collective-permute-done((bf16[4,144,512]{2,1,0:T(8,128)(2,1)S(1)}, bf16[4,144,512]{2,1,0:T(8,128)(2,1)S(1)}, u32[]{:S(2)}, u32[]{:S(2)}) %collective-permute-start.73) | collective-permute-done | bytes 589856 | tf_op jit(solution)/shard_map/ppermute | solution.py:664
  412.5 8.6 %collective-permute-done.48 = bf16[4,128,512]{2,1,0:T(8,128)(2,1)S(1)} collective-permute-done((bf16[4,128,512]{2,1,0:T(8,128)(2,1)S(1)}, bf16[4,128,512]{2,1,0:T(8,128)(2,1)S(1)}, u32[]{:S(2)}, u32[]{:S(2)}) %collective-permute-start.48) | collective-permute-done | bytes 524320 | tf_op jit(solution)/shard_map/ppermute | solution.py:664
  425.2 8.5 %collective-permute-done.75 = bf16[4,144,512]{2,1,0:T(8,128)(2,1)S(1)} collective-permute-done((bf16[4,144,512]{2,1,0:T(8,128)(2,1)S(1)}, bf16[4,144,512]{2,1,0:T(8,128)(2,1)S(1)}, u32[]{:S(2)}, u32[]{:S(2)}) %collective-permute-start.75) | collective-permute-done | bytes 589856 | tf_op jit(solution)/shard_map/ppermute | solution.py:664
  435.8 17.1 %spread.1 = (bf16[4,1024,512]{2,1,0:T(8,128)(2,1)}, f32[1024,16]{1,0:T(8,128)S(1)}) custom-call(f32[1024,16]{1,0:T(8,128)S(1)} %bitcast.383, bf16[8,4,128,512]{3,2,1,0:T(8,128)(2,1)S(1)} %bitcast_dynamic-update-slice_fusion.8.result_ref, bf16[4,1024,512]{2,1,0:T(8,128)(2,1)S(1)} %bitcast.375, f32[4,1024,512]{2,1,0:T(8,128)} %get-tuple-element.42.hidden_ref), custom_call_target="tpu_custom_call" | custom-call | flops 419430400 | bytes 20971520 | tf_op jit(solution)/shard_map/spread/pallas_call | solution.py:477
  459.1 14.6 %pull_gates.1 = (bf16[4,1024,512]{2,1,0:T(8,128)(2,1)S(1)}, f32[4,512]{1,0:T(4,128)S(1)}) custom-call(f32[1024,16]{1,0:T(8,128)S(1)} %bitcast.384, f32[1024,16]{1,0:T(8,128)S(1)} %copy.137.inner_ref, f32[1024,16]{1,0:T(8,128)S(1)} %copy-done.10, bf16[8,4,144,512]{3,2,1,0:T(8,128)(2,1)} %bitcast_dynamic-update-slice_fusion.pooled_ref, ...), custom_call_target="tpu_custom_call" | custom-call | flops 419430400 | bytes 20971520 | tf_op jit(solution)/shard_map/pull_gates/pallas_call | solution.py:541
  475.8 15.8 %pull_hidden.1 = (f32[4,1024,512]{2,1,0:T(8,128)}, bf16[4,1024,512]{2,1,0:T(8,128)(2,1)}, f32[512,512]{1,0:T(8,128)S(1)}, f32[8,512]{1,0:T(8,128)S(1)}) custom-call(bf16[4,1024,512]{2,1,0:T(8,128)(2,1)} %copy-done.5, f32[4,1024,512]{2,1,0:T(8,128)} %get-tuple-element.42.hidden_ref, bf16[4,1024,512]{2,1,0:T(8,128)(2,1)} %bitcast.373, ...), custom_call_target="tpu_custom_call" | custom-call | flops 4294967296 | bytes 33554432 | tf_op jit(solution)/shard_map/pull_hidden/pallas_call | solution.py:586
  496.1 61.9 %attend_back.1 = (bf16[4,1024,512]{2,1,0:T(8,128)(2,1)}, f32[4,1024,512]{2,1,0:T(8,128)}, f32[4,1024,512]{2,1,0:T(8,128)}) custom-call(s32[4,8]{1,0:T(4,128)} %copy-done.12, s32[4]{0:T(128)} %copy-done.13, s32[4,8,128]{2,1,0:T(8,128)} %copy-done.11, bf16[4,1024,1536]{2,1,0:T(8,128)(2,1)} %join.1.joined_ref, bf16[4,1024,512]{2,1,0:T(8,128)(2,1)} %get-tuple-element.51.grad_ref), custom_call_target="tpu_custom_call" | custom-call | flops 33554432000 | bytes 25165824 | tf_op jit(solution)/shard_map/attend_back/pallas_call | solution.py:195
  558.0 24.4 %pull_tokens.1 = (f32[4,1024,512]{2,1,0:T(8,128)}, f32[512,1536]{1,0:T(8,128)S(1)}, f32[8,512]{1,0:T(8,128)S(1)}) custom-call(bf16[4,1024,512]{2,1,0:T(8,128)(2,1)} %get-tuple-element.52.query_ref, f32[4,1024,512]{2,1,0:T(8,128)} %get-tuple-element.53.keys_ref, f32[4,1024,512]{2,1,0:T(8,128)} %get-tuple-element.54.values_ref, ...), custom_call_target="tpu_custom_call" | custom-call | flops 12884901888 | bytes 41943040 | tf_op jit(solution)/shard_map/pull_tokens/pallas_call | solution.py:635
  591.4 14.6 %collective-permute-done.78 = bf16[8,16,2176]{2,1,0:T(8,128)(2,1)S(1)} collective-permute-done((bf16[8,16,2176]{2,1,0:T(8,128)(2,1)S(1)}, bf16[8,16,2176]{2,1,0:T(8,128)(2,1)S(1)}, u32[]{:S(2)}, u32[]{:S(2)}) %collective-permute-start.78) | collective-permute-done | bytes 557088 | tf_op jit(solution)/shard_map/ppermute | solution.py:669
  615.5 5.9 collective-permute-done.82
  (369 shorter events, 229.1 us)
Async XLA Ops:
  5.4 41.5 %collective-permute-start = (bf16[16,2176]{1,0:T(8,128)(2,1)S(1)}, bf16[16,2176]{1,0:T(8,128)(2,1)S(1)}, u32[]{:S(2)}, u32[]{:S(2)}) collective-permute-start(bf16[16,2176]{1,0:T(8,128)(2,1)S(1)} %fusion.52), channel_id=1, source_target_pairs={{0,8},{8,16},{16,24},{24,28},{28,20},{20,12},{12,4},{4,0},{1,9},{9... | collective-permute-start | bytes 208904 | tf_op jit(solution)/shard_map/ppermute | solution.py:664
  8.4 40.6 %collective-permute-start.1 = (bf16[16,2176]{1,0:T(8,128)(2,1)S(1)}, bf16[16,2176]{1,0:T(8,128)(2,1)S(1)}, u32[]{:S(2)}, u32[]{:S(2)}) collective-permute-start(bf16[16,2176]{1,0:T(8,128)(2,1)S(1)} %fusion.52), channel_id=1, source_target_pairs={{0,4},{8,0},{16,8},{24,16},{28,24},{20,28},{12,20},{4,12},{1,5},{9... | collective-permute-start | bytes 208904 | tf_op jit(solution)/shard_map/ppermute | solution.py:664
  60.2 34.5 %collective-permute-start.7 = (bf16[8,1,16,2176]{3,2,1,0:T(8,128)(2,1)S(1)}, bf16[8,1,16,2176]{3,2,1,0:T(8,128)(2,1)S(1)}, u32[]{:S(2)}, u32[]{:S(2)}) collective-permute-start(bf16[8,1,16,2176]{3,2,1,0:T(8,128)(2,1)S(1)} %bitcast_dynamic-update-slice_fusion.36), channel_id=1, source_target_pairs={{0,2},{1,3},{2,0},{3,1},{4,6},{5,7},{6,4},{7,5},{8,10},{9,11},{10,... | collective-permute-start | bytes 1671176 | tf_op jit(solution)/shard_map/ppermute | solution.py:669
  172.3 31.7 %collective-permute-start.33 = (bf16[2,512,256]{2,1,0:T(8,128)(2,1)S(1)}, bf16[2,512,256]{2,1,0:T(8,128)(2,1)}, u32[]{:S(2)}, u32[]{:S(2)}) collective-permute-start(bf16[2,512,256]{2,1,0:T(8,128)(2,1)S(1)} %pad_maximum_fusion.3), channel_id=1, source_target_pairs={{0,8},{8,16},{16,24},{24,28},{28,20},{20,12},{12,4},{4,0},{1,9},{9... | collective-permute-start | bytes 1572872 | tf_op jit(solution)/shard_map/ppermute | solution.py:664
  173.9 33.1 %collective-permute-start.34 = (bf16[2,512,256]{2,1,0:T(8,128)(2,1)S(1)}, bf16[2,512,256]{2,1,0:T(8,128)(2,1)}, u32[]{:S(2)}, u32[]{:S(2)}) collective-permute-start(bf16[2,512,256]{2,1,0:T(8,128)(2,1)S(1)} %pad_maximum_fusion.3), channel_id=1, source_target_pairs={{0,4},{8,0},{16,8},{24,16},{28,24},{20,28},{12,20},{4,12},{1,5},{9... | collective-permute-start | bytes 1572872 | tf_op jit(solution)/shard_map/ppermute | solution.py:664
  206.9 33.9 %collective-permute-start.35 = (bf16[2,512,256]{2,1,0:T(8,128)(2,1)}, bf16[2,512,256]{2,1,0:T(8,128)(2,1)S(1)}, u32[]{:S(2)}, u32[]{:S(2)}) collective-permute-start(bf16[2,512,256]{2,1,0:T(8,128)(2,1)} %collective-permute-done.33), channel_id=1, source_target_pairs={{0,8},{8,16},{16,24},{24,28},{28,20},{20,12},{12,4},{4,0},{1,9},{9... | collective-permute-start | bytes 1572872 | tf_op jit(solution)/shard_map/ppermute | solution.py:664
  209.9 32.8 %collective-permute-start.36 = (bf16[2,512,256]{2,1,0:T(8,128)(2,1)}, bf16[2,512,256]{2,1,0:T(8,128)(2,1)S(1)}, u32[]{:S(2)}, u32[]{:S(2)}) collective-permute-start(bf16[2,512,256]{2,1,0:T(8,128)(2,1)} %collective-permute-done.34), channel_id=1, source_target_pairs={{0,4},{8,0},{16,8},{24,16},{28,24},{20,28},{12,20},{4,12},{1,5},{9... | collective-permute-start | bytes 1572872 | tf_op jit(solution)/shard_map/ppermute | solution.py:664
  242.7 33.5 %collective-permute-start.37 = (bf16[2,512,256]{2,1,0:T(8,128)(2,1)S(1)}, bf16[2,512,256]{2,1,0:T(8,128)(2,1)S(1)}, u32[]{:S(2)}, u32[]{:S(2)}) collective-permute-start(bf16[2,512,256]{2,1,0:T(8,128)(2,1)S(1)} %collective-permute-done.35), channel_id=1, source_target_pairs={{0,8},{8,16},{16,24},{24,28},{28,20},{20,12},{12,4},{4,0},{1,9},{9... | collective-permute-start | bytes 1572872 | tf_op jit(solution)/shard_map/ppermute | solution.py:664
  243.6 34.1 %collective-permute-start.38 = (bf16[2,512,256]{2,1,0:T(8,128)(2,1)S(1)}, bf16[2,512,256]{2,1,0:T(8,128)(2,1)S(1)}, u32[]{:S(2)}, u32[]{:S(2)}) collective-permute-start(bf16[2,512,256]{2,1,0:T(8,128)(2,1)S(1)} %collective-permute-done.36), channel_id=1, source_target_pairs={{0,4},{8,0},{16,8},{24,16},{28,24},{20,28},{12,20},{4,12},{1,5},{9... | collective-permute-start | bytes 1572872 | tf_op jit(solution)/shard_map/ppermute | solution.py:664
  277.7 35.4 %collective-permute-start.39 = (bf16[2,512,256]{2,1,0:T(8,128)(2,1)S(1)}, bf16[2,512,256]{2,1,0:T(8,128)(2,1)S(1)}, u32[]{:S(2)}, u32[]{:S(2)}) collective-permute-start(bf16[2,512,256]{2,1,0:T(8,128)(2,1)S(1)} %collective-permute-done.37), channel_id=1, source_target_pairs={{0,8},{8,16},{16,24},{24,28},{28,20},{20,12},{12,4},{4,0},{1,9},{9... | collective-permute-start | bytes 1572872 | tf_op jit(solution)/shard_map/ppermute | solution.py:664
  340.3 20.2 %collective-permute-start.68 = (bf16[144,512]{1,0:T(8,128)(2,1)S(1)}, bf16[144,512]{1,0:T(8,128)(2,1)S(1)}, u32[]{:S(2)}, u32[]{:S(2)}) collective-permute-start(bf16[144,512]{1,0:T(8,128)(2,1)S(1)} %get-tuple-element.132), channel_id=1, source_target_pairs={{0,2},{1,3},{2,0},{3,1},{4,6},{5,7},{6,4},{7,5},{8,10},{9,11},{10,... | collective-permute-start | bytes 442376 | tf_op jit(solution)/shard_map/ppermute | solution.py:669
  347.1 26.3 %collective-permute-start.44 = (bf16[4,128,512]{2,1,0:T(8,128)(2,1)S(1)}, bf16[4,128,512]{2,1,0:T(8,128)(2,1)S(1)}, u32[]{:S(2)}, u32[]{:S(2)}) collective-permute-start(bf16[4,128,512]{2,1,0:T(8,128)(2,1)S(1)} %bitcast_dynamic-update-slice_fusion.30), channel_id=1, source_target_pairs={{0,4},{8,0},{16,8},{24,16},{28,24},{20,28},{12,20},{4,12},{1,5},{9... | collective-permute-start | bytes 1572872 | tf_op jit(solution)/shard_map/ppermute | solution.py:664
  361.2 24.8 %collective-permute-start.71 = (bf16[4,144,512]{2,1,0:T(8,128)(2,1)S(1)}, bf16[4,144,512]{2,1,0:T(8,128)(2,1)S(1)}, u32[]{:S(2)}, u32[]{:S(2)}) collective-permute-start(bf16[4,144,512]{2,1,0:T(8,128)(2,1)S(1)} %bitcast_dynamic-update-slice_fusion.24), channel_id=1, source_target_pairs={{0,4},{8,0},{16,8},{24,16},{28,24},{20,28},{12,20},{4,12},{1,5},{9... | collective-permute-start | bytes 1769480 | tf_op jit(solution)/shard_map/ppermute | solution.py:664
  363.3 24.7 %collective-permute-start.45 = (bf16[4,128,512]{2,1,0:T(8,128)(2,1)S(1)}, bf16[4,128,512]{2,1,0:T(8,128)(2,1)S(1)}, u32[]{:S(2)}, u32[]{:S(2)}) collective-permute-start(bf16[4,128,512]{2,1,0:T(8,128)(2,1)S(1)} %collective-permute-done.43), channel_id=1, source_target_pairs={{0,8},{8,16},{16,24},{24,28},{28,20},{20,12},{12,4},{4,0},{1,9},{9... | collective-permute-start | bytes 1572872 | tf_op jit(solution)/shard_map/ppermute | solution.py:664
  373.4 23.9 %collective-permute-start.46 = (bf16[4,128,512]{2,1,0:T(8,128)(2,1)S(1)}, bf16[4,128,512]{2,1,0:T(8,128)(2,1)S(1)}, u32[]{:S(2)}, u32[]{:S(2)}) collective-permute-start(bf16[4,128,512]{2,1,0:T(8,128)(2,1)S(1)} %collective-permute-done.44), channel_id=1, source_target_pairs={{0,4},{8,0},{16,8},{24,16},{28,24},{20,28},{12,20},{4,12},{1,5},{9... | collective-permute-start | bytes 1572872 | tf_op jit(solution)/shard_map/ppermute | solution.py:664
  376.8 23.9 %collective-permute-start.72 = (bf16[4,144,512]{2,1,0:T(8,128)(2,1)S(1)}, bf16[4,144,512]{2,1,0:T(8,128)(2,1)S(1)}, u32[]{:S(2)}, u32[]{:S(2)}) collective-permute-start(bf16[4,144,512]{2,1,0:T(8,128)(2,1)S(1)} %collective-permute-done.70), channel_id=1, source_target_pairs={{0,8},{8,16},{16,24},{24,28},{28,20},{20,12},{12,4},{4,0},{1,9},{9... | collective-permute-start | bytes 1769480 | tf_op jit(solution)/shard_map/ppermute | solution.py:664
  386.0 23.9 %collective-permute-start.73 = (bf16[4,144,512]{2,1,0:T(8,128)(2,1)S(1)}, bf16[4,144,512]{2,1,0:T(8,128)(2,1)S(1)}, u32[]{:S(2)}, u32[]{:S(2)}) collective-permute-start(bf16[4,144,512]{2,1,0:T(8,128)(2,1)S(1)} %collective-permute-done.71), channel_id=1, source_target_pairs={{0,4},{8,0},{16,8},{24,16},{28,24},{20,28},{12,20},{4,12},{1,5},{9... | collective-permute-start | bytes 1769480 | tf_op jit(solution)/shard_map/ppermute | solution.py:664
  388.0 23.9 %collective-permute-start.47 = (bf16[4,128,512]{2,1,0:T(8,128)(2,1)S(1)}, bf16[4,128,512]{2,1,0:T(8,128)(2,1)S(1)}, u32[]{:S(2)}, u32[]{:S(2)}) collective-permute-start(bf16[4,128,512]{2,1,0:T(8,128)(2,1)S(1)} %collective-permute-done.45), channel_id=1, source_target_pairs={{0,8},{8,16},{16,24},{24,28},{28,20},{20,12},{12,4},{4,0},{1,9},{9... | collective-permute-start | bytes 1572872 | tf_op jit(solution)/shard_map/ppermute | solution.py:664
  397.2 23.9 %collective-permute-start.48 = (bf16[4,128,512]{2,1,0:T(8,128)(2,1)S(1)}, bf16[4,128,512]{2,1,0:T(8,128)(2,1)S(1)}, u32[]{:S(2)}, u32[]{:S(2)}) collective-permute-start(bf16[4,128,512]{2,1,0:T(8,128)(2,1)S(1)} %collective-permute-done.46), channel_id=1, source_target_pairs={{0,4},{8,0},{16,8},{24,16},{28,24},{20,28},{12,20},{4,12},{1,5},{9... | collective-permute-start | bytes 1572872 | tf_op jit(solution)/shard_map/ppermute | solution.py:664
  400.7 23.9 %collective-permute-start.74 = (bf16[4,144,512]{2,1,0:T(8,128)(2,1)S(1)}, bf16[4,144,512]{2,1,0:T(8,128)(2,1)S(1)}, u32[]{:S(2)}, u32[]{:S(2)}) collective-permute-start(bf16[4,144,512]{2,1,0:T(8,128)(2,1)S(1)} %collective-permute-done.72), channel_id=1, source_target_pairs={{0,8},{8,16},{16,24},{24,28},{28,20},{20,12},{12,4},{4,0},{1,9},{9... | collective-permute-start | bytes 1769480 | tf_op jit(solution)/shard_map/ppermute | solution.py:664
  409.9 23.8 %collective-permute-start.75 = (bf16[4,144,512]{2,1,0:T(8,128)(2,1)S(1)}, bf16[4,144,512]{2,1,0:T(8,128)(2,1)S(1)}, u32[]{:S(2)}, u32[]{:S(2)}) collective-permute-start(bf16[4,144,512]{2,1,0:T(8,128)(2,1)S(1)} %collective-permute-done.73), channel_id=1, source_target_pairs={{0,4},{8,0},{16,8},{24,16},{28,24},{20,28},{12,20},{4,12},{1,5},{9... | collective-permute-start | bytes 1769480 | tf_op jit(solution)/shard_map/ppermute | solution.py:664
  411.9 23.9 %collective-permute-start.49 = (bf16[4,128,512]{2,1,0:T(8,128)(2,1)S(1)}, bf16[4,128,512]{2,1,0:T(8,128)(2,1)S(1)}, u32[]{:S(2)}, u32[]{:S(2)}) collective-permute-start(bf16[4,128,512]{2,1,0:T(8,128)(2,1)S(1)} %collective-permute-done.47), channel_id=1, source_target_pairs={{0,8},{8,16},{16,24},{24,28},{28,20},{20,12},{12,4},{4,0},{1,9},{9... | collective-permute-start | bytes 1572872 | tf_op jit(solution)/shard_map/ppermute | solution.py:664
  424.5 29.2 %collective-permute-start.76 = (bf16[4,144,512]{2,1,0:T(8,128)(2,1)S(1)}, bf16[4,144,512]{2,1,0:T(8,128)(2,1)S(1)}, u32[]{:S(2)}, u32[]{:S(2)}) collective-permute-start(bf16[4,144,512]{2,1,0:T(8,128)(2,1)S(1)} %collective-permute-done.74), channel_id=1, source_target_pairs={{0,8},{8,16},{16,24},{24,28},{28,20},{20,12},{12,4},{4,0},{1,9},{9... | collective-permute-start | bytes 1769480 | tf_op jit(solution)/shard_map/ppermute | solution.py:664
  491.5 134.4 %all-to-all-start = ((bf16[8,2,512,256]{3,2,1,0:T(8,128)(2,1)}), bf16[8,2,512,256]{3,2,1,0:T(8,128)(2,1)}, u32[]{:S(2)}, u32[]{:S(2)}) async-start(bf16[8,2,512,256]{3,2,1,0:T(8,128)(2,1)} %copy-done.6), calls=%async_computation | async-start | bytes 8388608 | tf_op jit(solution)/shard_map/all_to_all | solution.py:841
  (83 other events, 976.6 us)

commit v2 on v1

v2 whole, which is shorter than its diff:
```python
import functools, math
import jax
import jax.numpy as jnp
import numpy as np
from jax import lax
from jax.experimental import pallas as pl
from jax.experimental.pallas import tpu as pltpu
from jax.sharding import PartitionSpec as P

NEGATIVE = -1e30
QB = 128
F32 = jnp.float32
BF16 = jnp.bfloat16
NT = (((1,), (1,)), ((), ()))
TN = (((0,), (0,)), ((), ()))


def dot(a, b):
    return jnp.dot(a, b, preferred_element_type=F32)


def dot_nt(a, b):
    return lax.dot_general(a, b, NT, preferred_element_type=F32)


def dot_tn(a, b):
    return lax.dot_general(a, b, TN, preferred_element_type=F32)


def iota(shape, axis):
    return lax.broadcasted_iota(jnp.int32, shape, axis)


def split_heads(x):
    low = iota(x.shape, 1) < 64
    zero = jnp.zeros_like(x)
    return jnp.concatenate([jnp.where(low, x, zero), jnp.where(low, zero, x)], axis=0)


def join_heads(x):
    half = x.shape[0] // 2
    low = iota((half, x.shape[1]), 1) < 64
    return jnp.where(low, x[:half], x[half:])


def attn_fwd_kernel(width, begin, count, lo_ref, vlen_ref, start_ref, joined_ref, out_ref, bias_ref):
    row = pl.program_id(0)
    vlen = vlen_ref[row]

    def block(step, _):
        qb = step + begin
        lo = lo_ref[row, qb]
        base = pl.multiple_of(qb * QB, QB)
        first = pl.multiple_of(lo * QB, QB)
        own = pl.ds(base, QB)
        target = pl.ds(pl.multiple_of(step * QB, QB), QB)

        def variant(blocks):
            span = blocks * QB
            keys = pl.ds(first, span)
            begins = jnp.broadcast_to(start_ref[0, pl.ds(qb, 1), :], (QB, QB)).T
            i = base + iota((QB, QB), 0)
            for b in range(blocks):
                j = first + b * QB + iota((QB, QB), 1)
                ok = ((j >= begins) & (j <= i) & (j < vlen)) | (j == i)
                bias_ref[:, b * QB:(b + 1) * QB] = jnp.where(ok, 0.0, NEGATIVE)
            bias = bias_ref[:, :span]
            bias = jnp.concatenate([bias, bias], axis=0)
            at = [pl.ds(lane, 128) for lane in range(0, width, 128)]
            key_at = [pl.ds(width + lane, 128) for lane in range(0, width, 128)]
            value_at = [pl.ds(2 * width + lane, 128) for lane in range(0, width, 128)]
            query = [split_heads(joined_ref[0, own, lanes] * jnp.asarray(0.125, BF16)) for lanes in at]
            scores = [dot_nt(q, joined_ref[0, keys, lanes]) for q, lanes in zip(query, key_at)]
            scores = [s + bias for s in scores]
            tops = [jnp.max(s, axis=1, keepdims=True) for s in scores]
            raised = [jnp.exp(s - top) for s, top in zip(scores, tops)]
            totals = [jnp.sum(p, axis=1, keepdims=True) for p in raised]
            out = [dot(p.astype(BF16), joined_ref[0, keys, lanes]) for p, lanes in zip(raised, value_at)]
            for o, total, lanes in zip(out, totals, at):
                out_ref[0, target, lanes] = join_heads(o * (1.0 / total)).astype(BF16)

        for blocks in range(1, 6):
            pl.when(qb - lo + 1 == blocks)(functools.partial(variant, blocks))
        return 0

    lax.fori_loop(0, count, block, 0)


def attn_fwd(joined, starts, lows, vlens, begin, count):
    rows, length, triple = joined.shape
    width = triple // 3
    spec = pltpu.PrefetchScalarGridSpec(
        num_scalar_prefetch=2,
        grid=(rows,),
        in_specs=[
            pl.BlockSpec((1, length // QB, QB), lambda r, *_: (r, 0, 0)),
            pl.BlockSpec((1, length, triple), lambda r, *_: (r, 0, 0)),
        ],
        out_specs=pl.BlockSpec((1, count * QB, width), lambda r, *_: (r, 0, 0)),
        scratch_shapes=[pltpu.VMEM((QB, 5 * QB), F32)],
    )
    return pl.pallas_call(
        functools.partial(attn_fwd_kernel, width, begin, count),
        grid_spec=spec,
        out_shape=jax.ShapeDtypeStruct((rows, count * QB, width), BF16),
        compiler_params=pltpu.CompilerParams(vmem_limit_bytes=48 << 20),
        cost_estimate=pl.CostEstimate(flops=rows * count * QB * 400 * 8 * 256 * 4, bytes_accessed=rows * length * triple * 2, transcendentals=0),
        name="attend",
    )(lows, vlens, starts, joined)


def attn_bwd_kernel(width, row_from, count, lo_ref, vlen_ref, start_ref, joined_ref, grad_ref, *rest):
    out_ref, dk_ref, dv_ref, bias_ref = rest[-4:]
    row = pl.program_id(0) + row_from
    vlen = vlen_ref[row]
    dk_ref[...] = jnp.zeros_like(dk_ref)
    dv_ref[...] = jnp.zeros_like(dv_ref)

    def block(step, _):
        qb = step
        lo = lo_ref[row, qb]
        base = pl.multiple_of(qb * QB, QB)
        first = pl.multiple_of(lo * QB, QB)
        own = pl.ds(base, QB)
        target = pl.ds(pl.multiple_of(step * QB, QB), QB)

        def variant(blocks):
            span = blocks * QB
            keys = pl.ds(first, span)
            begins = start_ref[0, pl.ds(qb, 1), :]
            i = base + iota((QB, QB), 1)
            for b in range(blocks):
                j = first + b * QB + iota((QB, QB), 0)
                ok = ((j >= begins) & (j <= i) & (j < vlen)) | (j == i)
                bias_ref[b * QB:(b + 1) * QB, :] = jnp.where(ok, 0.0, NEGATIVE)
            bias = bias_ref[:span, :]
            bias = jnp.concatenate([bias, bias], axis=1)
            at = [pl.ds(lane, 128) for lane in range(0, width, 128)]
            key_at = [pl.ds(width + lane, 128) for lane in range(0, width, 128)]
            value_at = [pl.ds(2 * width + lane, 128) for lane in range(0, width, 128)]
            query = [split_heads(joined_ref[0, own, lanes] * jnp.asarray(0.125, BF16)) for lanes in at]
            grads = [split_heads(grad_ref[0, target, lanes]) for lanes in at]
            scores = [dot_nt(joined_ref[0, keys, lanes], q) for q, lanes in zip(query, key_at)]
            change = [dot_nt(joined_ref[0, keys, lanes], g) for g, lanes in zip(grads, value_at)]
            scores = [s + bias for s in scores]
            tops = [jnp.max(s, axis=0, keepdims=True) for s in scores]
            prob = [jnp.exp(s - top) for s, top in zip(scores, tops)]
            totals = [1.0 / jnp.sum(p, axis=0, keepdims=True) for p in prob]
            prob = [p * total for p, total in zip(prob, totals)]
            scaled = [p * c for p, c in zip(prob, change)]
            sums = [jnp.sum(t, axis=0, keepdims=True) for t in scaled]
            moved = [(t - p * total).astype(BF16) for t, p, total in zip(scaled, prob, sums)]
            for p, g, lanes in zip(prob, grads, at):
                dv_ref[keys, lanes] += dot(p.astype(BF16), g)
            for m, q, lanes in zip(moved, query, at):
                dk_ref[keys, lanes] += dot(m, q)
            back = [dot_tn(m, joined_ref[0, keys, lanes]) for m, lanes in zip(moved, key_at)]
            for b, lanes in zip(back, at):
                out_ref[0, target, lanes] = (join_heads(b) * 0.125).astype(BF16)

        for blocks in range(1, 6):
            pl.when(qb - lo + 1 == blocks)(functools.partial(variant, blocks))
        return 0

    lax.fori_loop(0, count, block, 0)
    out_ref[0, :, width: 2 * width] = dk_ref[...].astype(BF16)
    out_ref[0, :, 2 * width:] = dv_ref[...].astype(BF16)


def attn_bwd(joined, grads, starts, lows, vlens, row_from, row_to, held=None):
    rows, length, triple = joined.shape
    width = triple // 3
    count = length // QB
    aliased = [] if held is None else [held]
    wide = pl.BlockSpec((1, length, triple), lambda r, *_: (r + row_from, 0, 0))
    return pl.pallas_call(
        functools.partial(attn_bwd_kernel, width, row_from, count),
        grid_spec=pltpu.PrefetchScalarGridSpec(
            num_scalar_prefetch=2,
            grid=(row_to - row_from,),
            in_specs=[
                pl.BlockSpec((1, count, QB), lambda r, *_: (r + row_from, 0, 0)),
                wide,
                pl.BlockSpec((1, length, width), lambda r, *_: (r + row_from, 0, 0)),
            ]
            + [pl.BlockSpec(memory_space=pltpu.HBM) for _ in aliased],
            out_specs=wide,
            scratch_shapes=[
                pltpu.VMEM((length, width), F32),
                pltpu.VMEM((length, width), F32),
                pltpu.VMEM((5 * QB, QB), F32),
            ],
        ),
        out_shape=jax.ShapeDtypeStruct(joined.shape, BF16),
        input_output_aliases={5: 0} if aliased else {},
        compiler_params=pltpu.CompilerParams(vmem_limit_bytes=48 << 20),
        cost_estimate=pl.CostEstimate(
            flops=(row_to - row_from) * length * 400 * 8 * 256 * 20,
            bytes_accessed=(row_to - row_from) * length * triple * 4,
            transcendentals=0,
        ),
        name="attend_back",
    )(lows, vlens, starts, joined, grads, *aliased)


def normalise(values):
    centred = values - jnp.mean(values, axis=-1, keepdims=True)
    inverse = lax.rsqrt(jnp.mean(centred * centred, axis=-1, keepdims=True) + 1e-05)
    return centred * inverse, inverse


def pull_norm(scaled, hat, inverse):
    return inverse * (
        scaled
        - jnp.mean(scaled, axis=-1, keepdims=True)
        - hat * jnp.mean(scaled * hat, axis=-1, keepdims=True)
    )


def constant_spec(shape, *where):
    where = where or (0,) * len(shape)
    return pl.BlockSpec(shape, lambda *_: where)


def join_kernel(tokens_ref, gains_ref, weight_ref, joined_ref):
    hat, _ = normalise(tokens_ref[0].astype(F32))
    normed = (hat * gains_ref[0:1] + gains_ref[1:2]).astype(BF16)
    joined_ref[0] = dot(normed, weight_ref[...]).astype(BF16)


def join_tokens(tokens, gains, packed, tile=512):
    rows, length, width = tokens.shape
    return pl.pallas_call(
        join_kernel,
        grid=(rows, length // tile),
        in_specs=[
            pl.BlockSpec((1, tile, width), lambda r, t: (r, t, 0)),
            constant_spec(gains.shape),
            constant_spec((width, 3 * width)),
        ],
        out_specs=pl.BlockSpec((1, tile, 3 * width), lambda r, t: (r, t, 0)),
        out_shape=jax.ShapeDtypeStruct((rows, length, 3 * width), BF16),
        compiler_params=pltpu.CompilerParams(vmem_limit_bytes=40 << 20),
        cost_estimate=pl.CostEstimate(
            flops=rows * length * width * width * 6, bytes_accessed=rows * length * width * 8, transcendentals=0
        ),
        name="join",
    )(tokens, gains, packed)


def mixed_kernel(attended_ref, tokens_ref, gains_ref, weight_ref, router_ref, hidden_ref, mixed_ref, logits_ref):
    hidden = tokens_ref[0].astype(F32) + dot(attended_ref[0], weight_ref[...])
    hidden_ref[0] = hidden
    hat, _ = normalise(hidden)
    mixed = (hat * gains_ref[2:3] + gains_ref[3:4]).astype(BF16)
    mixed_ref[0] = mixed
    logits_ref[0] = dot_nt(router_ref[...], mixed)


def mix_tokens(attended, tokens, gains, packed, router, offset, tile=512):
    rows, span, width = attended.shape
    block = pl.BlockSpec((1, tile, width), lambda r, t: (r, t, 0))
    return pl.pallas_call(
        mixed_kernel,
        grid=(rows, span // tile),
        in_specs=[
            block,
            pl.BlockSpec((1, tile, width), lambda r, t: (r, t + offset // tile, 0)),
            constant_spec(gains.shape),
            constant_spec((width, width), 0, 3),
            constant_spec(router.shape),
        ],
        out_specs=[block, block, pl.BlockSpec((1, router.shape[0], tile), lambda r, t: (r, 0, t))],
        out_shape=[
            jax.ShapeDtypeStruct((rows, span, width), F32),
            jax.ShapeDtypeStruct((rows, span, width), BF16),
            jax.ShapeDtypeStruct((rows, router.shape[0], span), F32),
        ],
        compiler_params=pltpu.CompilerParams(vmem_limit_bytes=40 << 20),
        cost_estimate=pl.CostEstimate(
            flops=rows * span * width * width * 2, bytes_accessed=rows * span * width * 10, transcendentals=0
        ),
        name="mix",
    )(attended, tokens, gains, packed, router)


def pool_kernel(experts, scale, slots_ref, gates_ref, values_ref, out_ref):
    rows, places = values_ref.shape[0], values_ref.shape[1]
    sub = 16

    def step(s, _):
        here = pl.ds(pl.multiple_of(s * sub, sub), sub)
        gates = gates_ref[here, :].astype(BF16).astype(F32)
        values = [values_ref[r, here, :].astype(F32) for r in range(rows)]
        for e in range(experts):
            total = sum(gates[:, r * experts + e: r * experts + e + 1] * values[r] for r in range(rows))
            out_ref[0, e, here, :] = (scale * total).astype(BF16)
        return 0

    lax.fori_loop(0, places // sub, step, 0, unroll=2)


def pool_tokens(slots, gates, values, experts, scale):
    rows, span, width = values.shape
    owners = slots.shape[0]
    places = span // owners
    return pl.pallas_call(
        functools.partial(pool_kernel, experts, scale),
        grid_spec=pltpu.PrefetchScalarGridSpec(
            num_scalar_prefetch=1,
            grid=(owners,),
            in_specs=[
                pl.BlockSpec((places, gates.shape[1]), lambda i, slots: (slots[i], 0)),
                pl.BlockSpec((rows, places, width), lambda i, slots: (0, slots[i], 0)),
            ],
            out_specs=pl.BlockSpec((1, experts, places, width), lambda i, slots: (i, 0, 0, 0)),
        ),
        out_shape=jax.ShapeDtypeStruct((owners, experts, places, width), BF16),
        compiler_params=pltpu.CompilerParams(vmem_limit_bytes=40 << 20),
        cost_estimate=pl.CostEstimate(
            flops=rows * span * width * 1000, bytes_accessed=rows * span * width * 8, transcendentals=0
        ),
        name="pool",
    )(slots, gates, values)


CUBIC = 0.044715
SLOPE = math.sqrt(2.0 / math.pi)


def expert_kernel(steps, pooled_ref, weights_ref, result_ref, act_ref, slope_ref, total_ref):
    step = pl.program_id(0)
    blocks, places, width = pooled_ref.shape
    pooled = pooled_ref[...].reshape(blocks * places, width)
    pre = dot(pooled, weights_ref[0, 0])
    square = pre * pre
    bent = jnp.tanh(SLOPE * pre * (1.0 + CUBIC * square))
    half = 0.5 * (1.0 + bent)
    act = (pre * half).astype(BF16)
    act_ref[0] = act
    slope_ref[0] = half + 0.5 * pre * (1.0 - bent * bent) * (SLOPE * (1.0 + 3.0 * CUBIC * square))
    result = dot_nt(act, weights_ref[0, 1])

    @pl.when(step == 0)
    def _():
        total_ref[...] = result

    @pl.when(step > 0)
    def _():
        total_ref[...] += result

    @pl.when(step == steps - 1)
    def _():
        result_ref[...] = total_ref[...].astype(BF16).reshape(blocks, places, width)


def run_experts(pooled, weights):
    blocks, places, width = pooled.shape
    steps, _, _, tile = weights.shape
    count = blocks * places
    return pl.pallas_call(
        functools.partial(expert_kernel, steps),
        grid=(steps,),
        in_specs=[constant_spec(pooled.shape), pl.BlockSpec((1, 2, width, tile), lambda i: (i, 0, 0, 0))],
        out_specs=[
            constant_spec(pooled.shape),
            pl.BlockSpec((1, count, tile), lambda i: (i, 0, 0)),
            pl.BlockSpec((1, count, tile), lambda i: (i, 0, 0)),
        ],
        out_shape=[
            jax.ShapeDtypeStruct(pooled.shape, BF16),
            jax.ShapeDtypeStruct((steps, count, tile), BF16),
            jax.ShapeDtypeStruct((steps, count, tile), F32),
        ],
        scratch_shapes=[pltpu.VMEM((count, width), F32)],
        compiler_params=pltpu.CompilerParams(vmem_limit_bytes=40 << 20),
        cost_estimate=pl.CostEstimate(
            flops=count * width * tile * steps * 8, bytes_accessed=width * tile * steps * 8, transcendentals=0
        ),
        name="experts",
    )(pooled, weights)


def expert_back_kernel(steps, slots_ref, pooled_ref, grads_ref, result_ref, act_ref, slope_ref, weights_ref, back_ref, grad_ref, total_ref):
    step = pl.program_id(0)
    blocks, places, width = pooled_ref.shape
    count = blocks * places
    pooled = pooled_ref[...].reshape(count, width)
    grads = grads_ref[...].reshape(count, width)
    act = act_ref[0]
    grad_pre = (dot(grads, weights_ref[0, 1]) * slope_ref[0]).astype(BF16)
    grad_ref[0, 0] = dot_tn(pooled, grad_pre).astype(BF16)
    grad_ref[0, 1] = dot_tn(grads, act).astype(BF16)
    part = dot_nt(grad_pre, weights_ref[0, 0])

    @pl.when(step == 0)
    def _():
        total_ref[...] = part

    @pl.when(step > 0)
    def _():
        total_ref[...] += part

    @pl.when(step == steps - 1)
    def _():
        grad_pooled = total_ref[...].astype(BF16)
        back_ref[:, :places] = grad_pooled.reshape(blocks, places, width)
        result = result_ref[...].reshape(count, width)
        product = result.astype(F32) * grads.astype(F32) + grad_pooled.astype(F32) * pooled.astype(F32)
        high = product.astype(BF16)
        rest = (product - high.astype(F32)).astype(BF16)
        ones = jnp.ones((16, width), BF16)
        sums = dot_nt(ones, high) + dot_nt(ones, rest)
        top = sums.astype(BF16)
        low = (sums - top.astype(F32)).astype(BF16)
        for b in range(blocks):
            here = slice(b * places, b * places + places)
            fill = jnp.zeros((16, width - 2 * places), BF16)
            back_ref[b, places:] = jnp.concatenate([top[:, here], low[:, here], fill], axis=1)


def pull_experts(slots, pooled, grads, result, act, slope, weights):
    blocks, places, width = pooled.shape
    steps, _, _, tile = weights.shape
    count = blocks * places
    return pl.pallas_call(
        functools.partial(expert_back_kernel, steps),
        grid_spec=pltpu.PrefetchScalarGridSpec(
            num_scalar_prefetch=1,
            grid=(steps,),
            in_specs=[constant_spec(pooled.shape)] * 3
            + [pl.BlockSpec((1, count, tile), lambda i, slots: (i, 0, 0))] * 2
            + [pl.BlockSpec((1, 2, width, tile), lambda i, slots: (i, 0, 0, 0))],
            out_specs=[
                constant_spec((blocks, places + 16, width)),
                pl.BlockSpec((1, 2, width, tile), lambda i, slots: (slots[i], 0, 0, 0)),
            ],
            scratch_shapes=[pltpu.VMEM((count, width), F32)],
        ),
        out_shape=[
            jax.ShapeDtypeStruct((blocks, places + 16, width), BF16),
            jax.ShapeDtypeStruct(weights.shape, BF16),
        ],
        compiler_params=pltpu.CompilerParams(vmem_limit_bytes=40 << 20),
        cost_estimate=pl.CostEstimate(
            flops=count * width * tile * steps * 12, bytes_accessed=width * tile * steps * 8, transcendentals=0
        ),
        name="pull_experts",
    )(slots, pooled, grads, result, act, slope, weights)


def spread_kernel(group, count, slots_ref, gates_ref, grads_ref, hidden_ref, *rest):
    parts, (out_ref, change_ref, result_ref) = rest[:count], rest[-3:]
    for k in range(count):
        @pl.when(pl.program_id(0) == k)
        def _():
            result_ref[...] = parts[k][...]

    rows, places = grads_ref.shape[0], grads_ref.shape[1]
    experts = result_ref.shape[0]
    sub = 16
    columns = gates_ref.shape[1]

    def step(s, _):
        here = pl.ds(pl.multiple_of(s * sub, sub), sub)
        results = [result_ref[e, here, :].astype(F32) * group for e in range(experts)]
        gates = gates_ref[here, :].astype(BF16).astype(F32)
        lane = iota((sub, columns), 1)
        changes = jnp.zeros((sub, columns), F32)
        for r in range(rows):
            grads = grads_ref[r, here, :].astype(F32)
            for e in range(experts):
                both = jnp.sum(grads * results[e], axis=1, keepdims=True)
                changes = jnp.where(lane == r * experts + e, both, changes)
            total = sum(gates[:, r * experts + e: r * experts + e + 1] * results[e] for e in range(experts))
            out_ref[r, here, :] = (hidden_ref[r, here, :] + total.astype(BF16).astype(F32)).astype(BF16)
        change_ref[0, here, :] = changes
        return 0

    lax.fori_loop(0, places // sub, step, 0, unroll=2)


def slot_of(found):
    found = list(found)
    step = found[-1] - found[0]
    return lambda i, slots: slots[found[0] + i * step]


def spread_tokens(found, slots, gates, cotangent, hidden, group, held):
    rows, span, width = hidden.shape
    parts = list(found.values())
    experts, places, _ = parts[0].shape
    at = slot_of(found)
    block = pl.BlockSpec((rows, places, width), lambda i, slots: (0, at(i, slots), 0))
    columns = gates.shape[1]
    aliased = [] if held is None else [held]
    return pl.pallas_call(
        functools.partial(spread_kernel, group, len(parts)),
        grid_spec=pltpu.PrefetchScalarGridSpec(
            num_scalar_prefetch=1,
            grid=(len(parts),),
            in_specs=[pl.BlockSpec((places, columns), lambda i, slots: (at(i, slots), 0)), block, block]
            + [constant_spec(part.shape) for part in parts]
            + [pl.BlockSpec(memory_space=pltpu.HBM) for _ in aliased],
            out_specs=[block, pl.BlockSpec((1, places, columns), lambda i, slots: (i, 0, 0))],
            scratch_shapes=[pltpu.VMEM(parts[0].shape, BF16)],
        ),
        out_shape=[
            jax.ShapeDtypeStruct((rows, span, width), BF16),
            jax.ShapeDtypeStruct((len(parts), places, columns), F32),
        ],
        input_output_aliases={4 + len(parts): 0} if aliased else {},
        compiler_params=pltpu.CompilerParams(vmem_limit_bytes=24 << 20),
        cost_estimate=pl.CostEstimate(
            flops=len(parts) * rows * places * width * 5000, bytes_accessed=rows * places * width * 10, transcendentals=0
        ),
        name="spread",
    )(slots, gates, cotangent, hidden, *parts, *aliased)


def pull_kernel(first, count, slots_ref, gates_ref, change_ref, mixed_ref, hidden_ref, cotangent_ref, attended_ref, router_ref, gains_ref, weight_ref, *rest):
    parts, rest = rest[:count], rest[count:]
    out_ref, low_ref, router_grad_ref, project_ref, sums_ref, pooled_ref, logits_ref, grad_ref = rest[-8:]

    @pl.when(pl.program_id(0) == 0)
    def _():
        if first:
            router_grad_ref[...] = jnp.zeros_like(router_grad_ref)
            project_ref[...] = jnp.zeros_like(project_ref)
            sums_ref[...] = jnp.zeros_like(sums_ref)
        else:
            router_grad_ref[...] = rest[2][...]
            project_ref[...] = rest[3][...]
            sums_ref[...] = rest[4][...]

    for k in range(count):
        @pl.when(pl.program_id(0) == k)
        def _():
            pooled_ref[...] = parts[k][...]

    rows, places, width = mixed_ref.shape
    experts = pooled_ref.shape[0]
    sub = 16
    columns = gates_ref.shape[1]
    inner = jnp.zeros((places, columns), F32)
    for e in range(experts):
        pick = (iota((16, columns), 0) == 0) & (iota((16, columns), 1) % experts == e)
        pick = jnp.where(pick, 1.0, 0.0).astype(BF16)
        inner += dot_tn(pooled_ref[e, places:, :places], pick) + dot_tn(pooled_ref[e, places:, places: 2 * places], pick)

    def change(s, _):
        here = pl.ds(pl.multiple_of(s * sub, sub), sub)
        pooled = [pooled_ref[e, here, :].astype(F32) for e in range(experts)]
        lane = iota((sub, columns), 1)
        changes = jnp.zeros((sub, columns), F32)
        for r in range(rows):
            mixed = mixed_ref[r, here, :].astype(F32)
            for e in range(experts):
                both = jnp.sum(pooled[e] * mixed, axis=1, keepdims=True)
                changes = jnp.where(lane == r * experts + e, both, changes)
        logits_ref[here, :] = changes
        return 0

    lax.fori_loop(0, places // sub, change, 0, unroll=2)
    changes = (logits_ref[...] + change_ref[0]).astype(BF16).astype(F32)
    low = (gates_ref[...] * (changes - inner)).astype(BF16)
    for r in range(rows):
        grad_ref[r] = dot(low, router_ref[r])
        router_grad_ref[...] += dot_tn(low, mixed_ref[r])[r * experts: r * experts + experts]

    def spread(s, _):
        here = pl.ds(pl.multiple_of(s * sub, sub), sub)
        pooled = [pooled_ref[e, here, :].astype(F32) for e in range(experts)]
        gates = gates_ref[here, :].astype(BF16).astype(F32)
        for r in range(rows):
            grad_ref[r, here, :] = sum(
                (gates[:, r * experts + e: r * experts + e + 1] * pooled[e] for e in range(experts)),
                grad_ref[r, here, :],
            )
        return 0

    lax.fori_loop(0, places // sub, spread, 0, unroll=2)

    for r in range(rows):
        grads = grad_ref[r].astype(BF16).astype(F32)
        hat, inverse = normalise(hidden_ref[r])
        sums_ref[0:1] += jnp.sum(grads * hat, axis=0, keepdims=True)
        sums_ref[1:2] += jnp.sum(grads, axis=0, keepdims=True)
        total = cotangent_ref[r].astype(F32) + pull_norm(grads * gains_ref[2:3], hat, inverse)
        out_ref[r] = total
        total = total.astype(BF16)
        project_ref[...] += dot_tn(attended_ref[r], total)
        low_ref[r] = dot_nt(total, weight_ref[...]).astype(BF16)


def pull_slots(found, slots, gates, change, mixed, hidden, cotangent, attended, router, gains, packed, held):
    rows, span, width = mixed.shape
    parts = list(found.values())
    experts, depth, _ = parts[0].shape
    places = span // slots.shape[0]
    at = slot_of(found)
    block = pl.BlockSpec((rows, places, width), lambda i, slots: (0, at(i, slots), 0))
    columns = gates.shape[1]
    sums = [(experts, width), (width, width), (8, width)]
    ins = [
        pl.BlockSpec((places, columns), lambda i, slots: (at(i, slots), 0)),
        pl.BlockSpec((1, places, columns), lambda i, slots: (i, 0, 0)),
        block,
        block,
        block,
        block,
        constant_spec(router.shape),
        constant_spec(gains.shape),
        constant_spec((width, width), 0, 3),
    ] + [constant_spec(part.shape) for part in parts]
    aliases = {}
    if held is not None:
        aliases = {len(ins) + 1: 0, len(ins) + 2: 1}
        ins += [pl.BlockSpec(memory_space=pltpu.HBM)] * 2 + [constant_spec(shape) for shape in sums]
    return pl.pallas_call(
        functools.partial(pull_kernel, held is None, len(parts)),
        grid_spec=pltpu.PrefetchScalarGridSpec(
            num_scalar_prefetch=1,
            grid=(len(parts),),
            in_specs=ins,
            out_specs=[block, block] + [constant_spec(shape) for shape in sums],
            scratch_shapes=[
                pltpu.VMEM(parts[0].shape, BF16),
                pltpu.VMEM((places, columns), F32),
                pltpu.VMEM((rows, places, width), F32),
            ],
        ),
        out_shape=[jax.ShapeDtypeStruct((rows, span, width), F32), jax.ShapeDtypeStruct((rows, span, width), BF16)]
        + [jax.ShapeDtypeStruct(shape, F32) for shape in sums],
        input_output_aliases=aliases,
        compiler_params=pltpu.CompilerParams(vmem_limit_bytes=32 << 20),
        cost_estimate=pl.CostEstimate(
            flops=len(parts) * rows * places * width * width * 20,
            bytes_accessed=rows * places * width * 20,
            transcendentals=0,
        ),
        name="pull_slots",
    )(slots, gates, change, mixed, hidden, cotangent, attended, router, gains, packed, *parts, *(held or ()))


def project_kernel(grads_ref, tokens_ref, product_ref, sums_ref):
    @pl.when((pl.program_id(0) == 0) & (pl.program_id(1) == 0))
    def _():
        product_ref[...] = jnp.zeros_like(product_ref)
        sums_ref[...] = jnp.zeros_like(sums_ref)

    hat = normalise(tokens_ref[0].astype(F32))[0].astype(BF16)
    ones = jnp.ones((hat.shape[0], 8), BF16)
    product_ref[...] += dot_tn(hat, grads_ref[0])
    sums_ref[...] += dot_tn(ones, grads_ref[0])


def project_grads(grads, tokens, tile=512):
    rows, length, width = tokens.shape
    shapes = [(width, 3 * width), (8, 3 * width)]
    return pl.pallas_call(
        project_kernel,
        grid=(rows, length // tile),
        in_specs=[
            pl.BlockSpec((1, tile, 3 * width), lambda r, t: (r, t, 0)),
            pl.BlockSpec((1, tile, width), lambda r, t: (r, t, 0)),
        ],
        out_specs=[constant_spec(shape) for shape in shapes],
        out_shape=[jax.ShapeDtypeStruct(shape, F32) for shape in shapes],
        compiler_params=pltpu.CompilerParams(vmem_limit_bytes=40 << 20),
        cost_estimate=pl.CostEstimate(
            flops=rows * length * width * width * 6, bytes_accessed=rows * length * width * 12, transcendentals=0
        ),
        name="project_grads",
    )(grads, tokens)


def tokens_kernel(grads_ref, tokens_ref, hidden_ref, gains_ref, weight_ref, out_ref):
    hat, inverse = normalise(tokens_ref[0].astype(F32))
    grads = dot_nt(grads_ref[0], weight_ref[...])
    out_ref[0] = hidden_ref[0] + pull_norm(grads * gains_ref[0:1], hat, inverse)


def pull_tokens(grads, tokens, hidden, gains, packed, tile=512):
    rows, length, width = tokens.shape
    block = pl.BlockSpec((1, tile, width), lambda r, t: (r, t, 0))
    return pl.pallas_call(
        tokens_kernel,
        grid=(rows, length // tile),
        in_specs=[
            pl.BlockSpec((1, tile, 3 * width), lambda r, t: (r, t, 0)),
            block,
            block,
            constant_spec(gains.shape),
            constant_spec((width, 3 * width)),
        ],
        out_specs=block,
        out_shape=jax.ShapeDtypeStruct((rows, length, width), F32),
        compiler_params=pltpu.CompilerParams(vmem_limit_bytes=40 << 20),
        cost_estimate=pl.CostEstimate(
            flops=rows * length * width * width * 20, bytes_accessed=rows * length * width * 16, transcendentals=0
        ),
        name="pull_tokens",
    )(grads, tokens, hidden, gains, packed)


def ring_order(size):
    inner = 2 if size % 2 == 0 and size > 2 else 1
    outer = size // inner
    up = [z * inner for z in range(outer)]
    if inner == 1:
        return up
    return up + [z * inner + 1 for z in reversed(range(outer))]


def shift(value, order, step):
    count = len(order)
    return lax.ppermute(value, "dp", [(order[i], order[(i + step) % count]) for i in range(count)])


def flip(value, bit, axis="fsdp"):
    count = lax.axis_size(axis)
    return lax.ppermute(value, axis, [(i, i ^ bit) for i in range(count)])


def turn(value, step, axis="dp"):
    count = lax.axis_size(axis)
    return lax.ppermute(value, axis, [(i, (i + step) % count) for i in range(count)])


def take(values, index):
    starts = (index,) + (jnp.uint32(0),) * (values.ndim - 1)
    return lax.dynamic_slice(values, starts, (1,) + values.shape[1:])[0]


def put(values, value, index):
    return lax.dynamic_update_slice(values, value[None], (index,) + (jnp.uint32(0),) * value.ndim)


def add(a, b):
    return (a.astype(F32) + b.astype(F32)).astype(BF16)


def together(*values):
    return lax.optimization_barrier(values)


class Ring:
    def __init__(self, value, order):
        self.order, self.done = order, 0
        self.ahead = self.behind = value

    def left(self):
        return self.done < len(self.order) // 2

    def step(self, *beside):
        count = len(self.order)
        self.done += 1
        found = {count - self.done: shift(self.ahead, self.order, 1)}
        if 2 * self.done < count:
            found[self.done] = shift(self.behind, self.order, -1)
        values = together(*found.values(), *beside)
        found = dict(zip(found, values))
        self.ahead = found[count - self.done]
        self.behind = found.get(self.done)
        return found, list(values[len(found):])


def gather_all(value, order, spots):
    count = len(order)
    size = lax.axis_size("fsdp")
    whole = put(jnp.zeros((count,) + value.shape, value.dtype), value, spots[0])
    ring = Ring(value, order)
    while ring.left():
        for slot, part in ring.step()[0].items():
            whole = put(whole, part, spots[slot])
    here = lax.axis_index("fsdp")
    whole = whole[:, None]
    bit = size // 2
    while bit:
        other = flip(whole, bit)
        upper = (here & bit) != 0
        whole = jnp.stack([jnp.where(upper, other, whole), jnp.where(upper, whole, other)], axis=1)
        whole = whole.swapaxes(1, 2).reshape((count, -1) + value.shape)
        bit //= 2
    return whole


def scatter_all(values, steps):
    owners, size = lax.axis_size("dp"), lax.axis_size("fsdp")
    bits = size.bit_length() - 1
    here = lax.axis_index("fsdp")
    width = values.shape[1]
    pair = pair_of(owners)
    held = values.reshape((owners // pair, pair) + (2,) * bits + (-1, width))
    for level in range(bits):
        axis = bits + 1 - level
        upper = ((here >> level) & 1) != 0
        low, high = (lax.index_in_dim(held, i, axis, keepdims=False) for i in (0, 1))
        held = add(jnp.where(upper, high, low), flip(jnp.where(upper, low, high), 1 << level))
    if pair == 2:
        upper = (lax.axis_index("dp") & 1) != 0
        low, high = held[:, 0], held[:, 1]
        held = add(jnp.where(upper, high, low), flip(jnp.where(upper, low, high), 1, "dp"))
    else:
        held = held[:, 0]
    return sum(
        (turn(take(held, steps[k]), k * pair).astype(F32) for k in range(1, owners // pair)),
        take(held, steps[0]).astype(F32),
    )


def pair_of(owners):
    return 2 if owners % 2 == 0 else 1


def exchange(values):
    return jnp.stack([values[0]] + [flip(values[k], k) for k in range(1, values.shape[0])])


def per_device(
    tokens,
    segment_ids,
    pad_tokens,
    cotangent,
    project_in,
    project_out,
    router_weight,
    expert_in,
    expert_out,
    first_gain,
    first_bias,
    second_gain,
    second_bias,
):
    blocks_here, rows, length, width = tokens.shape
    tokens = tokens.reshape(rows, length, width)
    cotangent = cotangent.reshape(rows, length, width)
    segments = segment_ids.reshape(rows, length)
    group = pad_tokens.shape[1]
    owners = lax.axis_size("dp")
    experts = router_weight.shape[1]
    order = ring_order(owners)
    data_index = lax.axis_index("dp")
    expert_index = lax.axis_index("fsdp")
    places = length // owners

    pair = pair_of(owners)
    lines = owners // pair
    ring = np.array([[order[(order.index(d) + k) % owners] for k in range(owners)] for d in range(owners)], np.int32)
    place = np.array(
        [[(o % pair ^ d % pair) * lines + (o // pair - d // pair) % lines for o in ring[d]] for d in range(owners)],
        np.int32,
    )
    line = np.array([[(d // pair + k) % lines for k in range(lines)] for d in range(owners)], np.int32)
    tables = np.concatenate([ring, place, line], axis=1)
    tables = lax.dynamic_slice(
        jnp.asarray(tables), (data_index.astype(jnp.uint32), jnp.uint32(0)), (1, tables.shape[1])
    )[0]
    slots, shares = tables[:owners], tables[owners: 2 * owners]
    spots = [tables[k].astype(jnp.uint32) for k in range(owners)]
    steps = [tables[2 * owners + k].astype(jnp.uint32) for k in range(lines)]

    vectors = jnp.stack([first_gain, first_bias, second_gain, second_bias], axis=1)
    small = jnp.concatenate([router_weight, vectors], axis=1)
    small = jnp.pad(small, ((0, 0), (0, 128 - small.shape[1])))
    packed = jnp.concatenate([project_in, project_out, small], axis=1)
    weights = jnp.stack([expert_in[0], expert_out[0].T])
    packed, weights = together(packed, weights)
    packed = gather_all(packed, order, spots)
    packed = packed.reshape(width, packed.shape[-1])
    packed, weights = together(packed, weights)
    kept = {0: weights}
    weights = Ring(weights, order)
    small = packed[:, 4 * width:].T
    mine = (jnp.arange(experts)[:, None] ^ jnp.arange(experts)[None, :]) == expert_index
    router = jnp.sum(jnp.where(mine[:, :, None], small[None, :experts], 0), axis=1).astype(BF16)
    spread_router = jnp.stack(
        [jnp.pad(router, ((r * experts, (rows - 1 - r) * experts), (0, 0))) for r in range(rows)]
    )
    gains = jnp.pad(small[experts: experts + 4].astype(F32), ((0, 4), (0, 0)))

    own_pads = lax.dynamic_slice_in_dim(pad_tokens[0], data_index * rows, rows, 0)
    vlens = (length - own_pads).astype(jnp.int32)
    starts = jnp.zeros_like(segments)
    for doc in range(1, 4):
        before = jnp.sum((segments < doc).astype(jnp.int32), axis=1, keepdims=True)
        starts = jnp.where(segments == doc, before, starts)
    starts = starts.reshape(rows, length // QB, QB)
    lows = starts[:, :, 0] // QB

    def meanwhile(value):
        if not weights.left():
            return value
        found, (value,) = weights.step(value)
        kept.update(found)
        return value

    joined = meanwhile(join_tokens(tokens, gains, packed))
    attended = meanwhile(attn_fwd(joined, starts, lows, vlens, 0, length // QB))
    hidden, mixed, logits = mix_tokens(
        attended, tokens, gains, packed, jnp.pad(router, ((0, 16 - experts), (0, 0))), 0
    )
    logits = meanwhile(logits)[:, :experts]
    valid = (jnp.arange(length)[None, :] < vlens[:, None])[:, None, :]
    highest = jnp.max(jnp.where(valid, logits, NEGATIVE), axis=0)
    total = jnp.sum(jnp.where(valid, jnp.exp(logits - highest), 0.0), axis=0)
    stats = jnp.stack([highest, total])[None]
    if pair == 2:
        stats = jnp.concatenate([stats, flip(stats, 1, "dp")])
    stats = jnp.concatenate([stats] + [turn(stats, k * pair) for k in range(1, lines)])
    tops = jnp.max(stats[:, 0], axis=0)
    total = jnp.sum(stats[:, 1] * jnp.exp(stats[:, 0] - tops), axis=0)
    gates = jnp.where(valid, jnp.exp(jnp.where(valid, logits - tops, NEGATIVE)) / total, 0.0)
    gates = gates.reshape(rows * experts, length).T
    pooled = meanwhile(pool_tokens(slots, gates, mixed, experts, 1.0))
    while weights.left():
        kept.update(weights.step()[0])
    weights = jnp.stack([kept[k] for k in range(owners)])
    grads = pool_tokens(slots, gates, cotangent, experts, float(group))

    half = experts // 2
    first = [(pooled[:, :half], 1), (pooled[:, half:], -1)]
    second = [(grads[:, :half], 1), (grads[:, half:], -1)]
    held = [part[-way % owners] for part, way in first]
    later = [part[-way % owners] for part, way in second]
    for step in range(owners - 1):
        came = [shift(value, order, way) for value, (_, way) in zip(held, first)]
        *came, one, two = together(*came, *later)
        held = [add(value, part[-way * (2 + step) % owners]) for value, (part, way) in zip(came, first)]
        came = [shift(value, order, way) for value, (_, way) in zip([one, two], second)]
        later = [add(value, part[-way * (2 + step) % owners]) for value, (part, way) in zip(came, second)]
    pooled = exchange(jnp.concatenate(held, axis=0))
    result, act, slope = run_experts(pooled, weights)
    grads = exchange(jnp.concatenate(later, axis=0))
    grad_pooled, grad_weights = pull_experts(shares, pooled, grads, result, act, slope, weights)

    result = exchange(result)
    back = exchange(grad_pooled)

    def spread(found, out):
        return spread_tokens(found, slots, gates, cotangent, hidden, group, out)

    def pull(found, change, out):
        return pull_slots(
            found, slots, gates, change, mixed, hidden, cotangent, attended, spread_router, gains, packed, out
        )

    turns = owners // 2
    ring, groups = Ring(result, order), [{0: result}]
    out, pulled, changes = None, None, []
    for step in range(turns):
        if step == 0:
            found, (grad_weights,) = ring.step(grad_weights)
        else:
            out, change = spread(groups[step - 1], out)
            found, (out, change) = ring.step(out, change)
            changes.append(change)
        groups.append(found)
    ring, arrived = Ring(together(back, *found.values())[0], order), [{0: back}]
    for step in range(turns):
        if step < 2:
            out, change = spread(groups[turns - 1 + step], out)
            changes.append(change)
        if step > 0:
            pulled = pull(arrived[step - 1], changes[step - 1], pulled)
        if step == turns - 1:
            pulled = pull(arrived[step], changes[step], pulled)
        found, (out, *held) = ring.step(out, *(pulled or ()))
        pulled = held or None
        arrived.append(found)
    pulled = pull(arrived[turns], changes[turns], pulled)
    layer_out = out
    grad_hidden, grad_attended, router_grad, grad_proj_out, sums_two = pulled
    grad_attended, grad_weights = together(grad_attended, grad_weights)
    split = rows - max(1, rows // 4)
    if pair == 2:
        came = flip(grad_weights[lines:], 1, "dp")
    grads = attn_bwd(joined, grad_attended, starts, lows, vlens, 0, split)
    grad_weights = grad_weights[:lines]
    if pair == 2:
        came, grads = together(came, grads)
        grad_weights = add(grad_weights, came)
    came = [turn(grad_weights[k], k * pair) for k in range(1, lines)]
    grads = attn_bwd(joined, grad_attended, starts, lows, vlens, split, rows, grads)
    product, sums_one = project_grads(grads, tokens)
    product, *came = together(product, *came)
    grad_weights = sum((value.astype(F32) for value in came), grad_weights[0].astype(F32))
    full_in = packed[:, : 3 * width].astype(F32)
    sums_one = sums_one[:1]
    grad_proj_in = gains[0][:, None] * product + gains[1][:, None] * sums_one
    sums_one = jnp.stack([jnp.sum(full_in * product, axis=1), jnp.sum(full_in * sums_one, axis=1)])
    tokens_grad = pull_tokens(grads, tokens, grad_hidden, gains, packed)
    router_grad = jnp.sum(jnp.where(mine[:, :, None], router_grad[None], 0.0), axis=1)

    late = jnp.concatenate([router_grad, sums_one, sums_two[:2]], axis=0).T
    late = jnp.pad(late, ((0, 0), (0, 128 - late.shape[1])))
    reduced = scatter_all(jnp.concatenate([grad_proj_in, grad_proj_out, late], axis=1).astype(BF16), steps)
    late = reduced[:, 4 * width:]
    return (
        layer_out[None],
        tokens_grad[None],
        reduced[:, : 3 * width],
        reduced[:, 3 * width: 4 * width],
        late[:, :experts],
        grad_weights[0][None],
        grad_weights[1].T[None],
        late[:, experts],
        late[:, experts + 1],
        late[:, experts + 2],
        late[:, experts + 3],
    )


def solution(mesh):
    in_specs = (
        P("fsdp", "dp", None, None),
        P("fsdp", "dp", None),
        P("fsdp", None),
        P("fsdp", "dp", None, None),
        P(("dp", "fsdp"), None),
        P(("dp", "fsdp"), None),
        P(("dp", "fsdp"), None),
        P("fsdp", None, "dp"),
        P("fsdp", "dp", None),
        P(("dp", "fsdp")),
        P(("dp", "fsdp")),
        P(("dp", "fsdp")),
        P(("dp", "fsdp")),
    )
    out_specs = (
        P("fsdp", "dp", None, None),
        P("fsdp", "dp", None, None),
        P(("dp", "fsdp"), None),
        P(("dp", "fsdp"), None),
        P(("dp", "fsdp"), None),
        P("fsdp", None, "dp"),
        P("fsdp", "dp", None),
        P(("dp", "fsdp")),
        P(("dp", "fsdp")),
        P(("dp", "fsdp")),
        P(("dp", "fsdp")),
    )
    return jax.shard_map(
        per_device, mesh=mesh, in_specs=in_specs, out_specs=out_specs, check_vma=False
    )
```

time: 641 us -> 566 us (0.88)
  between operations: 64.8 us -> 9.81 us
  waiting for transfers between devices: 179 us -> 127 us
  Pallas kernels: 213 us -> 242 us
    ppermute x56, waiting for transfers between devices: 136 us -> 83.5 us  [shift(): lax.ppermute(value, 'dp', [(order[i], order[(i + step) % count]) for i in...]
    pallas_call x8 -> x17, Pallas kernels: 155 us -> 187 us  [the longest x2 62.3 us: attn_bwd(): pl.pallas_call(functools.partial(attn_bwd_kernel, width, row_from, count)...]
    unnamed x52 -> x137, local copies, waits for them, and re-layouts: 25.2 us -> 48.8 us
    dynamic_update_slice x41 -> x8, local copies, waits for them, and re-layouts: 10.4 us -> 0.11 us  [put(): lax.dynamic_update_slice(values, value[None], (index,) + (jnp.uint32(0),)...]
    ppermute x16 -> x19, starting transfers between devices: 9 us -> 14.9 us  [flip(): return lax.ppermute(value, axis, [(i, i ^ bit) for i in range(count)])]
    ppermute x14 -> x9, starting transfers between devices: 19.7 us -> 22.2 us  [turn(): lax.ppermute(value, axis, [(i, (i + step) % count) for i in range(count)])]
    ppermute x16 -> x19, waiting for transfers between devices: 34.3 us -> 33.9 us  [flip(): return lax.ppermute(value, axis, [(i, i ^ bit) for i in range(count)])]
  transfers between devices with their start and end apart: 87 -> 84, of which waited for: 45 -> 51; matrix products, arithmetic and copies ran while one was open for 6% -> 3% of each run, Pallas kernels for 20% -> 42%
where the time goes in v2:
time: 566 us; the launch traced here: 557 us
  Pallas kernels  242 us (43%)
  waiting for transfers between devices  127 us (22%)
  starting transfers between devices  102 us (18%)
  local copies, waits for them, and re-layouts  58.5 us (10%)
  other arithmetic  18.1 us (3%)
  between operations  9.81 us (2%)
    ppermute x56, waiting for transfers between devices, shift(): lax.ppermute(value, 'dp', [(order[i], order[(i + step) % count]) for i in...  83.5 us
    ppermute x56, starting transfers between devices, shift(): lax.ppermute(value, 'dp', [(order[i], order[(i + step) % count]) for i in...  64.7 us
    pallas_call x2, Pallas kernels, attn_bwd(): pl.pallas_call(functools.partial(attn_bwd_kernel, width, row_from, count)...  62.3 us
    unnamed x137, local copies, waits for them, and re-layouts  48.8 us
    pallas_call x5, Pallas kernels, pull_slots(): pl.pallas_call(functools.partial(pull_kernel, held is None, len(parts)),...  46 us
    ppermute x19, waiting for transfers between devices, flip(): return lax.ppermute(value, axis, [(i, i ^ bit) for i in range(count)])  33.9 us
    pallas_call x1, Pallas kernels, attn_fwd(): pl.pallas_call(functools.partial(attn_fwd_kernel, width, begin, count), g...  27.1 us
    pallas_call x5, Pallas kernels, spread_tokens(): pl.pallas_call(functools.partial(spread_kernel, group, len(parts)), grid_...  24.2 us
  transfers between devices with their start and end apart: 84, of which 51 were waited for; matrix products, arithmetic and copies ran while one was open for 3% of the time, Pallas kernels for 42%

profile of v2, /device:TPU:0, one launch (start us, length us, event | category | flops | bytes accessed | tf_op | source)
XLA Modules:
  0.0 557.2 jit_solution(15533022169829829735)
XLA Ops:
  33.7 7.2 %collective-permute-done.7 = bf16[8,1,16,2176]{3,2,0,1:T(8,128)(2,1)S(1)} collective-permute-done((bf16[8,1,16,2176]{3,2,0,1:T(8,128)(2,1)S(1)}, bf16[8,1,16,2176]{3,2,0,1:T(8,128)(2,1)S(1)}, u32[]{:S(2)}, u32[]{:S(2)}) %collective-permute-start.7) | collective-permute-done | bytes 557088 | tf_op jit(solution)/shard_map/ppermute | solution.py:723
  49.2 11.4 %join.1.joined_ref = bf16[4,1024,1536]{2,1,0:T(8,128)(2,1)} custom-call(bf16[4,1024,512]{2,1,0:T(8,128)(2,1)S(1)} %bitcast.396, f32[8,512]{1,0:T(8,128)S(1)} %pad.31.clone.gains_ref, bf16[512,2176]{1,0:T(8,128)(2,1)S(1)} %bitcast.374), custom_call_target="tpu_custom_call" | custom-call | flops 6442450944 | bytes 16777216 | tf_op jit(solution)/shard_map/join/pallas_call | solution.py:233
  62.6 27.1 %attend.1.attended_ref = bf16[4,1024,512]{2,1,0:T(8,128)(2,1)S(1)} custom-call(s32[4,8]{1,0:T(4,128)S(1)} %add_select_fusion.lo_ref, s32[4]{0:T(128)S(1)} %subtract_bitcast_fusion.vlen_ref, s32[4,8,128]{2,1,0:T(8,128)S(1)} %select_select_fusion.start_ref, bf16[4,1024,1536]{2,1,0:T(8,128)(2,1)} %join.1.joined_ref), custom_call_target="tpu_custom_call" | custom-call | flops 13421772800 | bytes 12582912 | tf_op jit(solution)/shard_map/attend/pallas_call | solution.py:102
  94.1 9.2 %mix.1 = (f32[4,1024,512]{2,1,0:T(8,128)}, bf16[4,1024,512]{2,1,0:T(8,128)(2,1)S(1)}, f32[4,16,1024]{2,1,0:T(8,128)S(1)}) custom-call(bf16[4,1024,512]{2,1,0:T(8,128)(2,1)S(1)} %attend.1.attended_ref, bf16[4,1024,512]{2,1,0:T(8,128)(2,1)} %bitcast.395, f32[8,512]{1,0:T(8,128)S(1)} %pad.31.clone.gains_ref, bf16[512,2176]{1,0:T(8,128)(2,1)S(1)} %bitcast.375, ...), custom_call_target="tpu_custom_call" | custom-call | flops 2147483648 | bytes 20971520 | tf_op jit(solution)/shard_map/mix/pallas_call | solution.py:263
  114.0 5.9 %collective-permute-done.17 = f32[2,2,4,1024]{3,2,1,0:T(4,128)S(1)} collective-permute-done((f32[2,2,4,1024]{3,2,1,0:T(4,128)S(1)}, f32[2,2,4,1024]{3,2,1,0:T(4,128)S(1)}, u32[]{:S(2)}, u32[]{:S(2)}) %collective-permute-start.17) | collective-permute-done | bytes 65568 | tf_op jit(solution)/shard_map/ppermute | solution.py:728
  124.2 5.7 %pool.2 = bf16[8,4,128,512]{3,2,1,0:T(8,128)(2,1)S(1)} custom-call(s32[8]{0:T(128)S(1)} %get-tuple-element.457.slots_ref, f32[1024,16]{1,0:T(8,128)S(1)} %bitcast.383, bf16[4,1024,512]{2,1,0:T(8,128)(2,1)S(1)} %copy-done.9), custom_call_target="tpu_custom_call" | custom-call | flops 2097152000 | bytes 16777216 | tf_op jit(solution)/shard_map/pool/pallas_call | solution.py:307
  133.9 6.0 %pool.3 = bf16[8,4,128,512]{3,2,1,0:T(8,128)(2,1)S(1)} custom-call(s32[8]{0:T(128)S(1)} %get-tuple-element.457.slots_ref, f32[1024,16]{1,0:T(8,128)S(1)} %bitcast.384, bf16[4,1024,512]{2,1,0:T(8,128)(2,1)S(1)} %bitcast.362), custom_call_target="tpu_custom_call" | custom-call | flops 2097152000 | bytes 16777216 | tf_op jit(solution)/shard_map/pool/pallas_call | solution.py:307
  233.8 7.8 %experts.1 = (bf16[4,128,512]{2,1,0:T(8,128)(2,1)S(1)}, bf16[8,512,256]{2,1,0:T(8,128)(2,1)S(1)}, f32[8,512,256]{2,1,0:T(8,128)S(1)}) custom-call(bf16[4,128,512]{2,1,0:T(8,128)(2,1)S(1)} %pad_maximum_fusion.4.pooled_ref, bf16[8,2,512,256]{3,2,1,0:T(8,128)(2,1)S(1)} %copy-done.37), custom_call_target="tpu_custom_call" | custom-call | flops 4294967296 | bytes 8388608 | tf_op jit(solution)/shard_map/experts/pallas_call | solution.py:361
  260.4 11.6 %pull_experts.1 = (bf16[4,144,512]{2,1,0:T(8,128)(2,1)S(1)}, bf16[8,2,512,256]{3,2,1,0:T(8,128)(2,1)S(1)}) custom-call(s32[8]{0:T(128)S(1)} %get-tuple-element.458.slots_ref, bf16[4,128,512]{2,1,0:T(8,128)(2,1)S(1)} %pad_maximum_fusion.4.pooled_ref, bf16[4,128,512]{2,1,0:T(8,128)(2,1)S(1)} %pad_maximum_fusion.5.grads_ref, ...), custom_call_target="tpu_custom_call" | custom-call | flops 6442450944 | bytes 8388608 | tf_op jit(solution)/shard_map/pull_experts/pallas_call | solution.py:426
  280.5 6.5 %collective-permute-done.62.rest_0_ = bf16[4,128,512]{2,1,0:T(8,128)(2,1)S(1)} collective-permute-done((bf16[4,128,512]{2,1,0:T(8,128)(2,1)}, bf16[4,128,512]{2,1,0:T(8,128)(2,1)S(1)}, u32[]{:S(2)}, u32[]{:S(2)}) %collective-permute-start.62) | collective-permute-done | bytes 524320 | tf_op jit(solution)/shard_map/ppermute | solution.py:718
  289.7 6.3 %spread.6 = (bf16[4,1024,512]{2,1,0:T(8,128)(2,1)}, f32[2,128,16]{2,1,0:T(8,128)S(1)}) custom-call(s32[8]{0:T(128)S(1)} %get-tuple-element.457.slots_ref, f32[1024,16]{1,0:T(8,128)S(1)} %bitcast.386, bf16[4,1024,512]{2,1,0:T(8,128)(2,1)S(1)} %bitcast.364, f32[4,1024,512]{2,1,0:T(8,128)S(1)} %bitcast.361, ...), custom_call_target="tpu_custom_call", output_to_operand_aliasing={{0}: (6, {})} | custom-call | flops 2621440000 | bytes 2621440 | tf_op jit(solution)/shard_map/spread/pallas_call | solution.py:497
  296.0 5.3 collective-permute-done.64.rest_0_
  324.0 8.7 %collective-permute-done.67.rest_0_ = bf16[4,144,512]{2,1,0:T(8,128)(2,1)} collective-permute-done((bf16[4,144,512]{2,1,0:T(8,128)(2,1)S(1)}, bf16[4,144,512]{2,1,0:T(8,128)(2,1)}, u32[]{:S(2)}, u32[]{:S(2)}) %collective-permute-start.67) | collective-permute-done | bytes 589856 | tf_op jit(solution)/shard_map/ppermute | solution.py:718
  344.2 6.6 %pull_slots.5 = (f32[4,1024,512]{2,1,0:T(8,128)}, bf16[4,1024,512]{2,1,0:T(8,128)(2,1)S(1)}, f32[4,512]{1,0:T(4,128)S(1)}, f32[512,512]{1,0:T(8,128)S(1)}, f32[8,512]{1,0:T(8,128)S(1)}) custom-call(s32[8]{0:T(128)S(1)} %get-tuple-element.457.slots_ref, f32[1024,16]{1,0:T(8,128)S(1)} %bitcast.389, f32[1,128,16]{2,1,0:T(8,128)S(1)} %get-tuple-element.233.change_ref, ...), custom_call_target="tpu_custom_call" | custom-call | flops 2684354560 | bytes 5242880 | tf_op jit(solution)/shard_map/pull_slots/pallas_call | solution.py:620
  362.0 10.9 %pull_slots.6 = (f32[4,1024,512]{2,1,0:T(8,128)}, bf16[4,1024,512]{2,1,0:T(8,128)(2,1)S(1)}, f32[4,512]{1,0:T(4,128)S(1)}, f32[512,512]{1,0:T(8,128)S(1)}, f32[8,512]{1,0:T(8,128)S(1)}) custom-call(s32[8]{0:T(128)S(1)} %get-tuple-element.457.slots_ref, f32[1024,16]{1,0:T(8,128)S(1)} %bitcast.391, ...), custom_call_target="tpu_custom_call", output_to_operand_aliasing={{0}: (12, {}), {1}: (13, {})} | custom-call | flops 5368709120 | bytes 5242880 | tf_op jit(solution)/shard_map/pull_slots/pallas_call | solution.py:620
  374.4 10.9 %pull_slots.7 = (f32[4,1024,512]{2,1,0:T(8,128)}, bf16[4,1024,512]{2,1,0:T(8,128)(2,1)S(1)}, f32[4,512]{1,0:T(4,128)S(1)}, f32[512,512]{1,0:T(8,128)S(1)}, f32[8,512]{1,0:T(8,128)S(1)}) custom-call(s32[8]{0:T(128)S(1)} %get-tuple-element.457.slots_ref, f32[1024,16]{1,0:T(8,128)S(1)} %bitcast.392, ...), custom_call_target="tpu_custom_call", output_to_operand_aliasing={{0}: (12, {}), {1}: (13, {})} | custom-call | flops 5368709120 | bytes 5242880 | tf_op jit(solution)/shard_map/pull_slots/pallas_call | solution.py:620
  386.3 10.8 %pull_slots.8 = (f32[4,1024,512]{2,1,0:T(8,128)}, bf16[4,1024,512]{2,1,0:T(8,128)(2,1)S(1)}, f32[4,512]{1,0:T(4,128)S(1)}, f32[512,512]{1,0:T(8,128)S(1)}, f32[8,512]{1,0:T(8,128)S(1)}) custom-call(s32[8]{0:T(128)S(1)} %get-tuple-element.457.slots_ref, f32[1024,16]{1,0:T(8,128)S(1)} %bitcast.393, ...), custom_call_target="tpu_custom_call", output_to_operand_aliasing={{0}: (12, {}), {1}: (13, {})} | custom-call | flops 5368709120 | bytes 5242880 | tf_op jit(solution)/shard_map/pull_slots/pallas_call | solution.py:620
  401.3 6.9 %pull_slots.9 = (f32[4,1024,512]{2,1,0:T(8,128)}, bf16[4,1024,512]{2,1,0:T(8,128)(2,1)S(1)}, f32[4,512]{1,0:T(4,128)S(1)}, f32[512,512]{1,0:T(8,128)S(1)}, f32[8,512]{1,0:T(8,128)S(1)}) custom-call(s32[8]{0:T(128)S(1)} %get-tuple-element.457.slots_ref, f32[1024,16]{1,0:T(8,128)S(1)} %bitcast.394, ...), custom_call_target="tpu_custom_call", output_to_operand_aliasing={{0}: (11, {}), {1}: (12, {})} | custom-call | flops 2684354560 | bytes 5242880 | tf_op jit(solution)/shard_map/pull_slots/pallas_call | solution.py:620
  414.1 44.4 %attend_back.2.rest_0_ = bf16[4,1024,1536]{2,1,0:T(8,128)(2,1)} custom-call(s32[4,8]{1,0:T(4,128)S(1)} %add_select_fusion.lo_ref, s32[4]{0:T(128)S(1)} %subtract_bitcast_fusion.vlen_ref, s32[4,8,128]{2,1,0:T(8,128)S(1)} %select_select_fusion.start_ref, bf16[4,1024,1536]{2,1,0:T(8,128)(2,1)} %join.1.joined_ref, bf16[4,1024,512]{2,1,0:T(8,128)(2,1)S(1)} %copy-done.20), custom_call_target="tpu_custom_call" | custom-call | flops 50331648000 | bytes 18874368 | tf_op jit(solution)/shard_map/attend_back/pallas_call | solution.py:176
  466.2 17.9 %attend_back.3.grads_ref = bf16[4,1024,1536]{2,1,0:T(8,128)(2,1)} custom-call(s32[4,8]{1,0:T(4,128)S(1)} %add_select_fusion.lo_ref, s32[4]{0:T(128)S(1)} %subtract_bitcast_fusion.vlen_ref, s32[4,8,128]{2,1,0:T(8,128)S(1)} %select_select_fusion.start_ref, bf16[4,1024,1536]{2,1,0:T(8,128)(2,1)} %join.1.joined_ref, ...), custom_call_target="tpu_custom_call", output_to_operand_aliasing={{}: (5, {})} | custom-call | flops 16777216000 | bytes 6291456 | tf_op jit(solution)/shard_map/attend_back/pallas_call | solution.py:176
  484.2 14.9 %project_grads.1 = (f32[512,1536]{1,0:T(8,128)S(1)}, f32[8,1536]{1,0:T(8,128)S(1)}) custom-call(bf16[4,1024,1536]{2,1,0:T(8,128)(2,1)} %attend_back.3.grads_ref, bf16[4,1024,512]{2,1,0:T(8,128)(2,1)S(1)} %bitcast.397), custom_call_target="tpu_custom_call" | custom-call | flops 6442450944 | bytes 25165824 | tf_op jit(solution)/shard_map/project_grads/pallas_call | solution.py:661
  513.9 16.0 %pull_tokens.1 = f32[4,1024,512]{2,1,0:T(8,128)} custom-call(bf16[4,1024,1536]{2,1,0:T(8,128)(2,1)} %attend_back.3.grads_ref, bf16[4,1024,512]{2,1,0:T(8,128)(2,1)S(1)} %bitcast.398, f32[4,1024,512]{2,1,0:T(8,128)} %get-tuple-element.286.hidden_ref, f32[8,512]{1,0:T(8,128)S(1)} %pad.31.clone.gains_ref, bf16[512,2176]{1,0:T(8,128)(2,1)S(1)} %bitcast.382), custom_call_target="tpu_custom_call" | custom-call | flops 21474836480 | bytes 33554432 | tf_op jit(solution)/shard_map/pull_tokens/pallas_call | solution.py:687
  531.6 7.4 %collective-permute-done.80 = bf16[4,16,2176]{2,1,0:T(8,128)(2,1)S(1)} collective-permute-done((bf16[4,16,2176]{2,1,0:T(8,128)(2,1)S(1)}, bf16[4,16,2176]{2,1,0:T(8,128)(2,1)S(1)}, u32[]{:S(2)}, u32[]{:S(2)}) %collective-permute-start.80) | collective-permute-done | bytes 278560 | tf_op jit(solution)/shard_map/ppermute | solution.py:723
  539.1 8.8 %collective-permute-start.81 = (bf16[16,2176]{1,0:T(8,128)(2,1)S(1)}, bf16[16,2176]{1,0:T(8,128)(2,1)S(1)}, u32[]{:S(2)}, u32[]{:S(2)}) collective-permute-start(bf16[16,2176]{1,0:T(8,128)(2,1)S(1)} %get-tuple-element.424), channel_id=1, source_target_pairs={{0,8},{4,12},{8,16},{12,20},{16,24},{20,28},{24,0},{28,4},{1,9},{5... | collective-permute-start | bytes 208904 | tf_op jit(solution)/shard_map/ppermute | solution.py:728
  (404 shorter events, 273.3 us)
Async XLA Ops:
  44.4 16.1 %collective-permute-start.10 = (bf16[2,512,256]{2,1,0:T(8,128)(2,1)S(1)}, bf16[2,512,256]{2,1,0:T(8,128)(2,1)}, u32[]{:S(2)}, u32[]{:S(2)}) collective-permute-start(bf16[2,512,256]{2,1,0:T(8,128)(2,1)S(1)} %pad_maximum_fusion.3), channel_id=1, source_target_pairs={{0,4},{8,0},{16,8},{24,16},{28,24},{20,28},{12,20},{4,12},{1,5},{9... | collective-permute-start | bytes 1572872 | tf_op jit(solution)/shard_map/ppermute | solution.py:718
  44.9 15.6 %collective-permute-start.9 = (bf16[2,512,256]{2,1,0:T(8,128)(2,1)S(1)}, bf16[2,512,256]{2,1,0:T(8,128)(2,1)}, u32[]{:S(2)}, u32[]{:S(2)}) collective-permute-start(bf16[2,512,256]{2,1,0:T(8,128)(2,1)S(1)} %pad_maximum_fusion.3), channel_id=1, source_target_pairs={{0,8},{8,16},{16,24},{24,28},{28,20},{20,12},{12,4},{4,0},{1,9},{9... | collective-permute-start | bytes 1572872 | tf_op jit(solution)/shard_map/ppermute | solution.py:718
  60.6 29.2 %collective-permute-start.11 = (bf16[2,512,256]{2,1,0:T(8,128)(2,1)}, bf16[2,512,256]{2,1,0:T(8,128)(2,1)S(1)}, u32[]{:S(2)}, u32[]{:S(2)}) collective-permute-start(bf16[2,512,256]{2,1,0:T(8,128)(2,1)} %collective-permute-done.9), channel_id=1, source_target_pairs={{0,8},{8,16},{16,24},{24,28},{28,20},{20,12},{12,4},{4,0},{1,9},{9... | collective-permute-start | bytes 1572872 | tf_op jit(solution)/shard_map/ppermute | solution.py:718
  62.2 27.6 %collective-permute-start.12 = (bf16[2,512,256]{2,1,0:T(8,128)(2,1)}, bf16[2,512,256]{2,1,0:T(8,128)(2,1)S(1)}, u32[]{:S(2)}, u32[]{:S(2)}) collective-permute-start(bf16[2,512,256]{2,1,0:T(8,128)(2,1)} %collective-permute-done.10), channel_id=1, source_target_pairs={{0,4},{8,0},{16,8},{24,16},{28,24},{20,28},{12,20},{4,12},{1,5},{9... | collective-permute-start | bytes 1572872 | tf_op jit(solution)/shard_map/ppermute | solution.py:718
  89.8 15.6 %collective-permute-start.13 = (bf16[2,512,256]{2,1,0:T(8,128)(2,1)S(1)}, bf16[2,512,256]{2,1,0:T(8,128)(2,1)}, u32[]{:S(2)}, u32[]{:S(2)}) collective-permute-start(bf16[2,512,256]{2,1,0:T(8,128)(2,1)S(1)} %collective-permute-done.11), channel_id=1, source_target_pairs={{0,8},{8,16},{16,24},{24,28},{28,20},{20,12},{12,4},{4,0},{1,9},{9... | collective-permute-start | bytes 1572872 | tf_op jit(solution)/shard_map/ppermute | solution.py:718
  105.6 24.3 %collective-permute-start.15 = (bf16[2,512,256]{2,1,0:T(8,128)(2,1)}, bf16[2,512,256]{2,1,0:T(8,128)(2,1)}, u32[]{:S(2)}, u32[]{:S(2)}) collective-permute-start(bf16[2,512,256]{2,1,0:T(8,128)(2,1)} %collective-permute-done.13), channel_id=1, source_target_pairs={{0,8},{8,16},{16,24},{24,28},{28,20},{20,12},{12,4},{4,0},{1,9},{9... | collective-permute-start | bytes 1572872 | tf_op jit(solution)/shard_map/ppermute | solution.py:718
  228.1 17.1 %collective-permute-start.49 = (bf16[2,128,512]{2,1,0:T(8,128)(2,1)S(1)}, bf16[2,128,512]{2,1,0:T(8,128)(2,1)S(1)}, u32[]{:S(2)}, u32[]{:S(2)}) collective-permute-start(bf16[2,128,512]{2,1,0:T(8,128)(2,1)S(1)} %get-tuple-element.201), channel_id=1, source_target_pairs={{0,8},{8,16},{16,24},{24,28},{28,20},{20,12},{12,4},{4,0},{1,9},{9... | collective-permute-start | bytes 786440 | tf_op jit(solution)/shard_map/ppermute | solution.py:718
  229.0 16.2 %collective-permute-start.51 = (bf16[2,128,512]{2,1,0:T(8,128)(2,1)S(1)}, bf16[2,128,512]{2,1,0:T(8,128)(2,1)S(1)}, u32[]{:S(2)}, u32[]{:S(2)}) collective-permute-start(bf16[2,128,512]{2,1,0:T(8,128)(2,1)S(1)} %get-tuple-element.202), channel_id=1, source_target_pairs={{0,4},{8,0},{16,8},{24,16},{28,24},{20,28},{12,20},{4,12},{1,5},{9... | collective-permute-start | bytes 786440 | tf_op jit(solution)/shard_map/ppermute | solution.py:718
  252.7 19.3 %collective-permute-start.60 = (bf16[4,128,512]{2,1,0:T(8,128)(2,1)}, bf16[4,128,512]{2,1,0:T(8,128)(2,1)}, u32[]{:S(2)}, u32[]{:S(2)}) collective-permute-start(bf16[4,128,512]{2,1,0:T(8,128)(2,1)} %pad_maximum_fusion.6.rest_0_), channel_id=1, source_target_pairs={{0,8},{8,16},{16,24},{24,28},{28,20},{20,12},{12,4},{4,0},{1,9},{9... | collective-permute-start | bytes 1572872 | tf_op jit(solution)/shard_map/ppermute | solution.py:718
  253.6 18.4 %collective-permute-start.61 = (bf16[4,128,512]{2,1,0:T(8,128)(2,1)}, bf16[4,128,512]{2,1,0:T(8,128)(2,1)}, u32[]{:S(2)}, u32[]{:S(2)}) collective-permute-start(bf16[4,128,512]{2,1,0:T(8,128)(2,1)} %pad_maximum_fusion.6.rest_0_), channel_id=1, source_target_pairs={{0,4},{8,0},{16,8},{24,16},{28,24},{20,28},{12,20},{4,12},{1,5},{9... | collective-permute-start | bytes 1572872 | tf_op jit(solution)/shard_map/ppermute | solution.py:718
  272.0 15.1 %collective-permute-start.62 = (bf16[4,128,512]{2,1,0:T(8,128)(2,1)}, bf16[4,128,512]{2,1,0:T(8,128)(2,1)S(1)}, u32[]{:S(2)}, u32[]{:S(2)}) collective-permute-start(bf16[4,128,512]{2,1,0:T(8,128)(2,1)} %collective-permute-done.60.rest_0_), channel_id=1, source_target_pairs={{0,8},{8,16},{16,24},{24,28},{28,20},{20,12},{12,4},{4,0},{1,9},{9... | collective-permute-start | bytes 1572872 | tf_op jit(solution)/shard_map/ppermute | solution.py:718
  273.0 14.7 %collective-permute-start.63 = (bf16[4,128,512]{2,1,0:T(8,128)(2,1)}, bf16[4,128,512]{2,1,0:T(8,128)(2,1)S(1)}, u32[]{:S(2)}, u32[]{:S(2)}) collective-permute-start(bf16[4,128,512]{2,1,0:T(8,128)(2,1)} %collective-permute-done.61.rest_1_), channel_id=1, source_target_pairs={{0,4},{8,0},{16,8},{24,16},{28,24},{20,28},{12,20},{4,12},{1,5},{9... | collective-permute-start | bytes 1572872 | tf_op jit(solution)/shard_map/ppermute | solution.py:718
  301.7 15.1 %collective-permute-start.66 = (bf16[4,128,512]{2,1,0:T(8,128)(2,1)S(1)}, bf16[4,128,512]{2,1,0:T(8,128)(2,1)S(1)}, u32[]{:S(2)}, u32[]{:S(2)}) collective-permute-start(bf16[4,128,512]{2,1,0:T(8,128)(2,1)S(1)} %collective-permute-done.64.rest_0_), channel_id=1, source_target_pairs={{0,8},{8,16},{16,24},{24,28},{28,20},{20,12},{12,4},{4,0},{1,9},{9... | collective-permute-start | bytes 1572872 | tf_op jit(solution)/shard_map/ppermute | solution.py:718
  316.8 15.9 %collective-permute-start.67 = (bf16[4,144,512]{2,1,0:T(8,128)(2,1)S(1)}, bf16[4,144,512]{2,1,0:T(8,128)(2,1)}, u32[]{:S(2)}, u32[]{:S(2)}) collective-permute-start(bf16[4,144,512]{2,1,0:T(8,128)(2,1)S(1)} %pad_maximum_fusion.2.rest_0_), channel_id=1, source_target_pairs={{0,8},{8,16},{16,24},{24,28},{28,20},{20,12},{12,4},{4,0},{1,9},{9... | collective-permute-start | bytes 1769480 | tf_op jit(solution)/shard_map/ppermute | solution.py:718
  318.1 15.5 %collective-permute-start.68 = (bf16[4,144,512]{2,1,0:T(8,128)(2,1)S(1)}, bf16[4,144,512]{2,1,0:T(8,128)(2,1)}, u32[]{:S(2)}, u32[]{:S(2)}) collective-permute-start(bf16[4,144,512]{2,1,0:T(8,128)(2,1)S(1)} %pad_maximum_fusion.2.rest_0_), channel_id=1, source_target_pairs={{0,4},{8,0},{16,8},{24,16},{28,24},{20,28},{12,20},{4,12},{1,5},{9... | collective-permute-start | bytes 1769480 | tf_op jit(solution)/shard_map/ppermute | solution.py:718
  333.7 23.8 %collective-permute-start.69 = (bf16[4,144,512]{2,1,0:T(8,128)(2,1)}, bf16[4,144,512]{2,1,0:T(8,128)(2,1)}, u32[]{:S(2)}, u32[]{:S(2)}) collective-permute-start(bf16[4,144,512]{2,1,0:T(8,128)(2,1)} %collective-permute-done.67.rest_0_), channel_id=1, source_target_pairs={{0,8},{8,16},{16,24},{24,28},{28,20},{20,12},{12,4},{4,0},{1,9},{9... | collective-permute-start | bytes 1769480 | tf_op jit(solution)/shard_map/ppermute | solution.py:718
  335.1 22.3 %collective-permute-start.70 = (bf16[4,144,512]{2,1,0:T(8,128)(2,1)}, bf16[4,144,512]{2,1,0:T(8,128)(2,1)}, u32[]{:S(2)}, u32[]{:S(2)}) collective-permute-start(bf16[4,144,512]{2,1,0:T(8,128)(2,1)} %collective-permute-done.68.rest_1_), channel_id=1, source_target_pairs={{0,4},{8,0},{16,8},{24,16},{28,24},{20,28},{12,20},{4,12},{1,5},{9... | collective-permute-start | bytes 1769480 | tf_op jit(solution)/shard_map/ppermute | solution.py:718
  357.4 15.5 %collective-permute-start.71 = (bf16[4,144,512]{2,1,0:T(8,128)(2,1)}, bf16[4,144,512]{2,1,0:T(8,128)(2,1)S(1)}, u32[]{:S(2)}, u32[]{:S(2)}) collective-permute-start(bf16[4,144,512]{2,1,0:T(8,128)(2,1)} %collective-permute-done.69.rest_0_), channel_id=1, source_target_pairs={{0,8},{8,16},{16,24},{24,28},{28,20},{20,12},{12,4},{4,0},{1,9},{9... | collective-permute-start | bytes 1769480 | tf_op jit(solution)/shard_map/ppermute | solution.py:718
  372.9 26.2 %collective-permute-start.73 = (bf16[4,144,512]{2,1,0:T(8,128)(2,1)S(1)}, bf16[4,144,512]{2,1,0:T(8,128)(2,1)S(1)}, u32[]{:S(2)}, u32[]{:S(2)}) collective-permute-start(bf16[4,144,512]{2,1,0:T(8,128)(2,1)S(1)} %collective-permute-done.71.rest_0_), channel_id=1, source_target_pairs={{0,8},{8,16},{16,24},{24,28},{28,20},{20,12},{12,4},{4,0},{1,9},{9... | collective-permute-start | bytes 1769480 | tf_op jit(solution)/shard_map/ppermute | solution.py:718
  412.6 46.0 %collective-permute-start.74 = (bf16[4,2,512,256]{3,2,1,0:T(8,128)(2,1)}, bf16[4,2,512,256]{3,2,1,0:T(8,128)(2,1)S(1)}, u32[]{:S(2)}, u32[]{:S(2)}) collective-permute-start(bf16[4,2,512,256]{3,2,1,0:T(8,128)(2,1)} %slice.416), channel_id=1, source_target_pairs={{0,4},{4,0},{8,12},{12,8},{16,20},{20,16},{24,28},{28,24},{1,5},{5... | collective-permute-start | bytes 6291464 | tf_op jit(solution)/shard_map/ppermute | solution.py:723
  459.4 39.7 %collective-permute-start.75 = (bf16[2,512,256]{2,1,0:T(8,128)(2,1)S(1)}, bf16[2,512,256]{2,1,0:T(8,128)(2,1)S(1)}, u32[]{:S(2)}, u32[]{:S(2)}) collective-permute-start(bf16[2,512,256]{2,1,0:T(8,128)(2,1)S(1)} %get-tuple-element.411), channel_id=1, source_target_pairs={{0,8},{4,12},{8,16},{12,20},{16,24},{20,28},{24,0},{28,4},{1,9},{5... | collective-permute-start | bytes 1572872 | tf_op jit(solution)/shard_map/ppermute | solution.py:728
  462.9 36.2 %collective-permute-start.76 = (bf16[2,512,256]{2,1,0:T(8,128)(2,1)S(1)}, bf16[2,512,256]{2,1,0:T(8,128)(2,1)S(1)}, u32[]{:S(2)}, u32[]{:S(2)}) collective-permute-start(bf16[2,512,256]{2,1,0:T(8,128)(2,1)S(1)} %get-tuple-element.410), channel_id=1, source_target_pairs={{0,16},{4,20},{8,24},{12,28},{16,0},{20,4},{24,8},{28,12},{1,17},{... | collective-permute-start | bytes 1572872 | tf_op jit(solution)/shard_map/ppermute | solution.py:728
  465.6 33.5 %collective-permute-start.77 = (bf16[2,512,256]{2,1,0:T(8,128)(2,1)S(1)}, bf16[2,512,256]{2,1,0:T(8,128)(2,1)S(1)}, u32[]{:S(2)}, u32[]{:S(2)}) collective-permute-start(bf16[2,512,256]{2,1,0:T(8,128)(2,1)S(1)} %get-tuple-element.409), channel_id=1, source_target_pairs={{0,24},{4,28},{8,0},{12,4},{16,8},{20,12},{24,16},{28,20},{1,25},{... | collective-permute-start | bytes 1572872 | tf_op jit(solution)/shard_map/ppermute | solution.py:728
  510.8 19.2 %collective-permute-start.79 = (bf16[4,2,16,2176]{3,2,1,0:T(8,128)(2,1)S(1)}, bf16[4,2,16,2176]{3,2,1,0:T(8,128)(2,1)S(1)}, u32[]{:S(2)}, u32[]{:S(2)}) collective-permute-start(bf16[4,2,16,2176]{3,2,1,0:T(8,128)(2,1)S(1)} %select_bitcast_fusion.3), channel_id=1, source_target_pairs={{0,2},{1,3},{2,0},{3,1},{4,6},{5,7},{6,4},{7,5},{8,10},{9,11},{10,... | collective-permute-start | bytes 1671176 | tf_op jit(solution)/shard_map/ppermute | solution.py:723
  (121 other events, 1362.3 us)

commit v3 on v2

--- a/solution.py
+++ b/solution.py
@@ -43,41 +43,48 @@
     return jnp.where(low, x[:half], x[half:])
 
 
-def attn_fwd_kernel(width, begin, count, lo_ref, vlen_ref, start_ref, joined_ref, out_ref, bias_ref):
-    row = pl.program_id(0)
-    vlen = vlen_ref[row]
-
-    def block(step, _):
-        qb = step + begin
-        lo = lo_ref[row, qb]
+def attn_fwd_kernel(width, batch, count, lo_ref, vlen_ref, start_ref, joined_ref, out_ref, log_ref, bias_ref):
+    row = pl.program_id(0) * batch
+
+    def block(qb, _):
+        lo = functools.reduce(jnp.minimum, [lo_ref[row + r, qb] for r in range(batch)])
         base = pl.multiple_of(qb * QB, QB)
         first = pl.multiple_of(lo * QB, QB)
         own = pl.ds(base, QB)
-        target = pl.ds(pl.multiple_of(step * QB, QB), QB)
 
         def variant(blocks):
             span = blocks * QB
             keys = pl.ds(first, span)
-            begins = jnp.broadcast_to(start_ref[0, pl.ds(qb, 1), :], (QB, QB)).T
             i = base + iota((QB, QB), 0)
-            for b in range(blocks):
-                j = first + b * QB + iota((QB, QB), 1)
-                ok = ((j >= begins) & (j <= i) & (j < vlen)) | (j == i)
-                bias_ref[:, b * QB:(b + 1) * QB] = jnp.where(ok, 0.0, NEGATIVE)
-            bias = bias_ref[:, :span]
-            bias = jnp.concatenate([bias, bias], axis=0)
-            at = [pl.ds(lane, 128) for lane in range(0, width, 128)]
-            key_at = [pl.ds(width + lane, 128) for lane in range(0, width, 128)]
-            value_at = [pl.ds(2 * width + lane, 128) for lane in range(0, width, 128)]
-            query = [split_heads(joined_ref[0, own, lanes] * jnp.asarray(0.125, BF16)) for lanes in at]
-            scores = [dot_nt(q, joined_ref[0, keys, lanes]) for q, lanes in zip(query, key_at)]
-            scores = [s + bias for s in scores]
+            bias = []
+            for r in range(batch):
+                begins = jnp.broadcast_to(start_ref[r, pl.ds(qb, 1), :], (QB, QB)).T
+                for b in range(blocks):
+                    j = first + b * QB + iota((QB, QB), 1)
+                    ok = ((j >= begins) & (j <= i) & (j < vlen_ref[row + r])) | (j == i)
+                    bias_ref[r, :, b * QB:(b + 1) * QB] = jnp.where(ok, 0.0, NEGATIVE)
+                bias.append(jnp.concatenate([bias_ref[r, :, :span]] * 2, axis=0))
+            work = [(r, lane) for r in range(batch) for lane in range(0, width, 128)]
+            query = [split_heads(joined_ref[r, own, pl.ds(at, 128)] * jnp.asarray(0.125, BF16)) for r, at in work]
+            scores = [dot_nt(q, joined_ref[r, keys, pl.ds(width + at, 128)]) for q, (r, at) in zip(query, work)]
+            scores = [s + bias[r] for s, (r, _) in zip(scores, work)]
             tops = [jnp.max(s, axis=1, keepdims=True) for s in scores]
             raised = [jnp.exp(s - top) for s, top in zip(scores, tops)]
             totals = [jnp.sum(p, axis=1, keepdims=True) for p in raised]
-            out = [dot(p.astype(BF16), joined_ref[0, keys, lanes]) for p, lanes in zip(raised, value_at)]
-            for o, total, lanes in zip(out, totals, at):
-                out_ref[0, target, lanes] = join_heads(o * (1.0 / total)).astype(BF16)
+            out = [
+                dot(p.astype(BF16), joined_ref[r, keys, pl.ds(2 * width + at, 128)]) for p, (r, at) in zip(raised, work)
+            ]
+            for o, total, (r, at) in zip(out, totals, work):
+                out_ref[r, own, pl.ds(at, 128)] = join_heads(o * (1.0 / total)).astype(BF16)
+            lane = iota((QB, QB), 1)
+            for r in range(batch):
+                tile = jnp.zeros((QB, QB), F32)
+                for top, total, (other, at) in zip(tops, totals, work):
+                    if other == r:
+                        log = top + jnp.log(total)
+                        tile = jnp.where(lane == at // 64, log[:QB], tile)
+                        tile = jnp.where(lane == at // 64 + 1, log[QB:], tile)
+                log_ref[r, pl.ds(qb, 1)] = tile.T[None, : log_ref.shape[2]]
 
         for blocks in range(1, 6):
             pl.when(qb - lo + 1 == blocks)(functools.partial(variant, blocks))
@@ -86,113 +93,126 @@
     lax.fori_loop(0, count, block, 0)
 
 
-def attn_fwd(joined, starts, lows, vlens, begin, count):
+def attn_fwd(joined, starts, lows, vlens, batch=2):
     rows, length, triple = joined.shape
     width = triple // 3
-    spec = pltpu.PrefetchScalarGridSpec(
-        num_scalar_prefetch=2,
-        grid=(rows,),
-        in_specs=[
-            pl.BlockSpec((1, length // QB, QB), lambda r, *_: (r, 0, 0)),
-            pl.BlockSpec((1, length, triple), lambda r, *_: (r, 0, 0)),
+    count = length // QB
+    return pl.pallas_call(
+        functools.partial(attn_fwd_kernel, width, batch, count),
+        grid_spec=pltpu.PrefetchScalarGridSpec(
+            num_scalar_prefetch=2,
+            grid=(rows // batch,),
+            in_specs=[
+                pl.BlockSpec((batch, count, QB), lambda r, *_: (r, 0, 0)),
+                pl.BlockSpec((batch, length, triple), lambda r, *_: (r, 0, 0)),
+            ],
+            out_specs=[
+                pl.BlockSpec((batch, length, width), lambda r, *_: (r, 0, 0)),
+                pl.BlockSpec((batch, count, width // 64, QB), lambda r, *_: (r, 0, 0, 0)),
+            ],
+            scratch_shapes=[pltpu.VMEM((batch, QB, 5 * QB), F32)],
+        ),
+        out_shape=[
+            jax.ShapeDtypeStruct((rows, length, width), BF16),
+            jax.ShapeDtypeStruct((rows, count, width // 64, QB), F32),
         ],
-        out_specs=pl.BlockSpec((1, count * QB, width), lambda r, *_: (r, 0, 0)),
-        scratch_shapes=[pltpu.VMEM((QB, 5 * QB), F32)],
-    )
-    return pl.pallas_call(
-        functools.partial(attn_fwd_kernel, width, begin, count),
-        grid_spec=spec,
-        out_shape=jax.ShapeDtypeStruct((rows, count * QB, width), BF16),
         compiler_params=pltpu.CompilerParams(vmem_limit_bytes=48 << 20),
-        cost_estimate=pl.CostEstimate(flops=rows * count * QB * 400 * 8 * 256 * 4, bytes_accessed=rows * length * triple * 2, transcendentals=0),
+        cost_estimate=pl.CostEstimate(
+            flops=rows * length * 400 * 8 * 256 * 4, bytes_accessed=rows * length * triple * 2, transcendentals=0
+        ),
         name="attend",
     )(lows, vlens, starts, joined)
 
 
-def attn_bwd_kernel(width, row_from, count, lo_ref, vlen_ref, start_ref, joined_ref, grad_ref, *rest):
+def attn_bwd_kernel(width, row_from, batch, count, lo_ref, vlen_ref, start_ref, joined_ref, grad_ref, attended_ref, log_ref, *rest):
     out_ref, dk_ref, dv_ref, bias_ref = rest[-4:]
-    row = pl.program_id(0) + row_from
-    vlen = vlen_ref[row]
+    row = pl.program_id(0) * batch + row_from
     dk_ref[...] = jnp.zeros_like(dk_ref)
     dv_ref[...] = jnp.zeros_like(dv_ref)
 
-    def block(step, _):
-        qb = step
-        lo = lo_ref[row, qb]
+    def block(qb, _):
+        lo = functools.reduce(jnp.minimum, [lo_ref[row + r, qb] for r in range(batch)])
         base = pl.multiple_of(qb * QB, QB)
         first = pl.multiple_of(lo * QB, QB)
         own = pl.ds(base, QB)
-        target = pl.ds(pl.multiple_of(step * QB, QB), QB)
 
         def variant(blocks):
             span = blocks * QB
             keys = pl.ds(first, span)
-            begins = start_ref[0, pl.ds(qb, 1), :]
             i = base + iota((QB, QB), 1)
-            for b in range(blocks):
-                j = first + b * QB + iota((QB, QB), 0)
-                ok = ((j >= begins) & (j <= i) & (j < vlen)) | (j == i)
-                bias_ref[b * QB:(b + 1) * QB, :] = jnp.where(ok, 0.0, NEGATIVE)
-            bias = bias_ref[:span, :]
-            bias = jnp.concatenate([bias, bias], axis=1)
-            at = [pl.ds(lane, 128) for lane in range(0, width, 128)]
-            key_at = [pl.ds(width + lane, 128) for lane in range(0, width, 128)]
-            value_at = [pl.ds(2 * width + lane, 128) for lane in range(0, width, 128)]
-            query = [split_heads(joined_ref[0, own, lanes] * jnp.asarray(0.125, BF16)) for lanes in at]
-            grads = [split_heads(grad_ref[0, target, lanes]) for lanes in at]
-            scores = [dot_nt(joined_ref[0, keys, lanes], q) for q, lanes in zip(query, key_at)]
-            change = [dot_nt(joined_ref[0, keys, lanes], g) for g, lanes in zip(grads, value_at)]
-            scores = [s + bias for s in scores]
-            tops = [jnp.max(s, axis=0, keepdims=True) for s in scores]
-            prob = [jnp.exp(s - top) for s, top in zip(scores, tops)]
-            totals = [1.0 / jnp.sum(p, axis=0, keepdims=True) for p in prob]
-            prob = [p * total for p, total in zip(prob, totals)]
-            scaled = [p * c for p, c in zip(prob, change)]
-            sums = [jnp.sum(t, axis=0, keepdims=True) for t in scaled]
-            moved = [(t - p * total).astype(BF16) for t, p, total in zip(scaled, prob, sums)]
-            for p, g, lanes in zip(prob, grads, at):
-                dv_ref[keys, lanes] += dot(p.astype(BF16), g)
-            for m, q, lanes in zip(moved, query, at):
-                dk_ref[keys, lanes] += dot(m, q)
-            back = [dot_tn(m, joined_ref[0, keys, lanes]) for m, lanes in zip(moved, key_at)]
-            for b, lanes in zip(back, at):
-                out_ref[0, target, lanes] = (join_heads(b) * 0.125).astype(BF16)
+            pick = jnp.where(iota((16, width), 1) // 64 == iota((16, width), 0), 1.0, 0.0).astype(BF16)
+            bias, sums = [], []
+            for r in range(batch):
+                begins = start_ref[r, pl.ds(qb, 1), :]
+                for b in range(blocks):
+                    j = first + b * QB + iota((QB, QB), 0)
+                    ok = ((j >= begins) & (j <= i) & (j < vlen_ref[row + r])) | (j == i)
+                    bias_ref[r, b * QB:(b + 1) * QB, :] = jnp.where(ok, 0.0, NEGATIVE)
+                bias.append(jnp.concatenate([bias_ref[r, :span, :]] * 2, axis=1))
+                product = grad_ref[r, own, :].astype(F32) * attended_ref[r, own, :].astype(F32)
+                high = product.astype(BF16)
+                sums.append(dot_nt(pick, high) + dot_nt(pick, (product - high.astype(F32)).astype(BF16)))
+            work = [(r, lane) for r in range(batch) for lane in range(0, width, 128)]
+            query = [split_heads(joined_ref[r, own, pl.ds(at, 128)] * jnp.asarray(0.125, BF16)) for r, at in work]
+            grads = [split_heads(grad_ref[r, own, pl.ds(at, 128)]) for r, at in work]
+            prob, moved = [], []
+            for q, g, (r, at) in zip(query, grads, work):
+                head = at // 64
+                log = log_ref[r, qb]
+                log = jnp.concatenate([log[head: head + 1], log[head + 1: head + 2]], axis=1)
+                total = jnp.concatenate([sums[r][head: head + 1], sums[r][head + 1: head + 2]], axis=1)
+                scores = dot_nt(joined_ref[r, keys, pl.ds(width + at, 128)], q)
+                change = dot_nt(joined_ref[r, keys, pl.ds(2 * width + at, 128)], g)
+                p = jnp.exp(scores + bias[r] - log)
+                prob.append(p.astype(BF16))
+                moved.append((p * (change - total)).astype(BF16))
+            for p, g, (r, at) in zip(prob, grads, work):
+                dv_ref[r, keys, pl.ds(at, 128)] += dot(p, g)
+            for m, q, (r, at) in zip(moved, query, work):
+                dk_ref[r, keys, pl.ds(at, 128)] += dot(m, q)
+            back = [dot_tn(m, joined_ref[r, keys, pl.ds(width + at, 128)]) for m, (r, at) in zip(moved, work)]
+            for b, (r, at) in zip(back, work):
+                out_ref[r, own, pl.ds(at, 128)] = (join_heads(b) * 0.125).astype(BF16)
 
         for blocks in range(1, 6):
             pl.when(qb - lo + 1 == blocks)(functools.partial(variant, blocks))
         return 0
 
     lax.fori_loop(0, count, block, 0)
-    out_ref[0, :, width: 2 * width] = dk_ref[...].astype(BF16)
-    out_ref[0, :, 2 * width:] = dv_ref[...].astype(BF16)
-
-
-def attn_bwd(joined, grads, starts, lows, vlens, row_from, row_to, held=None):
+    out_ref[:, :, width: 2 * width] = dk_ref[...].astype(BF16)
+    out_ref[:, :, 2 * width:] = dv_ref[...].astype(BF16)
+
+
+def attn_bwd(joined, grads, attended, logs, starts, lows, vlens, row_from, row_to, held=None, batch=1):
     rows, length, triple = joined.shape
     width = triple // 3
     count = length // QB
     aliased = [] if held is None else [held]
-    wide = pl.BlockSpec((1, length, triple), lambda r, *_: (r + row_from, 0, 0))
+    skip = row_from // batch
+    wide = pl.BlockSpec((batch, length, triple), lambda r, *_: (r + skip, 0, 0))
+    slim = pl.BlockSpec((batch, length, width), lambda r, *_: (r + skip, 0, 0))
     return pl.pallas_call(
-        functools.partial(attn_bwd_kernel, width, row_from, count),
+        functools.partial(attn_bwd_kernel, width, row_from, batch, count),
         grid_spec=pltpu.PrefetchScalarGridSpec(
             num_scalar_prefetch=2,
-            grid=(row_to - row_from,),
+            grid=((row_to - row_from) // batch,),
             in_specs=[
-                pl.BlockSpec((1, count, QB), lambda r, *_: (r + row_from, 0, 0)),
+                pl.BlockSpec((batch, count, QB), lambda r, *_: (r + skip, 0, 0)),
                 wide,
-                pl.BlockSpec((1, length, width), lambda r, *_: (r + row_from, 0, 0)),
+                slim,
+                slim,
+                pl.BlockSpec((batch,) + logs.shape[1:], lambda r, *_: (r + skip, 0, 0, 0)),
             ]
             + [pl.BlockSpec(memory_space=pltpu.HBM) for _ in aliased],
             out_specs=wide,
             scratch_shapes=[
-                pltpu.VMEM((length, width), F32),
-                pltpu.VMEM((length, width), F32),
-                pltpu.VMEM((5 * QB, QB), F32),
+                pltpu.VMEM((batch, length, width), F32),
+                pltpu.VMEM((batch, length, width), F32),
+                pltpu.VMEM((batch, 5 * QB, QB), F32),
             ],
         ),
         out_shape=jax.ShapeDtypeStruct(joined.shape, BF16),
-        input_output_aliases={5: 0} if aliased else {},
+        input_output_aliases={7: 0} if aliased else {},
         compiler_params=pltpu.CompilerParams(vmem_limit_bytes=48 << 20),
         cost_estimate=pl.CostEstimate(
             flops=(row_to - row_from) * length * 400 * 8 * 256 * 20,
@@ -200,7 +220,7 @@
             transcendentals=0,
         ),
         name="attend_back",
-    )(lows, vlens, starts, joined, grads, *aliased)
+    )(lows, vlens, starts, joined, grads, attended, logs, *aliased)
 
 
 def normalise(values):
@@ -217,18 +237,26 @@
     )
 
 
+PIECE = 256
+
+
+def pieces(count):
+    return [slice(at, min(at + PIECE, count)) for at in range(0, count, PIECE)]
+
+
 def constant_spec(shape, *where):
     where = where or (0,) * len(shape)
     return pl.BlockSpec(shape, lambda *_: where)
 
 
 def join_kernel(tokens_ref, gains_ref, weight_ref, joined_ref):
-    hat, _ = normalise(tokens_ref[0].astype(F32))
-    normed = (hat * gains_ref[0:1] + gains_ref[1:2]).astype(BF16)
-    joined_ref[0] = dot(normed, weight_ref[...]).astype(BF16)
-
-
-def join_tokens(tokens, gains, packed, tile=512):
+    for at in pieces(tokens_ref.shape[1]):
+        hat, _ = normalise(tokens_ref[0, at].astype(F32))
+        normed = (hat * gains_ref[0:1] + gains_ref[1:2]).astype(BF16)
+        joined_ref[0, at] = dot(normed, weight_ref[...]).astype(BF16)
+
+
+def join_tokens(tokens, gains, packed, tile=1024):
     rows, length, width = tokens.shape
     return pl.pallas_call(
         join_kernel,
@@ -257,7 +285,7 @@
     logits_ref[0] = dot_nt(router_ref[...], mixed)
 
 
-def mix_tokens(attended, tokens, gains, packed, router, offset, tile=512):
+def mix_tokens(attended, tokens, gains, packed, router, offset, tile=1024):
     rows, span, width = attended.shape
     block = pl.BlockSpec((1, tile, width), lambda r, t: (r, t, 0))
     return pl.pallas_call(
@@ -297,7 +325,7 @@
             out_ref[0, e, here, :] = (scale * total).astype(BF16)
         return 0
 
-    lax.fori_loop(0, places // sub, step, 0, unroll=2)
+    lax.fori_loop(0, places // sub, step, 0, unroll=8)
 
 
 def pool_tokens(slots, gates, values, experts, scale):
@@ -477,7 +505,7 @@
         change_ref[0, here, :] = changes
         return 0
 
-    lax.fori_loop(0, places // sub, step, 0, unroll=2)
+    lax.fori_loop(0, places // sub, step, 0, unroll=8)
 
 
 def slot_of(found):
@@ -510,7 +538,7 @@
             jax.ShapeDtypeStruct((len(parts), places, columns), F32),
         ],
         input_output_aliases={4 + len(parts): 0} if aliased else {},
-        compiler_params=pltpu.CompilerParams(vmem_limit_bytes=24 << 20),
+        compiler_params=pltpu.CompilerParams(vmem_limit_bytes=58 << 20),
         cost_estimate=pl.CostEstimate(
             flops=len(parts) * rows * places * width * 5000, bytes_accessed=rows * places * width * 10, transcendentals=0
         ),
@@ -561,7 +589,7 @@
         logits_ref[here, :] = changes
         return 0
 
-    lax.fori_loop(0, places // sub, change, 0, unroll=2)
+    lax.fori_loop(0, places // sub, change, 0, unroll=8)
     changes = (logits_ref[...] + change_ref[0]).astype(BF16).astype(F32)
     low = (gates_ref[...] * (changes - inner)).astype(BF16)
     for r in range(rows):
@@ -579,7 +607,7 @@
             )
         return 0
 
-    lax.fori_loop(0, places // sub, spread, 0, unroll=2)
+    lax.fori_loop(0, places // sub, spread, 0, unroll=8)
 
     for r in range(rows):
         grads = grad_ref[r].astype(BF16).astype(F32)
@@ -633,7 +661,7 @@
         out_shape=[jax.ShapeDtypeStruct((rows, span, width), F32), jax.ShapeDtypeStruct((rows, span, width), BF16)]
         + [jax.ShapeDtypeStruct(shape, F32) for shape in sums],
         input_output_aliases=aliases,
-        compiler_params=pltpu.CompilerParams(vmem_limit_bytes=32 << 20),
+        compiler_params=pltpu.CompilerParams(vmem_limit_bytes=58 << 20),
         cost_estimate=pl.CostEstimate(
             flops=len(parts) * rows * places * width * width * 20,
             bytes_accessed=rows * places * width * 20,
@@ -655,7 +683,7 @@
     sums_ref[...] += dot_tn(ones, grads_ref[0])
 
 
-def project_grads(grads, tokens, tile=512):
+def project_grads(grads, tokens, tile=1024):
     rows, length, width = tokens.shape
     shapes = [(width, 3 * width), (8, 3 * width)]
     return pl.pallas_call(
@@ -669,39 +697,49 @@
         out_shape=[jax.ShapeDtypeStruct(shape, F32) for shape in shapes],
         compiler_params=pltpu.CompilerParams(vmem_limit_bytes=40 << 20),
         cost_estimate=pl.CostEstimate(
-            flops=rows * length * width * width * 6, bytes_accessed=rows * length * width * 12, transcendentals=0
+            flops=rows, bytes_accessed=rows, transcendentals=0
         ),
         name="project_grads",
     )(grads, tokens)
 
 
-def tokens_kernel(grads_ref, tokens_ref, hidden_ref, gains_ref, weight_ref, out_ref):
-    hat, inverse = normalise(tokens_ref[0].astype(F32))
-    grads = dot_nt(grads_ref[0], weight_ref[...])
-    out_ref[0] = hidden_ref[0] + pull_norm(grads * gains_ref[0:1], hat, inverse)
-
-
-def pull_tokens(grads, tokens, hidden, gains, packed, tile=512):
+def tokens_kernel(grads_ref, tokens_ref, hidden_ref, gains_ref, weight_ref, *rest):
+    out_ref = rest[-1]
+    for at in pieces(tokens_ref.shape[1]):
+        hat, inverse = normalise(tokens_ref[0, at].astype(F32))
+        grads = dot_nt(grads_ref[0, at], weight_ref[...])
+        out_ref[0, at] = hidden_ref[0, at] + pull_norm(grads * gains_ref[0:1], hat, inverse)
+
+
+def pull_tokens(grads, tokens, hidden, gains, packed, row_from, row_to, held=None, tile=1024):
     rows, length, width = tokens.shape
-    block = pl.BlockSpec((1, tile, width), lambda r, t: (r, t, 0))
+    block = pl.BlockSpec((1, tile, width), lambda r, t: (r + row_from, t, 0))
+    aliased = [] if held is None else [held]
     return pl.pallas_call(
         tokens_kernel,
-        grid=(rows, length // tile),
+        grid=(row_to - row_from, length // tile),
         in_specs=[
-            pl.BlockSpec((1, tile, 3 * width), lambda r, t: (r, t, 0)),
+            pl.BlockSpec((1, tile, 3 * width), lambda r, t: (r + row_from, t, 0)),
             block,
             block,
             constant_spec(gains.shape),
             constant_spec((width, 3 * width)),
-        ],
+        ]
+        + [pl.BlockSpec(memory_space=pltpu.HBM) for _ in aliased],
         out_specs=block,
         out_shape=jax.ShapeDtypeStruct((rows, length, width), F32),
-        compiler_params=pltpu.CompilerParams(vmem_limit_bytes=40 << 20),
+        input_output_aliases={5: 0} if aliased else {},
+        compiler_params=pltpu.CompilerParams(vmem_limit_bytes=58 << 20),
         cost_estimate=pl.CostEstimate(
-            flops=rows * length * width * width * 20, bytes_accessed=rows * length * width * 16, transcendentals=0
+            flops=(row_to - row_from) * length * width * width * 20,
+            bytes_accessed=(row_to - row_from) * length * width * 16,
+            transcendentals=0,
         ),
         name="pull_tokens",
-    )(grads, tokens, hidden, gains, packed)
+    )(grads, tokens, hidden, gains, packed, *aliased)
+
+
+LAG = 0
 
 
 def ring_order(size):
@@ -753,61 +791,76 @@
     def left(self):
         return self.done < len(self.order) // 2
 
+    def after(self, *values):
+        self.ahead, self.behind, *_ = together(self.ahead, self.behind, *values)
+
     def step(self, *beside):
         count = len(self.order)
         self.done += 1
-        found = {count - self.done: shift(self.ahead, self.order, 1)}
-        if 2 * self.done < count:
-            found[self.done] = shift(self.behind, self.order, -1)
-        values = together(*found.values(), *beside)
-        found = dict(zip(found, values))
-        self.ahead = found[count - self.done]
-        self.behind = found.get(self.done)
-        return found, list(values[len(found):])
-
-
-def gather_all(value, order, spots):
-    count = len(order)
+        slot = count - self.done
+        ahead, behind = self.ahead, self.behind
+        middle = 2 * self.done == count and ahead.shape[0] % 2 == 0
+        if middle:
+            half = ahead.shape[0] // 2
+            ahead, behind = ahead[:half], behind[half:]
+        ahead = shift(ahead, self.order, 1)
+        if 2 * self.done < count or middle:
+            behind = shift(behind, self.order, -1)
+        ahead, behind, *beside = together(ahead, behind, *beside)
+        self.ahead, self.behind = ahead, behind
+        if middle:
+            return {slot: jnp.concatenate([ahead, behind], axis=0)}, beside
+        return {slot: ahead, self.done: behind} if 2 * self.done < count else {slot: ahead}, beside
+
+
+def gather_all(value, steps):
+    pair = pair_of(lax.axis_size("dp"))
+    lines = lax.axis_size("dp") // pair
     size = lax.axis_size("fsdp")
-    whole = put(jnp.zeros((count,) + value.shape, value.dtype), value, spots[0])
-    ring = Ring(value, order)
-    while ring.left():
-        for slot, part in ring.step()[0].items():
-            whole = put(whole, part, spots[slot])
     here = lax.axis_index("fsdp")
-    whole = whole[:, None]
+
+    def both(value, bit, axis, index):
+        other = flip(value, bit, axis)
+        upper = (index & bit) != 0
+        return jnp.stack([jnp.where(upper, other, value), jnp.where(upper, value, other)])
+
+    value = both(value, 1, "dp", lax.axis_index("dp")) if pair == 2 else value[None]
+    whole = put(jnp.zeros((lines,) + value.shape, value.dtype), value, steps[0])
+    for k in range(1, lines):
+        whole = put(whole, turn(value, -k * pair), steps[k])
+    whole = whole.reshape((lines * pair, 1) + value.shape[1:])
     bit = size // 2
     while bit:
-        other = flip(whole, bit)
-        upper = (here & bit) != 0
-        whole = jnp.stack([jnp.where(upper, other, whole), jnp.where(upper, whole, other)], axis=1)
-        whole = whole.swapaxes(1, 2).reshape((count, -1) + value.shape)
+        whole = both(whole, bit, "fsdp", here)
+        whole = jnp.moveaxis(whole, 0, 2)
+        whole = whole.reshape((lines * pair, -1) + value.shape[1:])
         bit //= 2
     return whole
 
 
-def scatter_all(values, steps):
+def scatter_all(values, steps, work):
     owners, size = lax.axis_size("dp"), lax.axis_size("fsdp")
     bits = size.bit_length() - 1
     here = lax.axis_index("fsdp")
     width = values.shape[1]
     pair = pair_of(owners)
+    work = list(work)
+
+    def half(held, axis, upper, bit, name):
+        low, high = (lax.index_in_dim(held, i, axis, keepdims=False) for i in (0, 1))
+        came = flip(jnp.where(upper, low, high), bit, name)
+        if work:
+            came, = work.pop(0)(came)
+        return add(jnp.where(upper, high, low), came)
+
     held = values.reshape((owners // pair, pair) + (2,) * bits + (-1, width))
     for level in range(bits):
-        axis = bits + 1 - level
-        upper = ((here >> level) & 1) != 0
-        low, high = (lax.index_in_dim(held, i, axis, keepdims=False) for i in (0, 1))
-        held = add(jnp.where(upper, high, low), flip(jnp.where(upper, low, high), 1 << level))
-    if pair == 2:
-        upper = (lax.axis_index("dp") & 1) != 0
-        low, high = held[:, 0], held[:, 1]
-        held = add(jnp.where(upper, high, low), flip(jnp.where(upper, low, high), 1, "dp"))
-    else:
-        held = held[:, 0]
-    return sum(
-        (turn(take(held, steps[k]), k * pair).astype(F32) for k in range(1, owners // pair)),
-        take(held, steps[0]).astype(F32),
-    )
+        held = half(held, bits + 1 - level, ((here >> level) & 1) != 0, 1 << level, "fsdp")
+    held = half(held, 1, (lax.axis_index("dp") & 1) != 0, 1, "dp") if pair == 2 else held[:, 0]
+    came = [turn(take(held, steps[k]), k * pair) for k in range(1, owners // pair)]
+    while work:
+        came = work.pop(0)(*came)
+    return sum((value.astype(F32) for value in came), take(held, steps[0]).astype(F32))
 
 
 def pair_of(owners):
@@ -866,8 +919,7 @@
     small = jnp.pad(small, ((0, 0), (0, 128 - small.shape[1])))
     packed = jnp.concatenate([project_in, project_out, small], axis=1)
     weights = jnp.stack([expert_in[0], expert_out[0].T])
-    packed, weights = together(packed, weights)
-    packed = gather_all(packed, order, spots)
+    packed = gather_all(packed, steps)
     packed = packed.reshape(width, packed.shape[-1])
     packed, weights = together(packed, weights)
     kept = {0: weights}
@@ -897,7 +949,8 @@
         return value
 
     joined = meanwhile(join_tokens(tokens, gains, packed))
-    attended = meanwhile(attn_fwd(joined, starts, lows, vlens, 0, length // QB))
+    attended, logs = attn_fwd(joined, starts, lows, vlens, 1)
+    attended = meanwhile(attended)
     hidden, mixed, logits = mix_tokens(
         attended, tokens, gains, packed, jnp.pad(router, ((0, 16 - experts), (0, 0))), 0
     )
@@ -924,12 +977,16 @@
     second = [(grads[:, :half], 1), (grads[:, half:], -1)]
     held = [part[-way % owners] for part, way in first]
     later = [part[-way % owners] for part, way in second]
-    for step in range(owners - 1):
-        came = [shift(value, order, way) for value, (_, way) in zip(held, first)]
-        *came, one, two = together(*came, *later)
-        held = [add(value, part[-way * (2 + step) % owners]) for value, (part, way) in zip(came, first)]
-        came = [shift(value, order, way) for value, (_, way) in zip([one, two], second)]
-        later = [add(value, part[-way * (2 + step) % owners]) for value, (part, way) in zip(came, second)]
+    for step in range(owners - 1 + LAG):
+        if step < owners - 1:
+            came = [shift(value, order, way) for value, (_, way) in zip(held, first)]
+            *came, one, two = together(*came, *later)
+            later = [one, two]
+            held = [add(value, part[-way * (2 + step) % owners]) for value, (part, way) in zip(came, first)]
+        back = step - LAG
+        if back >= 0:
+            came = [shift(value, order, way) for value, (_, way) in zip(later, second)]
+            later = [add(value, part[-way * (2 + back) % owners]) for value, (part, way) in zip(came, second)]
     pooled = exchange(jnp.concatenate(held, axis=0))
     result, act, slope = run_experts(pooled, weights)
     grads = exchange(jnp.concatenate(later, axis=0))
@@ -938,51 +995,50 @@
     result = exchange(result)
     back = exchange(grad_pooled)
 
-    def spread(found, out):
-        return spread_tokens(found, slots, gates, cotangent, hidden, group, out)
-
     def pull(found, change, out):
         return pull_slots(
             found, slots, gates, change, mixed, hidden, cotangent, attended, spread_router, gains, packed, out
         )
 
+    def spread(found, out):
+        return spread_tokens(found, slots, gates, cotangent, hidden, group, out)
+
     turns = owners // 2
-    ring, groups = Ring(result, order), [{0: result}]
+    first, second = Ring(result, order), Ring(back, order)
+    found, (grad_weights,) = first.step(grad_weights)
+    groups, arrived = [{0: result}, found], [{0: back}]
     out, pulled, changes = None, None, []
-    for step in range(turns):
-        if step == 0:
-            found, (grad_weights,) = ring.step(grad_weights)
-        else:
-            out, change = spread(groups[step - 1], out)
-            found, (out, change) = ring.step(out, change)
-            changes.append(change)
-        groups.append(found)
-    ring, arrived = Ring(together(back, *found.values())[0], order), [{0: back}]
-    for step in range(turns):
-        if step < 2:
-            out, change = spread(groups[turns - 1 + step], out)
-            changes.append(change)
+    for step in range(turns + 1):
+        second.after(*groups[-1].values())
+        work = []
+        out, change = spread(groups[step], out)
+        work = [out, change]
         if step > 0:
             pulled = pull(arrived[step - 1], changes[step - 1], pulled)
-        if step == turns - 1:
-            pulled = pull(arrived[step], changes[step], pulled)
-        found, (out, *held) = ring.step(out, *(pulled or ()))
-        pulled = held or None
-        arrived.append(found)
+            work += pulled
+        if first.left():
+            found, work = first.step(*work)
+            groups.append(found)
+        if second.left():
+            found, work = second.step(*work)
+            arrived.append(found)
+        out, change, *pulled = work
+        pulled = pulled or None
+        changes.append(change)
+    layer_out = out
     pulled = pull(arrived[turns], changes[turns], pulled)
-    layer_out = out
     grad_hidden, grad_attended, router_grad, grad_proj_out, sums_two = pulled
     grad_attended, grad_weights = together(grad_attended, grad_weights)
     split = rows - max(1, rows // 4)
     if pair == 2:
         came = flip(grad_weights[lines:], 1, "dp")
-    grads = attn_bwd(joined, grad_attended, starts, lows, vlens, 0, split)
+    grads = attn_bwd(joined, grad_attended, attended, logs, starts, lows, vlens, 0, split)
     grad_weights = grad_weights[:lines]
     if pair == 2:
         came, grads = together(came, grads)
         grad_weights = add(grad_weights, came)
     came = [turn(grad_weights[k], k * pair) for k in range(1, lines)]
-    grads = attn_bwd(joined, grad_attended, starts, lows, vlens, split, rows, grads)
+    grads = attn_bwd(joined, grad_attended, attended, logs, starts, lows, vlens, split, rows, grads)
     product, sums_one = project_grads(grads, tokens)
     product, *came = together(product, *came)
     grad_weights = sum((value.astype(F32) for value in came), grad_weights[0].astype(F32))
@@ -990,12 +1046,25 @@
     sums_one = sums_one[:1]
     grad_proj_in = gains[0][:, None] * product + gains[1][:, None] * sums_one
     sums_one = jnp.stack([jnp.sum(full_in * product, axis=1), jnp.sum(full_in * sums_one, axis=1)])
-    tokens_grad = pull_tokens(grads, tokens, grad_hidden, gains, packed)
     router_grad = jnp.sum(jnp.where(mine[:, :, None], router_grad[None], 0.0), axis=1)
 
     late = jnp.concatenate([router_grad, sums_one, sums_two[:2]], axis=0).T
     late = jnp.pad(late, ((0, 0), (0, 128 - late.shape[1])))
-    reduced = scatter_all(jnp.concatenate([grad_proj_in, grad_proj_out, late], axis=1).astype(BF16), steps)
+    reduced = jnp.concatenate([grad_proj_in, grad_proj_out, late], axis=1).astype(BF16)
+    made = {"grad": None}
+
+    def rows_beside(start, stop):
+        def run(*came):
+            made["grad"] = pull_tokens(grads, tokens, grad_hidden, gains, packed, start, stop, made["grad"])
+            *came, made["grad"] = together(*came, made["grad"])
+            return came
+
+        return run
+
+    middle = rows - max(1, rows // 4)
+    work = [lambda *came: came, rows_beside(0, middle), rows_beside(middle, rows)]
+    reduced = scatter_all(reduced, steps, work)
+    tokens_grad = made["grad"]
     late = reduced[:, 4 * width:]
     return (
         layer_out[None],

time: 566 us -> 529 us (0.935)
  local copies, waits for them, and re-layouts: 58.5 us -> 28.6 us
  waiting for transfers between devices: 127 us -> 143 us
  Pallas kernels: 242 us -> 233 us
  starting transfers between devices: 102 us -> 94.4 us
    unnamed x137 -> x117, local copies, waits for them, and re-layouts: 48.8 us -> 19.4 us
    ppermute x9 -> x12, waiting for transfers between devices: 9.38 us -> 19.9 us  [turn(): lax.ppermute(value, axis, [(i, (i + step) % count) for i in range(count)])]
    ppermute x56 -> x52, starting transfers between devices: 64.7 us -> 54.2 us  [shift(): lax.ppermute(value, 'dp', [(order[i], order[(i + step) % count]) for i in...]
    pallas_call x4 -> x5, Pallas kernels: 105 us -> 98.4 us  [the longest x2 49.8 us: attn_bwd(): pl.pallas_call(functools.partial(attn_bwd_kernel, width, row_from, batch,...]
    ppermute x19 -> x20, waiting for transfers between devices: 33.9 us -> 39 us  [flip(): return lax.ppermute(value, axis, [(i, i ^ bit) for i in range(count)])]
    ppermute x9 -> x12, starting transfers between devices: 22.2 us -> 24.7 us  [turn(): lax.ppermute(value, axis, [(i, (i + step) % count) for i in range(count)])]
    ppermute x19 -> x20, starting transfers between devices: 14.9 us -> 15.5 us  [flip(): return lax.ppermute(value, axis, [(i, i ^ bit) for i in range(count)])]
    ppermute x56 -> x52, waiting for transfers between devices: 83.5 us -> 84.1 us  [shift(): lax.ppermute(value, 'dp', [(order[i], order[(i + step) % count]) for i in...]
  transfers between devices with their start and end apart: 84 -> 84, of which waited for: 51 -> 41; matrix products, arithmetic and copies ran while one was open for 3% -> 3% of each run, Pallas kernels for 42% -> 40%
where the time goes in v3:
time: 529 us; the launch traced here: 521 us
  Pallas kernels  233 us (44%)
  waiting for transfers between devices  143 us (27%)
  starting transfers between devices  94.4 us (18%)
  local copies, waits for them, and re-layouts  28.6 us (5%)
  other arithmetic  17.2 us (3%)
    ppermute x52, waiting for transfers between devices, shift(): lax.ppermute(value, 'dp', [(order[i], order[(i + step) % count]) for i in...  84.1 us
    ppermute x52, starting transfers between devices, shift(): lax.ppermute(value, 'dp', [(order[i], order[(i + step) % count]) for i in...  54.2 us
    pallas_call x2, Pallas kernels, attn_bwd(): pl.pallas_call(functools.partial(attn_bwd_kernel, width, row_from, batch,...  49.8 us
    pallas_call x5, Pallas kernels, pull_slots(): pl.pallas_call(functools.partial(pull_kernel, held is None, len(parts)),...  48.3 us
    ppermute x20, waiting for transfers between devices, flip(): return lax.ppermute(value, axis, [(i, i ^ bit) for i in range(count)])  39 us
    pallas_call x1, Pallas kernels, attn_fwd(): pl.pallas_call(functools.partial(attn_fwd_kernel, width, batch, count), g...  27.7 us
    pallas_call x5, Pallas kernels, spread_tokens(): pl.pallas_call(functools.partial(spread_kernel, group, len(parts)), grid_...  26.5 us
    ppermute x12, starting transfers between devices, turn(): lax.ppermute(value, axis, [(i, (i + step) % count) for i in range(count)])  24.7 us
  transfers between devices with their start and end apart: 84, of which 41 were waited for; matrix products, arithmetic and copies ran while one was open for 3% of the time, Pallas kernels for 40%

profile of v3, /device:TPU:0, one launch (start us, length us, event | category | flops | bytes accessed | tf_op | source)
XLA Modules:
  0.0 520.7 jit_solution(11799254512204993087)
XLA Ops:
  19.0 7.4 %collective-permute-done.2 = bf16[2,16,2176]{2,1,0:T(8,128)(2,1)S(1)} collective-permute-done((bf16[2,16,2176]{2,1,0:T(8,128)(2,1)S(1)}, bf16[2,16,2176]{2,1,0:T(8,128)(2,1)S(1)}, u32[]{:S(2)}, u32[]{:S(2)}) %collective-permute-start.2) | collective-permute-done | bytes 139296 | tf_op jit(solution)/shard_map/ppermute | solution.py:766
  30.3 10.0 %collective-permute-done.4 = bf16[8,1,16,2176]{3,2,0,1:T(8,128)(2,1)S(1)} collective-permute-done((bf16[8,1,16,2176]{3,2,0,1:T(8,128)(2,1)S(1)}, bf16[8,1,16,2176]{3,2,0,1:T(8,128)(2,1)S(1)}, u32[]{:S(2)}, u32[]{:S(2)}) %collective-permute-start.4) | collective-permute-done | bytes 557088 | tf_op jit(solution)/shard_map/ppermute | solution.py:761
  48.6 10.1 %join.1.joined_ref = bf16[4,1024,1536]{2,1,0:T(8,128)(2,1)} custom-call(bf16[4,1024,512]{2,1,0:T(8,128)(2,1)S(1)} %bitcast.376, f32[8,512]{1,0:T(8,128)S(1)} %pad.31.clone.gains_ref, bf16[512,2176]{1,0:T(8,128)(2,1)S(1)} %bitcast.351), custom_call_target="tpu_custom_call" | custom-call | flops 6442450944 | bytes 16777216 | tf_op jit(solution)/shard_map/join/pallas_call | solution.py:261
  61.2 27.7 %attend.1 = (bf16[4,1024,512]{2,1,0:T(8,128)(2,1)S(1)}, f32[4,8,8,128]{3,2,1,0:T(8,128)S(1)}) custom-call(s32[4,8]{1,0:T(4,128)S(1)} %add_select_fusion.lo_ref, s32[4]{0:T(128)S(1)} %subtract_bitcast_fusion.vlen_ref, s32[4,8,128]{2,1,0:T(8,128)S(1)} %select_select_fusion.start_ref, bf16[4,1024,1536]{2,1,0:T(8,128)(2,1)} %join.1.joined_ref), custom_call_target="tpu_custom_call" | custom-call | flops 13421772800 | bytes 12582912 | tf_op jit(solution)/shard_map/attend/pallas_call | solution.py:100
  91.9 7.6 %mix.1 = (f32[4,1024,512]{2,1,0:T(8,128)}, bf16[4,1024,512]{2,1,0:T(8,128)(2,1)S(1)}, f32[4,16,1024]{2,1,0:T(8,128)S(1)}) custom-call(bf16[4,1024,512]{2,1,0:T(8,128)(2,1)S(1)} %get-tuple-element.184.attended_ref, bf16[4,1024,512]{2,1,0:T(8,128)(2,1)} %bitcast.373, f32[8,512]{1,0:T(8,128)S(1)} %pad.31.clone.gains_ref, bf16[512,2176]{1,0:T(8,128)(2,1)S(1)} %bitcast.352, ...), custom_call_target="tpu_custom_call" | custom-call | flops 2147483648 | bytes 20971520 | tf_op jit(solution)/shard_map/mix/pallas_call | solution.py:291
  143.8 5.5 %collective-permute-done.20 = bf16[2,128,512]{2,1,0:T(8,128)(2,1)S(1)} collective-permute-done((bf16[2,128,512]{2,1,0:T(8,128)(2,1)S(1)}, bf16[2,128,512]{2,1,0:T(8,128)(2,1)S(1)}, u32[]{:S(2)}, u32[]{:S(2)}) %collective-permute-start.20) | collective-permute-done | bytes 262176 | tf_op jit(solution)/shard_map/ppermute | solution.py:756
  224.8 7.8 %experts.1 = (bf16[4,128,512]{2,1,0:T(8,128)(2,1)S(1)}, bf16[8,512,256]{2,1,0:T(8,128)(2,1)S(1)}, f32[8,512,256]{2,1,0:T(8,128)S(1)}) custom-call(bf16[4,128,512]{2,1,0:T(8,128)(2,1)S(1)} %pad_maximum_fusion.5.pooled_ref, bf16[8,2,512,256]{3,2,1,0:T(8,128)(2,1)S(1)} %copy-done.16), custom_call_target="tpu_custom_call" | custom-call | flops 4294967296 | bytes 8388608 | tf_op jit(solution)/shard_map/experts/pallas_call | solution.py:389
  247.0 11.4 %pull_experts.1 = (bf16[4,144,512]{2,1,0:T(8,128)(2,1)S(1)}, bf16[8,2,512,256]{3,2,1,0:T(8,128)(2,1)S(1)}) custom-call(s32[8]{0:T(128)S(1)} %get-tuple-element.491.slots_ref, bf16[4,128,512]{2,1,0:T(8,128)(2,1)S(1)} %pad_maximum_fusion.5.pooled_ref, bf16[4,128,512]{2,1,0:T(8,128)(2,1)S(1)} %pad_maximum_fusion.7.grads_ref, ...), custom_call_target="tpu_custom_call" | custom-call | flops 6442450944 | bytes 8388608 | tf_op jit(solution)/shard_map/pull_experts/pallas_call | solution.py:454
  279.4 17.2 %collective-permute-done.57.rest_0_ = bf16[4,128,512]{2,1,0:T(8,128)(2,1)} collective-permute-done((bf16[4,128,512]{2,1,0:T(8,128)(2,1)S(1)}, bf16[4,128,512]{2,1,0:T(8,128)(2,1)}, u32[]{:S(2)}, u32[]{:S(2)}) %collective-permute-start.57) | collective-permute-done | bytes 524320 | tf_op jit(solution)/shard_map/ppermute | solution.py:756
  301.5 6.1 %spread.6 = (bf16[4,1024,512]{2,1,0:T(8,128)(2,1)}, f32[2,128,16]{2,1,0:T(8,128)}) custom-call(s32[8]{0:T(128)} %copy-done.13, f32[1024,16]{1,0:T(8,128)} %bitcast.364, bf16[4,1024,512]{2,1,0:T(8,128)(2,1)} %bitcast.340, f32[4,1024,512]{2,1,0:T(8,128)} %get-tuple-element.187.hidden_ref, ...), custom_call_target="tpu_custom_call", output_to_operand_aliasing={{0}: (6, {})} | custom-call | flops 2621440000 | bytes 2621440 | tf_op jit(solution)/shard_map/spread/pallas_call | solution.py:525
  307.6 7.3 %pull_slots.5 = (f32[4,1024,512]{2,1,0:T(8,128)}, bf16[4,1024,512]{2,1,0:T(8,128)(2,1)}, f32[4,512]{1,0:T(4,128)}, f32[512,512]{1,0:T(8,128)}, f32[8,512]{1,0:T(8,128)}) custom-call(s32[8]{0:T(128)} %copy-done.13, f32[1024,16]{1,0:T(8,128)} %bitcast.365, f32[1,128,16]{2,1,0:T(8,128)} %get-tuple-element.240.change_ref, bf16[4,1024,512]{2,1,0:T(8,128)(2,1)} %copy-done.4, ...), custom_call_target="tpu_custom_call" | custom-call | flops 2684354560 | bytes 5242880 | tf_op jit(solution)/shard_map/pull_slots/pallas_call | solution.py:648
  317.1 7.4 %collective-permute-done.68.rest_0_ = bf16[4,144,512]{2,1,0:T(8,128)(2,1)S(1)} collective-permute-done((bf16[4,144,512]{2,1,0:T(8,128)(2,1)S(1)}, bf16[4,144,512]{2,1,0:T(8,128)(2,1)S(1)}, u32[]{:S(2)}, u32[]{:S(2)}) %collective-permute-start.68) | collective-permute-done | bytes 589856 | tf_op jit(solution)/shard_map/ppermute | solution.py:756
  328.1 11.0 %pull_slots.6 = (f32[4,1024,512]{2,1,0:T(8,128)}, bf16[4,1024,512]{2,1,0:T(8,128)(2,1)}, f32[4,512]{1,0:T(4,128)}, f32[512,512]{1,0:T(8,128)}, f32[8,512]{1,0:T(8,128)}) custom-call(s32[8]{0:T(128)} %copy-done.13, f32[1024,16]{1,0:T(8,128)} %bitcast.366, ...), custom_call_target="tpu_custom_call", output_to_operand_aliasing={{0}: (12, {}), {1}: (13, {})} | custom-call | flops 5368709120 | bytes 5242880 | tf_op jit(solution)/shard_map/pull_slots/pallas_call | solution.py:648
  339.1 6.1 %spread.7 = (bf16[4,1024,512]{2,1,0:T(8,128)(2,1)}, f32[2,128,16]{2,1,0:T(8,128)}) custom-call(s32[8]{0:T(128)} %copy-done.13, f32[1024,16]{1,0:T(8,128)} %bitcast.367, bf16[4,1024,512]{2,1,0:T(8,128)(2,1)} %bitcast.343, f32[4,1024,512]{2,1,0:T(8,128)} %get-tuple-element.187.hidden_ref, ...), custom_call_target="tpu_custom_call", output_to_operand_aliasing={{0}: (6, {})} | custom-call | flops 2621440000 | bytes 2621440 | tf_op jit(solution)/shard_map/spread/pallas_call | solution.py:525
  347.9 11.0 %pull_slots.7 = (f32[4,1024,512]{2,1,0:T(8,128)}, bf16[4,1024,512]{2,1,0:T(8,128)(2,1)}, f32[4,512]{1,0:T(4,128)}, f32[512,512]{1,0:T(8,128)}, f32[8,512]{1,0:T(8,128)}) custom-call(s32[8]{0:T(128)} %copy-done.13, f32[1024,16]{1,0:T(8,128)} %bitcast.368, ...), custom_call_target="tpu_custom_call", output_to_operand_aliasing={{0}: (12, {}), {1}: (13, {})} | custom-call | flops 5368709120 | bytes 5242880 | tf_op jit(solution)/shard_map/pull_slots/pallas_call | solution.py:648
  358.9 6.1 %spread.8 = (bf16[4,1024,512]{2,1,0:T(8,128)(2,1)}, f32[2,128,16]{2,1,0:T(8,128)}) custom-call(s32[8]{0:T(128)} %copy-done.13, f32[1024,16]{1,0:T(8,128)} %bitcast.369, bf16[4,1024,512]{2,1,0:T(8,128)(2,1)} %bitcast.345, f32[4,1024,512]{2,1,0:T(8,128)} %get-tuple-element.187.hidden_ref, ...), custom_call_target="tpu_custom_call", output_to_operand_aliasing={{0}: (6, {})} | custom-call | flops 2621440000 | bytes 2621440 | tf_op jit(solution)/shard_map/spread/pallas_call | solution.py:525
  370.0 11.0 %pull_slots.8 = (f32[4,1024,512]{2,1,0:T(8,128)}, bf16[4,1024,512]{2,1,0:T(8,128)(2,1)}, f32[4,512]{1,0:T(4,128)}, f32[512,512]{1,0:T(8,128)}, f32[8,512]{1,0:T(8,128)}) custom-call(s32[8]{0:T(128)} %copy-done.13, f32[1024,16]{1,0:T(8,128)} %bitcast.371, ...), custom_call_target="tpu_custom_call", output_to_operand_aliasing={{0}: (12, {}), {1}: (13, {})} | custom-call | flops 5368709120 | bytes 5242880 | tf_op jit(solution)/shard_map/pull_slots/pallas_call | solution.py:648
  381.1 8.0 %pull_slots.9 = (f32[4,1024,512]{2,1,0:T(8,128)}, bf16[4,1024,512]{2,1,0:T(8,128)(2,1)}, f32[4,512]{1,0:T(4,128)}, f32[512,512]{1,0:T(8,128)}, f32[8,512]{1,0:T(8,128)}) custom-call(s32[8]{0:T(128)} %copy-done.13, f32[1024,16]{1,0:T(8,128)} %bitcast.372, ...), custom_call_target="tpu_custom_call", output_to_operand_aliasing={{0}: (11, {}), {1}: (12, {})} | custom-call | flops 2684354560 | bytes 5242880 | tf_op jit(solution)/shard_map/pull_slots/pallas_call | solution.py:648
  391.3 33.4 %attend_back.2.rest_0_ = bf16[4,1024,1536]{2,1,0:T(8,128)(2,1)} custom-call(s32[4,8]{1,0:T(4,128)S(1)} %add_select_fusion.lo_ref, s32[4]{0:T(128)S(1)} %subtract_bitcast_fusion.vlen_ref, s32[4,8,128]{2,1,0:T(8,128)S(1)} %select_select_fusion.start_ref, bf16[4,1024,1536]{2,1,0:T(8,128)(2,1)} %join.1.joined_ref, bf16[4,1024,512]{2,1,0:T(8,128)(2,1)S(1)} %copy-done.7, ...), custom_call_target="tpu_custom_call" | custom-call | flops 50331648000 | bytes 18874368 | tf_op jit(solution)/shard_map/attend_back/pallas_call | solution.py:194
  436.9 16.4 %attend_back.3.grads_ref = bf16[4,1024,1536]{2,1,0:T(8,128)(2,1)} custom-call(s32[4,8]{1,0:T(4,128)S(1)} %add_select_fusion.lo_ref, s32[4]{0:T(128)S(1)} %subtract_bitcast_fusion.vlen_ref, s32[4,8,128]{2,1,0:T(8,128)S(1)} %select_select_fusion.start_ref, bf16[4,1024,1536]{2,1,0:T(8,128)(2,1)} %join.1.joined_ref, ...), custom_call_target="tpu_custom_call", output_to_operand_aliasing={{}: (7, {})} | custom-call | flops 16777216000 | bytes 6291456 | tf_op jit(solution)/shard_map/attend_back/pallas_call | solution.py:194
  453.4 13.5 %project_grads.1 = (f32[512,1536]{1,0:T(8,128)S(1)}, f32[8,1536]{1,0:T(8,128)S(1)}) custom-call(bf16[4,1024,1536]{2,1,0:T(8,128)(2,1)} %attend_back.3.grads_ref, bf16[4,1024,512]{2,1,0:T(8,128)(2,1)S(1)} %bitcast.377), custom_call_target="tpu_custom_call" | custom-call | flops 4 | bytes 4 | tf_op jit(solution)/shard_map/project_grads/pallas_call | solution.py:689
  475.8 14.0 %pull_tokens.2.rest_0_ = f32[4,1024,512]{2,1,0:T(8,128)} custom-call(bf16[4,1024,1536]{2,1,0:T(8,128)(2,1)} %attend_back.3.grads_ref, bf16[4,1024,512]{2,1,0:T(8,128)(2,1)} %bitcast.374, f32[4,1024,512]{2,1,0:T(8,128)} %get-tuple-element.333.hidden_ref, f32[8,512]{1,0:T(8,128)} %copy-done.12, bf16[512,2176]{1,0:T(8,128)(2,1)} %bitcast.358), custom_call_target="tpu_custom_call" | custom-call | flops 16106127360 | bytes 25165824 | tf_op jit(solution)/shard_map/pull_tokens/pallas_call | solution.py:718
  493.6 6.8 %pull_tokens.3 = f32[4,1024,512]{2,1,0:T(8,128)} custom-call(bf16[4,1024,1536]{2,1,0:T(8,128)(2,1)} %attend_back.3.grads_ref, bf16[4,1024,512]{2,1,0:T(8,128)(2,1)} %bitcast.375, f32[4,1024,512]{2,1,0:T(8,128)} %get-tuple-element.333.hidden_ref, f32[8,512]{1,0:T(8,128)} %copy-done.12, bf16[512,2176]{1,0:T(8,128)(2,1)} %bitcast.359, ...), custom_call_target="tpu_custom_call", output_to_operand_aliasing={{}: (5, {})} | custom-call | flops 5368709120 | bytes 8388608 | tf_op jit(solution)/shard_map/pull_tokens/pallas_call | solution.py:718
  500.5 9.2 %collective-permute-start.83 = (bf16[16,2176]{1,0:T(8,128)(2,1)S(1)}, bf16[16,2176]{1,0:T(8,128)(2,1)S(1)}, u32[]{:S(2)}, u32[]{:S(2)}) collective-permute-start(bf16[16,2176]{1,0:T(8,128)(2,1)S(1)} %get-tuple-element.469), channel_id=1, source_target_pairs={{0,24},{4,28},{8,0},{12,4},{16,8},{20,12},{24,16},{28,20},{1,25},{... | collective-permute-start | bytes 208904 | tf_op jit(solution)/shard_map/ppermute | solution.py:766
  (391 shorter events, 243.8 us)
Async XLA Ops:
  59.2 29.8 %collective-permute-start.8 = (bf16[2,512,256]{2,1,0:T(8,128)(2,1)}, bf16[2,512,256]{2,1,0:T(8,128)(2,1)S(1)}, u32[]{:S(2)}, u32[]{:S(2)}) collective-permute-start(bf16[2,512,256]{2,1,0:T(8,128)(2,1)} %collective-permute-done.6), channel_id=1, source_target_pairs={{0,8},{8,16},{16,24},{24,28},{28,20},{20,12},{12,4},{4,0},{1,9},{9... | collective-permute-start | bytes 1572872 | tf_op jit(solution)/shard_map/ppermute | solution.py:756
  60.9 28.1 %collective-permute-start.9 = (bf16[2,512,256]{2,1,0:T(8,128)(2,1)}, bf16[2,512,256]{2,1,0:T(8,128)(2,1)S(1)}, u32[]{:S(2)}, u32[]{:S(2)}) collective-permute-start(bf16[2,512,256]{2,1,0:T(8,128)(2,1)} %collective-permute-done.7), channel_id=1, source_target_pairs={{0,4},{8,0},{16,8},{24,16},{28,24},{20,28},{12,20},{4,12},{1,5},{9... | collective-permute-start | bytes 1572872 | tf_op jit(solution)/shard_map/ppermute | solution.py:756
  104.0 19.9 %collective-permute-start.16 = (bf16[1,512,256]{2,1,0:T(8,128)(2,1)S(1)}, bf16[1,512,256]{2,1,0:T(8,128)(2,1)S(1)}, u32[]{:S(2)}, u32[]{:S(2)}) collective-permute-start(bf16[1,512,256]{2,1,0:T(8,128)(2,1)S(1)} %slice.348), channel_id=1, source_target_pairs={{0,8},{8,16},{16,24},{24,28},{28,20},{20,12},{12,4},{4,0},{1,9},{9... | collective-permute-start | bytes 786440 | tf_op jit(solution)/shard_map/ppermute | solution.py:756
  105.1 18.9 %collective-permute-start.17 = (bf16[1,512,256]{2,1,0:T(8,128)(2,1)S(1)}, bf16[1,512,256]{2,1,0:T(8,128)(2,1)S(1)}, u32[]{:S(2)}, u32[]{:S(2)}) collective-permute-start(bf16[1,512,256]{2,1,0:T(8,128)(2,1)S(1)} %slice.349), channel_id=1, source_target_pairs={{0,4},{8,0},{16,8},{24,16},{28,24},{20,28},{12,20},{4,12},{1,5},{9... | collective-permute-start | bytes 786440 | tf_op jit(solution)/shard_map/ppermute | solution.py:756
  241.4 28.5 %collective-permute-start.50 = (bf16[4,128,512]{2,1,0:T(8,128)(2,1)S(1)}, bf16[4,128,512]{2,1,0:T(8,128)(2,1)S(1)}, u32[]{:S(2)}, u32[]{:S(2)}) collective-permute-start(bf16[4,128,512]{2,1,0:T(8,128)(2,1)S(1)} %pad_maximum_fusion.6.rest_0_), channel_id=1, source_target_pairs={{0,8},{8,16},{16,24},{24,28},{28,20},{20,12},{12,4},{4,0},{1,9},{9... | collective-permute-start | bytes 1572872 | tf_op jit(solution)/shard_map/ppermute | solution.py:756
  242.2 27.8 %collective-permute-start.51 = (bf16[4,128,512]{2,1,0:T(8,128)(2,1)S(1)}, bf16[4,128,512]{2,1,0:T(8,128)(2,1)}, u32[]{:S(2)}, u32[]{:S(2)}) collective-permute-start(bf16[4,128,512]{2,1,0:T(8,128)(2,1)S(1)} %pad_maximum_fusion.6.rest_0_), channel_id=1, source_target_pairs={{0,4},{8,0},{16,8},{24,16},{28,24},{20,28},{12,20},{4,12},{1,5},{9... | collective-permute-start | bytes 1572872 | tf_op jit(solution)/shard_map/ppermute | solution.py:756
  270.0 28.8 %collective-permute-start.64 = (bf16[4,144,512]{2,1,0:T(8,128)(2,1)S(1)}, bf16[4,144,512]{2,1,0:T(8,128)(2,1)S(1)}, u32[]{:S(2)}, u32[]{:S(2)}) collective-permute-start(bf16[4,144,512]{2,1,0:T(8,128)(2,1)S(1)} %pad_maximum_fusion.2.rest_0_), channel_id=1, source_target_pairs={{0,8},{8,16},{16,24},{24,28},{28,20},{20,12},{12,4},{4,0},{1,9},{9... | collective-permute-start | bytes 1769480 | tf_op jit(solution)/shard_map/ppermute | solution.py:756
  270.3 28.4 %collective-permute-start.65 = (bf16[4,144,512]{2,1,0:T(8,128)(2,1)S(1)}, bf16[4,144,512]{2,1,0:T(8,128)(2,1)S(1)}, u32[]{:S(2)}, u32[]{:S(2)}) collective-permute-start(bf16[4,144,512]{2,1,0:T(8,128)(2,1)S(1)} %pad_maximum_fusion.2.rest_0_), channel_id=1, source_target_pairs={{0,4},{8,0},{16,8},{24,16},{28,24},{20,28},{12,20},{4,12},{1,5},{9... | collective-permute-start | bytes 1769480 | tf_op jit(solution)/shard_map/ppermute | solution.py:756
  272.1 24.5 %collective-permute-start.57 = (bf16[4,128,512]{2,1,0:T(8,128)(2,1)S(1)}, bf16[4,128,512]{2,1,0:T(8,128)(2,1)}, u32[]{:S(2)}, u32[]{:S(2)}) collective-permute-start(bf16[4,128,512]{2,1,0:T(8,128)(2,1)S(1)} %collective-permute-done.50.rest_0_), channel_id=1, source_target_pairs={{0,8},{8,16},{16,24},{24,28},{28,20},{20,12},{12,4},{4,0},{1,9},{9... | collective-permute-start | bytes 1572872 | tf_op jit(solution)/shard_map/ppermute | solution.py:756
  272.4 24.4 %collective-permute-start.58 = (bf16[4,128,512]{2,1,0:T(8,128)(2,1)}, bf16[4,128,512]{2,1,0:T(8,128)(2,1)}, u32[]{:S(2)}, u32[]{:S(2)}) collective-permute-start(bf16[4,128,512]{2,1,0:T(8,128)(2,1)} %collective-permute-done.51.rest_1_), channel_id=1, source_target_pairs={{0,4},{8,0},{16,8},{24,16},{28,24},{20,28},{12,20},{4,12},{1,5},{9... | collective-permute-start | bytes 1572872 | tf_op jit(solution)/shard_map/ppermute | solution.py:756
  296.8 18.1 %collective-permute-start.59 = (bf16[4,128,512]{2,1,0:T(8,128)(2,1)}, bf16[4,128,512]{2,1,0:T(8,128)(2,1)S(1)}, u32[]{:S(2)}, u32[]{:S(2)}) collective-permute-start(bf16[4,128,512]{2,1,0:T(8,128)(2,1)} %collective-permute-done.57.rest_0_), channel_id=1, source_target_pairs={{0,8},{8,16},{16,24},{24,28},{28,20},{20,12},{12,4},{4,0},{1,9},{9... | collective-permute-start | bytes 1572872 | tf_op jit(solution)/shard_map/ppermute | solution.py:756
  298.3 16.5 %collective-permute-start.60 = (bf16[4,128,512]{2,1,0:T(8,128)(2,1)}, bf16[4,128,512]{2,1,0:T(8,128)(2,1)S(1)}, u32[]{:S(2)}, u32[]{:S(2)}) collective-permute-start(bf16[4,128,512]{2,1,0:T(8,128)(2,1)} %collective-permute-done.58.rest_1_), channel_id=1, source_target_pairs={{0,4},{8,0},{16,8},{24,16},{28,24},{20,28},{12,20},{4,12},{1,5},{9... | collective-permute-start | bytes 1572872 | tf_op jit(solution)/shard_map/ppermute | solution.py:756
  298.8 25.7 %collective-permute-start.68 = (bf16[4,144,512]{2,1,0:T(8,128)(2,1)S(1)}, bf16[4,144,512]{2,1,0:T(8,128)(2,1)S(1)}, u32[]{:S(2)}, u32[]{:S(2)}) collective-permute-start(bf16[4,144,512]{2,1,0:T(8,128)(2,1)S(1)} %collective-permute-done.64.rest_0_), channel_id=1, source_target_pairs={{0,8},{8,16},{16,24},{24,28},{28,20},{20,12},{12,4},{4,0},{1,9},{9... | collective-permute-start | bytes 1769480 | tf_op jit(solution)/shard_map/ppermute | solution.py:756
  300.4 25.6 %collective-permute-start.69 = (bf16[4,144,512]{2,1,0:T(8,128)(2,1)S(1)}, bf16[4,144,512]{2,1,0:T(8,128)(2,1)S(1)}, u32[]{:S(2)}, u32[]{:S(2)}) collective-permute-start(bf16[4,144,512]{2,1,0:T(8,128)(2,1)S(1)} %collective-permute-done.65.rest_1_), channel_id=1, source_target_pairs={{0,4},{8,0},{16,8},{24,16},{28,24},{20,28},{12,20},{4,12},{1,5},{9... | collective-permute-start | bytes 1769480 | tf_op jit(solution)/shard_map/ppermute | solution.py:756
  314.9 30.2 %collective-permute-start.66 = (bf16[2,128,512]{2,1,0:T(8,128)(2,1)S(1)}, bf16[2,128,512]{2,1,0:T(8,128)(2,1)S(1)}, u32[]{:S(2)}, u32[]{:S(2)}) collective-permute-start(bf16[2,128,512]{2,1,0:T(8,128)(2,1)S(1)} %slice.400), channel_id=1, source_target_pairs={{0,8},{8,16},{16,24},{24,28},{28,20},{20,12},{12,4},{4,0},{1,9},{9... | collective-permute-start | bytes 786440 | tf_op jit(solution)/shard_map/ppermute | solution.py:756
  316.5 28.7 %collective-permute-start.67 = (bf16[2,128,512]{2,1,0:T(8,128)(2,1)S(1)}, bf16[2,128,512]{2,1,0:T(8,128)(2,1)S(1)}, u32[]{:S(2)}, u32[]{:S(2)}) collective-permute-start(bf16[2,128,512]{2,1,0:T(8,128)(2,1)S(1)} %slice.401), channel_id=1, source_target_pairs={{0,4},{8,0},{16,8},{24,16},{28,24},{20,28},{12,20},{4,12},{1,5},{9... | collective-permute-start | bytes 786440 | tf_op jit(solution)/shard_map/ppermute | solution.py:756
  326.1 19.2 %collective-permute-start.70 = (bf16[4,144,512]{2,1,0:T(8,128)(2,1)S(1)}, bf16[4,144,512]{2,1,0:T(8,128)(2,1)S(1)}, u32[]{:S(2)}, u32[]{:S(2)}) collective-permute-start(bf16[4,144,512]{2,1,0:T(8,128)(2,1)S(1)} %collective-permute-done.68.rest_0_), channel_id=1, source_target_pairs={{0,8},{8,16},{16,24},{24,28},{28,20},{20,12},{12,4},{4,0},{1,9},{9... | collective-permute-start | bytes 1769480 | tf_op jit(solution)/shard_map/ppermute | solution.py:756
  327.0 18.3 %collective-permute-start.71 = (bf16[4,144,512]{2,1,0:T(8,128)(2,1)S(1)}, bf16[4,144,512]{2,1,0:T(8,128)(2,1)S(1)}, u32[]{:S(2)}, u32[]{:S(2)}) collective-permute-start(bf16[4,144,512]{2,1,0:T(8,128)(2,1)S(1)} %collective-permute-done.69.rest_1_), channel_id=1, source_target_pairs={{0,4},{8,0},{16,8},{24,16},{28,24},{20,28},{12,20},{4,12},{1,5},{9... | collective-permute-start | bytes 1769480 | tf_op jit(solution)/shard_map/ppermute | solution.py:756
  345.3 19.6 %collective-permute-start.72 = (bf16[2,144,512]{2,1,0:T(8,128)(2,1)S(1)}, bf16[2,144,512]{2,1,0:T(8,128)(2,1)S(1)}, u32[]{:S(2)}, u32[]{:S(2)}) collective-permute-start(bf16[2,144,512]{2,1,0:T(8,128)(2,1)S(1)} %slice.402), channel_id=1, source_target_pairs={{0,8},{8,16},{16,24},{24,28},{28,20},{20,12},{12,4},{4,0},{1,9},{9... | collective-permute-start | bytes 884744 | tf_op jit(solution)/shard_map/ppermute | solution.py:756
  346.4 18.6 %collective-permute-start.73 = (bf16[2,144,512]{2,1,0:T(8,128)(2,1)S(1)}, bf16[2,144,512]{2,1,0:T(8,128)(2,1)S(1)}, u32[]{:S(2)}, u32[]{:S(2)}) collective-permute-start(bf16[2,144,512]{2,1,0:T(8,128)(2,1)S(1)} %slice.403), channel_id=1, source_target_pairs={{0,4},{8,0},{16,8},{24,16},{28,24},{20,28},{12,20},{4,12},{1,5},{9... | collective-permute-start | bytes 884744 | tf_op jit(solution)/shard_map/ppermute | solution.py:756
  389.3 41.6 %collective-permute-start.74 = (bf16[4,2,512,256]{3,2,1,0:T(8,128)(2,1)S(1)}, bf16[4,2,512,256]{3,2,1,0:T(8,128)(2,1)S(1)}, u32[]{:S(2)}, u32[]{:S(2)}) collective-permute-start(bf16[4,2,512,256]{3,2,1,0:T(8,128)(2,1)S(1)} %slice.405), channel_id=1, source_target_pairs={{0,4},{4,0},{8,12},{12,8},{16,20},{20,16},{24,28},{28,24},{1,5},{5... | collective-permute-start | bytes 6291464 | tf_op jit(solution)/shard_map/ppermute | solution.py:761
  431.6 35.4 %collective-permute-start.75 = (bf16[2,512,256]{2,1,0:T(8,128)(2,1)S(1)}, bf16[2,512,256]{2,1,0:T(8,128)(2,1)S(1)}, u32[]{:S(2)}, u32[]{:S(2)}) collective-permute-start(bf16[2,512,256]{2,1,0:T(8,128)(2,1)S(1)} %get-tuple-element.455), channel_id=1, source_target_pairs={{0,8},{4,12},{8,16},{12,20},{16,24},{20,28},{24,0},{28,4},{1,9},{5... | collective-permute-start | bytes 1572872 | tf_op jit(solution)/shard_map/ppermute | solution.py:766
  432.9 34.1 %collective-permute-start.76 = (bf16[2,512,256]{2,1,0:T(8,128)(2,1)S(1)}, bf16[2,512,256]{2,1,0:T(8,128)(2,1)S(1)}, u32[]{:S(2)}, u32[]{:S(2)}) collective-permute-start(bf16[2,512,256]{2,1,0:T(8,128)(2,1)S(1)} %get-tuple-element.454), channel_id=1, source_target_pairs={{0,16},{4,20},{8,24},{12,28},{16,0},{20,4},{24,8},{28,12},{1,17},{... | collective-permute-start | bytes 1572872 | tf_op jit(solution)/shard_map/ppermute | solution.py:766
  434.8 32.2 %collective-permute-start.77 = (bf16[2,512,256]{2,1,0:T(8,128)(2,1)S(1)}, bf16[2,512,256]{2,1,0:T(8,128)(2,1)S(1)}, u32[]{:S(2)}, u32[]{:S(2)}) collective-permute-start(bf16[2,512,256]{2,1,0:T(8,128)(2,1)S(1)} %get-tuple-element.453), channel_id=1, source_target_pairs={{0,24},{4,28},{8,0},{12,4},{16,8},{20,12},{24,16},{28,20},{1,25},{... | collective-permute-start | bytes 1572872 | tf_op jit(solution)/shard_map/ppermute | solution.py:766
  (111 other events, 1357.7 us)

commit v4 on v3

--- a/solution.py
+++ b/solution.py
@@ -739,9 +739,6 @@
     )(grads, tokens, hidden, gains, packed, *aliased)
 
 
-LAG = 0
-
-
 def ring_order(size):
     inner = 2 if size % 2 == 0 and size > 2 else 1
     outer = size // inner
@@ -813,7 +810,7 @@
         return {slot: ahead, self.done: behind} if 2 * self.done < count else {slot: ahead}, beside
 
 
-def gather_all(value, steps):
+def gather_all(value, steps, *beside):
     pair = pair_of(lax.axis_size("dp"))
     lines = lax.axis_size("dp") // pair
     size = lax.axis_size("fsdp")
@@ -824,18 +821,21 @@
         upper = (index & bit) != 0
         return jnp.stack([jnp.where(upper, other, value), jnp.where(upper, value, other)])
 
-    value = both(value, 1, "dp", lax.axis_index("dp")) if pair == 2 else value[None]
     whole = put(jnp.zeros((lines,) + value.shape, value.dtype), value, steps[0])
     for k in range(1, lines):
         whole = put(whole, turn(value, -k * pair), steps[k])
-    whole = whole.reshape((lines * pair, 1) + value.shape[1:])
+    if beside:
+        whole, *beside = together(whole, *beside)
+    whole = both(whole, 1, "dp", lax.axis_index("dp")) if pair == 2 else whole[None]
+    whole = jnp.moveaxis(whole, 0, 1)
+    whole = whole.reshape((lines * pair, 1) + value.shape)
     bit = size // 2
     while bit:
         whole = both(whole, bit, "fsdp", here)
         whole = jnp.moveaxis(whole, 0, 2)
-        whole = whole.reshape((lines * pair, -1) + value.shape[1:])
+        whole = whole.reshape((lines * pair, -1) + value.shape)
         bit //= 2
-    return whole
+    return whole, beside
 
 
 def scatter_all(values, steps, work):
@@ -918,8 +918,8 @@
     small = jnp.concatenate([router_weight, vectors], axis=1)
     small = jnp.pad(small, ((0, 0), (0, 128 - small.shape[1])))
     packed = jnp.concatenate([project_in, project_out, small], axis=1)
+    packed, (expert_in, expert_out) = gather_all(packed, steps, expert_in, expert_out)
     weights = jnp.stack([expert_in[0], expert_out[0].T])
-    packed = gather_all(packed, steps)
     packed = packed.reshape(width, packed.shape[-1])
     packed, weights = together(packed, weights)
     kept = {0: weights}
@@ -977,16 +977,13 @@
     second = [(grads[:, :half], 1), (grads[:, half:], -1)]
     held = [part[-way % owners] for part, way in first]
     later = [part[-way % owners] for part, way in second]
-    for step in range(owners - 1 + LAG):
-        if step < owners - 1:
-            came = [shift(value, order, way) for value, (_, way) in zip(held, first)]
-            *came, one, two = together(*came, *later)
-            later = [one, two]
-            held = [add(value, part[-way * (2 + step) % owners]) for value, (part, way) in zip(came, first)]
-        back = step - LAG
-        if back >= 0:
-            came = [shift(value, order, way) for value, (_, way) in zip(later, second)]
-            later = [add(value, part[-way * (2 + back) % owners]) for value, (part, way) in zip(came, second)]
+    for step in range(owners - 1):
+        came = [shift(value, order, way) for value, (_, way) in zip(held, first)]
+        *came, one, two = together(*came, *later)
+        later = [one, two]
+        held = [add(value, part[-way * (2 + step) % owners]) for value, (part, way) in zip(came, first)]
+        came = [shift(value, order, way) for value, (_, way) in zip(later, second)]
+        later = [add(value, part[-way * (2 + step) % owners]) for value, (part, way) in zip(came, second)]
     pooled = exchange(jnp.concatenate(held, axis=0))
     result, act, slope = run_experts(pooled, weights)
     grads = exchange(jnp.concatenate(later, axis=0))
@@ -1009,22 +1006,27 @@
     groups, arrived = [{0: result}, found], [{0: back}]
     out, pulled, changes = None, None, []
     for step in range(turns + 1):
-        second.after(*groups[-1].values())
         work = []
-        out, change = spread(groups[step], out)
-        work = [out, change]
+        for k in [step] if step < turns - 1 else [turns - 1, turns] if step == turns - 1 else []:
+            out, change = spread(groups[k], out)
+            changes.append(change)
+            work = [out]
+        if 0 < step < turns - 1 or step == turns:
+            k = step - 1 if step < turns else turns - 2
+            pulled = pull(arrived[k], changes[k], pulled)
+            work += pulled
         if step > 0:
-            pulled = pull(arrived[step - 1], changes[step - 1], pulled)
-            work += pulled
+            second.after(*groups[min(step + 1, turns)].values())
         if first.left():
             found, work = first.step(*work)
             groups.append(found)
-        if second.left():
+        if second.left() and step > 0:
             found, work = second.step(*work)
             arrived.append(found)
-        out, change, *pulled = work
-        pulled = pulled or None
-        changes.append(change)
+        if step < turns:
+            out, *work = work
+        pulled = work or pulled
+    pulled = pull(arrived[turns - 1], changes[turns - 1], pulled)
     layer_out = out
     pulled = pull(arrived[turns], changes[turns], pulled)
     grad_hidden, grad_attended, router_grad, grad_proj_out, sums_two = pulled
@@ -1037,11 +1039,10 @@
     if pair == 2:
         came, grads = together(came, grads)
         grad_weights = add(grad_weights, came)
-    came = [turn(grad_weights[k], k * pair) for k in range(1, lines)]
+    grad_parts = [turn(grad_weights[k], k * pair) for k in range(1, lines)]
     grads = attn_bwd(joined, grad_attended, attended, logs, starts, lows, vlens, split, rows, grads)
     product, sums_one = project_grads(grads, tokens)
-    product, *came = together(product, *came)
-    grad_weights = sum((value.astype(F32) for value in came), grad_weights[0].astype(F32))
+    product, *grad_parts = together(product, *grad_parts)
     full_in = packed[:, : 3 * width].astype(F32)
     sums_one = sums_one[:1]
     grad_proj_in = gains[0][:, None] * product + gains[1][:, None] * sums_one
@@ -1051,20 +1052,20 @@
     late = jnp.concatenate([router_grad, sums_one, sums_two[:2]], axis=0).T
     late = jnp.pad(late, ((0, 0), (0, 128 - late.shape[1])))
     reduced = jnp.concatenate([grad_proj_in, grad_proj_out, late], axis=1).astype(BF16)
-    made = {"grad": None}
-
-    def rows_beside(start, stop):
-        def run(*came):
-            made["grad"] = pull_tokens(grads, tokens, grad_hidden, gains, packed, start, stop, made["grad"])
-            *came, made["grad"] = together(*came, made["grad"])
-            return came
-
-        return run
-
-    middle = rows - max(1, rows // 4)
-    work = [lambda *came: came, rows_beside(0, middle), rows_beside(middle, rows)]
-    reduced = scatter_all(reduced, steps, work)
-    tokens_grad = made["grad"]
+    made = []
+
+    def tokens_beside(*came):
+        *came, grad = together(*came, pull_tokens(grads, tokens, grad_hidden, gains, packed, 0, rows))
+        made.append(grad)
+        return came
+
+    def weights_beside(*came):
+        value, *parts = together(*came, *grad_parts)
+        made.append(sum((part.astype(F32) for part in parts), grad_weights[0].astype(F32)))
+        return [value]
+
+    reduced = scatter_all(reduced, steps, [lambda *came: came, tokens_beside, weights_beside])
+    tokens_grad, grad_weights = made
     late = reduced[:, 4 * width:]
     return (
         layer_out[None],

time: 529 us -> 508 us (0.960)
  waiting for transfers between devices: 143 us -> 119 us
  starting transfers between devices: 94.4 us -> 107 us
  Pallas kernels: 233 us -> 225 us
    ppermute x52, waiting for transfers between devices: 84.1 us -> 64.2 us  [shift(): lax.ppermute(value, 'dp', [(order[i], order[(i + step) % count]) for i in...]
    ppermute x12, waiting for transfers between devices: 19.9 us -> 8.12 us  [turn(): lax.ppermute(value, axis, [(i, (i + step) % count) for i in range(count)])]
    ppermute x20, starting transfers between devices: 15.5 us -> 23.4 us  [flip(): return lax.ppermute(value, axis, [(i, i ^ bit) for i in range(count)])]
    ppermute x20, waiting for transfers between devices: 39 us -> 46.3 us  [flip(): return lax.ppermute(value, axis, [(i, i ^ bit) for i in range(count)])]
    pallas_call x2 -> x1, Pallas kernels: 20.8 us -> 16.1 us  [pull_tokens(): pl.pallas_call(tokens_kernel, grid=(row_to - row_from, length // tile), i...]
    unnamed x117 -> x116, local copies, waits for them, and re-layouts: 19.4 us -> 17.7 us
  transfers between devices with their start and end apart: 84 -> 84, of which waited for: 41 -> 48; matrix products, arithmetic and copies ran while one was open for 3% -> 3% of each run, Pallas kernels for 40% -> 41%
where the time goes in v4:
time: 508 us; the launch traced here: 499 us
  Pallas kernels  225 us (44%)
  waiting for transfers between devices  119 us (23%)
  starting transfers between devices  107 us (21%)
  local copies, waits for them, and re-layouts  26.4 us (5%)
  other arithmetic  18.1 us (4%)
    ppermute x52, waiting for transfers between devices, shift(): lax.ppermute(value, 'dp', [(order[i], order[(i + step) % count]) for i in...  64.2 us
    ppermute x52, starting transfers between devices, shift(): lax.ppermute(value, 'dp', [(order[i], order[(i + step) % count]) for i in...  56.4 us
    pallas_call x5, Pallas kernels, pull_slots(): pl.pallas_call(functools.partial(pull_kernel, held is None, len(parts)),...  48.4 us
    pallas_call x2, Pallas kernels, attn_bwd(): pl.pallas_call(functools.partial(attn_bwd_kernel, width, row_from, batch,...  47.6 us
    ppermute x20, waiting for transfers between devices, flip(): return lax.ppermute(value, axis, [(i, i ^ bit) for i in range(count)])  46.3 us
    ppermute x12, starting transfers between devices, turn(): lax.ppermute(value, axis, [(i, (i + step) % count) for i in range(count)])  26.7 us
    pallas_call x1, Pallas kernels, attn_fwd(): pl.pallas_call(functools.partial(attn_fwd_kernel, width, batch, count), g...  26.6 us
    pallas_call x5, Pallas kernels, spread_tokens(): pl.pallas_call(functools.partial(spread_kernel, group, len(parts)), grid_...  26.6 us
  transfers between devices with their start and end apart: 84, of which 48 were waited for; matrix products, arithmetic and copies ran while one was open for 3% of the time, Pallas kernels for 41%

profile of v4, /device:TPU:0, one launch (start us, length us, event | category | flops | bytes accessed | tf_op | source)
XLA Modules:
  0.0 499.1 jit_solution(3457548276622147713)
XLA Ops:
  15.8 7.0 %collective-permute-done.3 = bf16[4,16,2176]{2,1,0:T(8,128)(2,1)S(1)} collective-permute-done((bf16[4,16,2176]{2,1,0:T(8,128)(2,1)S(1)}, bf16[4,16,2176]{2,1,0:T(8,128)(2,1)S(1)}, u32[]{:S(2)}, u32[]{:S(2)}) %collective-permute-start.3) | collective-permute-done | bytes 278560 | tf_op jit(solution)/shard_map/ppermute | solution.py:758
  26.8 9.8 %collective-permute-done.4 = bf16[8,1,16,2176]{3,2,0,1:T(8,128)(2,1)S(1)} collective-permute-done((bf16[8,1,16,2176]{3,2,0,1:T(8,128)(2,1)S(1)}, bf16[8,1,16,2176]{3,2,0,1:T(8,128)(2,1)S(1)}, u32[]{:S(2)}, u32[]{:S(2)}) %collective-permute-start.4) | collective-permute-done | bytes 557088 | tf_op jit(solution)/shard_map/ppermute | solution.py:758
  46.0 10.0 %join.1.joined_ref = bf16[4,1024,1536]{2,1,0:T(8,128)(2,1)} custom-call(bf16[4,1024,512]{2,1,0:T(8,128)(2,1)S(1)} %bitcast.379, f32[8,512]{1,0:T(8,128)S(1)} %pad.31.clone.gains_ref, bf16[512,2176]{1,0:T(8,128)(2,1)S(1)} %bitcast.356), custom_call_target="tpu_custom_call" | custom-call | flops 6442450944 | bytes 16777216 | tf_op jit(solution)/shard_map/join/pallas_call | solution.py:261
  58.0 26.6 %attend.1 = (bf16[4,1024,512]{2,1,0:T(8,128)(2,1)S(1)}, f32[4,8,8,128]{3,2,1,0:T(8,128)S(1)}) custom-call(s32[4,8]{1,0:T(4,128)S(1)} %add_select_fusion.lo_ref, s32[4]{0:T(128)S(1)} %subtract_bitcast_fusion.vlen_ref, s32[4,8,128]{2,1,0:T(8,128)S(1)} %select_select_fusion.start_ref, bf16[4,1024,1536]{2,1,0:T(8,128)(2,1)} %join.1.joined_ref), custom_call_target="tpu_custom_call" | custom-call | flops 13421772800 | bytes 12582912 | tf_op jit(solution)/shard_map/attend/pallas_call | solution.py:100
  88.4 7.6 %mix.1 = (f32[4,1024,512]{2,1,0:T(8,128)}, bf16[4,1024,512]{2,1,0:T(8,128)(2,1)S(1)}, f32[4,16,1024]{2,1,0:T(8,128)S(1)}) custom-call(bf16[4,1024,512]{2,1,0:T(8,128)(2,1)S(1)} %get-tuple-element.184.attended_ref, bf16[4,1024,512]{2,1,0:T(8,128)(2,1)} %bitcast.377, f32[8,512]{1,0:T(8,128)S(1)} %pad.31.clone.gains_ref, bf16[512,2176]{1,0:T(8,128)(2,1)S(1)} %bitcast.357, ...), custom_call_target="tpu_custom_call" | custom-call | flops 2147483648 | bytes 20971520 | tf_op jit(solution)/shard_map/mix/pallas_call | solution.py:291
  161.3 5.5 %collective-permute-done.28 = bf16[2,128,512]{2,1,0:T(8,128)(2,1)S(1)} collective-permute-done((bf16[2,128,512]{2,1,0:T(8,128)(2,1)S(1)}, bf16[2,128,512]{2,1,0:T(8,128)(2,1)S(1)}, u32[]{:S(2)}, u32[]{:S(2)}) %collective-permute-start.28) | collective-permute-done | bytes 262176 | tf_op jit(solution)/shard_map/ppermute | solution.py:753
  222.1 7.8 %experts.1 = (bf16[4,128,512]{2,1,0:T(8,128)(2,1)S(1)}, bf16[8,512,256]{2,1,0:T(8,128)(2,1)S(1)}, f32[8,512,256]{2,1,0:T(8,128)S(1)}) custom-call(bf16[4,128,512]{2,1,0:T(8,128)(2,1)S(1)} %pad_maximum_fusion.6.pooled_ref, bf16[8,2,512,256]{3,2,1,0:T(8,128)(2,1)S(1)} %copy-done.16), custom_call_target="tpu_custom_call" | custom-call | flops 4294967296 | bytes 8388608 | tf_op jit(solution)/shard_map/experts/pallas_call | solution.py:389
  243.7 11.4 %pull_experts.1 = (bf16[4,144,512]{2,1,0:T(8,128)(2,1)S(1)}, bf16[8,2,512,256]{3,2,1,0:T(8,128)(2,1)S(1)}) custom-call(s32[8]{0:T(128)S(1)} %get-tuple-element.486.slots_ref, bf16[4,128,512]{2,1,0:T(8,128)(2,1)S(1)} %pad_maximum_fusion.6.pooled_ref, bf16[4,128,512]{2,1,0:T(8,128)(2,1)S(1)} %pad_maximum_fusion.7.grads_ref, ...), custom_call_target="tpu_custom_call" | custom-call | flops 6442450944 | bytes 8388608 | tf_op jit(solution)/shard_map/pull_experts/pallas_call | solution.py:454
  277.9 7.2 %pull_slots.5 = (f32[4,1024,512]{2,1,0:T(8,128)}, bf16[4,1024,512]{2,1,0:T(8,128)(2,1)}, f32[4,512]{1,0:T(4,128)}, f32[512,512]{1,0:T(8,128)}, f32[8,512]{1,0:T(8,128)}) custom-call(s32[8]{0:T(128)} %copy-done.13, f32[1024,16]{1,0:T(8,128)} %bitcast.368, f32[1,128,16]{2,1,0:T(8,128)} %get-tuple-element.236.change_ref, bf16[4,1024,512]{2,1,0:T(8,128)(2,1)} %copy-done.2, ...), custom_call_target="tpu_custom_call" | custom-call | flops 2684354560 | bytes 5242880 | tf_op jit(solution)/shard_map/pull_slots/pallas_call | solution.py:648
  285.1 6.1 %spread.6 = (bf16[4,1024,512]{2,1,0:T(8,128)(2,1)}, f32[2,128,16]{2,1,0:T(8,128)}) custom-call(s32[8]{0:T(128)} %copy-done.13, f32[1024,16]{1,0:T(8,128)} %bitcast.369, bf16[4,1024,512]{2,1,0:T(8,128)(2,1)} %bitcast.346, f32[4,1024,512]{2,1,0:T(8,128)} %get-tuple-element.228.hidden_ref, ...), custom_call_target="tpu_custom_call", output_to_operand_aliasing={{0}: (6, {})} | custom-call | flops 2621440000 | bytes 2621440 | tf_op jit(solution)/shard_map/spread/pallas_call | solution.py:525
  293.4 6.9 %collective-permute-done.62.rest_0_ = bf16[4,144,512]{2,1,0:T(8,128)(2,1)S(1)} collective-permute-done((bf16[4,144,512]{2,1,0:T(8,128)(2,1)S(1)}, bf16[4,144,512]{2,1,0:T(8,128)(2,1)S(1)}, u32[]{:S(2)}, u32[]{:S(2)}) %collective-permute-start.62) | collective-permute-done | bytes 589856 | tf_op jit(solution)/shard_map/ppermute | solution.py:753
  303.2 11.0 %pull_slots.6 = (f32[4,1024,512]{2,1,0:T(8,128)}, bf16[4,1024,512]{2,1,0:T(8,128)(2,1)}, f32[4,512]{1,0:T(4,128)}, f32[512,512]{1,0:T(8,128)}, f32[8,512]{1,0:T(8,128)}) custom-call(s32[8]{0:T(128)} %copy-done.13, f32[1024,16]{1,0:T(8,128)} %bitcast.370, ...), custom_call_target="tpu_custom_call", output_to_operand_aliasing={{0}: (12, {}), {1}: (13, {})} | custom-call | flops 5368709120 | bytes 5242880 | tf_op jit(solution)/shard_map/pull_slots/pallas_call | solution.py:648
  314.3 6.1 %spread.7 = (bf16[4,1024,512]{2,1,0:T(8,128)(2,1)}, f32[2,128,16]{2,1,0:T(8,128)}) custom-call(s32[8]{0:T(128)} %copy-done.13, f32[1024,16]{1,0:T(8,128)} %bitcast.371, bf16[4,1024,512]{2,1,0:T(8,128)(2,1)} %bitcast.348, f32[4,1024,512]{2,1,0:T(8,128)} %get-tuple-element.228.hidden_ref, ...), custom_call_target="tpu_custom_call", output_to_operand_aliasing={{0}: (6, {})} | custom-call | flops 2621440000 | bytes 2621440 | tf_op jit(solution)/shard_map/spread/pallas_call | solution.py:525
  322.8 6.1 %spread.8 = (bf16[4,1024,512]{2,1,0:T(8,128)(2,1)}, f32[2,128,16]{2,1,0:T(8,128)}) custom-call(s32[8]{0:T(128)} %copy-done.13, f32[1024,16]{1,0:T(8,128)} %bitcast.372, bf16[4,1024,512]{2,1,0:T(8,128)(2,1)} %bitcast.349, f32[4,1024,512]{2,1,0:T(8,128)} %get-tuple-element.228.hidden_ref, ...), custom_call_target="tpu_custom_call", output_to_operand_aliasing={{0}: (6, {})} | custom-call | flops 2621440000 | bytes 2621440 | tf_op jit(solution)/shard_map/spread/pallas_call | solution.py:525
  335.8 11.1 %pull_slots.7 = (f32[4,1024,512]{2,1,0:T(8,128)}, bf16[4,1024,512]{2,1,0:T(8,128)(2,1)}, f32[4,512]{1,0:T(4,128)}, f32[512,512]{1,0:T(8,128)}, f32[8,512]{1,0:T(8,128)}) custom-call(s32[8]{0:T(128)} %copy-done.13, f32[1024,16]{1,0:T(8,128)} %bitcast.374, ...), custom_call_target="tpu_custom_call", output_to_operand_aliasing={{0}: (12, {}), {1}: (13, {})} | custom-call | flops 5368709120 | bytes 5242880 | tf_op jit(solution)/shard_map/pull_slots/pallas_call | solution.py:648
  347.8 11.0 %pull_slots.8 = (f32[4,1024,512]{2,1,0:T(8,128)}, bf16[4,1024,512]{2,1,0:T(8,128)(2,1)}, f32[4,512]{1,0:T(4,128)}, f32[512,512]{1,0:T(8,128)}, f32[8,512]{1,0:T(8,128)}) custom-call(s32[8]{0:T(128)} %copy-done.13, f32[1024,16]{1,0:T(8,128)} %bitcast.375, ...), custom_call_target="tpu_custom_call", output_to_operand_aliasing={{0}: (12, {}), {1}: (13, {})} | custom-call | flops 5368709120 | bytes 5242880 | tf_op jit(solution)/shard_map/pull_slots/pallas_call | solution.py:648
  358.9 8.0 %pull_slots.9 = (f32[4,1024,512]{2,1,0:T(8,128)}, bf16[4,1024,512]{2,1,0:T(8,128)(2,1)}, f32[4,512]{1,0:T(4,128)}, f32[512,512]{1,0:T(8,128)}, f32[8,512]{1,0:T(8,128)}) custom-call(s32[8]{0:T(128)} %copy-done.13, f32[1024,16]{1,0:T(8,128)} %bitcast.376, ...), custom_call_target="tpu_custom_call", output_to_operand_aliasing={{0}: (11, {}), {1}: (12, {})} | custom-call | flops 2684354560 | bytes 5242880 | tf_op jit(solution)/shard_map/pull_slots/pallas_call | solution.py:648
  369.1 33.9 %attend_back.2.rest_0_ = bf16[4,1024,1536]{2,1,0:T(8,128)(2,1)} custom-call(s32[4,8]{1,0:T(4,128)S(1)} %add_select_fusion.lo_ref, s32[4]{0:T(128)S(1)} %subtract_bitcast_fusion.vlen_ref, s32[4,8,128]{2,1,0:T(8,128)S(1)} %select_select_fusion.start_ref, bf16[4,1024,1536]{2,1,0:T(8,128)(2,1)} %join.1.joined_ref, bf16[4,1024,512]{2,1,0:T(8,128)(2,1)S(1)} %copy-done.7, ...), custom_call_target="tpu_custom_call" | custom-call | flops 50331648000 | bytes 18874368 | tf_op jit(solution)/shard_map/attend_back/pallas_call | solution.py:194
  403.8 5.9 %collective-permute-done.74 = bf16[4,2,512,256]{3,2,1,0:T(8,128)(2,1)S(1)} collective-permute-done((bf16[4,2,512,256]{3,2,1,0:T(8,128)(2,1)S(1)}, bf16[4,2,512,256]{3,2,1,0:T(8,128)(2,1)S(1)}, u32[]{:S(2)}, u32[]{:S(2)}) %collective-permute-start.74) | collective-permute-done | bytes 2097184 | tf_op jit(solution)/shard_map/ppermute | solution.py:758
  415.4 13.7 %attend_back.3.grads_ref = bf16[4,1024,1536]{2,1,0:T(8,128)(2,1)} custom-call(s32[4,8]{1,0:T(4,128)S(1)} %add_select_fusion.lo_ref, s32[4]{0:T(128)S(1)} %subtract_bitcast_fusion.vlen_ref, s32[4,8,128]{2,1,0:T(8,128)S(1)} %select_select_fusion.start_ref, bf16[4,1024,1536]{2,1,0:T(8,128)(2,1)} %join.1.joined_ref, ...), custom_call_target="tpu_custom_call", output_to_operand_aliasing={{}: (7, {})} | custom-call | flops 16777216000 | bytes 6291456 | tf_op jit(solution)/shard_map/attend_back/pallas_call | solution.py:194
  429.3 13.5 %project_grads.1 = (f32[512,1536]{1,0:T(8,128)S(1)}, f32[8,1536]{1,0:T(8,128)S(1)}) custom-call(bf16[4,1024,1536]{2,1,0:T(8,128)(2,1)} %attend_back.3.grads_ref, bf16[4,1024,512]{2,1,0:T(8,128)(2,1)S(1)} %bitcast.380), custom_call_target="tpu_custom_call" | custom-call | flops 4 | bytes 4 | tf_op jit(solution)/shard_map/project_grads/pallas_call | solution.py:689
  455.1 16.1 %pull_tokens.1 = f32[4,1024,512]{2,1,0:T(8,128)} custom-call(bf16[4,1024,1536]{2,1,0:T(8,128)(2,1)} %attend_back.3.grads_ref, bf16[4,1024,512]{2,1,0:T(8,128)(2,1)} %bitcast.378, f32[4,1024,512]{2,1,0:T(8,128)} %get-tuple-element.325.hidden_ref, f32[8,512]{1,0:T(8,128)} %copy-done.12, bf16[512,2176]{1,0:T(8,128)(2,1)} %bitcast.363), custom_call_target="tpu_custom_call" | custom-call | flops 21474836480 | bytes 33554432 | tf_op jit(solution)/shard_map/pull_tokens/pallas_call | solution.py:718
  473.2 6.8 %collective-permute-done.80 = bf16[4,16,2176]{2,1,0:T(8,128)(2,1)S(1)} collective-permute-done((bf16[4,16,2176]{2,1,0:T(8,128)(2,1)S(1)}, bf16[4,16,2176]{2,1,0:T(8,128)(2,1)S(1)}, u32[]{:S(2)}, u32[]{:S(2)}) %collective-permute-start.80) | collective-permute-done | bytes 278560 | tf_op jit(solution)/shard_map/ppermute | solution.py:758
  480.1 9.4 %collective-permute-start.81 = (bf16[16,2176]{1,0:T(8,128)(2,1)S(1)}, bf16[16,2176]{1,0:T(8,128)(2,1)S(1)}, u32[]{:S(2)}, u32[]{:S(2)}) collective-permute-start(bf16[16,2176]{1,0:T(8,128)(2,1)S(1)} %get-tuple-element.464), channel_id=1, source_target_pairs={{0,8},{4,12},{8,16},{12,20},{16,24},{20,28},{24,0},{28,4},{1,9},{5... | collective-permute-start | bytes 208904 | tf_op jit(solution)/shard_map/ppermute | solution.py:763
  (390 shorter events, 235.9 us)
Async XLA Ops:
  41.3 14.7 %collective-permute-start.6 = (bf16[2,512,256]{2,1,0:T(8,128)(2,1)S(1)}, bf16[2,512,256]{2,1,0:T(8,128)(2,1)}, u32[]{:S(2)}, u32[]{:S(2)}) collective-permute-start(bf16[2,512,256]{2,1,0:T(8,128)(2,1)S(1)} %pad_maximum_fusion.5), channel_id=1, source_target_pairs={{0,8},{8,16},{16,24},{24,28},{28,20},{20,12},{12,4},{4,0},{1,9},{9... | collective-permute-start | bytes 1572872 | tf_op jit(solution)/shard_map/ppermute | solution.py:753
  56.0 28.6 %collective-permute-start.8 = (bf16[2,512,256]{2,1,0:T(8,128)(2,1)}, bf16[2,512,256]{2,1,0:T(8,128)(2,1)S(1)}, u32[]{:S(2)}, u32[]{:S(2)}) collective-permute-start(bf16[2,512,256]{2,1,0:T(8,128)(2,1)} %collective-permute-done.6), channel_id=1, source_target_pairs={{0,8},{8,16},{16,24},{24,28},{28,20},{20,12},{12,4},{4,0},{1,9},{9... | collective-permute-start | bytes 1572872 | tf_op jit(solution)/shard_map/ppermute | solution.py:753
  56.3 28.3 %collective-permute-start.9 = (bf16[2,512,256]{2,1,0:T(8,128)(2,1)}, bf16[2,512,256]{2,1,0:T(8,128)(2,1)S(1)}, u32[]{:S(2)}, u32[]{:S(2)}) collective-permute-start(bf16[2,512,256]{2,1,0:T(8,128)(2,1)} %collective-permute-done.7), channel_id=1, source_target_pairs={{0,4},{8,0},{16,8},{24,16},{28,24},{20,28},{12,20},{4,12},{1,5},{9... | collective-permute-start | bytes 1572872 | tf_op jit(solution)/shard_map/ppermute | solution.py:753
  102.0 19.6 %collective-permute-start.12 = (bf16[1,512,256]{2,1,0:T(8,128)(2,1)S(1)}, bf16[1,512,256]{2,1,0:T(8,128)(2,1)S(1)}, u32[]{:S(2)}, u32[]{:S(2)}) collective-permute-start(bf16[1,512,256]{2,1,0:T(8,128)(2,1)S(1)} %slice.345), channel_id=1, source_target_pairs={{0,8},{8,16},{16,24},{24,28},{28,20},{20,12},{12,4},{4,0},{1,9},{9... | collective-permute-start | bytes 786440 | tf_op jit(solution)/shard_map/ppermute | solution.py:753
  102.8 18.8 %collective-permute-start.13 = (bf16[1,512,256]{2,1,0:T(8,128)(2,1)S(1)}, bf16[1,512,256]{2,1,0:T(8,128)(2,1)S(1)}, u32[]{:S(2)}, u32[]{:S(2)}) collective-permute-start(bf16[1,512,256]{2,1,0:T(8,128)(2,1)S(1)} %slice.346), channel_id=1, source_target_pairs={{0,4},{8,0},{16,8},{24,16},{28,24},{20,28},{12,20},{4,12},{1,5},{9... | collective-permute-start | bytes 786440 | tf_op jit(solution)/shard_map/ppermute | solution.py:753
  216.3 15.8 %collective-permute-start.47 = (bf16[2,128,512]{2,1,0:T(8,128)(2,1)S(1)}, bf16[2,128,512]{2,1,0:T(8,128)(2,1)S(1)}, u32[]{:S(2)}, u32[]{:S(2)}) collective-permute-start(bf16[2,128,512]{2,1,0:T(8,128)(2,1)S(1)} %get-tuple-element.217), channel_id=1, source_target_pairs={{0,8},{8,16},{16,24},{24,28},{28,20},{20,12},{12,4},{4,0},{1,9},{9... | collective-permute-start | bytes 786440 | tf_op jit(solution)/shard_map/ppermute | solution.py:753
  217.4 14.7 %collective-permute-start.49 = (bf16[2,128,512]{2,1,0:T(8,128)(2,1)S(1)}, bf16[2,128,512]{2,1,0:T(8,128)(2,1)S(1)}, u32[]{:S(2)}, u32[]{:S(2)}) collective-permute-start(bf16[2,128,512]{2,1,0:T(8,128)(2,1)S(1)} %get-tuple-element.218), channel_id=1, source_target_pairs={{0,4},{8,0},{16,8},{24,16},{28,24},{20,28},{12,20},{4,12},{1,5},{9... | collective-permute-start | bytes 786440 | tf_op jit(solution)/shard_map/ppermute | solution.py:753
  238.9 18.3 %collective-permute-start.58 = (bf16[4,128,512]{2,1,0:T(8,128)(2,1)S(1)}, bf16[4,128,512]{2,1,0:T(8,128)(2,1)S(1)}, u32[]{:S(2)}, u32[]{:S(2)}) collective-permute-start(bf16[4,128,512]{2,1,0:T(8,128)(2,1)S(1)} %pad_maximum_fusion.8.rest_0_), channel_id=1, source_target_pairs={{0,8},{8,16},{16,24},{24,28},{28,20},{20,12},{12,4},{4,0},{1,9},{9... | collective-permute-start | bytes 1572872 | tf_op jit(solution)/shard_map/ppermute | solution.py:753
  240.0 17.1 %collective-permute-start.59 = (bf16[4,128,512]{2,1,0:T(8,128)(2,1)S(1)}, bf16[4,128,512]{2,1,0:T(8,128)(2,1)S(1)}, u32[]{:S(2)}, u32[]{:S(2)}) collective-permute-start(bf16[4,128,512]{2,1,0:T(8,128)(2,1)S(1)} %pad_maximum_fusion.8.rest_0_), channel_id=1, source_target_pairs={{0,4},{8,0},{16,8},{24,16},{28,24},{20,28},{12,20},{4,12},{1,5},{9... | collective-permute-start | bytes 1572872 | tf_op jit(solution)/shard_map/ppermute | solution.py:753
  257.2 14.8 %collective-permute-start.60 = (bf16[4,128,512]{2,1,0:T(8,128)(2,1)S(1)}, bf16[4,128,512]{2,1,0:T(8,128)(2,1)S(1)}, u32[]{:S(2)}, u32[]{:S(2)}) collective-permute-start(bf16[4,128,512]{2,1,0:T(8,128)(2,1)S(1)} %collective-permute-done.58.rest_0_), channel_id=1, source_target_pairs={{0,8},{8,16},{16,24},{24,28},{28,20},{20,12},{12,4},{4,0},{1,9},{9... | collective-permute-start | bytes 1572872 | tf_op jit(solution)/shard_map/ppermute | solution.py:753
  272.8 18.4 %collective-permute-start.64 = (bf16[4,128,512]{2,1,0:T(8,128)(2,1)S(1)}, bf16[4,128,512]{2,1,0:T(8,128)(2,1)S(1)}, u32[]{:S(2)}, u32[]{:S(2)}) collective-permute-start(bf16[4,128,512]{2,1,0:T(8,128)(2,1)S(1)} %collective-permute-done.60.rest_0_), channel_id=1, source_target_pairs={{0,8},{8,16},{16,24},{24,28},{28,20},{20,12},{12,4},{4,0},{1,9},{9... | collective-permute-start | bytes 1572872 | tf_op jit(solution)/shard_map/ppermute | solution.py:753
  273.7 17.5 %collective-permute-start.65 = (bf16[4,128,512]{2,1,0:T(8,128)(2,1)S(1)}, bf16[4,128,512]{2,1,0:T(8,128)(2,1)S(1)}, u32[]{:S(2)}, u32[]{:S(2)}) collective-permute-start(bf16[4,128,512]{2,1,0:T(8,128)(2,1)S(1)} %collective-permute-done.61.rest_1_), channel_id=1, source_target_pairs={{0,4},{8,0},{16,8},{24,16},{28,24},{20,28},{12,20},{4,12},{1,5},{9... | collective-permute-start | bytes 1572872 | tf_op jit(solution)/shard_map/ppermute | solution.py:753
  274.8 25.4 %collective-permute-start.62 = (bf16[4,144,512]{2,1,0:T(8,128)(2,1)S(1)}, bf16[4,144,512]{2,1,0:T(8,128)(2,1)S(1)}, u32[]{:S(2)}, u32[]{:S(2)}) collective-permute-start(bf16[4,144,512]{2,1,0:T(8,128)(2,1)S(1)} %pad_maximum_fusion.2.rest_0_), channel_id=1, source_target_pairs={{0,8},{8,16},{16,24},{24,28},{28,20},{20,12},{12,4},{4,0},{1,9},{9... | collective-permute-start | bytes 1769480 | tf_op jit(solution)/shard_map/ppermute | solution.py:753
  275.7 25.5 %collective-permute-start.63 = (bf16[4,144,512]{2,1,0:T(8,128)(2,1)S(1)}, bf16[4,144,512]{2,1,0:T(8,128)(2,1)S(1)}, u32[]{:S(2)}, u32[]{:S(2)}) collective-permute-start(bf16[4,144,512]{2,1,0:T(8,128)(2,1)S(1)} %pad_maximum_fusion.2.rest_0_), channel_id=1, source_target_pairs={{0,4},{8,0},{16,8},{24,16},{28,24},{20,28},{12,20},{4,12},{1,5},{9... | collective-permute-start | bytes 1769480 | tf_op jit(solution)/shard_map/ppermute | solution.py:753
  291.2 29.1 %collective-permute-start.68 = (bf16[2,128,512]{2,1,0:T(8,128)(2,1)S(1)}, bf16[2,128,512]{2,1,0:T(8,128)(2,1)S(1)}, u32[]{:S(2)}, u32[]{:S(2)}) collective-permute-start(bf16[2,128,512]{2,1,0:T(8,128)(2,1)S(1)} %slice.400), channel_id=1, source_target_pairs={{0,8},{8,16},{16,24},{24,28},{28,20},{20,12},{12,4},{4,0},{1,9},{9... | collective-permute-start | bytes 786440 | tf_op jit(solution)/shard_map/ppermute | solution.py:753
  292.2 28.2 %collective-permute-start.69 = (bf16[2,128,512]{2,1,0:T(8,128)(2,1)S(1)}, bf16[2,128,512]{2,1,0:T(8,128)(2,1)S(1)}, u32[]{:S(2)}, u32[]{:S(2)}) collective-permute-start(bf16[2,128,512]{2,1,0:T(8,128)(2,1)S(1)} %slice.401), channel_id=1, source_target_pairs={{0,4},{8,0},{16,8},{24,16},{28,24},{20,28},{12,20},{4,12},{1,5},{9... | collective-permute-start | bytes 786440 | tf_op jit(solution)/shard_map/ppermute | solution.py:753
  301.2 19.2 %collective-permute-start.66 = (bf16[4,144,512]{2,1,0:T(8,128)(2,1)S(1)}, bf16[4,144,512]{2,1,0:T(8,128)(2,1)}, u32[]{:S(2)}, u32[]{:S(2)}) collective-permute-start(bf16[4,144,512]{2,1,0:T(8,128)(2,1)S(1)} %collective-permute-done.62.rest_0_), channel_id=1, source_target_pairs={{0,8},{8,16},{16,24},{24,28},{28,20},{20,12},{12,4},{4,0},{1,9},{9... | collective-permute-start | bytes 1769480 | tf_op jit(solution)/shard_map/ppermute | solution.py:753
  302.3 18.2 %collective-permute-start.67 = (bf16[4,144,512]{2,1,0:T(8,128)(2,1)S(1)}, bf16[4,144,512]{2,1,0:T(8,128)(2,1)}, u32[]{:S(2)}, u32[]{:S(2)}) collective-permute-start(bf16[4,144,512]{2,1,0:T(8,128)(2,1)S(1)} %collective-permute-done.63.rest_1_), channel_id=1, source_target_pairs={{0,4},{8,0},{16,8},{24,16},{28,24},{20,28},{12,20},{4,12},{1,5},{9... | collective-permute-start | bytes 1769480 | tf_op jit(solution)/shard_map/ppermute | solution.py:753
  367.1 42.7 %collective-permute-start.74 = (bf16[4,2,512,256]{3,2,1,0:T(8,128)(2,1)S(1)}, bf16[4,2,512,256]{3,2,1,0:T(8,128)(2,1)S(1)}, u32[]{:S(2)}, u32[]{:S(2)}) collective-permute-start(bf16[4,2,512,256]{3,2,1,0:T(8,128)(2,1)S(1)} %slice.405), channel_id=1, source_target_pairs={{0,4},{4,0},{8,12},{12,8},{16,20},{20,16},{24,28},{28,24},{1,5},{5... | collective-permute-start | bytes 6291464 | tf_op jit(solution)/shard_map/ppermute | solution.py:758
  410.5 32.3 %collective-permute-start.75 = (bf16[2,512,256]{2,1,0:T(8,128)(2,1)S(1)}, bf16[2,512,256]{2,1,0:T(8,128)(2,1)S(1)}, u32[]{:S(2)}, u32[]{:S(2)}) collective-permute-start(bf16[2,512,256]{2,1,0:T(8,128)(2,1)S(1)} %get-tuple-element.449), channel_id=1, source_target_pairs={{0,8},{4,12},{8,16},{12,20},{16,24},{20,28},{24,0},{28,4},{1,9},{5... | collective-permute-start | bytes 1572872 | tf_op jit(solution)/shard_map/ppermute | solution.py:763
  411.6 31.4 %collective-permute-start.76 = (bf16[2,512,256]{2,1,0:T(8,128)(2,1)S(1)}, bf16[2,512,256]{2,1,0:T(8,128)(2,1)S(1)}, u32[]{:S(2)}, u32[]{:S(2)}) collective-permute-start(bf16[2,512,256]{2,1,0:T(8,128)(2,1)S(1)} %get-tuple-element.448), channel_id=1, source_target_pairs={{0,16},{4,20},{8,24},{12,28},{16,0},{20,4},{24,8},{28,12},{1,17},{... | collective-permute-start | bytes 1572872 | tf_op jit(solution)/shard_map/ppermute | solution.py:763
  413.6 29.5 %collective-permute-start.77 = (bf16[2,512,256]{2,1,0:T(8,128)(2,1)S(1)}, bf16[2,512,256]{2,1,0:T(8,128)(2,1)S(1)}, u32[]{:S(2)}, u32[]{:S(2)}) collective-permute-start(bf16[2,512,256]{2,1,0:T(8,128)(2,1)S(1)} %get-tuple-element.447), channel_id=1, source_target_pairs={{0,24},{4,28},{8,0},{12,4},{16,8},{20,12},{24,16},{28,20},{1,25},{... | collective-permute-start | bytes 1572872 | tf_op jit(solution)/shard_map/ppermute | solution.py:763
  451.7 19.6 %collective-permute-start.79 = (bf16[4,2,16,2176]{3,2,1,0:T(8,128)(2,1)S(1)}, bf16[4,2,16,2176]{3,2,1,0:T(8,128)(2,1)S(1)}, u32[]{:S(2)}, u32[]{:S(2)}) collective-permute-start(bf16[4,2,16,2176]{3,2,1,0:T(8,128)(2,1)S(1)} %select_bitcast_fusion.3), channel_id=1, source_target_pairs={{0,2},{1,3},{2,0},{3,1},{4,6},{5,7},{6,4},{7,5},{8,10},{9,11},{10,... | collective-permute-start | bytes 1671176 | tf_op jit(solution)/shard_map/ppermute | solution.py:758
  480.1 15.0 %collective-permute-start.81 = (bf16[16,2176]{1,0:T(8,128)(2,1)S(1)}, bf16[16,2176]{1,0:T(8,128)(2,1)S(1)}, u32[]{:S(2)}, u32[]{:S(2)}) collective-permute-start(bf16[16,2176]{1,0:T(8,128)(2,1)S(1)} %get-tuple-element.464), channel_id=1, source_target_pairs={{0,8},{4,12},{8,16},{12,20},{16,24},{20,28},{24,0},{28,4},{1,9},{5... | collective-permute-start | bytes 208904 | tf_op jit(solution)/shard_map/ppermute | solution.py:763
  (111 other events, 1324.5 us)

commit v5 on v4

--- a/solution.py
+++ b/solution.py
@@ -215,8 +215,8 @@
         input_output_aliases={7: 0} if aliased else {},
         compiler_params=pltpu.CompilerParams(vmem_limit_bytes=48 << 20),
         cost_estimate=pl.CostEstimate(
-            flops=(row_to - row_from) * length * 400 * 8 * 256 * 20,
-            bytes_accessed=(row_to - row_from) * length * triple * 4,
+            flops=row_to * length * 400 * 8 * 256 * 20 if aliased else rows,
+            bytes_accessed=rows * length,
             transcendentals=0,
         ),
         name="attend_back",
@@ -621,7 +621,7 @@
         low_ref[r] = dot_nt(total, weight_ref[...]).astype(BF16)
 
 
-def pull_slots(found, slots, gates, change, mixed, hidden, cotangent, attended, router, gains, packed, held):
+def pull_slots(found, slots, gates, change, mixed, hidden, cotangent, attended, router, gains, packed, held, weight=20):
     rows, span, width = mixed.shape
     parts = list(found.values())
     experts, depth, _ = parts[0].shape
@@ -663,16 +663,20 @@
         input_output_aliases=aliases,
         compiler_params=pltpu.CompilerParams(vmem_limit_bytes=58 << 20),
         cost_estimate=pl.CostEstimate(
-            flops=len(parts) * rows * places * width * width * 20,
-            bytes_accessed=rows * places * width * 20,
+            flops=len(parts) * rows * places * width * width * weight,
+            bytes_accessed=rows * places * weight,
             transcendentals=0,
         ),
         name="pull_slots",
     )(slots, gates, change, mixed, hidden, cotangent, attended, router, gains, packed, *parts, *(held or ()))
 
 
-def project_kernel(grads_ref, tokens_ref, product_ref, sums_ref):
-    @pl.when((pl.program_id(0) == 0) & (pl.program_id(1) == 0))
+def project_kernel(experts, grads_ref, tokens_ref, gains_ref, weight_ref, project_ref, late_ref, out_ref, product_ref, sums_ref):
+    width, wide = product_ref.shape
+    steps = pl.num_programs(0) * pl.num_programs(1)
+    step = pl.program_id(0) * pl.num_programs(1) + pl.program_id(1)
+
+    @pl.when(step == 0)
     def _():
         product_ref[...] = jnp.zeros_like(product_ref)
         sums_ref[...] = jnp.zeros_like(sums_ref)
@@ -682,25 +686,43 @@
     product_ref[...] += dot_tn(hat, grads_ref[0])
     sums_ref[...] += dot_tn(ones, grads_ref[0])
 
-
-def project_grads(grads, tokens, tile=1024):
+    @pl.when(step == steps - 1)
+    def _():
+        sums = sums_ref[0:1, :]
+        for at in range(0, width, 64):
+            here = slice(at, at + 64)
+            product = product_ref[here, :]
+            weights = weight_ref[here, :].astype(F32)
+            out_ref[here, :wide] = (gains_ref[here, 0:1] * product + gains_ref[here, 1:2] * sums).astype(BF16)
+            out_ref[here, wide: wide + width] = project_ref[here, :].astype(BF16)
+            late = late_ref[here, :]
+            lane = iota(late.shape, 1)
+            late = jnp.where(lane == experts, jnp.sum(weights * product, axis=1, keepdims=True), late)
+            late = jnp.where(lane == experts + 1, jnp.sum(weights * sums, axis=1, keepdims=True), late)
+            out_ref[here, wide + width:] = late.astype(BF16)
+
+
+def project_grads(grads, tokens, gains, packed, project, late, experts, tile=1024):
     rows, length, width = tokens.shape
-    shapes = [(width, 3 * width), (8, 3 * width)]
+    wide = 3 * width
     return pl.pallas_call(
-        project_kernel,
+        functools.partial(project_kernel, experts),
         grid=(rows, length // tile),
         in_specs=[
-            pl.BlockSpec((1, tile, 3 * width), lambda r, t: (r, t, 0)),
+            pl.BlockSpec((1, tile, wide), lambda r, t: (r, t, 0)),
             pl.BlockSpec((1, tile, width), lambda r, t: (r, t, 0)),
+            constant_spec(gains.shape),
+            constant_spec((width, wide)),
+            constant_spec(project.shape),
+            constant_spec(late.shape),
         ],
-        out_specs=[constant_spec(shape) for shape in shapes],
-        out_shape=[jax.ShapeDtypeStruct(shape, F32) for shape in shapes],
-        compiler_params=pltpu.CompilerParams(vmem_limit_bytes=40 << 20),
-        cost_estimate=pl.CostEstimate(
-            flops=rows, bytes_accessed=rows, transcendentals=0
-        ),
+        out_specs=constant_spec(packed.shape),
+        out_shape=jax.ShapeDtypeStruct(packed.shape, BF16),
+        scratch_shapes=[pltpu.VMEM((width, wide), F32), pltpu.VMEM((8, wide), F32)],
+        compiler_params=pltpu.CompilerParams(vmem_limit_bytes=48 << 20),
+        cost_estimate=pl.CostEstimate(flops=rows, bytes_accessed=rows, transcendentals=0),
         name="project_grads",
-    )(grads, tokens)
+    )(grads, tokens, gains, packed, project, late)
 
 
 def tokens_kernel(grads_ref, tokens_ref, hidden_ref, gains_ref, weight_ref, *rest):
@@ -992,9 +1014,9 @@
     result = exchange(result)
     back = exchange(grad_pooled)
 
-    def pull(found, change, out):
+    def pull(found, change, out, *weight):
         return pull_slots(
-            found, slots, gates, change, mixed, hidden, cotangent, attended, spread_router, gains, packed, out
+            found, slots, gates, change, mixed, hidden, cotangent, attended, spread_router, gains, packed, out, *weight
         )
 
     def spread(found, out):
@@ -1028,12 +1050,12 @@
         pulled = work or pulled
     pulled = pull(arrived[turns - 1], changes[turns - 1], pulled)
     layer_out = out
-    pulled = pull(arrived[turns], changes[turns], pulled)
-    grad_hidden, grad_attended, router_grad, grad_proj_out, sums_two = pulled
-    grad_attended, grad_weights = together(grad_attended, grad_weights)
-    split = rows - max(1, rows // 4)
+    grad_weights, *_ = together(grad_weights, *arrived[turns].values())
     if pair == 2:
         came = flip(grad_weights[lines:], 1, "dp")
+    pulled = pull(arrived[turns], changes[turns], pulled, 0)
+    grad_hidden, grad_attended, router_grad, grad_proj_out, sums_two = pulled
+    split = rows - max(1, rows // 2)
     grads = attn_bwd(joined, grad_attended, attended, logs, starts, lows, vlens, 0, split)
     grad_weights = grad_weights[:lines]
     if pair == 2:
@@ -1041,17 +1063,11 @@
         grad_weights = add(grad_weights, came)
     grad_parts = [turn(grad_weights[k], k * pair) for k in range(1, lines)]
     grads = attn_bwd(joined, grad_attended, attended, logs, starts, lows, vlens, split, rows, grads)
-    product, sums_one = project_grads(grads, tokens)
-    product, *grad_parts = together(product, *grad_parts)
-    full_in = packed[:, : 3 * width].astype(F32)
-    sums_one = sums_one[:1]
-    grad_proj_in = gains[0][:, None] * product + gains[1][:, None] * sums_one
-    sums_one = jnp.stack([jnp.sum(full_in * product, axis=1), jnp.sum(full_in * sums_one, axis=1)])
     router_grad = jnp.sum(jnp.where(mine[:, :, None], router_grad[None], 0.0), axis=1)
-
-    late = jnp.concatenate([router_grad, sums_one, sums_two[:2]], axis=0).T
+    late = jnp.concatenate([router_grad, jnp.zeros((2, width), F32), sums_two[:2]], axis=0).T
     late = jnp.pad(late, ((0, 0), (0, 128 - late.shape[1])))
-    reduced = jnp.concatenate([grad_proj_in, grad_proj_out, late], axis=1).astype(BF16)
+    reduced = project_grads(grads, tokens, gains.T, packed, grad_proj_out, late, experts)
+    reduced, *grad_parts = together(reduced, *grad_parts)
     made = []
 
     def tokens_beside(*came):

time: 508 us -> 499 us (0.982)
  starting transfers between devices: 107 us -> 90.2 us
  local copies, waits for them, and re-layouts: 26.4 us -> 32.3 us
    ppermute x12, starting transfers between devices: 26.7 us -> 18.4 us  [turn(): lax.ppermute(value, axis, [(i, (i + step) % count) for i in range(count)])]
    ppermute x20, starting transfers between devices: 23.4 us -> 16.1 us  [flip(): return lax.ppermute(value, axis, [(i, i ^ bit) for i in range(count)])]
    unnamed x116 -> x100, local copies, waits for them, and re-layouts: 17.7 us -> 15 us
  transfers between devices with their start and end apart: 84 -> 84, of which waited for: 48 -> 48; matrix products, arithmetic and copies ran while one was open for 3% -> 5% of each run, Pallas kernels for 41% -> 47%
where the time goes in v5:
time: 499 us; the launch traced here: 489 us
  Pallas kernels  228 us (46%)
  waiting for transfers between devices  118 us (24%)
  starting transfers between devices  90.2 us (18%)
  local copies, waits for them, and re-layouts  32.3 us (6%)
  other arithmetic  15.9 us (3%)
    ppermute x52, waiting for transfers between devices, shift(): lax.ppermute(value, 'dp', [(order[i], order[(i + step) % count]) for i in...  63.6 us
    ppermute x52, starting transfers between devices, shift(): lax.ppermute(value, 'dp', [(order[i], order[(i + step) % count]) for i in...  55.7 us
    pallas_call x2, Pallas kernels, attn_bwd(): pl.pallas_call(functools.partial(attn_bwd_kernel, width, row_from, batch,...  49.4 us
    pallas_call x5, Pallas kernels, pull_slots(): pl.pallas_call(functools.partial(pull_kernel, held is None, len(parts)),...  47.7 us
    ppermute x20, waiting for transfers between devices, flip(): return lax.ppermute(value, axis, [(i, i ^ bit) for i in range(count)])  45 us
    pallas_call x1, Pallas kernels, attn_fwd(): pl.pallas_call(functools.partial(attn_fwd_kernel, width, batch, count), g...  27.9 us
    pallas_call x5, Pallas kernels, spread_tokens(): pl.pallas_call(functools.partial(spread_kernel, group, len(parts)), grid_...  26.5 us
    ppermute x12, starting transfers between devices, turn(): lax.ppermute(value, axis, [(i, (i + step) % count) for i in range(count)])  18.4 us
  transfers between devices with their start and end apart: 84, of which 48 were waited for; matrix products, arithmetic and copies ran while one was open for 5% of the time, Pallas kernels for 47%

profile of v5, /device:TPU:0, one launch (start us, length us, event | category | flops | bytes accessed | tf_op | source)
XLA Modules:
  0.0 489.0 jit_solution(9124729212005987849)
XLA Ops:
  2.4 5.0 %collective-permute-start = (bf16[16,2176]{1,0:T(8,128)(2,1)S(1)}, bf16[16,2176]{1,0:T(8,128)(2,1)S(1)}, u32[]{:S(2)}, u32[]{:S(2)}) collective-permute-start(bf16[16,2176]{1,0:T(8,128)(2,1)S(1)} %fusion.40), channel_id=1, source_target_pairs={{0,24},{4,28},{8,0},{12,4},{16,8},{20,12},{24,16},{28,20},{1,25},{... | collective-permute-start | bytes 208904 | tf_op jit(solution)/shard_map/ppermute | solution.py:785
  15.8 7.0 %collective-permute-done.3 = bf16[4,16,2176]{2,1,0:T(8,128)(2,1)S(1)} collective-permute-done((bf16[4,16,2176]{2,1,0:T(8,128)(2,1)S(1)}, bf16[4,16,2176]{2,1,0:T(8,128)(2,1)S(1)}, u32[]{:S(2)}, u32[]{:S(2)}) %collective-permute-start.3) | collective-permute-done | bytes 278560 | tf_op jit(solution)/shard_map/ppermute | solution.py:780
  26.8 9.8 %collective-permute-done.4 = bf16[8,1,16,2176]{3,2,0,1:T(8,128)(2,1)S(1)} collective-permute-done((bf16[8,1,16,2176]{3,2,0,1:T(8,128)(2,1)S(1)}, bf16[8,1,16,2176]{3,2,0,1:T(8,128)(2,1)S(1)}, u32[]{:S(2)}, u32[]{:S(2)}) %collective-permute-start.4) | collective-permute-done | bytes 557088 | tf_op jit(solution)/shard_map/ppermute | solution.py:780
  47.5 10.1 %join.1.joined_ref = bf16[4,1024,1536]{2,1,0:T(8,128)(2,1)} custom-call(bf16[4,1024,512]{2,1,0:T(8,128)(2,1)S(1)} %bitcast.382, f32[8,512]{1,0:T(8,128)S(1)} %copy.150.gains_ref, bf16[512,2176]{1,0:T(8,128)(2,1)S(1)} %bitcast.356), custom_call_target="tpu_custom_call" | custom-call | flops 6442450944 | bytes 16777216 | tf_op jit(solution)/shard_map/join/pallas_call | solution.py:261
  59.6 27.9 %attend.1 = (bf16[4,1024,512]{2,1,0:T(8,128)(2,1)S(1)}, f32[4,8,8,128]{3,2,1,0:T(8,128)S(1)}) custom-call(s32[4,8]{1,0:T(4,128)S(1)} %add_select_fusion.lo_ref, s32[4]{0:T(128)S(1)} %subtract_bitcast_fusion.vlen_ref, s32[4,8,128]{2,1,0:T(8,128)S(1)} %select_select_fusion.start_ref, bf16[4,1024,1536]{2,1,0:T(8,128)(2,1)} %join.1.joined_ref), custom_call_target="tpu_custom_call" | custom-call | flops 13421772800 | bytes 12582912 | tf_op jit(solution)/shard_map/attend/pallas_call | solution.py:100
  90.5 7.5 %mix.1 = (f32[4,1024,512]{2,1,0:T(8,128)}, bf16[4,1024,512]{2,1,0:T(8,128)(2,1)S(1)}, f32[4,16,1024]{2,1,0:T(8,128)S(1)}) custom-call(bf16[4,1024,512]{2,1,0:T(8,128)(2,1)S(1)} %get-tuple-element.181.attended_ref, bf16[4,1024,512]{2,1,0:T(8,128)(2,1)} %bitcast.379, f32[8,512]{1,0:T(8,128)S(1)} %copy.150.gains_ref, bf16[512,2176]{1,0:T(8,128)(2,1)S(1)} %bitcast.357, ...), custom_call_target="tpu_custom_call" | custom-call | flops 2147483648 | bytes 20971520 | tf_op jit(solution)/shard_map/mix/pallas_call | solution.py:291
  109.7 4.9 %collective-permute-done.15 = f32[2,2,4,1024]{3,2,1,0:T(4,128)S(1)} collective-permute-done((f32[2,2,4,1024]{3,2,1,0:T(4,128)S(1)}, f32[2,2,4,1024]{3,2,1,0:T(4,128)S(1)}, u32[]{:S(2)}, u32[]{:S(2)}) %collective-permute-start.15) | collective-permute-done | bytes 65568 | tf_op jit(solution)/shard_map/ppermute | solution.py:785
  193.4 5.0 %collective-permute-done.38 = bf16[2,128,512]{2,1,0:T(8,128)(2,1)S(1)} collective-permute-done((bf16[2,128,512]{2,1,0:T(8,128)(2,1)S(1)}, bf16[2,128,512]{2,1,0:T(8,128)(2,1)S(1)}, u32[]{:S(2)}, u32[]{:S(2)}) %collective-permute-start.38) | collective-permute-done | bytes 262176 | tf_op jit(solution)/shard_map/ppermute | solution.py:775
  220.9 7.8 %experts.1 = (bf16[4,128,512]{2,1,0:T(8,128)(2,1)S(1)}, bf16[8,512,256]{2,1,0:T(8,128)(2,1)S(1)}, f32[8,512,256]{2,1,0:T(8,128)S(1)}) custom-call(bf16[4,128,512]{2,1,0:T(8,128)(2,1)S(1)} %pad_maximum_fusion.4.pooled_ref, bf16[8,2,512,256]{3,2,1,0:T(8,128)(2,1)S(1)} %bitcast_dynamic-update-slice_fusion.weights_ref), custom_call_target="tpu_custom_call" | custom-call | flops 4294967296 | bytes 8388608 | tf_op jit(solution)/shard_map/experts/pallas_call | solution.py:389
  242.5 11.2 %pull_experts.1 = (bf16[4,144,512]{2,1,0:T(8,128)(2,1)S(1)}, bf16[8,2,512,256]{3,2,1,0:T(8,128)(2,1)S(1)}) custom-call(s32[8]{0:T(128)S(1)} %get-tuple-element.477.slots_ref, bf16[4,128,512]{2,1,0:T(8,128)(2,1)S(1)} %pad_maximum_fusion.4.pooled_ref, bf16[4,128,512]{2,1,0:T(8,128)(2,1)S(1)} %pad_maximum_fusion.5.grads_ref, ...), custom_call_target="tpu_custom_call" | custom-call | flops 6442450944 | bytes 8388608 | tf_op jit(solution)/shard_map/pull_experts/pallas_call | solution.py:454
  275.6 7.2 %pull_slots.5 = (f32[4,1024,512]{2,1,0:T(8,128)}, bf16[4,1024,512]{2,1,0:T(8,128)(2,1)}, f32[4,512]{1,0:T(4,128)}, f32[512,512]{1,0:T(8,128)}, f32[8,512]{1,0:T(8,128)}) custom-call(s32[8]{0:T(128)} %copy-done.13, f32[1024,16]{1,0:T(8,128)} %bitcast.368, f32[1,128,16]{2,1,0:T(8,128)} %get-tuple-element.233.change_ref, bf16[4,1024,512]{2,1,0:T(8,128)(2,1)} %copy-done.2, ...), custom_call_target="tpu_custom_call" | custom-call | flops 2684354560 | bytes 10240 | tf_op jit(solution)/shard_map/pull_slots/pallas_call | solution.py:648
  282.8 6.1 %spread.6 = (bf16[4,1024,512]{2,1,0:T(8,128)(2,1)}, f32[2,128,16]{2,1,0:T(8,128)}) custom-call(s32[8]{0:T(128)} %copy-done.13, f32[1024,16]{1,0:T(8,128)} %bitcast.369, bf16[4,1024,512]{2,1,0:T(8,128)(2,1)} %bitcast.346, f32[4,1024,512]{2,1,0:T(8,128)} %get-tuple-element.225.hidden_ref, ...), custom_call_target="tpu_custom_call", output_to_operand_aliasing={{0}: (6, {})} | custom-call | flops 2621440000 | bytes 2621440 | tf_op jit(solution)/shard_map/spread/pallas_call | solution.py:525
  293.4 5.2 %collective-permute-done.62.rest_0_ = bf16[4,144,512]{2,1,0:T(8,128)(2,1)} collective-permute-done((bf16[4,144,512]{2,1,0:T(8,128)(2,1)S(1)}, bf16[4,144,512]{2,1,0:T(8,128)(2,1)}, u32[]{:S(2)}, u32[]{:S(2)}) %collective-permute-start.62) | collective-permute-done | bytes 589856 | tf_op jit(solution)/shard_map/ppermute | solution.py:775
  302.1 11.0 %pull_slots.6 = (f32[4,1024,512]{2,1,0:T(8,128)}, bf16[4,1024,512]{2,1,0:T(8,128)(2,1)}, f32[4,512]{1,0:T(4,128)}, f32[512,512]{1,0:T(8,128)}, f32[8,512]{1,0:T(8,128)}) custom-call(s32[8]{0:T(128)} %copy-done.13, f32[1024,16]{1,0:T(8,128)} %bitcast.370, ...), custom_call_target="tpu_custom_call", output_to_operand_aliasing={{0}: (12, {}), {1}: (13, {})} | custom-call | flops 5368709120 | bytes 10240 | tf_op jit(solution)/shard_map/pull_slots/pallas_call | solution.py:648
  313.1 6.1 %spread.7 = (bf16[4,1024,512]{2,1,0:T(8,128)(2,1)}, f32[2,128,16]{2,1,0:T(8,128)}) custom-call(s32[8]{0:T(128)} %copy-done.13, f32[1024,16]{1,0:T(8,128)} %bitcast.371, bf16[4,1024,512]{2,1,0:T(8,128)(2,1)} %bitcast.348, f32[4,1024,512]{2,1,0:T(8,128)} %get-tuple-element.225.hidden_ref, ...), custom_call_target="tpu_custom_call", output_to_operand_aliasing={{0}: (6, {})} | custom-call | flops 2621440000 | bytes 2621440 | tf_op jit(solution)/shard_map/spread/pallas_call | solution.py:525
  323.1 6.1 %spread.8 = (bf16[4,1024,512]{2,1,0:T(8,128)(2,1)}, f32[2,128,16]{2,1,0:T(8,128)}) custom-call(s32[8]{0:T(128)} %copy-done.13, f32[1024,16]{1,0:T(8,128)} %bitcast.372, bf16[4,1024,512]{2,1,0:T(8,128)(2,1)} %bitcast.349, f32[4,1024,512]{2,1,0:T(8,128)} %get-tuple-element.225.hidden_ref, ...), custom_call_target="tpu_custom_call", output_to_operand_aliasing={{0}: (6, {})} | custom-call | flops 2621440000 | bytes 2621440 | tf_op jit(solution)/shard_map/spread/pallas_call | solution.py:525
  337.8 11.0 %pull_slots.7 = (f32[4,1024,512]{2,1,0:T(8,128)}, bf16[4,1024,512]{2,1,0:T(8,128)(2,1)}, f32[4,512]{1,0:T(4,128)}, f32[512,512]{1,0:T(8,128)}, f32[8,512]{1,0:T(8,128)}) custom-call(s32[8]{0:T(128)} %copy-done.13, f32[1024,16]{1,0:T(8,128)} %bitcast.374, ...), custom_call_target="tpu_custom_call", output_to_operand_aliasing={{0}: (12, {}), {1}: (13, {})} | custom-call | flops 5368709120 | bytes 10240 | tf_op jit(solution)/shard_map/pull_slots/pallas_call | solution.py:648
  352.1 11.0 %pull_slots.8 = (f32[4,1024,512]{2,1,0:T(8,128)}, bf16[4,1024,512]{2,1,0:T(8,128)(2,1)}, f32[4,512]{1,0:T(4,128)}, f32[512,512]{1,0:T(8,128)}, f32[8,512]{1,0:T(8,128)}) custom-call(s32[8]{0:T(128)} %copy-done.13, f32[1024,16]{1,0:T(8,128)} %bitcast.375, ...), custom_call_target="tpu_custom_call", output_to_operand_aliasing={{0}: (12, {}), {1}: (13, {})} | custom-call | flops 5368709120 | bytes 10240 | tf_op jit(solution)/shard_map/pull_slots/pallas_call | solution.py:648
  363.1 7.5 %pull_slots.9 = (f32[4,1024,512]{2,1,0:T(8,128)}, bf16[4,1024,512]{2,1,0:T(8,128)(2,1)}, f32[4,512]{1,0:T(4,128)}, f32[512,512]{1,0:T(8,128)}, f32[8,512]{1,0:T(8,128)}) custom-call(s32[8]{0:T(128)} %copy-done.13, f32[1024,16]{1,0:T(8,128)} %bitcast.376, ...), custom_call_target="tpu_custom_call", output_to_operand_aliasing={{0}: (11, {}), {1}: (12, {})} | custom-call | tf_op jit(solution)/shard_map/pull_slots/pallas_call | solution.py:648
  372.8 25.0 %attend_back.2.rest_0_ = bf16[4,1024,1536]{2,1,0:T(8,128)(2,1)} custom-call(s32[4,8]{1,0:T(4,128)S(1)} %add_select_fusion.lo_ref, s32[4]{0:T(128)S(1)} %subtract_bitcast_fusion.vlen_ref, s32[4,8,128]{2,1,0:T(8,128)S(1)} %select_select_fusion.start_ref, bf16[4,1024,1536]{2,1,0:T(8,128)(2,1)} %join.1.joined_ref, bf16[4,1024,512]{2,1,0:T(8,128)(2,1)S(1)} %copy-done.6, ...), custom_call_target="tpu_custom_call" | custom-call | flops 4 | bytes 4096 | tf_op jit(solution)/shard_map/attend_back/pallas_call | solution.py:194
  405.5 24.4 %attend_back.3.grads_ref = bf16[4,1024,1536]{2,1,0:T(8,128)(2,1)} custom-call(s32[4,8]{1,0:T(4,128)S(1)} %add_select_fusion.lo_ref, s32[4]{0:T(128)S(1)} %subtract_bitcast_fusion.vlen_ref, s32[4,8,128]{2,1,0:T(8,128)S(1)} %select_select_fusion.start_ref, bf16[4,1024,1536]{2,1,0:T(8,128)(2,1)} %join.1.joined_ref, ...), custom_call_target="tpu_custom_call", output_to_operand_aliasing={{}: (7, {})} | custom-call | flops 67108864000 | bytes 4096 | tf_op jit(solution)/shard_map/attend_back/pallas_call | solution.py:194
  429.9 14.8 %project_grads.1 = bf16[512,2176]{1,0:T(8,128)(2,1)S(1)} custom-call(bf16[4,1024,1536]{2,1,0:T(8,128)(2,1)} %attend_back.3.grads_ref, bf16[4,1024,512]{2,1,0:T(8,128)(2,1)} %bitcast.380, f32[512,8]{1,0:T(8,128)S(1)} %get-tuple-element.464.gains_ref, bf16[512,2176]{1,0:T(8,128)(2,1)S(1)} %bitcast.364, f32[512,512]{1,0:T(8,128)S(1)} %copy-done.11, ...), custom_call_target="tpu_custom_call" | custom-call | flops 4 | bytes 4 | tf_op jit(solution)/shard_map/project_grads/pallas_call | solution.py:708
  452.8 16.1 %pull_tokens.1 = f32[4,1024,512]{2,1,0:T(8,128)} custom-call(bf16[4,1024,1536]{2,1,0:T(8,128)(2,1)} %attend_back.3.grads_ref, bf16[4,1024,512]{2,1,0:T(8,128)(2,1)} %bitcast.381, f32[4,1024,512]{2,1,0:T(8,128)} %get-tuple-element.319.hidden_ref, f32[8,512]{1,0:T(8,128)} %copy-done.12, bf16[512,2176]{1,0:T(8,128)(2,1)} %bitcast.363), custom_call_target="tpu_custom_call" | custom-call | flops 21474836480 | bytes 33554432 | tf_op jit(solution)/shard_map/pull_tokens/pallas_call | solution.py:740
  469.2 8.4 %collective-permute-done.80 = bf16[4,16,2176]{2,1,0:T(8,128)(2,1)S(1)} collective-permute-done((bf16[4,16,2176]{2,1,0:T(8,128)(2,1)S(1)}, bf16[4,16,2176]{2,1,0:T(8,128)(2,1)S(1)}, u32[]{:S(2)}, u32[]{:S(2)}) %collective-permute-start.80) | collective-permute-done | bytes 278560 | tf_op jit(solution)/shard_map/ppermute | solution.py:780
  (370 shorter events, 228.1 us)
Async XLA Ops:
  41.3 16.3 %collective-permute-start.6 = (bf16[2,512,256]{2,1,0:T(8,128)(2,1)S(1)}, bf16[2,512,256]{2,1,0:T(8,128)(2,1)}, u32[]{:S(2)}, u32[]{:S(2)}) collective-permute-start(bf16[2,512,256]{2,1,0:T(8,128)(2,1)S(1)} %pad_maximum_fusion.3), channel_id=1, source_target_pairs={{0,8},{8,16},{16,24},{24,28},{28,20},{20,12},{12,4},{4,0},{1,9},{9... | collective-permute-start | bytes 1572872 | tf_op jit(solution)/shard_map/ppermute | solution.py:775
  41.3 16.3 %collective-permute-start.7 = (bf16[2,512,256]{2,1,0:T(8,128)(2,1)S(1)}, bf16[2,512,256]{2,1,0:T(8,128)(2,1)}, u32[]{:S(2)}, u32[]{:S(2)}) collective-permute-start(bf16[2,512,256]{2,1,0:T(8,128)(2,1)S(1)} %pad_maximum_fusion.3), channel_id=1, source_target_pairs={{0,4},{8,0},{16,8},{24,16},{28,24},{20,28},{12,20},{4,12},{1,5},{9... | collective-permute-start | bytes 1572872 | tf_op jit(solution)/shard_map/ppermute | solution.py:775
  57.6 29.9 %collective-permute-start.8 = (bf16[2,512,256]{2,1,0:T(8,128)(2,1)}, bf16[2,512,256]{2,1,0:T(8,128)(2,1)S(1)}, u32[]{:S(2)}, u32[]{:S(2)}) collective-permute-start(bf16[2,512,256]{2,1,0:T(8,128)(2,1)} %collective-permute-done.6), channel_id=1, source_target_pairs={{0,8},{8,16},{16,24},{24,28},{28,20},{20,12},{12,4},{4,0},{1,9},{9... | collective-permute-start | bytes 1572872 | tf_op jit(solution)/shard_map/ppermute | solution.py:775
  57.7 29.9 %collective-permute-start.9 = (bf16[2,512,256]{2,1,0:T(8,128)(2,1)}, bf16[2,512,256]{2,1,0:T(8,128)(2,1)S(1)}, u32[]{:S(2)}, u32[]{:S(2)}) collective-permute-start(bf16[2,512,256]{2,1,0:T(8,128)(2,1)} %collective-permute-done.7), channel_id=1, source_target_pairs={{0,4},{8,0},{16,8},{24,16},{28,24},{20,28},{12,20},{4,12},{1,5},{9... | collective-permute-start | bytes 1572872 | tf_op jit(solution)/shard_map/ppermute | solution.py:775
  101.9 22.1 %collective-permute-start.12 = (bf16[1,512,256]{2,1,0:T(8,128)(2,1)S(1)}, bf16[1,512,256]{2,1,0:T(8,128)(2,1)S(1)}, u32[]{:S(2)}, u32[]{:S(2)}) collective-permute-start(bf16[1,512,256]{2,1,0:T(8,128)(2,1)S(1)} %slice.330), channel_id=1, source_target_pairs={{0,8},{8,16},{16,24},{24,28},{28,20},{20,12},{12,4},{4,0},{1,9},{9... | collective-permute-start | bytes 786440 | tf_op jit(solution)/shard_map/ppermute | solution.py:775
  103.7 20.4 %collective-permute-start.13 = (bf16[1,512,256]{2,1,0:T(8,128)(2,1)S(1)}, bf16[1,512,256]{2,1,0:T(8,128)(2,1)S(1)}, u32[]{:S(2)}, u32[]{:S(2)}) collective-permute-start(bf16[1,512,256]{2,1,0:T(8,128)(2,1)S(1)} %slice.331), channel_id=1, source_target_pairs={{0,4},{8,0},{16,8},{24,16},{28,24},{20,28},{12,20},{4,12},{1,5},{9... | collective-permute-start | bytes 786440 | tf_op jit(solution)/shard_map/ppermute | solution.py:775
  215.5 15.5 %collective-permute-start.47 = (bf16[2,128,512]{2,1,0:T(8,128)(2,1)S(1)}, bf16[2,128,512]{2,1,0:T(8,128)(2,1)S(1)}, u32[]{:S(2)}, u32[]{:S(2)}) collective-permute-start(bf16[2,128,512]{2,1,0:T(8,128)(2,1)S(1)} %get-tuple-element.214), channel_id=1, source_target_pairs={{0,8},{8,16},{16,24},{24,28},{28,20},{20,12},{12,4},{4,0},{1,9},{9... | collective-permute-start | bytes 786440 | tf_op jit(solution)/shard_map/ppermute | solution.py:775
  237.7 16.1 %collective-permute-start.58 = (bf16[4,128,512]{2,1,0:T(8,128)(2,1)S(1)}, bf16[4,128,512]{2,1,0:T(8,128)(2,1)}, u32[]{:S(2)}, u32[]{:S(2)}) collective-permute-start(bf16[4,128,512]{2,1,0:T(8,128)(2,1)S(1)} %pad_maximum_fusion.6.rest_0_), channel_id=1, source_target_pairs={{0,8},{8,16},{16,24},{24,28},{28,20},{20,12},{12,4},{4,0},{1,9},{9... | collective-permute-start | bytes 1572872 | tf_op jit(solution)/shard_map/ppermute | solution.py:775
  238.9 14.9 %collective-permute-start.59 = (bf16[4,128,512]{2,1,0:T(8,128)(2,1)S(1)}, bf16[4,128,512]{2,1,0:T(8,128)(2,1)}, u32[]{:S(2)}, u32[]{:S(2)}) collective-permute-start(bf16[4,128,512]{2,1,0:T(8,128)(2,1)S(1)} %pad_maximum_fusion.6.rest_0_), channel_id=1, source_target_pairs={{0,4},{8,0},{16,8},{24,16},{28,24},{20,28},{12,20},{4,12},{1,5},{9... | collective-permute-start | bytes 1572872 | tf_op jit(solution)/shard_map/ppermute | solution.py:775
  253.8 15.0 %collective-permute-start.60 = (bf16[4,128,512]{2,1,0:T(8,128)(2,1)}, bf16[4,128,512]{2,1,0:T(8,128)(2,1)}, u32[]{:S(2)}, u32[]{:S(2)}) collective-permute-start(bf16[4,128,512]{2,1,0:T(8,128)(2,1)} %collective-permute-done.58.rest_0_), channel_id=1, source_target_pairs={{0,8},{8,16},{16,24},{24,28},{28,20},{20,12},{12,4},{4,0},{1,9},{9... | collective-permute-start | bytes 1572872 | tf_op jit(solution)/shard_map/ppermute | solution.py:775
  255.0 15.1 %collective-permute-start.61 = (bf16[4,128,512]{2,1,0:T(8,128)(2,1)}, bf16[4,128,512]{2,1,0:T(8,128)(2,1)S(1)}, u32[]{:S(2)}, u32[]{:S(2)}) collective-permute-start(bf16[4,128,512]{2,1,0:T(8,128)(2,1)} %collective-permute-done.59.rest_1_), channel_id=1, source_target_pairs={{0,4},{8,0},{16,8},{24,16},{28,24},{20,28},{12,20},{4,12},{1,5},{9... | collective-permute-start | bytes 1572872 | tf_op jit(solution)/shard_map/ppermute | solution.py:775
  270.9 18.0 %collective-permute-start.64 = (bf16[4,128,512]{2,1,0:T(8,128)(2,1)}, bf16[4,128,512]{2,1,0:T(8,128)(2,1)S(1)}, u32[]{:S(2)}, u32[]{:S(2)}) collective-permute-start(bf16[4,128,512]{2,1,0:T(8,128)(2,1)} %collective-permute-done.60.rest_0_), channel_id=1, source_target_pairs={{0,8},{8,16},{16,24},{24,28},{28,20},{20,12},{12,4},{4,0},{1,9},{9... | collective-permute-start | bytes 1572872 | tf_op jit(solution)/shard_map/ppermute | solution.py:775
  272.2 16.6 %collective-permute-start.65 = (bf16[4,128,512]{2,1,0:T(8,128)(2,1)}, bf16[4,128,512]{2,1,0:T(8,128)(2,1)}, u32[]{:S(2)}, u32[]{:S(2)}) collective-permute-start(bf16[4,128,512]{2,1,0:T(8,128)(2,1)} %copy-done.38), channel_id=1, source_target_pairs={{0,4},{8,0},{16,8},{24,16},{28,24},{20,28},{12,20},{4,12},{1,5},{9... | collective-permute-start | bytes 1572872 | tf_op jit(solution)/shard_map/ppermute | solution.py:775
  272.9 25.7 %collective-permute-start.62 = (bf16[4,144,512]{2,1,0:T(8,128)(2,1)S(1)}, bf16[4,144,512]{2,1,0:T(8,128)(2,1)}, u32[]{:S(2)}, u32[]{:S(2)}) collective-permute-start(bf16[4,144,512]{2,1,0:T(8,128)(2,1)S(1)} %pad_maximum_fusion.1.rest_0_), channel_id=1, source_target_pairs={{0,8},{8,16},{16,24},{24,28},{28,20},{20,12},{12,4},{4,0},{1,9},{9... | collective-permute-start | bytes 1769480 | tf_op jit(solution)/shard_map/ppermute | solution.py:775
  274.3 25.8 %collective-permute-start.63 = (bf16[4,144,512]{2,1,0:T(8,128)(2,1)S(1)}, bf16[4,144,512]{2,1,0:T(8,128)(2,1)}, u32[]{:S(2)}, u32[]{:S(2)}) collective-permute-start(bf16[4,144,512]{2,1,0:T(8,128)(2,1)S(1)} %pad_maximum_fusion.1.rest_0_), channel_id=1, source_target_pairs={{0,4},{8,0},{16,8},{24,16},{28,24},{20,28},{12,20},{4,12},{1,5},{9... | collective-permute-start | bytes 1769480 | tf_op jit(solution)/shard_map/ppermute | solution.py:775
  289.7 29.4 %collective-permute-start.68 = (bf16[2,128,512]{2,1,0:T(8,128)(2,1)}, bf16[2,128,512]{2,1,0:T(8,128)(2,1)S(1)}, u32[]{:S(2)}, u32[]{:S(2)}) collective-permute-start(bf16[2,128,512]{2,1,0:T(8,128)(2,1)} %slice.385), channel_id=1, source_target_pairs={{0,8},{8,16},{16,24},{24,28},{28,20},{20,12},{12,4},{4,0},{1,9},{9... | collective-permute-start | bytes 786440 | tf_op jit(solution)/shard_map/ppermute | solution.py:775
  292.7 26.5 %collective-permute-start.69 = (bf16[2,128,512]{2,1,0:T(8,128)(2,1)}, bf16[2,128,512]{2,1,0:T(8,128)(2,1)}, u32[]{:S(2)}, u32[]{:S(2)}) collective-permute-start(bf16[2,128,512]{2,1,0:T(8,128)(2,1)} %slice.386), channel_id=1, source_target_pairs={{0,4},{8,0},{16,8},{24,16},{28,24},{20,28},{12,20},{4,12},{1,5},{9... | collective-permute-start | bytes 786440 | tf_op jit(solution)/shard_map/ppermute | solution.py:775
  300.1 20.1 %collective-permute-start.66 = (bf16[4,144,512]{2,1,0:T(8,128)(2,1)}, bf16[4,144,512]{2,1,0:T(8,128)(2,1)}, u32[]{:S(2)}, u32[]{:S(2)}) collective-permute-start(bf16[4,144,512]{2,1,0:T(8,128)(2,1)} %collective-permute-done.62.rest_0_), channel_id=1, source_target_pairs={{0,8},{8,16},{16,24},{24,28},{28,20},{20,12},{12,4},{4,0},{1,9},{9... | collective-permute-start | bytes 1769480 | tf_op jit(solution)/shard_map/ppermute | solution.py:775
  301.1 19.1 %collective-permute-start.67 = (bf16[4,144,512]{2,1,0:T(8,128)(2,1)}, bf16[4,144,512]{2,1,0:T(8,128)(2,1)}, u32[]{:S(2)}, u32[]{:S(2)}) collective-permute-start(bf16[4,144,512]{2,1,0:T(8,128)(2,1)} %collective-permute-done.63.rest_1_), channel_id=1, source_target_pairs={{0,4},{8,0},{16,8},{24,16},{28,24},{20,28},{12,20},{4,12},{1,5},{9... | collective-permute-start | bytes 1769480 | tf_op jit(solution)/shard_map/ppermute | solution.py:775
  351.3 47.6 %collective-permute-start.74 = (bf16[4,2,512,256]{3,2,1,0:T(8,128)(2,1)}, bf16[4,2,512,256]{3,2,1,0:T(8,128)(2,1)S(1)}, u32[]{:S(2)}, u32[]{:S(2)}) collective-permute-start(bf16[4,2,512,256]{3,2,1,0:T(8,128)(2,1)} %slice.389), channel_id=1, source_target_pairs={{0,4},{4,0},{8,12},{12,8},{16,20},{20,16},{24,28},{28,24},{1,5},{5... | collective-permute-start | bytes 6291464 | tf_op jit(solution)/shard_map/ppermute | solution.py:780
  401.3 43.4 %collective-permute-start.75 = (bf16[2,512,256]{2,1,0:T(8,128)(2,1)S(1)}, bf16[2,512,256]{2,1,0:T(8,128)(2,1)S(1)}, u32[]{:S(2)}, u32[]{:S(2)}) collective-permute-start(bf16[2,512,256]{2,1,0:T(8,128)(2,1)S(1)} %get-tuple-element.438), channel_id=1, source_target_pairs={{0,8},{4,12},{8,16},{12,20},{16,24},{20,28},{24,0},{28,4},{1,9},{5... | collective-permute-start | bytes 1572872 | tf_op jit(solution)/shard_map/ppermute | solution.py:785
  401.3 43.4 %collective-permute-start.76 = (bf16[2,512,256]{2,1,0:T(8,128)(2,1)S(1)}, bf16[2,512,256]{2,1,0:T(8,128)(2,1)S(1)}, u32[]{:S(2)}, u32[]{:S(2)}) collective-permute-start(bf16[2,512,256]{2,1,0:T(8,128)(2,1)S(1)} %get-tuple-element.437), channel_id=1, source_target_pairs={{0,16},{4,20},{8,24},{12,28},{16,0},{20,4},{24,8},{28,12},{1,17},{... | collective-permute-start | bytes 1572872 | tf_op jit(solution)/shard_map/ppermute | solution.py:785
  404.3 40.4 %collective-permute-start.77 = (bf16[2,512,256]{2,1,0:T(8,128)(2,1)S(1)}, bf16[2,512,256]{2,1,0:T(8,128)(2,1)S(1)}, u32[]{:S(2)}, u32[]{:S(2)}) collective-permute-start(bf16[2,512,256]{2,1,0:T(8,128)(2,1)S(1)} %get-tuple-element.436), channel_id=1, source_target_pairs={{0,24},{4,28},{8,0},{12,4},{16,8},{20,12},{24,16},{28,20},{1,25},{... | collective-permute-start | bytes 1572872 | tf_op jit(solution)/shard_map/ppermute | solution.py:785
  450.1 18.8 %collective-permute-start.79 = (bf16[4,2,16,2176]{3,2,1,0:T(8,128)(2,1)S(1)}, bf16[4,2,16,2176]{3,2,1,0:T(8,128)(2,1)S(1)}, u32[]{:S(2)}, u32[]{:S(2)}) collective-permute-start(bf16[4,2,16,2176]{3,2,1,0:T(8,128)(2,1)S(1)} %select_bitcast_fusion.3), channel_id=1, source_target_pairs={{0,2},{1,3},{2,0},{3,1},{4,6},{5,7},{6,4},{7,5},{8,10},{9,11},{10,... | collective-permute-start | bytes 1671176 | tf_op jit(solution)/shard_map/ppermute | solution.py:780
  (103 other events, 1287.7 us)

commit v6 on v5

--- a/solution.py
+++ b/solution.py
@@ -1001,8 +1001,9 @@
     later = [part[-way % owners] for part, way in second]
     for step in range(owners - 1):
         came = [shift(value, order, way) for value, (_, way) in zip(held, first)]
-        *came, one, two = together(*came, *later)
-        later = [one, two]
+        if step == 0:
+            *came, one, two = together(*came, *later)
+            later = [one, two]
         held = [add(value, part[-way * (2 + step) % owners]) for value, (part, way) in zip(came, first)]
         came = [shift(value, order, way) for value, (_, way) in zip(later, second)]
         later = [add(value, part[-way * (2 + step) % owners]) for value, (part, way) in zip(came, second)]
@@ -1038,7 +1039,8 @@
             pulled = pull(arrived[k], changes[k], pulled)
             work += pulled
         if step > 0:
-            second.after(*groups[min(step + 1, turns)].values())
+            if step == 1:
+                second.after(*groups[2].values())
         if first.left():
             found, work = first.step(*work)
             groups.append(found)

time: 499 us -> 481 us (0.964)
  waiting for transfers between devices: 118 us -> 103 us
    ppermute x52, waiting for transfers between devices: 63.6 us -> 49.7 us  [shift(): lax.ppermute(value, 'dp', [(order[i], order[(i + step) % count]) for i in...]
    unnamed x100 -> x97, local copies, waits for them, and re-layouts: 15 us -> 13.5 us
  transfers between devices with their start and end apart: 84 -> 84, of which waited for: 48 -> 49; matrix products, arithmetic and copies ran while one was open for 5% -> 5% of each run, Pallas kernels for 47% -> 48%
where the time goes in v6:
time: 481 us; the launch traced here: 472 us
  Pallas kernels  228 us (47%)
  waiting for transfers between devices  103 us (21%)
  starting transfers between devices  90.2 us (19%)
  local copies, waits for them, and re-layouts  29 us (6%)
  other arithmetic  17.7 us (4%)
    ppermute x52, starting transfers between devices, shift(): lax.ppermute(value, 'dp', [(order[i], order[(i + step) % count]) for i in...  54.3 us
    ppermute x52, waiting for transfers between devices, shift(): lax.ppermute(value, 'dp', [(order[i], order[(i + step) % count]) for i in...  49.7 us
    pallas_call x2, Pallas kernels, attn_bwd(): pl.pallas_call(functools.partial(attn_bwd_kernel, width, row_from, batch,...  49.3 us
    pallas_call x5, Pallas kernels, pull_slots(): pl.pallas_call(functools.partial(pull_kernel, held is None, len(parts)),...  47.8 us
    ppermute x20, waiting for transfers between devices, flip(): return lax.ppermute(value, axis, [(i, i ^ bit) for i in range(count)])  44.4 us
    pallas_call x1, Pallas kernels, attn_fwd(): pl.pallas_call(functools.partial(attn_fwd_kernel, width, batch, count), g...  27.9 us
    pallas_call x5, Pallas kernels, spread_tokens(): pl.pallas_call(functools.partial(spread_kernel, group, len(parts)), grid_...  26.6 us
    ppermute x12, starting transfers between devices, turn(): lax.ppermute(value, axis, [(i, (i + step) % count) for i in range(count)])  19 us
  transfers between devices with their start and end apart: 84, of which 49 were waited for; matrix products, arithmetic and copies ran while one was open for 5% of the time, Pallas kernels for 48%

profile of v6, /device:TPU:0, one launch (start us, length us, event | category | flops | bytes accessed | tf_op | source)
XLA Modules:
  0.0 472.4 jit_solution(13736255095840849214)
XLA Ops:
  2.4 5.0 %collective-permute-start = (bf16[16,2176]{1,0:T(8,128)(2,1)S(1)}, bf16[16,2176]{1,0:T(8,128)(2,1)S(1)}, u32[]{:S(2)}, u32[]{:S(2)}) collective-permute-start(bf16[16,2176]{1,0:T(8,128)(2,1)S(1)} %fusion.40), channel_id=1, source_target_pairs={{0,24},{4,28},{8,0},{12,4},{16,8},{20,12},{24,16},{28,20},{1,25},{... | collective-permute-start | bytes 208904 | tf_op jit(solution)/shard_map/ppermute | solution.py:785
  15.8 7.0 %collective-permute-done.3 = bf16[4,16,2176]{2,1,0:T(8,128)(2,1)S(1)} collective-permute-done((bf16[4,16,2176]{2,1,0:T(8,128)(2,1)S(1)}, bf16[4,16,2176]{2,1,0:T(8,128)(2,1)S(1)}, u32[]{:S(2)}, u32[]{:S(2)}) %collective-permute-start.3) | collective-permute-done | bytes 278560 | tf_op jit(solution)/shard_map/ppermute | solution.py:780
  26.8 9.8 %collective-permute-done.4 = bf16[8,1,16,2176]{3,2,0,1:T(8,128)(2,1)S(1)} collective-permute-done((bf16[8,1,16,2176]{3,2,0,1:T(8,128)(2,1)S(1)}, bf16[8,1,16,2176]{3,2,0,1:T(8,128)(2,1)S(1)}, u32[]{:S(2)}, u32[]{:S(2)}) %collective-permute-start.4) | collective-permute-done | bytes 557088 | tf_op jit(solution)/shard_map/ppermute | solution.py:780
  47.5 10.1 %join.1.joined_ref = bf16[4,1024,1536]{2,1,0:T(8,128)(2,1)} custom-call(bf16[4,1024,512]{2,1,0:T(8,128)(2,1)S(1)} %bitcast.382, f32[8,512]{1,0:T(8,128)S(1)} %copy.150.gains_ref, bf16[512,2176]{1,0:T(8,128)(2,1)S(1)} %bitcast.356), custom_call_target="tpu_custom_call" | custom-call | flops 6442450944 | bytes 16777216 | tf_op jit(solution)/shard_map/join/pallas_call | solution.py:261
  59.6 27.9 %attend.1 = (bf16[4,1024,512]{2,1,0:T(8,128)(2,1)S(1)}, f32[4,8,8,128]{3,2,1,0:T(8,128)S(1)}) custom-call(s32[4,8]{1,0:T(4,128)S(1)} %add_select_fusion.lo_ref, s32[4]{0:T(128)S(1)} %subtract_bitcast_fusion.vlen_ref, s32[4,8,128]{2,1,0:T(8,128)S(1)} %select_select_fusion.start_ref, bf16[4,1024,1536]{2,1,0:T(8,128)(2,1)} %join.1.joined_ref), custom_call_target="tpu_custom_call" | custom-call | flops 13421772800 | bytes 12582912 | tf_op jit(solution)/shard_map/attend/pallas_call | solution.py:100
  90.6 7.5 %mix.1 = (f32[4,1024,512]{2,1,0:T(8,128)}, bf16[4,1024,512]{2,1,0:T(8,128)(2,1)S(1)}, f32[4,16,1024]{2,1,0:T(8,128)S(1)}) custom-call(bf16[4,1024,512]{2,1,0:T(8,128)(2,1)S(1)} %get-tuple-element.151.attended_ref, bf16[4,1024,512]{2,1,0:T(8,128)(2,1)} %bitcast.379, f32[8,512]{1,0:T(8,128)S(1)} %copy.150.gains_ref, bf16[512,2176]{1,0:T(8,128)(2,1)S(1)} %bitcast.357, ...), custom_call_target="tpu_custom_call" | custom-call | flops 2147483648 | bytes 20971520 | tf_op jit(solution)/shard_map/mix/pallas_call | solution.py:291
  118.2 4.4 pool.2
  124.7 4.6 pool.3
  204.5 7.8 %experts.1 = (bf16[4,128,512]{2,1,0:T(8,128)(2,1)S(1)}, bf16[8,512,256]{2,1,0:T(8,128)(2,1)S(1)}, f32[8,512,256]{2,1,0:T(8,128)S(1)}) custom-call(bf16[4,128,512]{2,1,0:T(8,128)(2,1)S(1)} %pad_maximum_fusion.4.pooled_ref, bf16[8,2,512,256]{3,2,1,0:T(8,128)(2,1)S(1)} %bitcast_dynamic-update-slice_fusion.weights_ref), custom_call_target="tpu_custom_call" | custom-call | flops 4294967296 | bytes 8388608 | tf_op jit(solution)/shard_map/experts/pallas_call | solution.py:389
  226.1 11.2 %pull_experts.1 = (bf16[4,144,512]{2,1,0:T(8,128)(2,1)S(1)}, bf16[8,2,512,256]{3,2,1,0:T(8,128)(2,1)S(1)}) custom-call(s32[8]{0:T(128)S(1)} %get-tuple-element.417.slots_ref, bf16[4,128,512]{2,1,0:T(8,128)(2,1)S(1)} %pad_maximum_fusion.4.pooled_ref, bf16[4,128,512]{2,1,0:T(8,128)(2,1)S(1)} %pad_maximum_fusion.5.grads_ref, ...), custom_call_target="tpu_custom_call" | custom-call | flops 6442450944 | bytes 8388608 | tf_op jit(solution)/shard_map/pull_experts/pallas_call | solution.py:454
  258.2 7.2 %pull_slots.5 = (f32[4,1024,512]{2,1,0:T(8,128)}, bf16[4,1024,512]{2,1,0:T(8,128)(2,1)}, f32[4,512]{1,0:T(4,128)}, f32[512,512]{1,0:T(8,128)}, f32[8,512]{1,0:T(8,128)}) custom-call(s32[8]{0:T(128)} %copy-done.13, f32[1024,16]{1,0:T(8,128)} %bitcast.368, f32[1,128,16]{2,1,0:T(8,128)} %get-tuple-element.179.change_ref, bf16[4,1024,512]{2,1,0:T(8,128)(2,1)} %copy-done.2, ...), custom_call_target="tpu_custom_call" | custom-call | flops 2684354560 | bytes 10240 | tf_op jit(solution)/shard_map/pull_slots/pallas_call | solution.py:648
  265.5 6.1 %spread.6 = (bf16[4,1024,512]{2,1,0:T(8,128)(2,1)}, f32[2,128,16]{2,1,0:T(8,128)}) custom-call(s32[8]{0:T(128)} %copy-done.13, f32[1024,16]{1,0:T(8,128)} %bitcast.369, bf16[4,1024,512]{2,1,0:T(8,128)(2,1)} %bitcast.346, f32[4,1024,512]{2,1,0:T(8,128)} %get-tuple-element.171.hidden_ref, ...), custom_call_target="tpu_custom_call", output_to_operand_aliasing={{0}: (6, {})} | custom-call | flops 2621440000 | bytes 2621440 | tf_op jit(solution)/shard_map/spread/pallas_call | solution.py:525
  275.3 6.0 %collective-permute-done.62.rest_0_ = bf16[4,144,512]{2,1,0:T(8,128)(2,1)} collective-permute-done((bf16[4,144,512]{2,1,0:T(8,128)(2,1)S(1)}, bf16[4,144,512]{2,1,0:T(8,128)(2,1)}, u32[]{:S(2)}, u32[]{:S(2)}) %collective-permute-start.62) | collective-permute-done | bytes 589856 | tf_op jit(solution)/shard_map/ppermute | solution.py:775
  285.1 11.0 %pull_slots.6 = (f32[4,1024,512]{2,1,0:T(8,128)}, bf16[4,1024,512]{2,1,0:T(8,128)(2,1)}, f32[4,512]{1,0:T(4,128)}, f32[512,512]{1,0:T(8,128)}, f32[8,512]{1,0:T(8,128)}) custom-call(s32[8]{0:T(128)} %copy-done.13, f32[1024,16]{1,0:T(8,128)} %bitcast.370, ...), custom_call_target="tpu_custom_call", output_to_operand_aliasing={{0}: (12, {}), {1}: (13, {})} | custom-call | flops 5368709120 | bytes 10240 | tf_op jit(solution)/shard_map/pull_slots/pallas_call | solution.py:648
  296.1 6.1 %spread.7 = (bf16[4,1024,512]{2,1,0:T(8,128)(2,1)}, f32[2,128,16]{2,1,0:T(8,128)}) custom-call(s32[8]{0:T(128)} %copy-done.13, f32[1024,16]{1,0:T(8,128)} %bitcast.371, bf16[4,1024,512]{2,1,0:T(8,128)(2,1)} %bitcast.348, f32[4,1024,512]{2,1,0:T(8,128)} %get-tuple-element.171.hidden_ref, ...), custom_call_target="tpu_custom_call", output_to_operand_aliasing={{0}: (6, {})} | custom-call | flops 2621440000 | bytes 2621440 | tf_op jit(solution)/shard_map/spread/pallas_call | solution.py:525
  306.3 6.1 %spread.8 = (bf16[4,1024,512]{2,1,0:T(8,128)(2,1)}, f32[2,128,16]{2,1,0:T(8,128)}) custom-call(s32[8]{0:T(128)} %copy-done.13, f32[1024,16]{1,0:T(8,128)} %bitcast.372, bf16[4,1024,512]{2,1,0:T(8,128)(2,1)} %bitcast.349, f32[4,1024,512]{2,1,0:T(8,128)} %get-tuple-element.171.hidden_ref, ...), custom_call_target="tpu_custom_call", output_to_operand_aliasing={{0}: (6, {})} | custom-call | flops 2621440000 | bytes 2621440 | tf_op jit(solution)/shard_map/spread/pallas_call | solution.py:525
  320.2 11.0 %pull_slots.7 = (f32[4,1024,512]{2,1,0:T(8,128)}, bf16[4,1024,512]{2,1,0:T(8,128)(2,1)}, f32[4,512]{1,0:T(4,128)}, f32[512,512]{1,0:T(8,128)}, f32[8,512]{1,0:T(8,128)}) custom-call(s32[8]{0:T(128)} %copy-done.13, f32[1024,16]{1,0:T(8,128)} %bitcast.374, ...), custom_call_target="tpu_custom_call", output_to_operand_aliasing={{0}: (12, {}), {1}: (13, {})} | custom-call | flops 5368709120 | bytes 10240 | tf_op jit(solution)/shard_map/pull_slots/pallas_call | solution.py:648
  334.1 11.0 %pull_slots.8 = (f32[4,1024,512]{2,1,0:T(8,128)}, bf16[4,1024,512]{2,1,0:T(8,128)(2,1)}, f32[4,512]{1,0:T(4,128)}, f32[512,512]{1,0:T(8,128)}, f32[8,512]{1,0:T(8,128)}) custom-call(s32[8]{0:T(128)} %copy-done.13, f32[1024,16]{1,0:T(8,128)} %bitcast.375, ...), custom_call_target="tpu_custom_call", output_to_operand_aliasing={{0}: (12, {}), {1}: (13, {})} | custom-call | flops 5368709120 | bytes 10240 | tf_op jit(solution)/shard_map/pull_slots/pallas_call | solution.py:648
  345.1 7.5 %pull_slots.9 = (f32[4,1024,512]{2,1,0:T(8,128)}, bf16[4,1024,512]{2,1,0:T(8,128)(2,1)}, f32[4,512]{1,0:T(4,128)}, f32[512,512]{1,0:T(8,128)}, f32[8,512]{1,0:T(8,128)}) custom-call(s32[8]{0:T(128)} %copy-done.13, f32[1024,16]{1,0:T(8,128)} %bitcast.376, ...), custom_call_target="tpu_custom_call", output_to_operand_aliasing={{0}: (11, {}), {1}: (12, {})} | custom-call | tf_op jit(solution)/shard_map/pull_slots/pallas_call | solution.py:648
  354.9 23.9 %attend_back.2.rest_0_ = bf16[4,1024,1536]{2,1,0:T(8,128)(2,1)} custom-call(s32[4,8]{1,0:T(4,128)S(1)} %add_select_fusion.lo_ref, s32[4]{0:T(128)S(1)} %subtract_bitcast_fusion.vlen_ref, s32[4,8,128]{2,1,0:T(8,128)S(1)} %select_select_fusion.start_ref, bf16[4,1024,1536]{2,1,0:T(8,128)(2,1)} %join.1.joined_ref, bf16[4,1024,512]{2,1,0:T(8,128)(2,1)S(1)} %copy-done.6, ...), custom_call_target="tpu_custom_call" | custom-call | flops 4 | bytes 4096 | tf_op jit(solution)/shard_map/attend_back/pallas_call | solution.py:194
  387.2 25.4 %attend_back.3.grads_ref = bf16[4,1024,1536]{2,1,0:T(8,128)(2,1)} custom-call(s32[4,8]{1,0:T(4,128)S(1)} %add_select_fusion.lo_ref, s32[4]{0:T(128)S(1)} %subtract_bitcast_fusion.vlen_ref, s32[4,8,128]{2,1,0:T(8,128)S(1)} %select_select_fusion.start_ref, bf16[4,1024,1536]{2,1,0:T(8,128)(2,1)} %join.1.joined_ref, ...), custom_call_target="tpu_custom_call", output_to_operand_aliasing={{}: (7, {})} | custom-call | flops 67108864000 | bytes 4096 | tf_op jit(solution)/shard_map/attend_back/pallas_call | solution.py:194
  412.6 14.8 %project_grads.1 = bf16[512,2176]{1,0:T(8,128)(2,1)S(1)} custom-call(bf16[4,1024,1536]{2,1,0:T(8,128)(2,1)} %attend_back.3.grads_ref, bf16[4,1024,512]{2,1,0:T(8,128)(2,1)} %bitcast.380, f32[512,8]{1,0:T(8,128)S(1)} %get-tuple-element.404.gains_ref, bf16[512,2176]{1,0:T(8,128)(2,1)S(1)} %bitcast.364, f32[512,512]{1,0:T(8,128)S(1)} %copy-done.11, ...), custom_call_target="tpu_custom_call" | custom-call | flops 4 | bytes 4 | tf_op jit(solution)/shard_map/project_grads/pallas_call | solution.py:708
  435.6 16.1 %pull_tokens.1 = f32[4,1024,512]{2,1,0:T(8,128)} custom-call(bf16[4,1024,1536]{2,1,0:T(8,128)(2,1)} %attend_back.3.grads_ref, bf16[4,1024,512]{2,1,0:T(8,128)(2,1)} %bitcast.381, f32[4,1024,512]{2,1,0:T(8,128)} %get-tuple-element.259.hidden_ref, f32[8,512]{1,0:T(8,128)} %copy-done.12, bf16[512,2176]{1,0:T(8,128)(2,1)} %bitcast.363), custom_call_target="tpu_custom_call" | custom-call | flops 21474836480 | bytes 33554432 | tf_op jit(solution)/shard_map/pull_tokens/pallas_call | solution.py:740
  452.1 8.4 %collective-permute-done.80 = bf16[4,16,2176]{2,1,0:T(8,128)(2,1)S(1)} collective-permute-done((bf16[4,16,2176]{2,1,0:T(8,128)(2,1)S(1)}, bf16[4,16,2176]{2,1,0:T(8,128)(2,1)S(1)}, u32[]{:S(2)}, u32[]{:S(2)}) %collective-permute-start.80) | collective-permute-done | bytes 278560 | tf_op jit(solution)/shard_map/ppermute | solution.py:780
  (367 shorter events, 211.6 us)
Async XLA Ops:
  41.3 16.3 %collective-permute-start.6 = (bf16[2,512,256]{2,1,0:T(8,128)(2,1)S(1)}, bf16[2,512,256]{2,1,0:T(8,128)(2,1)}, u32[]{:S(2)}, u32[]{:S(2)}) collective-permute-start(bf16[2,512,256]{2,1,0:T(8,128)(2,1)S(1)} %pad_maximum_fusion.3), channel_id=1, source_target_pairs={{0,8},{8,16},{16,24},{24,28},{28,20},{20,12},{12,4},{4,0},{1,9},{9... | collective-permute-start | bytes 1572872 | tf_op jit(solution)/shard_map/ppermute | solution.py:775
  41.3 16.3 %collective-permute-start.7 = (bf16[2,512,256]{2,1,0:T(8,128)(2,1)S(1)}, bf16[2,512,256]{2,1,0:T(8,128)(2,1)}, u32[]{:S(2)}, u32[]{:S(2)}) collective-permute-start(bf16[2,512,256]{2,1,0:T(8,128)(2,1)S(1)} %pad_maximum_fusion.3), channel_id=1, source_target_pairs={{0,4},{8,0},{16,8},{24,16},{28,24},{20,28},{12,20},{4,12},{1,5},{9... | collective-permute-start | bytes 1572872 | tf_op jit(solution)/shard_map/ppermute | solution.py:775
  57.6 30.0 %collective-permute-start.8 = (bf16[2,512,256]{2,1,0:T(8,128)(2,1)}, bf16[2,512,256]{2,1,0:T(8,128)(2,1)S(1)}, u32[]{:S(2)}, u32[]{:S(2)}) collective-permute-start(bf16[2,512,256]{2,1,0:T(8,128)(2,1)} %collective-permute-done.6), channel_id=1, source_target_pairs={{0,8},{8,16},{16,24},{24,28},{28,20},{20,12},{12,4},{4,0},{1,9},{9... | collective-permute-start | bytes 1572872 | tf_op jit(solution)/shard_map/ppermute | solution.py:775
  57.7 29.9 %collective-permute-start.9 = (bf16[2,512,256]{2,1,0:T(8,128)(2,1)}, bf16[2,512,256]{2,1,0:T(8,128)(2,1)S(1)}, u32[]{:S(2)}, u32[]{:S(2)}) collective-permute-start(bf16[2,512,256]{2,1,0:T(8,128)(2,1)} %collective-permute-done.7), channel_id=1, source_target_pairs={{0,4},{8,0},{16,8},{24,16},{28,24},{20,28},{12,20},{4,12},{1,5},{9... | collective-permute-start | bytes 1572872 | tf_op jit(solution)/shard_map/ppermute | solution.py:775
  102.3 20.3 %collective-permute-start.12 = (bf16[1,512,256]{2,1,0:T(8,128)(2,1)S(1)}, bf16[1,512,256]{2,1,0:T(8,128)(2,1)S(1)}, u32[]{:S(2)}, u32[]{:S(2)}) collective-permute-start(bf16[1,512,256]{2,1,0:T(8,128)(2,1)S(1)} %slice.330), channel_id=1, source_target_pairs={{0,8},{8,16},{16,24},{24,28},{28,20},{20,12},{12,4},{4,0},{1,9},{9... | collective-permute-start | bytes 786440 | tf_op jit(solution)/shard_map/ppermute | solution.py:775
  104.1 18.5 %collective-permute-start.13 = (bf16[1,512,256]{2,1,0:T(8,128)(2,1)S(1)}, bf16[1,512,256]{2,1,0:T(8,128)(2,1)S(1)}, u32[]{:S(2)}, u32[]{:S(2)}) collective-permute-start(bf16[1,512,256]{2,1,0:T(8,128)(2,1)S(1)} %slice.331), channel_id=1, source_target_pairs={{0,4},{8,0},{16,8},{24,16},{28,24},{20,28},{12,20},{4,12},{1,5},{9... | collective-permute-start | bytes 786440 | tf_op jit(solution)/shard_map/ppermute | solution.py:775
  199.3 15.2 %collective-permute-start.41 = (bf16[2,128,512]{2,1,0:T(8,128)(2,1)S(1)}, bf16[2,128,512]{2,1,0:T(8,128)(2,1)S(1)}, u32[]{:S(2)}, u32[]{:S(2)}) collective-permute-start(bf16[2,128,512]{2,1,0:T(8,128)(2,1)S(1)} %get-tuple-element.344), channel_id=1, source_target_pairs={{0,8},{8,16},{16,24},{24,28},{28,20},{20,12},{12,4},{4,0},{1,9},{9... | collective-permute-start | bytes 786440 | tf_op jit(solution)/shard_map/ppermute | solution.py:775
  221.3 16.1 %collective-permute-start.58 = (bf16[4,128,512]{2,1,0:T(8,128)(2,1)S(1)}, bf16[4,128,512]{2,1,0:T(8,128)(2,1)}, u32[]{:S(2)}, u32[]{:S(2)}) collective-permute-start(bf16[4,128,512]{2,1,0:T(8,128)(2,1)S(1)} %pad_maximum_fusion.6.rest_0_), channel_id=1, source_target_pairs={{0,8},{8,16},{16,24},{24,28},{28,20},{20,12},{12,4},{4,0},{1,9},{9... | collective-permute-start | bytes 1572872 | tf_op jit(solution)/shard_map/ppermute | solution.py:775
  221.9 15.4 %collective-permute-start.59 = (bf16[4,128,512]{2,1,0:T(8,128)(2,1)S(1)}, bf16[4,128,512]{2,1,0:T(8,128)(2,1)}, u32[]{:S(2)}, u32[]{:S(2)}) collective-permute-start(bf16[4,128,512]{2,1,0:T(8,128)(2,1)S(1)} %pad_maximum_fusion.6.rest_0_), channel_id=1, source_target_pairs={{0,4},{8,0},{16,8},{24,16},{28,24},{20,28},{12,20},{4,12},{1,5},{9... | collective-permute-start | bytes 1572872 | tf_op jit(solution)/shard_map/ppermute | solution.py:775
  237.4 15.1 %collective-permute-start.60 = (bf16[4,128,512]{2,1,0:T(8,128)(2,1)}, bf16[4,128,512]{2,1,0:T(8,128)(2,1)S(1)}, u32[]{:S(2)}, u32[]{:S(2)}) collective-permute-start(bf16[4,128,512]{2,1,0:T(8,128)(2,1)} %collective-permute-done.58.rest_0_), channel_id=1, source_target_pairs={{0,8},{8,16},{16,24},{24,28},{28,20},{20,12},{12,4},{4,0},{1,9},{9... | collective-permute-start | bytes 1572872 | tf_op jit(solution)/shard_map/ppermute | solution.py:775
  238.1 15.4 %collective-permute-start.61 = (bf16[4,128,512]{2,1,0:T(8,128)(2,1)}, bf16[4,128,512]{2,1,0:T(8,128)(2,1)}, u32[]{:S(2)}, u32[]{:S(2)}) collective-permute-start(bf16[4,128,512]{2,1,0:T(8,128)(2,1)} %collective-permute-done.59.rest_1_), channel_id=1, source_target_pairs={{0,4},{8,0},{16,8},{24,16},{28,24},{20,28},{12,20},{4,12},{1,5},{9... | collective-permute-start | bytes 1572872 | tf_op jit(solution)/shard_map/ppermute | solution.py:775
  253.5 18.0 %collective-permute-start.64 = (bf16[4,128,512]{2,1,0:T(8,128)(2,1)}, bf16[4,128,512]{2,1,0:T(8,128)(2,1)S(1)}, u32[]{:S(2)}, u32[]{:S(2)}) collective-permute-start(bf16[4,128,512]{2,1,0:T(8,128)(2,1)} %copy-done.37), channel_id=1, source_target_pairs={{0,8},{8,16},{16,24},{24,28},{28,20},{20,12},{12,4},{4,0},{1,9},{9... | collective-permute-start | bytes 1572872 | tf_op jit(solution)/shard_map/ppermute | solution.py:775
  255.3 16.3 %collective-permute-start.65 = (bf16[4,128,512]{2,1,0:T(8,128)(2,1)}, bf16[4,128,512]{2,1,0:T(8,128)(2,1)}, u32[]{:S(2)}, u32[]{:S(2)}) collective-permute-start(bf16[4,128,512]{2,1,0:T(8,128)(2,1)} %collective-permute-done.61.rest_1_), channel_id=1, source_target_pairs={{0,4},{8,0},{16,8},{24,16},{28,24},{20,28},{12,20},{4,12},{1,5},{9... | collective-permute-start | bytes 1572872 | tf_op jit(solution)/shard_map/ppermute | solution.py:775
  255.6 25.7 %collective-permute-start.62 = (bf16[4,144,512]{2,1,0:T(8,128)(2,1)S(1)}, bf16[4,144,512]{2,1,0:T(8,128)(2,1)}, u32[]{:S(2)}, u32[]{:S(2)}) collective-permute-start(bf16[4,144,512]{2,1,0:T(8,128)(2,1)S(1)} %pad_maximum_fusion.1.rest_0_), channel_id=1, source_target_pairs={{0,8},{8,16},{16,24},{24,28},{28,20},{20,12},{12,4},{4,0},{1,9},{9... | collective-permute-start | bytes 1769480 | tf_op jit(solution)/shard_map/ppermute | solution.py:775
  257.3 25.8 %collective-permute-start.63 = (bf16[4,144,512]{2,1,0:T(8,128)(2,1)S(1)}, bf16[4,144,512]{2,1,0:T(8,128)(2,1)}, u32[]{:S(2)}, u32[]{:S(2)}) collective-permute-start(bf16[4,144,512]{2,1,0:T(8,128)(2,1)S(1)} %pad_maximum_fusion.1.rest_0_), channel_id=1, source_target_pairs={{0,4},{8,0},{16,8},{24,16},{28,24},{20,28},{12,20},{4,12},{1,5},{9... | collective-permute-start | bytes 1769480 | tf_op jit(solution)/shard_map/ppermute | solution.py:775
  271.6 30.6 %collective-permute-start.68 = (bf16[2,128,512]{2,1,0:T(8,128)(2,1)S(1)}, bf16[2,128,512]{2,1,0:T(8,128)(2,1)}, u32[]{:S(2)}, u32[]{:S(2)}) collective-permute-start(bf16[2,128,512]{2,1,0:T(8,128)(2,1)S(1)} %slice.385), channel_id=1, source_target_pairs={{0,8},{8,16},{16,24},{24,28},{28,20},{20,12},{12,4},{4,0},{1,9},{9... | collective-permute-start | bytes 786440 | tf_op jit(solution)/shard_map/ppermute | solution.py:775
  275.0 27.2 %collective-permute-start.69 = (bf16[2,128,512]{2,1,0:T(8,128)(2,1)}, bf16[2,128,512]{2,1,0:T(8,128)(2,1)}, u32[]{:S(2)}, u32[]{:S(2)}) collective-permute-start(bf16[2,128,512]{2,1,0:T(8,128)(2,1)} %slice.386), channel_id=1, source_target_pairs={{0,4},{8,0},{16,8},{24,16},{28,24},{20,28},{12,20},{4,12},{1,5},{9... | collective-permute-start | bytes 786440 | tf_op jit(solution)/shard_map/ppermute | solution.py:775
  283.1 19.1 %collective-permute-start.66 = (bf16[4,144,512]{2,1,0:T(8,128)(2,1)}, bf16[4,144,512]{2,1,0:T(8,128)(2,1)}, u32[]{:S(2)}, u32[]{:S(2)}) collective-permute-start(bf16[4,144,512]{2,1,0:T(8,128)(2,1)} %collective-permute-done.62.rest_0_), channel_id=1, source_target_pairs={{0,8},{8,16},{16,24},{24,28},{28,20},{20,12},{12,4},{4,0},{1,9},{9... | collective-permute-start | bytes 1769480 | tf_op jit(solution)/shard_map/ppermute | solution.py:775
  284.1 18.1 %collective-permute-start.67 = (bf16[4,144,512]{2,1,0:T(8,128)(2,1)}, bf16[4,144,512]{2,1,0:T(8,128)(2,1)}, u32[]{:S(2)}, u32[]{:S(2)}) collective-permute-start(bf16[4,144,512]{2,1,0:T(8,128)(2,1)} %collective-permute-done.63.rest_1_), channel_id=1, source_target_pairs={{0,4},{8,0},{16,8},{24,16},{28,24},{20,28},{12,20},{4,12},{1,5},{9... | collective-permute-start | bytes 1769480 | tf_op jit(solution)/shard_map/ppermute | solution.py:775
  333.7 46.1 %collective-permute-start.74 = (bf16[4,2,512,256]{3,2,1,0:T(8,128)(2,1)}, bf16[4,2,512,256]{3,2,1,0:T(8,128)(2,1)S(1)}, u32[]{:S(2)}, u32[]{:S(2)}) collective-permute-start(bf16[4,2,512,256]{3,2,1,0:T(8,128)(2,1)} %slice.389), channel_id=1, source_target_pairs={{0,4},{4,0},{8,12},{12,8},{16,20},{20,16},{24,28},{28,24},{1,5},{5... | collective-permute-start | bytes 6291464 | tf_op jit(solution)/shard_map/ppermute | solution.py:780
  382.2 45.2 %collective-permute-start.75 = (bf16[2,512,256]{2,1,0:T(8,128)(2,1)S(1)}, bf16[2,512,256]{2,1,0:T(8,128)(2,1)S(1)}, u32[]{:S(2)}, u32[]{:S(2)}) collective-permute-start(bf16[2,512,256]{2,1,0:T(8,128)(2,1)S(1)} %get-tuple-element.378), channel_id=1, source_target_pairs={{0,8},{4,12},{8,16},{12,20},{16,24},{20,28},{24,0},{28,4},{1,9},{5... | collective-permute-start | bytes 1572872 | tf_op jit(solution)/shard_map/ppermute | solution.py:785
  384.5 42.9 %collective-permute-start.76 = (bf16[2,512,256]{2,1,0:T(8,128)(2,1)S(1)}, bf16[2,512,256]{2,1,0:T(8,128)(2,1)S(1)}, u32[]{:S(2)}, u32[]{:S(2)}) collective-permute-start(bf16[2,512,256]{2,1,0:T(8,128)(2,1)S(1)} %get-tuple-element.377), channel_id=1, source_target_pairs={{0,16},{4,20},{8,24},{12,28},{16,0},{20,4},{24,8},{28,12},{1,17},{... | collective-permute-start | bytes 1572872 | tf_op jit(solution)/shard_map/ppermute | solution.py:785
  385.8 41.6 %collective-permute-start.77 = (bf16[2,512,256]{2,1,0:T(8,128)(2,1)S(1)}, bf16[2,512,256]{2,1,0:T(8,128)(2,1)S(1)}, u32[]{:S(2)}, u32[]{:S(2)}) collective-permute-start(bf16[2,512,256]{2,1,0:T(8,128)(2,1)S(1)} %get-tuple-element.376), channel_id=1, source_target_pairs={{0,24},{4,28},{8,0},{12,4},{16,8},{20,12},{24,16},{28,20},{1,25},{... | collective-permute-start | bytes 1572872 | tf_op jit(solution)/shard_map/ppermute | solution.py:785
  432.7 19.0 %collective-permute-start.79 = (bf16[4,2,16,2176]{3,2,1,0:T(8,128)(2,1)S(1)}, bf16[4,2,16,2176]{3,2,1,0:T(8,128)(2,1)S(1)}, u32[]{:S(2)}, u32[]{:S(2)}) collective-permute-start(bf16[4,2,16,2176]{3,2,1,0:T(8,128)(2,1)S(1)} %select_bitcast_fusion.3), channel_id=1, source_target_pairs={{0,2},{1,3},{2,0},{3,1},{4,6},{5,7},{6,4},{7,5},{8,10},{9,11},{10,... | collective-permute-start | bytes 1671176 | tf_op jit(solution)/shard_map/ppermute | solution.py:780
  (102 other events, 1286.8 us)

commit v7 on v6

--- a/solution.py
+++ b/solution.py
@@ -213,7 +213,7 @@
         ),
         out_shape=jax.ShapeDtypeStruct(joined.shape, BF16),
         input_output_aliases={7: 0} if aliased else {},
-        compiler_params=pltpu.CompilerParams(vmem_limit_bytes=48 << 20),
+        compiler_params=pltpu.CompilerParams(vmem_limit_bytes=58 << 20),
         cost_estimate=pl.CostEstimate(
             flops=row_to * length * 400 * 8 * 256 * 20 if aliased else rows,
             bytes_accessed=rows * length,
@@ -719,7 +719,7 @@
         out_specs=constant_spec(packed.shape),
         out_shape=jax.ShapeDtypeStruct(packed.shape, BF16),
         scratch_shapes=[pltpu.VMEM((width, wide), F32), pltpu.VMEM((8, wide), F32)],
-        compiler_params=pltpu.CompilerParams(vmem_limit_bytes=48 << 20),
+        compiler_params=pltpu.CompilerParams(vmem_limit_bytes=58 << 20),
         cost_estimate=pl.CostEstimate(flops=rows, bytes_accessed=rows, transcendentals=0),
         name="project_grads",
     )(grads, tokens, gains, packed, project, late)
@@ -1042,7 +1042,7 @@
             if step == 1:
                 second.after(*groups[2].values())
         if first.left():
-            found, work = first.step(*work)
+            found, _ = first.step()
             groups.append(found)
         if second.left() and step > 0:
             found, work = second.step(*work)
@@ -1050,11 +1050,11 @@
         if step < turns:
             out, *work = work
         pulled = work or pulled
-    pulled = pull(arrived[turns - 1], changes[turns - 1], pulled)
-    layer_out = out
     grad_weights, *_ = together(grad_weights, *arrived[turns].values())
     if pair == 2:
         came = flip(grad_weights[lines:], 1, "dp")
+    pulled = pull(arrived[turns - 1], changes[turns - 1], pulled, 0)
+    layer_out = out
     pulled = pull(arrived[turns], changes[turns], pulled, 0)
     grad_hidden, grad_attended, router_grad, grad_proj_out, sums_two = pulled
     split = rows - max(1, rows // 2)

time: 481 us -> 485 us (level)
  Pallas kernels: 228 us -> 233 us
  transfers between devices with their start and end apart: 84 -> 84, of which waited for: 49 -> 48; matrix products, arithmetic and copies ran while one was open for 5% -> 4% of each run, Pallas kernels for 48% -> 49%
where the time goes in v7:
time: 485 us; the launch traced here: 476 us
  Pallas kernels  233 us (48%)
  waiting for transfers between devices  102 us (21%)
  starting transfers between devices  91 us (19%)
  local copies, waits for them, and re-layouts  26.4 us (5%)
  other arithmetic  19.3 us (4%)
    ppermute x52, starting transfers between devices, shift(): lax.ppermute(value, 'dp', [(order[i], order[(i + step) % count]) for i in...  54.3 us
    pallas_call x2, Pallas kernels, attn_bwd(): pl.pallas_call(functools.partial(attn_bwd_kernel, width, row_from, batch,...  51.1 us
    ppermute x52, waiting for transfers between devices, shift(): lax.ppermute(value, 'dp', [(order[i], order[(i + step) % count]) for i in...  48.2 us
    pallas_call x5, Pallas kernels, pull_slots(): pl.pallas_call(functools.partial(pull_kernel, held is None, len(parts)),...  47.8 us
    ppermute x20, waiting for transfers between devices, flip(): return lax.ppermute(value, axis, [(i, i ^ bit) for i in range(count)])  46.2 us
    pallas_call x1, Pallas kernels, attn_fwd(): pl.pallas_call(functools.partial(attn_fwd_kernel, width, batch, count), g...  28.3 us
    pallas_call x5, Pallas kernels, spread_tokens(): pl.pallas_call(functools.partial(spread_kernel, group, len(parts)), grid_...  26.6 us
    ppermute x20, starting transfers between devices, flip(): return lax.ppermute(value, axis, [(i, i ^ bit) for i in range(count)])  18.7 us
  transfers between devices with their start and end apart: 84, of which 48 were waited for; matrix products, arithmetic and copies ran while one was open for 4% of the time, Pallas kernels for 49%

profile of v7, /device:TPU:0, one launch (start us, length us, event | category | flops | bytes accessed | tf_op | source)
XLA Modules:
  0.0 476.1 jit_solution(16125941360618280373)
XLA Ops:
  2.4 5.0 %collective-permute-start = (bf16[16,2176]{1,0:T(8,128)(2,1)S(1)}, bf16[16,2176]{1,0:T(8,128)(2,1)S(1)}, u32[]{:S(2)}, u32[]{:S(2)}) collective-permute-start(bf16[16,2176]{1,0:T(8,128)(2,1)S(1)} %fusion.40), channel_id=1, source_target_pairs={{0,24},{4,28},{8,0},{12,4},{16,8},{20,12},{24,16},{28,20},{1,25},{... | collective-permute-start | bytes 208904 | tf_op jit(solution)/shard_map/ppermute | solution.py:785
  15.8 7.0 %collective-permute-done.3 = bf16[4,16,2176]{2,1,0:T(8,128)(2,1)S(1)} collective-permute-done((bf16[4,16,2176]{2,1,0:T(8,128)(2,1)S(1)}, bf16[4,16,2176]{2,1,0:T(8,128)(2,1)S(1)}, u32[]{:S(2)}, u32[]{:S(2)}) %collective-permute-start.3) | collective-permute-done | bytes 278560 | tf_op jit(solution)/shard_map/ppermute | solution.py:780
  26.8 9.8 %collective-permute-done.4 = bf16[8,1,16,2176]{3,2,0,1:T(8,128)(2,1)S(1)} collective-permute-done((bf16[8,1,16,2176]{3,2,0,1:T(8,128)(2,1)S(1)}, bf16[8,1,16,2176]{3,2,0,1:T(8,128)(2,1)S(1)}, u32[]{:S(2)}, u32[]{:S(2)}) %collective-permute-start.4) | collective-permute-done | bytes 557088 | tf_op jit(solution)/shard_map/ppermute | solution.py:780
  46.7 10.1 %join.1.joined_ref = bf16[4,1024,1536]{2,1,0:T(8,128)(2,1)} custom-call(bf16[4,1024,512]{2,1,0:T(8,128)(2,1)S(1)} %bitcast.380, f32[8,512]{1,0:T(8,128)S(1)} %copy.150.gains_ref, bf16[512,2176]{1,0:T(8,128)(2,1)S(1)} %bitcast.356), custom_call_target="tpu_custom_call" | custom-call | flops 6442450944 | bytes 16777216 | tf_op jit(solution)/shard_map/join/pallas_call | solution.py:261
  58.9 28.3 %attend.1 = (bf16[4,1024,512]{2,1,0:T(8,128)(2,1)S(1)}, f32[4,8,8,128]{3,2,1,0:T(8,128)S(1)}) custom-call(s32[4,8]{1,0:T(4,128)S(1)} %add_select_fusion.lo_ref, s32[4]{0:T(128)S(1)} %subtract_bitcast_fusion.vlen_ref, s32[4,8,128]{2,1,0:T(8,128)S(1)} %select_select_fusion.start_ref, bf16[4,1024,1536]{2,1,0:T(8,128)(2,1)} %join.1.joined_ref), custom_call_target="tpu_custom_call" | custom-call | flops 13421772800 | bytes 12582912 | tf_op jit(solution)/shard_map/attend/pallas_call | solution.py:100
  90.2 7.5 %mix.1 = (f32[4,1024,512]{2,1,0:T(8,128)}, bf16[4,1024,512]{2,1,0:T(8,128)(2,1)S(1)}, f32[4,16,1024]{2,1,0:T(8,128)S(1)}) custom-call(bf16[4,1024,512]{2,1,0:T(8,128)(2,1)S(1)} %get-tuple-element.138.attended_ref, bf16[4,1024,512]{2,1,0:T(8,128)(2,1)} %bitcast.377, f32[8,512]{1,0:T(8,128)S(1)} %copy.150.gains_ref, bf16[512,2176]{1,0:T(8,128)(2,1)S(1)} %bitcast.357, ...), custom_call_target="tpu_custom_call" | custom-call | flops 2147483648 | bytes 20971520 | tf_op jit(solution)/shard_map/mix/pallas_call | solution.py:291
  116.6 4.4 pool.2
  123.2 4.6 pool.3
  203.4 7.8 %experts.1 = (bf16[4,128,512]{2,1,0:T(8,128)(2,1)S(1)}, bf16[8,512,256]{2,1,0:T(8,128)(2,1)S(1)}, f32[8,512,256]{2,1,0:T(8,128)S(1)}) custom-call(bf16[4,128,512]{2,1,0:T(8,128)(2,1)S(1)} %pad_maximum_fusion.4.pooled_ref, bf16[8,2,512,256]{3,2,1,0:T(8,128)(2,1)S(1)} %bitcast_dynamic-update-slice_fusion.weights_ref), custom_call_target="tpu_custom_call" | custom-call | flops 4294967296 | bytes 8388608 | tf_op jit(solution)/shard_map/experts/pallas_call | solution.py:389
  225.0 11.2 %pull_experts.1 = (bf16[4,144,512]{2,1,0:T(8,128)(2,1)S(1)}, bf16[8,2,512,256]{3,2,1,0:T(8,128)(2,1)S(1)}) custom-call(s32[8]{0:T(128)S(1)} %get-tuple-element.391.slots_ref, bf16[4,128,512]{2,1,0:T(8,128)(2,1)S(1)} %pad_maximum_fusion.4.pooled_ref, bf16[4,128,512]{2,1,0:T(8,128)(2,1)S(1)} %pad_maximum_fusion.5.grads_ref, ...), custom_call_target="tpu_custom_call" | custom-call | flops 6442450944 | bytes 8388608 | tf_op jit(solution)/shard_map/pull_experts/pallas_call | solution.py:454
  261.3 7.2 %pull_slots.5 = (f32[4,1024,512]{2,1,0:T(8,128)}, bf16[4,1024,512]{2,1,0:T(8,128)(2,1)}, f32[4,512]{1,0:T(4,128)}, f32[512,512]{1,0:T(8,128)}, f32[8,512]{1,0:T(8,128)}) custom-call(s32[8]{0:T(128)} %copy-done.11, f32[1024,16]{1,0:T(8,128)} %bitcast.368, f32[1,128,16]{2,1,0:T(8,128)} %get-tuple-element.165.change_ref, bf16[4,1024,512]{2,1,0:T(8,128)(2,1)} %copy-done.2, ...), custom_call_target="tpu_custom_call" | custom-call | flops 2684354560 | bytes 10240 | tf_op jit(solution)/shard_map/pull_slots/pallas_call | solution.py:648
  268.5 6.1 %spread.6 = (bf16[4,1024,512]{2,1,0:T(8,128)(2,1)}, f32[2,128,16]{2,1,0:T(8,128)}) custom-call(s32[8]{0:T(128)} %copy-done.11, f32[1024,16]{1,0:T(8,128)} %bitcast.369, bf16[4,1024,512]{2,1,0:T(8,128)(2,1)} %bitcast.346, f32[4,1024,512]{2,1,0:T(8,128)} %get-tuple-element.162.hidden_ref, ...), custom_call_target="tpu_custom_call", output_to_operand_aliasing={{0}: (6, {})} | custom-call | flops 2621440000 | bytes 2621440 | tf_op jit(solution)/shard_map/spread/pallas_call | solution.py:525
  284.2 11.0 %pull_slots.6 = (f32[4,1024,512]{2,1,0:T(8,128)}, bf16[4,1024,512]{2,1,0:T(8,128)(2,1)}, f32[4,512]{1,0:T(4,128)}, f32[512,512]{1,0:T(8,128)}, f32[8,512]{1,0:T(8,128)}) custom-call(s32[8]{0:T(128)} %copy-done.11, f32[1024,16]{1,0:T(8,128)} %bitcast.370, ...), custom_call_target="tpu_custom_call", output_to_operand_aliasing={{0}: (12, {}), {1}: (13, {})} | custom-call | flops 5368709120 | bytes 10240 | tf_op jit(solution)/shard_map/pull_slots/pallas_call | solution.py:648
  295.2 6.1 %spread.7 = (bf16[4,1024,512]{2,1,0:T(8,128)(2,1)}, f32[2,128,16]{2,1,0:T(8,128)}) custom-call(s32[8]{0:T(128)} %copy-done.11, f32[1024,16]{1,0:T(8,128)} %bitcast.371, bf16[4,1024,512]{2,1,0:T(8,128)(2,1)} %bitcast.348, f32[4,1024,512]{2,1,0:T(8,128)} %get-tuple-element.162.hidden_ref, ...), custom_call_target="tpu_custom_call", output_to_operand_aliasing={{0}: (6, {})} | custom-call | flops 2621440000 | bytes 2621440 | tf_op jit(solution)/shard_map/spread/pallas_call | solution.py:525
  305.4 6.1 %spread.8 = (bf16[4,1024,512]{2,1,0:T(8,128)(2,1)}, f32[2,128,16]{2,1,0:T(8,128)}) custom-call(s32[8]{0:T(128)} %copy-done.11, f32[1024,16]{1,0:T(8,128)} %bitcast.372, bf16[4,1024,512]{2,1,0:T(8,128)(2,1)} %bitcast.349, f32[4,1024,512]{2,1,0:T(8,128)} %get-tuple-element.162.hidden_ref, ...), custom_call_target="tpu_custom_call", output_to_operand_aliasing={{0}: (6, {})} | custom-call | flops 2621440000 | bytes 2621440 | tf_op jit(solution)/shard_map/spread/pallas_call | solution.py:525
  319.2 11.0 %pull_slots.7 = (f32[4,1024,512]{2,1,0:T(8,128)}, bf16[4,1024,512]{2,1,0:T(8,128)(2,1)}, f32[4,512]{1,0:T(4,128)}, f32[512,512]{1,0:T(8,128)}, f32[8,512]{1,0:T(8,128)}) custom-call(s32[8]{0:T(128)} %copy-done.11, f32[1024,16]{1,0:T(8,128)} %bitcast.374, ...), custom_call_target="tpu_custom_call", output_to_operand_aliasing={{0}: (12, {}), {1}: (13, {})} | custom-call | flops 5368709120 | bytes 10240 | tf_op jit(solution)/shard_map/pull_slots/pallas_call | solution.py:648
  333.3 11.0 %pull_slots.8 = (f32[4,1024,512]{2,1,0:T(8,128)}, bf16[4,1024,512]{2,1,0:T(8,128)(2,1)}, f32[4,512]{1,0:T(4,128)}, f32[512,512]{1,0:T(8,128)}, f32[8,512]{1,0:T(8,128)}) custom-call(s32[8]{0:T(128)} %copy-done.11, f32[1024,16]{1,0:T(8,128)} %bitcast.375, ...), custom_call_target="tpu_custom_call", output_to_operand_aliasing={{0}: (12, {}), {1}: (13, {})} | custom-call | tf_op jit(solution)/shard_map/pull_slots/pallas_call | solution.py:648
  344.3 7.5 %pull_slots.9 = (f32[4,1024,512]{2,1,0:T(8,128)}, bf16[4,1024,512]{2,1,0:T(8,128)(2,1)}, f32[4,512]{1,0:T(4,128)}, f32[512,512]{1,0:T(8,128)}, f32[8,512]{1,0:T(8,128)}) custom-call(s32[8]{0:T(128)} %copy-done.11, f32[1024,16]{1,0:T(8,128)} %bitcast.376, ...), custom_call_target="tpu_custom_call", output_to_operand_aliasing={{0}: (11, {}), {1}: (12, {})} | custom-call | tf_op jit(solution)/shard_map/pull_slots/pallas_call | solution.py:648
  351.8 24.5 %attend_back.2.rest_0_ = bf16[4,1024,1536]{2,1,0:T(8,128)(2,1)} custom-call(s32[4,8]{1,0:T(4,128)} %copy-done.14, s32[4]{0:T(128)} %copy-done.15, s32[4,8,128]{2,1,0:T(8,128)} %copy-done.9, bf16[4,1024,1536]{2,1,0:T(8,128)(2,1)} %join.1.joined_ref, bf16[4,1024,512]{2,1,0:T(8,128)(2,1)} %get-tuple-element.223.grad_ref, bf16[4,1024,512]{2,1,0:T(8,128)(2,1)} %copy-done.1, ...), custom_call_target="tpu_custom_call" | custom-call | flops 4 | bytes 4096 | tf_op jit(solution)/shard_map/attend_back/pallas_call | solution.py:194
  385.5 26.6 %attend_back.3.grads_ref = bf16[4,1024,1536]{2,1,0:T(8,128)(2,1)} custom-call(s32[4,8]{1,0:T(4,128)} %copy-done.14, s32[4]{0:T(128)} %copy-done.15, s32[4,8,128]{2,1,0:T(8,128)} %copy-done.9, bf16[4,1024,1536]{2,1,0:T(8,128)(2,1)} %join.1.joined_ref, bf16[4,1024,512]{2,1,0:T(8,128)(2,1)} %get-tuple-element.223.grad_ref, ...), custom_call_target="tpu_custom_call", output_to_operand_aliasing={{}: (7, {})} | custom-call | flops 67108864000 | bytes 4096 | tf_op jit(solution)/shard_map/attend_back/pallas_call | solution.py:194
  412.1 17.0 %project_grads.1 = bf16[512,2176]{1,0:T(8,128)(2,1)} custom-call(bf16[4,1024,1536]{2,1,0:T(8,128)(2,1)} %attend_back.3.grads_ref, bf16[4,1024,512]{2,1,0:T(8,128)(2,1)} %bitcast.378, f32[512,8]{1,0:T(8,128)} %get-tuple-element.378.gains_ref, bf16[512,2176]{1,0:T(8,128)(2,1)} %bitcast.363, f32[512,512]{1,0:T(8,128)} %get-tuple-element.228.project_ref, ...), custom_call_target="tpu_custom_call" | custom-call | flops 4 | bytes 4 | tf_op jit(solution)/shard_map/project_grads/pallas_call | solution.py:708
  436.6 16.1 %pull_tokens.1 = f32[4,1024,512]{2,1,0:T(8,128)} custom-call(bf16[4,1024,1536]{2,1,0:T(8,128)(2,1)} %attend_back.3.grads_ref, bf16[4,1024,512]{2,1,0:T(8,128)(2,1)} %bitcast.379, f32[4,1024,512]{2,1,0:T(8,128)} %get-tuple-element.233.hidden_ref, f32[8,512]{1,0:T(8,128)} %copy-done.8, bf16[512,2176]{1,0:T(8,128)(2,1)} %bitcast.364), custom_call_target="tpu_custom_call" | custom-call | flops 21474836480 | bytes 33554432 | tf_op jit(solution)/shard_map/pull_tokens/pallas_call | solution.py:740
  453.0 4.9 %collective-permute-start.80 = (bf16[4,16,2176]{2,1,0:T(8,128)(2,1)S(1)}, bf16[4,16,2176]{2,1,0:T(8,128)(2,1)S(1)}, u32[]{:S(2)}, u32[]{:S(2)}) collective-permute-start(bf16[4,16,2176]{2,1,0:T(8,128)(2,1)S(1)} %select_bitcast_fusion.6), channel_id=1, source_target_pairs={{0,4},{4,0},{8,12},{12,8},{16,20},{20,16},{24,28},{28,24},{1,5},{5... | collective-permute-start | bytes 835592 | tf_op jit(solution)/shard_map/ppermute | solution.py:780
  457.9 6.7 %collective-permute-done.80 = bf16[4,16,2176]{2,1,0:T(8,128)(2,1)S(1)} collective-permute-done((bf16[4,16,2176]{2,1,0:T(8,128)(2,1)S(1)}, bf16[4,16,2176]{2,1,0:T(8,128)(2,1)S(1)}, u32[]{:S(2)}, u32[]{:S(2)}) %collective-permute-start.80) | collective-permute-done | bytes 278560 | tf_op jit(solution)/shard_map/ppermute | solution.py:780
  (367 shorter events, 213.5 us)
Async XLA Ops:
  41.3 15.6 %collective-permute-start.6 = (bf16[2,512,256]{2,1,0:T(8,128)(2,1)S(1)}, bf16[2,512,256]{2,1,0:T(8,128)(2,1)}, u32[]{:S(2)}, u32[]{:S(2)}) collective-permute-start(bf16[2,512,256]{2,1,0:T(8,128)(2,1)S(1)} %pad_maximum_fusion.3), channel_id=1, source_target_pairs={{0,8},{8,16},{16,24},{24,28},{28,20},{20,12},{12,4},{4,0},{1,9},{9... | collective-permute-start | bytes 1572872 | tf_op jit(solution)/shard_map/ppermute | solution.py:775
  41.3 15.5 %collective-permute-start.7 = (bf16[2,512,256]{2,1,0:T(8,128)(2,1)S(1)}, bf16[2,512,256]{2,1,0:T(8,128)(2,1)}, u32[]{:S(2)}, u32[]{:S(2)}) collective-permute-start(bf16[2,512,256]{2,1,0:T(8,128)(2,1)S(1)} %pad_maximum_fusion.3), channel_id=1, source_target_pairs={{0,4},{8,0},{16,8},{24,16},{28,24},{20,28},{12,20},{4,12},{1,5},{9... | collective-permute-start | bytes 1572872 | tf_op jit(solution)/shard_map/ppermute | solution.py:775
  56.8 30.4 %collective-permute-start.8 = (bf16[2,512,256]{2,1,0:T(8,128)(2,1)}, bf16[2,512,256]{2,1,0:T(8,128)(2,1)S(1)}, u32[]{:S(2)}, u32[]{:S(2)}) collective-permute-start(bf16[2,512,256]{2,1,0:T(8,128)(2,1)} %collective-permute-done.6), channel_id=1, source_target_pairs={{0,8},{8,16},{16,24},{24,28},{28,20},{20,12},{12,4},{4,0},{1,9},{9... | collective-permute-start | bytes 1572872 | tf_op jit(solution)/shard_map/ppermute | solution.py:775
  56.9 30.4 %collective-permute-start.9 = (bf16[2,512,256]{2,1,0:T(8,128)(2,1)}, bf16[2,512,256]{2,1,0:T(8,128)(2,1)S(1)}, u32[]{:S(2)}, u32[]{:S(2)}) collective-permute-start(bf16[2,512,256]{2,1,0:T(8,128)(2,1)} %collective-permute-done.7), channel_id=1, source_target_pairs={{0,4},{8,0},{16,8},{24,16},{28,24},{20,28},{12,20},{4,12},{1,5},{9... | collective-permute-start | bytes 1572872 | tf_op jit(solution)/shard_map/ppermute | solution.py:775
  101.1 19.9 %collective-permute-start.12 = (bf16[1,512,256]{2,1,0:T(8,128)(2,1)S(1)}, bf16[1,512,256]{2,1,0:T(8,128)(2,1)S(1)}, u32[]{:S(2)}, u32[]{:S(2)}) collective-permute-start(bf16[1,512,256]{2,1,0:T(8,128)(2,1)S(1)} %slice.330), channel_id=1, source_target_pairs={{0,8},{8,16},{16,24},{24,28},{28,20},{20,12},{12,4},{4,0},{1,9},{9... | collective-permute-start | bytes 786440 | tf_op jit(solution)/shard_map/ppermute | solution.py:775
  102.4 18.6 %collective-permute-start.13 = (bf16[1,512,256]{2,1,0:T(8,128)(2,1)S(1)}, bf16[1,512,256]{2,1,0:T(8,128)(2,1)S(1)}, u32[]{:S(2)}, u32[]{:S(2)}) collective-permute-start(bf16[1,512,256]{2,1,0:T(8,128)(2,1)S(1)} %slice.331), channel_id=1, source_target_pairs={{0,4},{8,0},{16,8},{24,16},{28,24},{20,28},{12,20},{4,12},{1,5},{9... | collective-permute-start | bytes 786440 | tf_op jit(solution)/shard_map/ppermute | solution.py:775
  198.4 14.8 %collective-permute-start.41 = (bf16[2,128,512]{2,1,0:T(8,128)(2,1)S(1)}, bf16[2,128,512]{2,1,0:T(8,128)(2,1)S(1)}, u32[]{:S(2)}, u32[]{:S(2)}) collective-permute-start(bf16[2,128,512]{2,1,0:T(8,128)(2,1)S(1)} %get-tuple-element.318), channel_id=1, source_target_pairs={{0,8},{8,16},{16,24},{24,28},{28,20},{20,12},{12,4},{4,0},{1,9},{9... | collective-permute-start | bytes 786440 | tf_op jit(solution)/shard_map/ppermute | solution.py:775
  219.8 16.4 %collective-permute-start.58 = (bf16[4,128,512]{2,1,0:T(8,128)(2,1)S(1)}, bf16[4,128,512]{2,1,0:T(8,128)(2,1)S(1)}, u32[]{:S(2)}, u32[]{:S(2)}) collective-permute-start(bf16[4,128,512]{2,1,0:T(8,128)(2,1)S(1)} %pad_maximum_fusion.6.rest_0_), channel_id=1, source_target_pairs={{0,8},{8,16},{16,24},{24,28},{28,20},{20,12},{12,4},{4,0},{1,9},{9... | collective-permute-start | bytes 1572872 | tf_op jit(solution)/shard_map/ppermute | solution.py:775
  221.7 14.6 %collective-permute-start.59 = (bf16[4,128,512]{2,1,0:T(8,128)(2,1)S(1)}, bf16[4,128,512]{2,1,0:T(8,128)(2,1)S(1)}, u32[]{:S(2)}, u32[]{:S(2)}) collective-permute-start(bf16[4,128,512]{2,1,0:T(8,128)(2,1)S(1)} %pad_maximum_fusion.6.rest_0_), channel_id=1, source_target_pairs={{0,4},{8,0},{16,8},{24,16},{28,24},{20,28},{12,20},{4,12},{1,5},{9... | collective-permute-start | bytes 1572872 | tf_op jit(solution)/shard_map/ppermute | solution.py:775
  236.3 14.9 %collective-permute-start.60 = (bf16[4,128,512]{2,1,0:T(8,128)(2,1)S(1)}, bf16[4,128,512]{2,1,0:T(8,128)(2,1)}, u32[]{:S(2)}, u32[]{:S(2)}) collective-permute-start(bf16[4,128,512]{2,1,0:T(8,128)(2,1)S(1)} %collective-permute-done.58.rest_0_), channel_id=1, source_target_pairs={{0,8},{8,16},{16,24},{24,28},{28,20},{20,12},{12,4},{4,0},{1,9},{9... | collective-permute-start | bytes 1572872 | tf_op jit(solution)/shard_map/ppermute | solution.py:775
  238.2 14.5 %collective-permute-start.61 = (bf16[4,128,512]{2,1,0:T(8,128)(2,1)S(1)}, bf16[4,128,512]{2,1,0:T(8,128)(2,1)}, u32[]{:S(2)}, u32[]{:S(2)}) collective-permute-start(bf16[4,128,512]{2,1,0:T(8,128)(2,1)S(1)} %collective-permute-done.59.rest_1_), channel_id=1, source_target_pairs={{0,4},{8,0},{16,8},{24,16},{28,24},{20,28},{12,20},{4,12},{1,5},{9... | collective-permute-start | bytes 1572872 | tf_op jit(solution)/shard_map/ppermute | solution.py:775
  252.7 21.9 %collective-permute-start.68 = (bf16[4,128,512]{2,1,0:T(8,128)(2,1)}, bf16[4,128,512]{2,1,0:T(8,128)(2,1)S(1)}, u32[]{:S(2)}, u32[]{:S(2)}) collective-permute-start(bf16[4,128,512]{2,1,0:T(8,128)(2,1)} %collective-permute-done.60.rest_0_), channel_id=1, source_target_pairs={{0,8},{8,16},{16,24},{24,28},{28,20},{20,12},{12,4},{4,0},{1,9},{9... | collective-permute-start | bytes 1572872 | tf_op jit(solution)/shard_map/ppermute | solution.py:775
  254.4 20.2 %collective-permute-start.69 = (bf16[4,128,512]{2,1,0:T(8,128)(2,1)}, bf16[4,128,512]{2,1,0:T(8,128)(2,1)S(1)}, u32[]{:S(2)}, u32[]{:S(2)}) collective-permute-start(bf16[4,128,512]{2,1,0:T(8,128)(2,1)} %collective-permute-done.61.rest_1_), channel_id=1, source_target_pairs={{0,4},{8,0},{16,8},{24,16},{28,24},{20,28},{12,20},{4,12},{1,5},{9... | collective-permute-start | bytes 1572872 | tf_op jit(solution)/shard_map/ppermute | solution.py:775
  254.7 25.7 %collective-permute-start.62 = (bf16[4,144,512]{2,1,0:T(8,128)(2,1)S(1)}, bf16[4,144,512]{2,1,0:T(8,128)(2,1)}, u32[]{:S(2)}, u32[]{:S(2)}) collective-permute-start(bf16[4,144,512]{2,1,0:T(8,128)(2,1)S(1)} %pad_maximum_fusion.1.rest_0_), channel_id=1, source_target_pairs={{0,8},{8,16},{16,24},{24,28},{28,20},{20,12},{12,4},{4,0},{1,9},{9... | collective-permute-start | bytes 1769480 | tf_op jit(solution)/shard_map/ppermute | solution.py:775
  256.4 25.8 %collective-permute-start.63 = (bf16[4,144,512]{2,1,0:T(8,128)(2,1)S(1)}, bf16[4,144,512]{2,1,0:T(8,128)(2,1)}, u32[]{:S(2)}, u32[]{:S(2)}) collective-permute-start(bf16[4,144,512]{2,1,0:T(8,128)(2,1)S(1)} %pad_maximum_fusion.1.rest_0_), channel_id=1, source_target_pairs={{0,4},{8,0},{16,8},{24,16},{28,24},{20,28},{12,20},{4,12},{1,5},{9... | collective-permute-start | bytes 1769480 | tf_op jit(solution)/shard_map/ppermute | solution.py:775
  274.6 28.9 %collective-permute-start.70 = (bf16[2,128,512]{2,1,0:T(8,128)(2,1)S(1)}, bf16[2,128,512]{2,1,0:T(8,128)(2,1)}, u32[]{:S(2)}, u32[]{:S(2)}) collective-permute-start(bf16[2,128,512]{2,1,0:T(8,128)(2,1)S(1)} %slice.385), channel_id=1, source_target_pairs={{0,8},{8,16},{16,24},{24,28},{28,20},{20,12},{12,4},{4,0},{1,9},{9... | collective-permute-start | bytes 786440 | tf_op jit(solution)/shard_map/ppermute | solution.py:775
  277.0 26.5 %collective-permute-start.71 = (bf16[2,128,512]{2,1,0:T(8,128)(2,1)}, bf16[2,128,512]{2,1,0:T(8,128)(2,1)}, u32[]{:S(2)}, u32[]{:S(2)}) collective-permute-start(bf16[2,128,512]{2,1,0:T(8,128)(2,1)} %slice.386), channel_id=1, source_target_pairs={{0,4},{8,0},{16,8},{24,16},{28,24},{20,28},{12,20},{4,12},{1,5},{9... | collective-permute-start | bytes 786440 | tf_op jit(solution)/shard_map/ppermute | solution.py:775
  282.2 19.2 %collective-permute-start.64 = (bf16[4,144,512]{2,1,0:T(8,128)(2,1)}, bf16[4,144,512]{2,1,0:T(8,128)(2,1)}, u32[]{:S(2)}, u32[]{:S(2)}) collective-permute-start(bf16[4,144,512]{2,1,0:T(8,128)(2,1)} %collective-permute-done.62.rest_0_), channel_id=1, source_target_pairs={{0,8},{8,16},{16,24},{24,28},{28,20},{20,12},{12,4},{4,0},{1,9},{9... | collective-permute-start | bytes 1769480 | tf_op jit(solution)/shard_map/ppermute | solution.py:775
  282.6 18.7 %collective-permute-start.65 = (bf16[4,144,512]{2,1,0:T(8,128)(2,1)}, bf16[4,144,512]{2,1,0:T(8,128)(2,1)}, u32[]{:S(2)}, u32[]{:S(2)}) collective-permute-start(bf16[4,144,512]{2,1,0:T(8,128)(2,1)} %collective-permute-done.63.rest_1_), channel_id=1, source_target_pairs={{0,4},{8,0},{16,8},{24,16},{28,24},{20,28},{12,20},{4,12},{1,5},{9... | collective-permute-start | bytes 1769480 | tf_op jit(solution)/shard_map/ppermute | solution.py:775
  332.8 45.3 %collective-permute-start.74 = (bf16[4,2,512,256]{3,2,1,0:T(8,128)(2,1)}, bf16[4,2,512,256]{3,2,1,0:T(8,128)(2,1)S(1)}, u32[]{:S(2)}, u32[]{:S(2)}) collective-permute-start(bf16[4,2,512,256]{3,2,1,0:T(8,128)(2,1)} %slice.389), channel_id=1, source_target_pairs={{0,4},{4,0},{8,12},{12,8},{16,20},{20,16},{24,28},{28,24},{1,5},{5... | collective-permute-start | bytes 6291464 | tf_op jit(solution)/shard_map/ppermute | solution.py:780
  381.6 47.5 %collective-permute-start.75 = (bf16[2,512,256]{2,1,0:T(8,128)(2,1)S(1)}, bf16[2,512,256]{2,1,0:T(8,128)(2,1)S(1)}, u32[]{:S(2)}, u32[]{:S(2)}) collective-permute-start(bf16[2,512,256]{2,1,0:T(8,128)(2,1)S(1)} %get-tuple-element.352), channel_id=1, source_target_pairs={{0,8},{4,12},{8,16},{12,20},{16,24},{20,28},{24,0},{28,4},{1,9},{5... | collective-permute-start | bytes 1572872 | tf_op jit(solution)/shard_map/ppermute | solution.py:785
  383.0 46.1 %collective-permute-start.76 = (bf16[2,512,256]{2,1,0:T(8,128)(2,1)S(1)}, bf16[2,512,256]{2,1,0:T(8,128)(2,1)S(1)}, u32[]{:S(2)}, u32[]{:S(2)}) collective-permute-start(bf16[2,512,256]{2,1,0:T(8,128)(2,1)S(1)} %get-tuple-element.351), channel_id=1, source_target_pairs={{0,16},{4,20},{8,24},{12,28},{16,0},{20,4},{24,8},{28,12},{1,17},{... | collective-permute-start | bytes 1572872 | tf_op jit(solution)/shard_map/ppermute | solution.py:785
  383.6 45.6 %collective-permute-start.77 = (bf16[2,512,256]{2,1,0:T(8,128)(2,1)S(1)}, bf16[2,512,256]{2,1,0:T(8,128)(2,1)S(1)}, u32[]{:S(2)}, u32[]{:S(2)}) collective-permute-start(bf16[2,512,256]{2,1,0:T(8,128)(2,1)S(1)} %get-tuple-element.350), channel_id=1, source_target_pairs={{0,24},{4,28},{8,0},{12,4},{16,8},{20,12},{24,16},{28,20},{1,25},{... | collective-permute-start | bytes 1572872 | tf_op jit(solution)/shard_map/ppermute | solution.py:785
  436.5 16.2 %collective-permute-start.79 = (bf16[4,2,16,2176]{3,2,1,0:T(8,128)(2,1)S(1)}, bf16[4,2,16,2176]{3,2,1,0:T(8,128)(2,1)S(1)}, u32[]{:S(2)}, u32[]{:S(2)}) collective-permute-start(bf16[4,2,16,2176]{3,2,1,0:T(8,128)(2,1)S(1)} %select_bitcast_fusion.3), channel_id=1, source_target_pairs={{0,2},{1,3},{2,0},{3,1},{4,6},{5,7},{6,4},{7,5},{8,10},{9,11},{10,... | collective-permute-start | bytes 1671176 | tf_op jit(solution)/shard_map/ppermute | solution.py:780
  (102 other events, 1344.5 us)

commit v8 on v6

--- a/solution.py
+++ b/solution.py
@@ -213,7 +213,7 @@
         ),
         out_shape=jax.ShapeDtypeStruct(joined.shape, BF16),
         input_output_aliases={7: 0} if aliased else {},
-        compiler_params=pltpu.CompilerParams(vmem_limit_bytes=48 << 20),
+        compiler_params=pltpu.CompilerParams(vmem_limit_bytes=58 << 20),
         cost_estimate=pl.CostEstimate(
             flops=row_to * length * 400 * 8 * 256 * 20 if aliased else rows,
             bytes_accessed=rows * length,
@@ -1042,7 +1042,7 @@
             if step == 1:
                 second.after(*groups[2].values())
         if first.left():
-            found, work = first.step(*work)
+            found, _ = first.step()
             groups.append(found)
         if second.left() and step > 0:
             found, work = second.step(*work)

time: 481 us -> 479 us (level)
    unnamed x97 -> x91, local copies, waits for them, and re-layouts: 13.5 us -> 12.6 us
  transfers between devices with their start and end apart: 84 -> 84, of which waited for: 49 -> 48; matrix products, arithmetic and copies ran while one was open for 5% -> 5% of each run, Pallas kernels for 48% -> 48%
where the time goes in v8:
time: 479 us; the launch traced here: 470 us
  Pallas kernels  226 us (47%)
  waiting for transfers between devices  98.3 us (21%)
  starting transfers between devices  94.9 us (20%)
  local copies, waits for them, and re-layouts  27.8 us (6%)
  other arithmetic  17.9 us (4%)
    ppermute x52, starting transfers between devices, shift(): lax.ppermute(value, 'dp', [(order[i], order[(i + step) % count]) for i in...  54.6 us
    pallas_call x2, Pallas kernels, attn_bwd(): pl.pallas_call(functools.partial(attn_bwd_kernel, width, row_from, batch,...  48.7 us
    pallas_call x5, Pallas kernels, pull_slots(): pl.pallas_call(functools.partial(pull_kernel, held is None, len(parts)),...  47.6 us
    ppermute x52, waiting for transfers between devices, shift(): lax.ppermute(value, 'dp', [(order[i], order[(i + step) % count]) for i in...  46.2 us
    ppermute x20, waiting for transfers between devices, flip(): return lax.ppermute(value, axis, [(i, i ^ bit) for i in range(count)])  45.8 us
    pallas_call x1, Pallas kernels, attn_fwd(): pl.pallas_call(functools.partial(attn_fwd_kernel, width, batch, count), g...  27 us
    pallas_call x5, Pallas kernels, spread_tokens(): pl.pallas_call(functools.partial(spread_kernel, group, len(parts)), grid_...  26.5 us
    ppermute x20, starting transfers between devices, flip(): return lax.ppermute(value, axis, [(i, i ^ bit) for i in range(count)])  20.4 us
  transfers between devices with their start and end apart: 84, of which 48 were waited for; matrix products, arithmetic and copies ran while one was open for 5% of the time, Pallas kernels for 48%

profile of v8, /device:TPU:0, one launch (start us, length us, event | category | flops | bytes accessed | tf_op | source)
XLA Modules:
  0.0 470.1 jit_solution(13777295398685768175)
XLA Ops:
  2.4 5.0 %collective-permute-start = (bf16[16,2176]{1,0:T(8,128)(2,1)S(1)}, bf16[16,2176]{1,0:T(8,128)(2,1)S(1)}, u32[]{:S(2)}, u32[]{:S(2)}) collective-permute-start(bf16[16,2176]{1,0:T(8,128)(2,1)S(1)} %fusion.40), channel_id=1, source_target_pairs={{0,24},{4,28},{8,0},{12,4},{16,8},{20,12},{24,16},{28,20},{1,25},{... | collective-permute-start | bytes 208904 | tf_op jit(solution)/shard_map/ppermute | solution.py:785
  15.8 7.0 %collective-permute-done.3 = bf16[4,16,2176]{2,1,0:T(8,128)(2,1)S(1)} collective-permute-done((bf16[4,16,2176]{2,1,0:T(8,128)(2,1)S(1)}, bf16[4,16,2176]{2,1,0:T(8,128)(2,1)S(1)}, u32[]{:S(2)}, u32[]{:S(2)}) %collective-permute-start.3) | collective-permute-done | bytes 278560 | tf_op jit(solution)/shard_map/ppermute | solution.py:780
  26.8 9.8 %collective-permute-done.4 = bf16[8,1,16,2176]{3,2,0,1:T(8,128)(2,1)S(1)} collective-permute-done((bf16[8,1,16,2176]{3,2,0,1:T(8,128)(2,1)S(1)}, bf16[8,1,16,2176]{3,2,0,1:T(8,128)(2,1)S(1)}, u32[]{:S(2)}, u32[]{:S(2)}) %collective-permute-start.4) | collective-permute-done | bytes 557088 | tf_op jit(solution)/shard_map/ppermute | solution.py:780
  46.0 10.1 %join.1.joined_ref = bf16[4,1024,1536]{2,1,0:T(8,128)(2,1)} custom-call(bf16[4,1024,512]{2,1,0:T(8,128)(2,1)S(1)} %bitcast.382, f32[8,512]{1,0:T(8,128)S(1)} %copy.150.gains_ref, bf16[512,2176]{1,0:T(8,128)(2,1)S(1)} %bitcast.356), custom_call_target="tpu_custom_call" | custom-call | flops 6442450944 | bytes 16777216 | tf_op jit(solution)/shard_map/join/pallas_call | solution.py:261
  58.2 27.0 %attend.1 = (bf16[4,1024,512]{2,1,0:T(8,128)(2,1)S(1)}, f32[4,8,8,128]{3,2,1,0:T(8,128)S(1)}) custom-call(s32[4,8]{1,0:T(4,128)S(1)} %add_select_fusion.lo_ref, s32[4]{0:T(128)S(1)} %subtract_bitcast_fusion.vlen_ref, s32[4,8,128]{2,1,0:T(8,128)S(1)} %select_select_fusion.start_ref, bf16[4,1024,1536]{2,1,0:T(8,128)(2,1)} %join.1.joined_ref), custom_call_target="tpu_custom_call" | custom-call | flops 13421772800 | bytes 12582912 | tf_op jit(solution)/shard_map/attend/pallas_call | solution.py:100
  88.5 7.5 %mix.1 = (f32[4,1024,512]{2,1,0:T(8,128)}, bf16[4,1024,512]{2,1,0:T(8,128)(2,1)S(1)}, f32[4,16,1024]{2,1,0:T(8,128)S(1)}) custom-call(bf16[4,1024,512]{2,1,0:T(8,128)(2,1)S(1)} %get-tuple-element.138.attended_ref, bf16[4,1024,512]{2,1,0:T(8,128)(2,1)} %bitcast.379, f32[8,512]{1,0:T(8,128)S(1)} %copy.150.gains_ref, bf16[512,2176]{1,0:T(8,128)(2,1)S(1)} %bitcast.357, ...), custom_call_target="tpu_custom_call" | custom-call | flops 2147483648 | bytes 20971520 | tf_op jit(solution)/shard_map/mix/pallas_call | solution.py:291
  115.9 4.4 pool.2
  122.4 4.6 pool.3
  203.0 7.8 %experts.1 = (bf16[4,128,512]{2,1,0:T(8,128)(2,1)S(1)}, bf16[8,512,256]{2,1,0:T(8,128)(2,1)S(1)}, f32[8,512,256]{2,1,0:T(8,128)S(1)}) custom-call(bf16[4,128,512]{2,1,0:T(8,128)(2,1)S(1)} %pad_maximum_fusion.4.pooled_ref, bf16[8,2,512,256]{3,2,1,0:T(8,128)(2,1)S(1)} %bitcast_dynamic-update-slice_fusion.weights_ref), custom_call_target="tpu_custom_call" | custom-call | flops 4294967296 | bytes 8388608 | tf_op jit(solution)/shard_map/experts/pallas_call | solution.py:389
  224.7 11.2 %pull_experts.1 = (bf16[4,144,512]{2,1,0:T(8,128)(2,1)S(1)}, bf16[8,2,512,256]{3,2,1,0:T(8,128)(2,1)S(1)}) custom-call(s32[8]{0:T(128)S(1)} %get-tuple-element.391.slots_ref, bf16[4,128,512]{2,1,0:T(8,128)(2,1)S(1)} %pad_maximum_fusion.4.pooled_ref, bf16[4,128,512]{2,1,0:T(8,128)(2,1)S(1)} %pad_maximum_fusion.5.grads_ref, ...), custom_call_target="tpu_custom_call" | custom-call | flops 6442450944 | bytes 8388608 | tf_op jit(solution)/shard_map/pull_experts/pallas_call | solution.py:454
  260.5 7.2 %pull_slots.5 = (f32[4,1024,512]{2,1,0:T(8,128)}, bf16[4,1024,512]{2,1,0:T(8,128)(2,1)}, f32[4,512]{1,0:T(4,128)}, f32[512,512]{1,0:T(8,128)}, f32[8,512]{1,0:T(8,128)}) custom-call(s32[8]{0:T(128)} %copy-done.13, f32[1024,16]{1,0:T(8,128)} %bitcast.368, f32[1,128,16]{2,1,0:T(8,128)} %get-tuple-element.165.change_ref, bf16[4,1024,512]{2,1,0:T(8,128)(2,1)} %copy-done.2, ...), custom_call_target="tpu_custom_call" | custom-call | flops 2684354560 | bytes 10240 | tf_op jit(solution)/shard_map/pull_slots/pallas_call | solution.py:648
  267.8 6.1 %spread.6 = (bf16[4,1024,512]{2,1,0:T(8,128)(2,1)}, f32[2,128,16]{2,1,0:T(8,128)}) custom-call(s32[8]{0:T(128)} %copy-done.13, f32[1024,16]{1,0:T(8,128)} %bitcast.369, bf16[4,1024,512]{2,1,0:T(8,128)(2,1)} %bitcast.346, f32[4,1024,512]{2,1,0:T(8,128)} %get-tuple-element.162.hidden_ref, ...), custom_call_target="tpu_custom_call", output_to_operand_aliasing={{0}: (6, {})} | custom-call | flops 2621440000 | bytes 2621440 | tf_op jit(solution)/shard_map/spread/pallas_call | solution.py:525
  283.1 11.0 %pull_slots.6 = (f32[4,1024,512]{2,1,0:T(8,128)}, bf16[4,1024,512]{2,1,0:T(8,128)(2,1)}, f32[4,512]{1,0:T(4,128)}, f32[512,512]{1,0:T(8,128)}, f32[8,512]{1,0:T(8,128)}) custom-call(s32[8]{0:T(128)} %copy-done.13, f32[1024,16]{1,0:T(8,128)} %bitcast.370, ...), custom_call_target="tpu_custom_call", output_to_operand_aliasing={{0}: (12, {}), {1}: (13, {})} | custom-call | flops 5368709120 | bytes 10240 | tf_op jit(solution)/shard_map/pull_slots/pallas_call | solution.py:648
  294.1 6.1 %spread.7 = (bf16[4,1024,512]{2,1,0:T(8,128)(2,1)}, f32[2,128,16]{2,1,0:T(8,128)}) custom-call(s32[8]{0:T(128)} %copy-done.13, f32[1024,16]{1,0:T(8,128)} %bitcast.371, bf16[4,1024,512]{2,1,0:T(8,128)(2,1)} %bitcast.348, f32[4,1024,512]{2,1,0:T(8,128)} %get-tuple-element.162.hidden_ref, ...), custom_call_target="tpu_custom_call", output_to_operand_aliasing={{0}: (6, {})} | custom-call | flops 2621440000 | bytes 2621440 | tf_op jit(solution)/shard_map/spread/pallas_call | solution.py:525
  304.3 6.1 %spread.8 = (bf16[4,1024,512]{2,1,0:T(8,128)(2,1)}, f32[2,128,16]{2,1,0:T(8,128)}) custom-call(s32[8]{0:T(128)} %copy-done.13, f32[1024,16]{1,0:T(8,128)} %bitcast.372, bf16[4,1024,512]{2,1,0:T(8,128)(2,1)} %bitcast.349, f32[4,1024,512]{2,1,0:T(8,128)} %get-tuple-element.162.hidden_ref, ...), custom_call_target="tpu_custom_call", output_to_operand_aliasing={{0}: (6, {})} | custom-call | flops 2621440000 | bytes 2621440 | tf_op jit(solution)/shard_map/spread/pallas_call | solution.py:525
  310.4 4.2 spread.9
  318.1 10.9 %pull_slots.7 = (f32[4,1024,512]{2,1,0:T(8,128)}, bf16[4,1024,512]{2,1,0:T(8,128)(2,1)}, f32[4,512]{1,0:T(4,128)}, f32[512,512]{1,0:T(8,128)}, f32[8,512]{1,0:T(8,128)}) custom-call(s32[8]{0:T(128)} %copy-done.13, f32[1024,16]{1,0:T(8,128)} %bitcast.374, ...), custom_call_target="tpu_custom_call", output_to_operand_aliasing={{0}: (12, {}), {1}: (13, {})} | custom-call | flops 5368709120 | bytes 10240 | tf_op jit(solution)/shard_map/pull_slots/pallas_call | solution.py:648
  332.2 11.0 %pull_slots.8 = (f32[4,1024,512]{2,1,0:T(8,128)}, bf16[4,1024,512]{2,1,0:T(8,128)(2,1)}, f32[4,512]{1,0:T(4,128)}, f32[512,512]{1,0:T(8,128)}, f32[8,512]{1,0:T(8,128)}) custom-call(s32[8]{0:T(128)} %copy-done.13, f32[1024,16]{1,0:T(8,128)} %bitcast.375, ...), custom_call_target="tpu_custom_call", output_to_operand_aliasing={{0}: (12, {}), {1}: (13, {})} | custom-call | flops 5368709120 | bytes 10240 | tf_op jit(solution)/shard_map/pull_slots/pallas_call | solution.py:648
  343.2 7.5 %pull_slots.9 = (f32[4,1024,512]{2,1,0:T(8,128)}, bf16[4,1024,512]{2,1,0:T(8,128)(2,1)}, f32[4,512]{1,0:T(4,128)}, f32[512,512]{1,0:T(8,128)}, f32[8,512]{1,0:T(8,128)}) custom-call(s32[8]{0:T(128)} %copy-done.13, f32[1024,16]{1,0:T(8,128)} %bitcast.376, ...), custom_call_target="tpu_custom_call", output_to_operand_aliasing={{0}: (11, {}), {1}: (12, {})} | custom-call | tf_op jit(solution)/shard_map/pull_slots/pallas_call | solution.py:648
  350.7 25.6 %attend_back.2.rest_0_ = bf16[4,1024,1536]{2,1,0:T(8,128)(2,1)} custom-call(s32[4,8]{1,0:T(4,128)} %copy-done.16, s32[4]{0:T(128)} %copy-done.17, s32[4,8,128]{2,1,0:T(8,128)} %copy-done.11, bf16[4,1024,1536]{2,1,0:T(8,128)(2,1)} %join.1.joined_ref, bf16[4,1024,512]{2,1,0:T(8,128)(2,1)} %get-tuple-element.223.grad_ref, bf16[4,1024,512]{2,1,0:T(8,128)(2,1)} %copy-done.1, ...), custom_call_target="tpu_custom_call" | custom-call | flops 4 | bytes 4096 | tf_op jit(solution)/shard_map/attend_back/pallas_call | solution.py:194
  384.7 23.1 %attend_back.3.grads_ref = bf16[4,1024,1536]{2,1,0:T(8,128)(2,1)} custom-call(s32[4,8]{1,0:T(4,128)} %copy-done.16, s32[4]{0:T(128)} %copy-done.17, s32[4,8,128]{2,1,0:T(8,128)} %copy-done.11, bf16[4,1024,1536]{2,1,0:T(8,128)(2,1)} %join.1.joined_ref, bf16[4,1024,512]{2,1,0:T(8,128)(2,1)} %get-tuple-element.223.grad_ref, ...), custom_call_target="tpu_custom_call", output_to_operand_aliasing={{}: (7, {})} | custom-call | flops 67108864000 | bytes 4096 | tf_op jit(solution)/shard_map/attend_back/pallas_call | solution.py:194
  409.0 14.8 %project_grads.1 = bf16[512,2176]{1,0:T(8,128)(2,1)S(1)} custom-call(bf16[4,1024,1536]{2,1,0:T(8,128)(2,1)} %attend_back.3.grads_ref, bf16[4,1024,512]{2,1,0:T(8,128)(2,1)} %bitcast.380, f32[512,8]{1,0:T(8,128)S(1)} %get-tuple-element.378.gains_ref, bf16[512,2176]{1,0:T(8,128)(2,1)S(1)} %bitcast.364, f32[512,512]{1,0:T(8,128)S(1)} %copy-done.9, ...), custom_call_target="tpu_custom_call" | custom-call | flops 4 | bytes 4 | tf_op jit(solution)/shard_map/project_grads/pallas_call | solution.py:708
  432.9 16.1 %pull_tokens.1 = f32[4,1024,512]{2,1,0:T(8,128)} custom-call(bf16[4,1024,1536]{2,1,0:T(8,128)(2,1)} %attend_back.3.grads_ref, bf16[4,1024,512]{2,1,0:T(8,128)(2,1)} %bitcast.381, f32[4,1024,512]{2,1,0:T(8,128)} %get-tuple-element.233.hidden_ref, f32[8,512]{1,0:T(8,128)} %copy-done.10, bf16[512,2176]{1,0:T(8,128)(2,1)} %bitcast.363), custom_call_target="tpu_custom_call" | custom-call | flops 21474836480 | bytes 33554432 | tf_op jit(solution)/shard_map/pull_tokens/pallas_call | solution.py:740
  450.3 7.4 %collective-permute-done.80 = bf16[4,16,2176]{2,1,0:T(8,128)(2,1)S(1)} collective-permute-done((bf16[4,16,2176]{2,1,0:T(8,128)(2,1)S(1)}, bf16[4,16,2176]{2,1,0:T(8,128)(2,1)S(1)}, u32[]{:S(2)}, u32[]{:S(2)}) %collective-permute-start.80) | collective-permute-done | bytes 278560 | tf_op jit(solution)/shard_map/ppermute | solution.py:780
  (361 shorter events, 213.8 us)
Async XLA Ops:
  41.3 14.8 %collective-permute-start.6 = (bf16[2,512,256]{2,1,0:T(8,128)(2,1)S(1)}, bf16[2,512,256]{2,1,0:T(8,128)(2,1)}, u32[]{:S(2)}, u32[]{:S(2)}) collective-permute-start(bf16[2,512,256]{2,1,0:T(8,128)(2,1)S(1)} %pad_maximum_fusion.3), channel_id=1, source_target_pairs={{0,8},{8,16},{16,24},{24,28},{28,20},{20,12},{12,4},{4,0},{1,9},{9... | collective-permute-start | bytes 1572872 | tf_op jit(solution)/shard_map/ppermute | solution.py:775
  41.3 14.8 %collective-permute-start.7 = (bf16[2,512,256]{2,1,0:T(8,128)(2,1)S(1)}, bf16[2,512,256]{2,1,0:T(8,128)(2,1)}, u32[]{:S(2)}, u32[]{:S(2)}) collective-permute-start(bf16[2,512,256]{2,1,0:T(8,128)(2,1)S(1)} %pad_maximum_fusion.3), channel_id=1, source_target_pairs={{0,4},{8,0},{16,8},{24,16},{28,24},{20,28},{12,20},{4,12},{1,5},{9... | collective-permute-start | bytes 1572872 | tf_op jit(solution)/shard_map/ppermute | solution.py:775
  56.1 29.1 %collective-permute-start.8 = (bf16[2,512,256]{2,1,0:T(8,128)(2,1)}, bf16[2,512,256]{2,1,0:T(8,128)(2,1)S(1)}, u32[]{:S(2)}, u32[]{:S(2)}) collective-permute-start(bf16[2,512,256]{2,1,0:T(8,128)(2,1)} %collective-permute-done.6), channel_id=1, source_target_pairs={{0,8},{8,16},{16,24},{24,28},{28,20},{20,12},{12,4},{4,0},{1,9},{9... | collective-permute-start | bytes 1572872 | tf_op jit(solution)/shard_map/ppermute | solution.py:775
  56.3 28.9 %collective-permute-start.9 = (bf16[2,512,256]{2,1,0:T(8,128)(2,1)}, bf16[2,512,256]{2,1,0:T(8,128)(2,1)S(1)}, u32[]{:S(2)}, u32[]{:S(2)}) collective-permute-start(bf16[2,512,256]{2,1,0:T(8,128)(2,1)} %collective-permute-done.7), channel_id=1, source_target_pairs={{0,4},{8,0},{16,8},{24,16},{28,24},{20,28},{12,20},{4,12},{1,5},{9... | collective-permute-start | bytes 1572872 | tf_op jit(solution)/shard_map/ppermute | solution.py:775
  100.7 19.6 %collective-permute-start.12 = (bf16[1,512,256]{2,1,0:T(8,128)(2,1)S(1)}, bf16[1,512,256]{2,1,0:T(8,128)(2,1)S(1)}, u32[]{:S(2)}, u32[]{:S(2)}) collective-permute-start(bf16[1,512,256]{2,1,0:T(8,128)(2,1)S(1)} %slice.330), channel_id=1, source_target_pairs={{0,8},{8,16},{16,24},{24,28},{28,20},{20,12},{12,4},{4,0},{1,9},{9... | collective-permute-start | bytes 786440 | tf_op jit(solution)/shard_map/ppermute | solution.py:775
  101.5 18.8 %collective-permute-start.13 = (bf16[1,512,256]{2,1,0:T(8,128)(2,1)S(1)}, bf16[1,512,256]{2,1,0:T(8,128)(2,1)S(1)}, u32[]{:S(2)}, u32[]{:S(2)}) collective-permute-start(bf16[1,512,256]{2,1,0:T(8,128)(2,1)S(1)} %slice.331), channel_id=1, source_target_pairs={{0,4},{8,0},{16,8},{24,16},{28,24},{20,28},{12,20},{4,12},{1,5},{9... | collective-permute-start | bytes 786440 | tf_op jit(solution)/shard_map/ppermute | solution.py:775
  197.5 15.6 %collective-permute-start.41 = (bf16[2,128,512]{2,1,0:T(8,128)(2,1)S(1)}, bf16[2,128,512]{2,1,0:T(8,128)(2,1)S(1)}, u32[]{:S(2)}, u32[]{:S(2)}) collective-permute-start(bf16[2,128,512]{2,1,0:T(8,128)(2,1)S(1)} %get-tuple-element.318), channel_id=1, source_target_pairs={{0,8},{8,16},{16,24},{24,28},{28,20},{20,12},{12,4},{4,0},{1,9},{9... | collective-permute-start | bytes 786440 | tf_op jit(solution)/shard_map/ppermute | solution.py:775
  219.8 16.1 %collective-permute-start.58 = (bf16[4,128,512]{2,1,0:T(8,128)(2,1)S(1)}, bf16[4,128,512]{2,1,0:T(8,128)(2,1)S(1)}, u32[]{:S(2)}, u32[]{:S(2)}) collective-permute-start(bf16[4,128,512]{2,1,0:T(8,128)(2,1)S(1)} %pad_maximum_fusion.6.rest_0_), channel_id=1, source_target_pairs={{0,8},{8,16},{16,24},{24,28},{28,20},{20,12},{12,4},{4,0},{1,9},{9... | collective-permute-start | bytes 1572872 | tf_op jit(solution)/shard_map/ppermute | solution.py:775
  221.3 14.7 %collective-permute-start.59 = (bf16[4,128,512]{2,1,0:T(8,128)(2,1)S(1)}, bf16[4,128,512]{2,1,0:T(8,128)(2,1)S(1)}, u32[]{:S(2)}, u32[]{:S(2)}) collective-permute-start(bf16[4,128,512]{2,1,0:T(8,128)(2,1)S(1)} %pad_maximum_fusion.6.rest_0_), channel_id=1, source_target_pairs={{0,4},{8,0},{16,8},{24,16},{28,24},{20,28},{12,20},{4,12},{1,5},{9... | collective-permute-start | bytes 1572872 | tf_op jit(solution)/shard_map/ppermute | solution.py:775
  236.0 14.8 %collective-permute-start.60 = (bf16[4,128,512]{2,1,0:T(8,128)(2,1)S(1)}, bf16[4,128,512]{2,1,0:T(8,128)(2,1)}, u32[]{:S(2)}, u32[]{:S(2)}) collective-permute-start(bf16[4,128,512]{2,1,0:T(8,128)(2,1)S(1)} %collective-permute-done.58.rest_0_), channel_id=1, source_target_pairs={{0,8},{8,16},{16,24},{24,28},{28,20},{20,12},{12,4},{4,0},{1,9},{9... | collective-permute-start | bytes 1572872 | tf_op jit(solution)/shard_map/ppermute | solution.py:775
  237.4 14.5 %collective-permute-start.61 = (bf16[4,128,512]{2,1,0:T(8,128)(2,1)S(1)}, bf16[4,128,512]{2,1,0:T(8,128)(2,1)}, u32[]{:S(2)}, u32[]{:S(2)}) collective-permute-start(bf16[4,128,512]{2,1,0:T(8,128)(2,1)S(1)} %collective-permute-done.59.rest_1_), channel_id=1, source_target_pairs={{0,4},{8,0},{16,8},{24,16},{28,24},{20,28},{12,20},{4,12},{1,5},{9... | collective-permute-start | bytes 1572872 | tf_op jit(solution)/shard_map/ppermute | solution.py:775
  251.9 21.9 %collective-permute-start.68 = (bf16[4,128,512]{2,1,0:T(8,128)(2,1)}, bf16[4,128,512]{2,1,0:T(8,128)(2,1)S(1)}, u32[]{:S(2)}, u32[]{:S(2)}) collective-permute-start(bf16[4,128,512]{2,1,0:T(8,128)(2,1)} %collective-permute-done.60.rest_0_), channel_id=1, source_target_pairs={{0,8},{8,16},{16,24},{24,28},{28,20},{20,12},{12,4},{4,0},{1,9},{9... | collective-permute-start | bytes 1572872 | tf_op jit(solution)/shard_map/ppermute | solution.py:775
  253.4 20.4 %collective-permute-start.69 = (bf16[4,128,512]{2,1,0:T(8,128)(2,1)}, bf16[4,128,512]{2,1,0:T(8,128)(2,1)}, u32[]{:S(2)}, u32[]{:S(2)}) collective-permute-start(bf16[4,128,512]{2,1,0:T(8,128)(2,1)} %collective-permute-done.61.rest_1_), channel_id=1, source_target_pairs={{0,4},{8,0},{16,8},{24,16},{28,24},{20,28},{12,20},{4,12},{1,5},{9... | collective-permute-start | bytes 1572872 | tf_op jit(solution)/shard_map/ppermute | solution.py:775
  253.9 25.7 %collective-permute-start.62 = (bf16[4,144,512]{2,1,0:T(8,128)(2,1)S(1)}, bf16[4,144,512]{2,1,0:T(8,128)(2,1)}, u32[]{:S(2)}, u32[]{:S(2)}) collective-permute-start(bf16[4,144,512]{2,1,0:T(8,128)(2,1)S(1)} %pad_maximum_fusion.1.rest_0_), channel_id=1, source_target_pairs={{0,8},{8,16},{16,24},{24,28},{28,20},{20,12},{12,4},{4,0},{1,9},{9... | collective-permute-start | bytes 1769480 | tf_op jit(solution)/shard_map/ppermute | solution.py:775
  255.4 25.6 %collective-permute-start.63 = (bf16[4,144,512]{2,1,0:T(8,128)(2,1)S(1)}, bf16[4,144,512]{2,1,0:T(8,128)(2,1)}, u32[]{:S(2)}, u32[]{:S(2)}) collective-permute-start(bf16[4,144,512]{2,1,0:T(8,128)(2,1)S(1)} %pad_maximum_fusion.1.rest_0_), channel_id=1, source_target_pairs={{0,4},{8,0},{16,8},{24,16},{28,24},{20,28},{12,20},{4,12},{1,5},{9... | collective-permute-start | bytes 1769480 | tf_op jit(solution)/shard_map/ppermute | solution.py:775
  273.9 28.6 %collective-permute-start.70 = (bf16[2,128,512]{2,1,0:T(8,128)(2,1)S(1)}, bf16[2,128,512]{2,1,0:T(8,128)(2,1)}, u32[]{:S(2)}, u32[]{:S(2)}) collective-permute-start(bf16[2,128,512]{2,1,0:T(8,128)(2,1)S(1)} %slice.385), channel_id=1, source_target_pairs={{0,8},{8,16},{16,24},{24,28},{28,20},{20,12},{12,4},{4,0},{1,9},{9... | collective-permute-start | bytes 786440 | tf_op jit(solution)/shard_map/ppermute | solution.py:775
  277.0 25.4 %collective-permute-start.71 = (bf16[2,128,512]{2,1,0:T(8,128)(2,1)}, bf16[2,128,512]{2,1,0:T(8,128)(2,1)}, u32[]{:S(2)}, u32[]{:S(2)}) collective-permute-start(bf16[2,128,512]{2,1,0:T(8,128)(2,1)} %slice.386), channel_id=1, source_target_pairs={{0,4},{8,0},{16,8},{24,16},{28,24},{20,28},{12,20},{4,12},{1,5},{9... | collective-permute-start | bytes 786440 | tf_op jit(solution)/shard_map/ppermute | solution.py:775
  281.0 19.1 %collective-permute-start.64 = (bf16[4,144,512]{2,1,0:T(8,128)(2,1)}, bf16[4,144,512]{2,1,0:T(8,128)(2,1)}, u32[]{:S(2)}, u32[]{:S(2)}) collective-permute-start(bf16[4,144,512]{2,1,0:T(8,128)(2,1)} %collective-permute-done.62.rest_0_), channel_id=1, source_target_pairs={{0,8},{8,16},{16,24},{24,28},{28,20},{20,12},{12,4},{4,0},{1,9},{9... | collective-permute-start | bytes 1769480 | tf_op jit(solution)/shard_map/ppermute | solution.py:775
  282.1 18.1 %collective-permute-start.65 = (bf16[4,144,512]{2,1,0:T(8,128)(2,1)}, bf16[4,144,512]{2,1,0:T(8,128)(2,1)}, u32[]{:S(2)}, u32[]{:S(2)}) collective-permute-start(bf16[4,144,512]{2,1,0:T(8,128)(2,1)} %collective-permute-done.63.rest_1_), channel_id=1, source_target_pairs={{0,4},{8,0},{16,8},{24,16},{28,24},{20,28},{12,20},{4,12},{1,5},{9... | collective-permute-start | bytes 1769480 | tf_op jit(solution)/shard_map/ppermute | solution.py:775
  331.6 45.8 %collective-permute-start.74 = (bf16[4,2,512,256]{3,2,1,0:T(8,128)(2,1)}, bf16[4,2,512,256]{3,2,1,0:T(8,128)(2,1)S(1)}, u32[]{:S(2)}, u32[]{:S(2)}) collective-permute-start(bf16[4,2,512,256]{3,2,1,0:T(8,128)(2,1)} %slice.389), channel_id=1, source_target_pairs={{0,4},{4,0},{8,12},{12,8},{16,20},{20,16},{24,28},{28,24},{1,5},{5... | collective-permute-start | bytes 6291464 | tf_op jit(solution)/shard_map/ppermute | solution.py:780
  380.8 43.0 %collective-permute-start.75 = (bf16[2,512,256]{2,1,0:T(8,128)(2,1)}, bf16[2,512,256]{2,1,0:T(8,128)(2,1)S(1)}, u32[]{:S(2)}, u32[]{:S(2)}) collective-permute-start(bf16[2,512,256]{2,1,0:T(8,128)(2,1)} %get-tuple-element.352), channel_id=1, source_target_pairs={{0,8},{4,12},{8,16},{12,20},{16,24},{20,28},{24,0},{28,4},{1,9},{5... | collective-permute-start | bytes 1572872 | tf_op jit(solution)/shard_map/ppermute | solution.py:785
  380.8 43.0 %collective-permute-start.76 = (bf16[2,512,256]{2,1,0:T(8,128)(2,1)}, bf16[2,512,256]{2,1,0:T(8,128)(2,1)}, u32[]{:S(2)}, u32[]{:S(2)}) collective-permute-start(bf16[2,512,256]{2,1,0:T(8,128)(2,1)} %get-tuple-element.351), channel_id=1, source_target_pairs={{0,16},{4,20},{8,24},{12,28},{16,0},{20,4},{24,8},{28,12},{1,17},{... | collective-permute-start | bytes 1572872 | tf_op jit(solution)/shard_map/ppermute | solution.py:785
  381.4 42.5 %collective-permute-start.77 = (bf16[2,512,256]{2,1,0:T(8,128)(2,1)}, bf16[2,512,256]{2,1,0:T(8,128)(2,1)}, u32[]{:S(2)}, u32[]{:S(2)}) collective-permute-start(bf16[2,512,256]{2,1,0:T(8,128)(2,1)} %get-tuple-element.350), channel_id=1, source_target_pairs={{0,24},{4,28},{8,0},{12,4},{16,8},{20,12},{24,16},{28,20},{1,25},{... | collective-permute-start | bytes 1572872 | tf_op jit(solution)/shard_map/ppermute | solution.py:785
  429.2 19.8 %collective-permute-start.79 = (bf16[4,2,16,2176]{3,2,1,0:T(8,128)(2,1)S(1)}, bf16[4,2,16,2176]{3,2,1,0:T(8,128)(2,1)S(1)}, u32[]{:S(2)}, u32[]{:S(2)}) collective-permute-start(bf16[4,2,16,2176]{3,2,1,0:T(8,128)(2,1)S(1)} %select_bitcast_fusion.3), channel_id=1, source_target_pairs={{0,2},{1,3},{2,0},{3,1},{4,6},{5,7},{6,4},{7,5},{8,10},{9,11},{10,... | collective-permute-start | bytes 1671176 | tf_op jit(solution)/shard_map/ppermute | solution.py:780
  (99 other events, 1302.4 us)
